TPU v7x, 512 devices: a whole 4x4x16 slice. The times are simulated.
512 devices in a mesh: dp: 64 (over z, x), tensor: 8 (over y, core).
Axes of the slice: x: 4, y: 4, z: 16, core: 2. Of those that a mesh axis runs over, the one named last changes fastest.
Arguments:
- states: float32 [256, 64, 128, 128], P('dp', 'tensor'), may hold values from -90 to 90
- from_shard: int32 [128], replicated, may hold values from 0 to 63, as said below
- from_slot: int32 [128], replicated, may hold values from 0 to 3
- projected: bfloat16 [3, 128, 4, 8192], P(None, 'dp', None, 'tensor'), may hold values from -6 to 6
- decay_rate: float32 [64], P('tensor'), may hold values from 0.01 to 1
- norm_gain: float32 [8192], P('tensor'), may hold values from 0.5 to 1.5
Outputs:
- attended: bfloat16 [3, 128, 8192], P(None, 'dp', 'tensor')
- final_states: float32 [128, 64, 128, 128], P('dp', 'tensor')
Inputs may be any that keep to these rules, and one draw needn't show every extreme that they name: Row r belongs to dp shard r // 2. No pair (from_shard, from_slot) repeats. from_shard[r] lies within 2 shards of r // 2 along dp, counted around the cycle. At most 1 row of one shard comes from any one other shard; in every draw some shard takes 1 row from each of the two shards above it, and another takes 1 from each of the two below it.
All inputs are finite; a program needn't handle non-finite values.
Results may differ from a plain program's by a relative error of at most 0.0014.
Values sent between devices are 32-bit elements; how exact they have to be, the bound alone decides.
No kernel may reach another device: no remote copies, remote signals or barrier semaphores. Data moves between devices by JAX's collectives and lax.ppermute only.
A program may use at most 64 MiB of HBM per device.

v0:
```python
import jax
import jax.numpy as jnp
from jax import lax
from jax.sharding import PartitionSpec as P


def shifted(block, axis, distance):
    devices = range(lax.axis_size(axis))
    route = [((i - distance) % len(devices), i) for i in devices]
    return lax.ppermute(block, axis, route)


def on_device(states, from_shard, from_slot, projected, decay_rate, norm_gain):
    shards = lax.axis_size("dp")
    device = lax.axis_index("dp")
    step_count = projected.shape[0]
    live_rows = projected.shape[1]
    per_pair = live_rows // 2
    local_heads = states.shape[1]
    head_dim = states.shape[2]
    features = local_heads * head_dim * lax.axis_size("tensor")
    row_span = jnp.arange(live_rows, dtype=jnp.int32)
    highest = lax.Precision.HIGHEST

    def outgoing(stride):
        target = (device + stride) % shards
        target_root = lax.dynamic_slice_in_dim(from_shard, target * live_rows, live_rows)
        target_slots = lax.dynamic_slice_in_dim(from_slot, target * live_rows, live_rows)
        is_mine = target_root == device
        mine_rank = jnp.cumsum(is_mine.astype(jnp.int32)) - 1
        matched = is_mine[None, :] & (
            mine_rank[None, :] == jnp.arange(per_pair, dtype=jnp.int32)[:, None]
        )
        picked = jnp.sum(jnp.where(matched, target_slots[None, :], 0), axis=1)
        return jnp.take(states, picked, axis=0)

    strides = (-2, -1, 1, 2)
    received = [shifted(outgoing(stride), "dp", stride) for stride in strides]
    my_root = lax.dynamic_slice_in_dim(from_shard, device * live_rows, live_rows)
    my_slots = lax.dynamic_slice_in_dim(from_slot, device * live_rows, live_rows)
    is_local = my_root == device
    same_root = (my_root[:, None] == my_root[None, :]) & (row_span[:, None] > row_span[None, :])
    arrival_rank = jnp.sum(same_root.astype(jnp.int32), axis=1)
    distance = (device - my_root) % shards
    signed = jnp.where(distance > shards // 2, distance - shards, distance)
    column = jnp.where(signed < 0, signed + 2, signed + 1)
    position = jnp.where(is_local, row_span, live_rows + column * per_pair + arrival_rank)
    candidates = jnp.concatenate([jnp.take(states, my_slots, axis=0)] + received, axis=0)
    moved = jnp.take(candidates, position, axis=0)
    activity = projected.astype(jnp.float32)
    queries = jax.nn.silu(activity[:, :, 0]).reshape(step_count, live_rows, local_heads, head_dim)
    keys_all = jax.nn.silu(activity[:, :, 1]).reshape(step_count, live_rows, local_heads, head_dim)
    values_all = jax.nn.silu(activity[:, :, 2]).reshape(
        step_count, live_rows, local_heads, head_dim
    )
    gates = jax.nn.sigmoid(activity[:, :, 3])
    retain = jnp.exp(-decay_rate)
    running = moved
    pieces = []
    norm_terms = []
    for step_idx in range(step_count):
        running = (
            retain[None, :, None, None] * running
            + keys_all[step_idx][:, :, :, None] * values_all[step_idx][:, :, None, :]
        )
        attn_now = jnp.einsum(
            "rhi,rhij->rhj", queries[step_idx], running, precision=highest
        ).reshape(live_rows, -1)
        pieces.append(attn_now)
        norm_terms.append(lax.psum(jnp.sum(attn_now * attn_now, axis=1), "tensor"))
    attn_all = jnp.stack(pieces)
    totals = jnp.stack(norm_terms)
    scale = lax.rsqrt(totals / features + 1e-05)
    attended = (attn_all * scale[:, :, None] * norm_gain * gates).astype(jnp.bfloat16)
    return (attended, running)


def solution(mesh):
    return jax.shard_map(
        on_device,
        mesh=mesh,
        in_specs=(
            P("dp", "tensor", None, None),
            P(),
            P(),
            P(None, "dp", None, "tensor"),
            P("tensor"),
            P("tensor"),
        ),
        out_specs=(P(None, "dp", "tensor"), P("dp", "tensor", None, None)),
        check_vma=False,
    )
```

profile of v0, /device:TPU:102, one launch (start us, length us, event | category | flops | bytes accessed | tf_op | source)
XLA Modules:
  0.0 89.2 jit_solution(4015049036760988476)
XLA Ops:
  0.7 0.9 %fusion.30 = (s32[2,1]{0,1:T(1,128)S(1)}, s32[2,1]{0,1:T(1,128)S(1)}, s32[2,1]{0,1:T(1,128)S(1)}, s32[2,1]{0,1:T(1,128)S(1)}) fusion(s32[]{:T(128)S(6)} %axis_index.15, s32[128]{0:T(128)} %param.9, s32[]{:T(128)S(6)} %select_n.118, s32[]{:T(128)S(6)} %select_n.121, s32[]{:T(128)S(6)} %select_n.115, s32[]{:T(128)S(6)} %select_n.112), kind=kLoop, calls=%fused_computation.96 | loop fusion | flops 16 | bytes 84 | tf_op jit(solution)/shard_map/convert.2
  2.4 1.6 %fusion.38 = (s32[]{:T(128)}, s32[]{:T(128)}, s32[]{:T(128)}, s32[]{:T(128)}, s32[2]{0:T(128)S(1)}) fusion(s32[128]{0:T(128)} %param.10, s32[]{:T(128)S(6)} %select_n.121, s32[2,1]{0,1:T(1,128)S(1)} %reduce-window.39, s32[]{:T(128)S(6)} %axis_index.15, s32[128]{0:T(128)} %param.9, s32[]{:T(128)S(6)} %select_n.115, s32[2,1]{0,1:T(1,128)S(1)} %reduce-window.37, ...), kind=kLoop, calls=%fused_computation.105 | loop fusion | flops 44 | bytes 152 | tf_op jit(solution)/shard_map/reduce_sum | solution.py:34
  11.5 3.2 %dynamic-slice_select_fusion = (f32[1,8,128,128]{3,2,1,0:T(8,128)}, f32[1,8,128,128]{3,2,1,0:T(8,128)}, f32[1,8,128,128]{3,2,1,0:T(8,128)}, f32[1,8,128,128]{3,2,1,0:T(8,128)}) fusion(f32[4,8,128,128]{3,2,1,0:T(8,128)} %param.8, s32[]{:T(128)} %bitcast.21, pred[]{:T(512)} %bitcast.20, s32[]{:T(128)} %bitcast.11, pred[]{:T(512)} %bitcast.10, s32[]{:T(128)} %bitcast.6, ...), kind=kLoop, calls=%fused_computation.8 | loop fusion | flops 524288 | bytes 4194324 | tf_op jit(solution)/shard_map/jit(_take)/select_n | solution.py:35
  14.6 3.1 %collective-permute-start = (f32[1,8,128,128]{3,2,1,0:T(8,128)}, f32[1,8,128,128]{3,2,1,0:T(8,128)}, u32[]{:S(2)}, u32[]{:S(2)}) collective-permute-start(f32[1,8,128,128]{3,2,1,0:T(8,128)} %get-tuple-element.27), channel_id=1, source_target_pairs={{16,0},{24,8},{32,16},{40,24},{48,32},{56,40},{64,48},{72,56},{80,... | collective-permute-start | bytes 1572872 | tf_op jit(solution)/shard_map/ppermute | solution.py:10
  17.8 2.1 %collective-permute-start.1 = (f32[1,8,128,128]{3,2,1,0:T(8,128)}, f32[1,8,128,128]{3,2,1,0:T(8,128)}, u32[]{:S(2)}, u32[]{:S(2)}) collective-permute-start(f32[1,8,128,128]{3,2,1,0:T(8,128)} %get-tuple-element.26), channel_id=1, source_target_pairs={{8,0},{16,8},{24,16},{32,24},{40,32},{48,40},{56,48},{64,56},{72,6... | collective-permute-start | bytes 1572872 | tf_op jit(solution)/shard_map/ppermute | solution.py:10
  19.9 7.0 %collective-permute-start.2 = (f32[1,8,128,128]{3,2,1,0:T(8,128)}, f32[1,8,128,128]{3,2,1,0:T(8,128)}, u32[]{:S(2)}, u32[]{:S(2)}) collective-permute-start(f32[1,8,128,128]{3,2,1,0:T(8,128)} %get-tuple-element.28), channel_id=1, source_target_pairs={{504,0},{0,8},{8,16},{16,24},{24,32},{32,40},{40,48},{48,56},{56,6... | collective-permute-start | bytes 1572872 | tf_op jit(solution)/shard_map/ppermute | solution.py:10
  27.0 3.1 %collective-permute-start.3 = (f32[1,8,128,128]{3,2,1,0:T(8,128)}, f32[1,8,128,128]{3,2,1,0:T(8,128)}, u32[]{:S(2)}, u32[]{:S(2)}) collective-permute-start(f32[1,8,128,128]{3,2,1,0:T(8,128)} %get-tuple-element.25), channel_id=1, source_target_pairs={{496,0},{504,8},{0,16},{8,24},{16,32},{24,40},{32,48},{40,56},{48,... | collective-permute-start | bytes 1572872 | tf_op jit(solution)/shard_map/ppermute | solution.py:10
  30.2 0.6 gather_fusion
  30.8 0.2 fusion.27
  31.2 1.2 %select_dynamic-update-slice_fusion = f32[6,8,128,128]{3,2,1,0:T(8,128)} fusion(f32[2,8,128,128]{3,2,1,0:T(8,128)S(1)} %gather_fusion, pred[2]{0:T(512)(128)(4,1)S(1)} %get-tuple-element.23), kind=kLoop, calls=%fused_computation.5 | loop fusion | flops 262143 | bytes 2097154
  32.5 2.6 %collective-permute-done = f32[1,8,128,128]{3,2,1,0:T(8,128)} collective-permute-done((f32[1,8,128,128]{3,2,1,0:T(8,128)}, f32[1,8,128,128]{3,2,1,0:T(8,128)}, u32[]{:S(2)}, u32[]{:S(2)}) %collective-permute-start) | collective-permute-done | bytes 524320 | tf_op jit(solution)/shard_map/ppermute | solution.py:10
  35.1 1.9 %constant_dynamic-update-slice_fusion.3 = f32[6,8,128,128]{3,2,1,0:T(8,128)} fusion(f32[6,8,128,128]{3,2,1,0:T(8,128)} %select_dynamic-update-slice_fusion, f32[1,8,128,128]{3,2,1,0:T(8,128)} %collective-permute-done), kind=kLoop, calls=%fused_computation.43 | loop fusion | bytes 1048576
  37.0 8.7 %collective-permute-done.1 = f32[1,8,128,128]{3,2,1,0:T(8,128)} collective-permute-done((f32[1,8,128,128]{3,2,1,0:T(8,128)}, f32[1,8,128,128]{3,2,1,0:T(8,128)}, u32[]{:S(2)}, u32[]{:S(2)}) %collective-permute-start.1) | collective-permute-done | bytes 524320 | tf_op jit(solution)/shard_map/ppermute | solution.py:10
  45.7 1.9 %constant_dynamic-update-slice_fusion.2 = f32[6,8,128,128]{3,2,1,0:T(8,128)} fusion(f32[6,8,128,128]{3,2,1,0:T(8,128)} %constant_dynamic-update-slice_fusion.3, f32[1,8,128,128]{3,2,1,0:T(8,128)} %collective-permute-done.1), kind=kLoop, calls=%fused_computation.42 | loop fusion | bytes 1048576
  47.5 15.7 %collective-permute-done.2 = f32[1,8,128,128]{3,2,1,0:T(8,128)} collective-permute-done((f32[1,8,128,128]{3,2,1,0:T(8,128)}, f32[1,8,128,128]{3,2,1,0:T(8,128)}, u32[]{:S(2)}, u32[]{:S(2)}) %collective-permute-start.2) | collective-permute-done | bytes 524320 | tf_op jit(solution)/shard_map/ppermute | solution.py:10
  63.3 1.9 %constant_dynamic-update-slice_fusion.1 = f32[6,8,128,128]{3,2,1,0:T(8,128)} fusion(f32[6,8,128,128]{3,2,1,0:T(8,128)} %constant_dynamic-update-slice_fusion.2, f32[1,8,128,128]{3,2,1,0:T(8,128)} %collective-permute-done.2), kind=kLoop, calls=%fused_computation.41 | loop fusion | bytes 1048576
  65.1 1.9 %constant_dynamic-update-slice_fusion = f32[6,8,128,128]{3,2,1,0:T(8,128)} fusion(f32[6,8,128,128]{3,2,1,0:T(8,128)} %constant_dynamic-update-slice_fusion.1, f32[1,8,128,128]{3,2,1,0:T(8,128)} %collective-permute-done.3), kind=kLoop, calls=%fused_computation.40 | loop fusion | bytes 1048576 | tf_op jit(solution)/shard_map/concatenate | solution.py:48
  67.0 2.5 %gather_fusion.1 = f32[2,8,128,128]{3,2,1,0:T(8,128)S(1)} fusion(f32[6,8,128,128]{3,2,1,0:T(8,128)} %constant_dynamic-update-slice_fusion, s32[1024]{0:T(1024)S(1)} %pad_clamp_fusion), kind=kCustom, calls=%fused_computation.1 | custom fusion | bytes 2097160 | tf_op jit(solution)/shard_map/jit(_take)/gather | solution.py:49
  69.5 1.1 %fusion.1 = f32[2,8,1,128]{3,2,1,0:T(1,128)S(1)} fusion(f32[2,8,128,1]{2,3,1,0:T(1,128)S(1)} %bitcast.156, f32[2,8,128,128]{3,2,1,0:T(8,128)S(1)} %gather_fusion.1, f32[2,8,128]{2,1,0:T(8,128)S(1)} %bitcast.138, f32[2,8,128]{2,1,0:T(8,128)S(1)} %bitcast.141, f32[8]{0:T(128)S(1)} %negate_exponential_fusion, pred[2]{0:T(512)(128)(4,1)S(1)} %get-tuple-element.21), kind=kOutput, calls=%fused_computation.7 | convolution fusion | flops 4194304 | bytes 1081378 | tf_op jit(solution)/shard_map/rhi,rhij->rhj/dot_general | solution.py:66
  70.8 1.4 %fusion = f32[2,8,1,128]{3,2,1,0:T(1,128)S(1)} fusion(f32[2,8,128,1]{2,3,1,0:T(1,128)S(1)} %bitcast.155, f32[2,8,128,128]{3,2,1,0:T(8,128)S(1)} %gather_fusion.1, f32[2,8,128]{2,1,0:T(8,128)S(1)} %bitcast.144, f32[2,8,128]{2,1,0:T(8,128)S(1)} %bitcast.146, f32[2,8,128]{2,1,0:T(8,128)S(1)} %bitcast.139, f32[2,8,128]{2,1,0:T(8,128)S(1)} %bitcast.142, ...), kind=kOutput, calls=%fused_computation.6 | convolution fusion | flops 4980736 | bytes 1097762 | tf_op jit(solution)/shard_map/rhi,rhij->rhj/dot_general | solution.py:66
  72.3 1.0 %multiply_add_fusion = f32[2,8,128,128]{3,2,1,0:T(8,128)S(1)} fusion(f32[2,8,128,128]{3,2,1,0:T(8,128)S(1)} %gather_fusion.1, f32[2,8,128]{2,1,0:T(8,128)S(1)} %bitcast.148, f32[2,8,128]{2,1,0:T(8,128)S(1)} %bitcast.149, f32[2,8,128]{2,1,0:T(8,128)S(1)} %bitcast.145, f32[2,8,128]{2,1,0:T(8,128)S(1)} %bitcast.147, f32[2,8,128]{2,1,0:T(8,128)S(1)} %bitcast.140, ...), kind=kLoop, calls=%fused_computation.2 | loop fusion | flops 2621440 | bytes 2146338 | tf_op jit(solution)/shard_map/add | solution.py:63
  73.4 1.0 %fusion.41 = f32[2,8,1,128]{3,2,1,0:T(1,128)S(1)} fusion(f32[2,8,128,1]{2,3,1,0:T(1,128)S(1)} %bitcast.150, f32[2,8,128,128]{3,2,1,0:T(8,128)S(1)} %multiply_add_fusion), kind=kOutput, calls=%fused_computation.108 | convolution fusion | flops 3145728 | bytes 1064960 | tf_op jit(solution)/shard_map/rhi,rhij->rhj/dot_general | solution.py:66
  74.5 14.0 %all-reduce = (f32[1,2]{1,0:T(1,128)S(1)}, f32[1,2]{1,0:T(1,128)S(1)}, f32[1,2]{1,0:T(1,128)S(1)}) all-reduce(f32[1,2]{1,0:T(1,128)S(1)} %bitcast.159, f32[1,2]{1,0:T(1,128)S(1)} %bitcast.158, f32[1,2]{1,0:T(1,128)S(1)} %bitcast.157), channel_id=1, replica_groups=mesh['dp'=64,'tensor'=8] {'tensor'}, use_global_device_ids=true, to_apply=%region_14.16 | all-reduce | flops 6 | bytes 48 | tf_op jit(solution)/shard_map/psum | solution.py:70
  88.5 0.7 fusion.20
  (41 shorter events, 1.4 us)
Async XLA Ops:
  0.6 29.5 %copy-start.3 = (s32[128]{0:T(128)S(1)}, s32[128]{0:T(128)}, u32[]{:S(2)}) copy-start(s32[128]{0:T(128)} %param.10) | copy-start | bytes 1540
  0.6 29.6 %copy-start = (f32[4,8,128,128]{3,2,1,0:T(8,128)S(1)}, f32[4,8,128,128]{3,2,1,0:T(8,128)}, u32[]{:S(2)}) copy-start(f32[4,8,128,128]{3,2,1,0:T(8,128)} %param.8) | copy-start | bytes 6291460
  11.5 19.6 %copy-start.2 = (bf16[3,2,4,1024]{3,2,1,0:T(4,128)(2,1)S(1)}, bf16[3,2,4,1024]{3,2,1,0:T(4,128)(2,1)}, u32[]{:S(2)}) copy-start(bf16[3,2,4,1024]{3,2,1,0:T(4,128)(2,1)} %param.11) | copy-start | bytes 147460
  14.6 17.7 %copy-start.5 = (f32[8]{0:T(128)S(1)}, f32[8]{0:T(128)}, u32[]{:S(2)}) copy-start(f32[8]{0:T(128)} %param.12) | copy-start | bytes 100
  14.6 20.4 %collective-permute-start = (f32[1,8,128,128]{3,2,1,0:T(8,128)}, f32[1,8,128,128]{3,2,1,0:T(8,128)}, u32[]{:S(2)}, u32[]{:S(2)}) collective-permute-start(f32[1,8,128,128]{3,2,1,0:T(8,128)} %get-tuple-element.27), channel_id=1, source_target_pairs={{16,0},{24,8},{32,16},{40,24},{48,32},{56,40},{64,48},{72,56},{80,... | collective-permute-start | bytes 1572872 | tf_op jit(solution)/shard_map/ppermute | solution.py:10
  17.8 27.9 %collective-permute-start.1 = (f32[1,8,128,128]{3,2,1,0:T(8,128)}, f32[1,8,128,128]{3,2,1,0:T(8,128)}, u32[]{:S(2)}, u32[]{:S(2)}) collective-permute-start(f32[1,8,128,128]{3,2,1,0:T(8,128)} %get-tuple-element.26), channel_id=1, source_target_pairs={{8,0},{16,8},{24,16},{32,24},{40,32},{48,40},{56,48},{64,56},{72,6... | collective-permute-start | bytes 1572872 | tf_op jit(solution)/shard_map/ppermute | solution.py:10
  19.9 43.3 %collective-permute-start.2 = (f32[1,8,128,128]{3,2,1,0:T(8,128)}, f32[1,8,128,128]{3,2,1,0:T(8,128)}, u32[]{:S(2)}, u32[]{:S(2)}) collective-permute-start(f32[1,8,128,128]{3,2,1,0:T(8,128)} %get-tuple-element.28), channel_id=1, source_target_pairs={{504,0},{0,8},{8,16},{16,24},{24,32},{32,40},{40,48},{48,56},{56,6... | collective-permute-start | bytes 1572872 | tf_op jit(solution)/shard_map/ppermute | solution.py:10
  27.0 38.2 %collective-permute-start.3 = (f32[1,8,128,128]{3,2,1,0:T(8,128)}, f32[1,8,128,128]{3,2,1,0:T(8,128)}, u32[]{:S(2)}, u32[]{:S(2)}) collective-permute-start(f32[1,8,128,128]{3,2,1,0:T(8,128)} %get-tuple-element.25), channel_id=1, source_target_pairs={{496,0},{504,8},{0,16},{8,24},{16,32},{24,40},{32,48},{40,56},{48,... | collective-permute-start | bytes 1572872 | tf_op jit(solution)/shard_map/ppermute | solution.py:10
  69.5 18.9 %copy-start.4 = (f32[1024]{0:T(1024)S(1)}, f32[1024]{0:T(1024)}, u32[]{:S(2)}) copy-start(f32[1024]{0:T(1024)} %param.13) | copy-start | bytes 12292
  73.4 15.8 %copy-start.1 = (f32[2,8,128,128]{3,2,1,0:T(8,128)}, f32[2,8,128,128]{3,2,1,0:T(8,128)S(1)}, u32[]{:S(2)}) copy-start(f32[2,8,128,128]{3,2,1,0:T(8,128)S(1)} %multiply_add_fusion) | copy-start | bytes 3145732
where the time goes:
time: 89.8 us; the launch traced here: 89.2 us
  waiting for transfers between devices  27 us (30%)
  starting transfers between devices  15.4 us (17%)
  blocking collectives  14 us (16%)
  local copies, waits for them, and re-layouts  10.8 us (12%)
  other arithmetic  10 us (11%)
  between operations  8.43 us (9%)
  matrix products  3.52 us (4%)
    ppermute x4, waiting for transfers between devices, shifted(): return lax.ppermute(block, axis, route)  27 us
    ppermute x4, starting transfers between devices, shifted(): return lax.ppermute(block, axis, route)  15.4 us
    psum x1, blocking collectives, on_device(): norm_terms.append(lax.psum(jnp.sum(attn_now * attn_now, axis=1), 'tensor'))  14 us
    unnamed x24, local copies, waits for them, and re-layouts  5.73 us
    dot_general x3, matrix products, on_device(): jnp.einsum('rhi,rhij->rhj', queries[step_idx], running, precision=highest)  3.52 us
    select_n x1, other arithmetic, outgoing(): return jnp.take(states, picked, axis=0)  3.17 us
    gather x1, local copies, waits for them, and re-layouts, on_device(): moved = jnp.take(candidates, position, axis=0)  2.5 us
    concatenate x1, local copies, waits for them, and re-layouts, on_device(): jnp.concatenate([jnp.take(states, my_slots, axis=0)] + received, axis=0)  1.89 us
  transfers between devices with their start and end apart: 4, of which 3 were waited for; matrix products, arithmetic and copies ran while one was open for 9% of the time, Pallas kernels for 0%

commit v1 on v0

v1 whole, which is shorter than its diff:
```python
import functools
import jax
import jax.numpy as jnp
from jax import lax
from jax.experimental import pallas as pl
from jax.experimental.pallas import tpu as pltpu
from jax.sharding import PartitionSpec as P

EPS = 1e-05


def shifted(block, axis, distance):
    size = lax.axis_size(axis)
    route = [((i - distance) % size, i) for i in range(size)]
    return lax.ppermute(block, axis, route)


def split(x):
    high = lax.reduce_precision(x, 8, 7)
    return high.astype(jnp.bfloat16), (x - high).astype(jnp.bfloat16)


def pick_kernel(shards, live, strides, place, shard_ref, slot_ref, states, *refs):
    outs, sems = refs[:-1], refs[-1]
    device = place[0]
    copies = []
    for n, stride in enumerate(strides):
        target = lax.rem(device + stride + shards, shards)
        slot = jnp.int32(0)
        for row in range(live):
            mine = shard_ref[target * live + row] == device
            slot = jnp.where(mine, slot_ref[target * live + row], slot)
        copy = pltpu.make_async_copy(states.at[slot], outs[n], sems.at[n])
        copy.start()
        copies.append(copy)
    for copy in copies:
        copy.wait()


def pick(place, from_shard, from_slot, states, shards, live, strides):
    row = jax.ShapeDtypeStruct(states.shape[1:], states.dtype)
    smem = pl.BlockSpec(memory_space=pltpu.SMEM)
    return pl.pallas_call(
        functools.partial(pick_kernel, shards, live, strides),
        out_shape=[row] * len(strides),
        in_specs=[smem] * 3 + [pl.BlockSpec(memory_space=pltpu.HBM)],
        out_specs=[pl.BlockSpec(memory_space=pl.ANY)] * len(strides),
        scratch_shapes=[pltpu.SemaphoreType.DMA((len(strides),))],
        name="pick_rows",
    )(place, from_shard, from_slot, states)


def step_kernel(
    shards, live, strides, place, shard_ref, slot_ref, states, *refs
):
    n = len(strides)
    arrived = refs[:n]
    qs, ks, vs, base, decay, final, raw, sums, held, made, sem_in, sem_out = refs[n:]
    device = place[0]
    heads = held.shape[1]
    half = heads // 2

    def fetch(row, part):
        owner = shard_ref[device * live + row]
        slot = slot_ref[device * live + row]
        gap = lax.rem(device - owner + shards, shards)
        span = pl.ds(part * half, half)
        target = held.at[row, span]
        sem = sem_in.at[row, part]

        @pl.when(gap == 0)
        def _():
            pltpu.make_async_copy(states.at[slot, span], target, sem).start()

        for k, stride in enumerate(strides):

            @pl.when(gap == stride % shards)
            def _():
                pltpu.make_async_copy(arrived[k].at[span], target, sem).start()

    parts = [(row, part) for row in range(live) for part in range(2)]
    for row, part in parts:
        fetch(row, part)
    out_copies = []
    for row, part in parts:
        span = pl.ds(part * half, half)
        pltpu.make_async_copy(
            arrived[0].at[span], held.at[row, span], sem_in.at[row, part]
        ).wait()
        for head in range(part * half, (part + 1) * half):
            state = held[row, head]
            high = state.astype(jnp.bfloat16)
            low = (state - high.astype(jnp.float32)).astype(jnp.bfloat16)
            q = qs[row, head]
            first = jnp.dot(q, high, preferred_element_type=jnp.float32)
            second = jnp.dot(q, low, preferred_element_type=jnp.float32)
            raw[row, head] = first[:8] + first[8:] + second[:8] + base[row, head]
            outer = lax.dot_general(
                ks[row, head],
                vs[row, head],
                (((0,), (0,)), ((), ())),
                preferred_element_type=jnp.float32,
            )
            made[row, head] = decay[row, head] * state + outer
        copy = pltpu.make_async_copy(
            made.at[row, span], final.at[row, span], sem_out.at[row, part]
        )
        copy.start()
        out_copies.append(copy)
    for row in range(live):
        total = raw[row, 0] * raw[row, 0]
        for head in range(1, heads):
            total = total + raw[row, head] * raw[row, head]
        sums[row] = jnp.broadcast_to(jnp.sum(total, axis=1, keepdims=True), sums.shape[1:])
    for copy in out_copies:
        copy.wait()


def run_steps(place, from_shard, from_slot, states, arrived, small, shards, live, strides):
    heads, dim = states.shape[1], states.shape[2]
    smem = pl.BlockSpec(memory_space=pltpu.SMEM)
    hbm = pl.BlockSpec(memory_space=pl.ANY)
    vmem = pl.BlockSpec(memory_space=pltpu.VMEM)
    f32 = jnp.float32
    return pl.pallas_call(
        functools.partial(step_kernel, shards, live, strides),
        out_shape=[
            jax.ShapeDtypeStruct((live, heads, dim, dim), f32),
            jax.ShapeDtypeStruct((live, heads, 8, dim), f32),
            jax.ShapeDtypeStruct((live, 8, dim), f32),
        ],
        in_specs=[smem] * 3 + [pl.BlockSpec(memory_space=pltpu.HBM)] + [hbm] * len(strides) + [vmem] * len(small),
        out_specs=[hbm, vmem, vmem],
        scratch_shapes=[
            pltpu.VMEM((live, heads, dim, dim), f32),
            pltpu.VMEM((live, heads, dim, dim), f32),
            pltpu.SemaphoreType.DMA((live, 2)),
            pltpu.SemaphoreType.DMA((live, 2)),
        ],
        compiler_params=pltpu.CompilerParams(vmem_limit_bytes=16 * 1024 * 1024),
        name="decode_steps",
    )(place, from_shard, from_slot, states, *arrived, *small)


def on_device(states, from_shard, from_slot, projected, decay_rate, norm_gain):
    shards = lax.axis_size("dp")
    steps, live = projected.shape[:2]
    heads, dim = states.shape[1], states.shape[2]
    features = heads * dim * lax.axis_size("tensor")
    place = lax.axis_index("dp").astype(jnp.int32).reshape(1)
    strides = (2, -2, 1, -1)
    rows = pick(place, from_shard, from_slot, states, shards, live, strides)
    near_up, near_down = shifted(rows[0], "dp", 1), shifted(rows[1], "dp", -1)
    up, down = shifted(rows[2], "dp", 1), shifted(rows[3], "dp", -1)
    far_up, far_down = shifted(near_up, "dp", 1), shifted(near_down, "dp", -1)
    arrived = [far_up, far_down, up, down]

    activity = projected.astype(jnp.float32)
    by_head = jnp.transpose(
        activity.reshape(steps, live, 4, heads, dim), (2, 1, 3, 0, 4)
    )
    queries, keys, values = (jax.nn.silu(by_head[i]) for i in range(3))
    gates = jax.nn.sigmoid(by_head[3])
    retain = jnp.exp(-decay_rate)
    power = [jnp.ones_like(retain)]
    for _ in range(steps):
        power.append(power[-1] * retain)
    grown = queries * jnp.stack(power[1:], axis=1)[None, :, :, None]
    faded = keys * jnp.stack(power[steps - 1 :: -1], axis=1)[None, :, :, None]
    base = []
    for t in range(steps):
        total = 0.0
        for u in range(t + 1):
            match = jnp.sum(queries[:, :, t] * keys[:, :, u], axis=-1, keepdims=True)
            total = total + power[t - u][None, :, None] * match * values[:, :, u]
        base.append(total)

    def rows_of(parts, count):
        whole = jnp.concatenate(parts, axis=2)
        return jnp.pad(whole, ((0, 0), (0, 0), (0, count - whole.shape[2]), (0, 0)))

    q_high, q_low = split(grown)
    k_high, k_low = split(faded)
    v_high, v_low = split(values)
    small = [
        jnp.concatenate([rows_of([q_high], 8), rows_of([q_low], 8)], axis=2),
        rows_of([k_high, k_low, k_high], 16),
        rows_of([v_high, v_high, v_low], 16),
        rows_of([jnp.stack(base, axis=2)], 8),
        jnp.broadcast_to(power[steps][None, :, None, None], (live, heads, 1, dim)),
    ]
    final, raw, sums = run_steps(
        place, from_shard, from_slot, states, arrived, small, shards, live, strides
    )
    group = lax.axis_size("tensor")
    mine = sums[:, :steps, 0].reshape(1, live * steps)
    mine = jnp.pad(mine, ((0, 0), (0, dim - live * steps)))
    everyone = lax.all_to_all(
        jnp.broadcast_to(mine[None], (group, 1, dim)), "tensor", 0, 0
    )
    totals = jnp.sum(everyone, axis=0)[0, : live * steps].reshape(live, 1, steps, 1)
    scale = lax.rsqrt(totals / features + EPS)
    gain = norm_gain.reshape(1, heads, 1, dim)
    attended = raw[:, :, :steps] * scale * gain * gates
    attended = jnp.transpose(attended, (2, 0, 1, 3)).reshape(steps, live, heads * dim)
    return attended.astype(jnp.bfloat16), final


def solution(mesh):
    return jax.shard_map(
        on_device,
        mesh=mesh,
        in_specs=(
            P("dp", "tensor", None, None),
            P(),
            P(),
            P(None, "dp", None, "tensor"),
            P("tensor"),
            P("tensor"),
        ),
        out_specs=(P(None, "dp", "tensor"), P("dp", "tensor", None, None)),
        check_vma=False,
    )
```

time: 89.8 us -> 130 us (1.45)
  the two profiles are of different devices: /device:TPU:102 before, /device:TPU:1 now
where the time goes in v1:
time: 130 us
  Pallas kernels  68 us (52%)
  starting transfers between devices  33.3 us (26%)
  waiting for transfers between devices  14.8 us (11%)
  blocking collectives  10.4 us (8%)
  local copies, waits for them, and re-layouts  1.31 us (1%)
    pallas_call x1, Pallas kernels, pick(): pl.pallas_call(functools.partial(pick_kernel, shards, live, strides), out...  65.5 us
    ppermute x6, starting transfers between devices, shifted(): return lax.ppermute(block, axis, route)  33.3 us
    ppermute x6, waiting for transfers between devices, shifted(): return lax.ppermute(block, axis, route)  14.8 us
    all_to_all x1, blocking collectives, on_device(): lax.all_to_all(jnp.broadcast_to(mine[None], (group, 1, dim)), 'tensor', 0...  10.4 us
  transfers between devices with their start and end apart: 6, of which 5 were waited for; matrix products, arithmetic and copies ran while one was open for 1% of the time, Pallas kernels for 0%

profile of v1, /device:TPU:1, one launch (start us, length us, event | category | flops | bytes accessed | tf_op | source)
XLA Modules:
  0.0 129.6 jit_solution(10830125307077672024)
XLA Ops:
  0.7 65.5 %pick_rows.1 = (f32[8,128,128]{2,1,0:T(8,128)}, f32[8,128,128]{2,1,0:T(8,128)}, f32[8,128,128]{2,1,0:T(8,128)}, f32[8,128,128]{2,1,0:T(8,128)}) custom-call(s32[1]{0:T(128)} %bitcast.place, s32[128]{0:T(128)} %shard_ref.3, s32[128]{0:T(128)} %slot_ref.3, f32[4,8,128,128]{3,2,1,0:T(8,128)} %states.3), custom_call_target="tpu_custom_call" | custom-call | tf_op jit(solution)/shard_map/pick_rows/pallas_call | solution.py:43
  66.2 4.0 %collective-permute-start = (f32[8,128,128]{2,1,0:T(8,128)}, f32[8,128,128]{2,1,0:T(8,128)}, u32[]{:S(2)}, u32[]{:S(2)}) collective-permute-start(f32[8,128,128]{2,1,0:T(8,128)} %get-tuple-element.9), channel_id=1, source_target_pairs={{504,0},{0,8},{8,16},{16,24},{24,32},{32,40},{40,48},{48,56},{56,6... | collective-permute-start | bytes 1572872 | tf_op jit(solution)/shard_map/ppermute | solution.py:15
  70.1 12.1 %collective-permute-start.2 = (f32[8,128,128]{2,1,0:T(8,128)}, f32[8,128,128]{2,1,0:T(8,128)}, u32[]{:S(2)}, u32[]{:S(2)}) collective-permute-start(f32[8,128,128]{2,1,0:T(8,128)} %get-tuple-element.10), channel_id=1, source_target_pairs={{8,0},{16,8},{24,16},{32,24},{40,32},{48,40},{56,48},{64,56},{72,6... | collective-permute-start | bytes 1572872 | tf_op jit(solution)/shard_map/ppermute | solution.py:15
  82.3 1.9 %collective-permute-start.4 = (f32[8,128,128]{2,1,0:T(8,128)}, f32[8,128,128]{2,1,0:T(8,128)S(1)}, u32[]{:S(2)}, u32[]{:S(2)}) collective-permute-start(f32[8,128,128]{2,1,0:T(8,128)} %get-tuple-element.11), channel_id=1, source_target_pairs={{504,0},{0,8},{8,16},{16,24},{24,32},{32,40},{40,48},{48,56},{56,6... | collective-permute-start | bytes 1572872 | tf_op jit(solution)/shard_map/ppermute | solution.py:15
  84.2 6.7 %collective-permute-start.5 = (f32[8,128,128]{2,1,0:T(8,128)}, f32[8,128,128]{2,1,0:T(8,128)S(1)}, u32[]{:S(2)}, u32[]{:S(2)}) collective-permute-start(f32[8,128,128]{2,1,0:T(8,128)} %get-tuple-element.12), channel_id=1, source_target_pairs={{8,0},{16,8},{24,16},{32,24},{40,32},{48,40},{56,48},{64,56},{72,6... | collective-permute-start | bytes 1572872 | tf_op jit(solution)/shard_map/ppermute | solution.py:15
  91.0 0.1 copy.20
  91.1 0.1 copy.19
  91.3 0.1 reduce-precision_convert_fusion
  91.4 0.3 fusion.24
  91.8 0.2 broadcast_multiply_fusion
  92.0 0.3 collective-permute-done
  92.3 1.9 %collective-permute-start.1 = (f32[8,128,128]{2,1,0:T(8,128)}, f32[8,128,128]{2,1,0:T(8,128)S(1)}, u32[]{:S(2)}, u32[]{:S(2)}) collective-permute-start(f32[8,128,128]{2,1,0:T(8,128)} %collective-permute-done), channel_id=1, source_target_pairs={{504,0},{0,8},{8,16},{16,24},{24,32},{32,40},{40,48},{48,56},{56,6... | collective-permute-start | bytes 1572872 | tf_op jit(solution)/shard_map/ppermute | solution.py:15
  94.2 6.7 %collective-permute-start.3 = (f32[8,128,128]{2,1,0:T(8,128)}, f32[8,128,128]{2,1,0:T(8,128)S(1)}, u32[]{:S(2)}, u32[]{:S(2)}) collective-permute-start(f32[8,128,128]{2,1,0:T(8,128)} %collective-permute-done.2), channel_id=1, source_target_pairs={{8,0},{16,8},{24,16},{32,24},{40,32},{48,40},{56,48},{64,56},{72,6... | collective-permute-start | bytes 1572872 | tf_op jit(solution)/shard_map/ppermute | solution.py:15
  101.1 2.3 %collective-permute-done.4.refs_2_ = f32[8,128,128]{2,1,0:T(8,128)S(1)} collective-permute-done((f32[8,128,128]{2,1,0:T(8,128)}, f32[8,128,128]{2,1,0:T(8,128)S(1)}, u32[]{:S(2)}, u32[]{:S(2)}) %collective-permute-start.4) | collective-permute-done | bytes 524320 | tf_op jit(solution)/shard_map/ppermute | solution.py:15
  103.4 1.0 collective-permute-done.5.refs_3_
  104.4 10.3 %collective-permute-done.1.refs_0_ = f32[8,128,128]{2,1,0:T(8,128)S(1)} collective-permute-done((f32[8,128,128]{2,1,0:T(8,128)}, f32[8,128,128]{2,1,0:T(8,128)S(1)}, u32[]{:S(2)}, u32[]{:S(2)}) %collective-permute-start.1) | collective-permute-done | bytes 524320 | tf_op jit(solution)/shard_map/ppermute | solution.py:15
  114.6 1.0 collective-permute-done.3.refs_1_
  115.7 2.5 %decode_steps.1 = (f32[2,8,128,128]{3,2,1,0:T(8,128)}, f32[2,8,8,128]{3,2,1,0:T(8,128)S(1)}, f32[2,8,128]{2,1,0:T(8,128)S(1)}) custom-call(s32[1]{0:T(128)} %bitcast.place, s32[128]{0:T(128)S(1)} %copy-done.1, s32[128]{0:T(128)S(1)} %copy-done.2, f32[4,8,128,128]{3,2,1,0:T(8,128)S(1)} %copy-done, f32[8,128,128]{2,1,0:T(8,128)S(1)} %collective-permute-done.1.refs_0_, ...), custom_call_target="tpu_custom_call" | custom-call | tf_op jit(solution)/shard_map/decode_steps/pallas_call | solution.py:125
  118.2 0.1 slice_reduce_fusion
  118.3 0.1 reshape_squeeze.4
  118.4 10.4 %all_to_all.5 = f32[8,1,128]{2,1,0:T(1,128)S(1)} all-to-all(f32[8,1,128]{2,1,0:T(1,128)S(1)} %broadcast_in_dim.8), channel_id=1, replica_groups=mesh['dp'=64,'tensor'=8] {'tensor'}, dimensions={0} | all-to-all | bytes 8192 | tf_op jit(solution)/shard_map/all_to_all | solution.py:198
  128.8 0.1 rsqrt.12
  128.9 0.1 fusion.22
  129.0 0.6 convert_element_type.46
  (31 shorter events, 0.7 us)
Async XLA Ops:
  0.6 115.1 %copy-start.2 = (s32[128]{0:T(128)S(1)}, s32[128]{0:T(128)}, u32[]{:S(2)}) copy-start(s32[128]{0:T(128)} %slot_ref.3) | copy-start | bytes 1540
  0.6 115.0 %copy-start.1 = (s32[128]{0:T(128)S(1)}, s32[128]{0:T(128)}, u32[]{:S(2)}) copy-start(s32[128]{0:T(128)} %shard_ref.3) | copy-start | bytes 1540
  0.7 115.0 %copy-start = (f32[4,8,128,128]{3,2,1,0:T(8,128)S(1)}, f32[4,8,128,128]{3,2,1,0:T(8,128)}, u32[]{:S(2)}) copy-start(f32[4,8,128,128]{3,2,1,0:T(8,128)} %states.3) | copy-start | bytes 6291460
  0.7 90.2 %copy-start.5 = (f32[8]{0:T(128)S(1)}, f32[8]{0:T(128)}, u32[]{:S(2)}) copy-start(f32[8]{0:T(128)} %param.10) | copy-start | bytes 100
  0.7 90.5 %copy-start.3 = (bf16[3,2,4,1024]{3,2,1,0:T(4,128)(2,1)S(1)}, bf16[3,2,4,1024]{3,2,1,0:T(4,128)(2,1)}, u32[]{:S(2)}) copy-start(bf16[3,2,4,1024]{3,2,1,0:T(4,128)(2,1)} %param.9) | copy-start | bytes 147460
  66.2 26.1 %collective-permute-start = (f32[8,128,128]{2,1,0:T(8,128)}, f32[8,128,128]{2,1,0:T(8,128)}, u32[]{:S(2)}, u32[]{:S(2)}) collective-permute-start(f32[8,128,128]{2,1,0:T(8,128)} %get-tuple-element.9), channel_id=1, source_target_pairs={{504,0},{0,8},{8,16},{16,24},{24,32},{32,40},{40,48},{48,56},{56,6... | collective-permute-start | bytes 1572872 | tf_op jit(solution)/shard_map/ppermute | solution.py:15
  70.1 24.1 %collective-permute-start.2 = (f32[8,128,128]{2,1,0:T(8,128)}, f32[8,128,128]{2,1,0:T(8,128)}, u32[]{:S(2)}, u32[]{:S(2)}) collective-permute-start(f32[8,128,128]{2,1,0:T(8,128)} %get-tuple-element.10), channel_id=1, source_target_pairs={{8,0},{16,8},{24,16},{32,24},{40,32},{48,40},{56,48},{64,56},{72,6... | collective-permute-start | bytes 1572872 | tf_op jit(solution)/shard_map/ppermute | solution.py:15
  82.3 21.2 %collective-permute-start.4 = (f32[8,128,128]{2,1,0:T(8,128)}, f32[8,128,128]{2,1,0:T(8,128)S(1)}, u32[]{:S(2)}, u32[]{:S(2)}) collective-permute-start(f32[8,128,128]{2,1,0:T(8,128)} %get-tuple-element.11), channel_id=1, source_target_pairs={{504,0},{0,8},{8,16},{16,24},{24,32},{32,40},{40,48},{48,56},{56,6... | collective-permute-start | bytes 1572872 | tf_op jit(solution)/shard_map/ppermute | solution.py:15
  84.2 20.2 %collective-permute-start.5 = (f32[8,128,128]{2,1,0:T(8,128)}, f32[8,128,128]{2,1,0:T(8,128)S(1)}, u32[]{:S(2)}, u32[]{:S(2)}) collective-permute-start(f32[8,128,128]{2,1,0:T(8,128)} %get-tuple-element.12), channel_id=1, source_target_pairs={{8,0},{16,8},{24,16},{32,24},{40,32},{48,40},{56,48},{64,56},{72,6... | collective-permute-start | bytes 1572872 | tf_op jit(solution)/shard_map/ppermute | solution.py:15
  92.3 22.4 %collective-permute-start.1 = (f32[8,128,128]{2,1,0:T(8,128)}, f32[8,128,128]{2,1,0:T(8,128)S(1)}, u32[]{:S(2)}, u32[]{:S(2)}) collective-permute-start(f32[8,128,128]{2,1,0:T(8,128)} %collective-permute-done), channel_id=1, source_target_pairs={{504,0},{0,8},{8,16},{16,24},{24,32},{32,40},{40,48},{48,56},{56,6... | collective-permute-start | bytes 1572872 | tf_op jit(solution)/shard_map/ppermute | solution.py:15
  94.2 21.4 %collective-permute-start.3 = (f32[8,128,128]{2,1,0:T(8,128)}, f32[8,128,128]{2,1,0:T(8,128)S(1)}, u32[]{:S(2)}, u32[]{:S(2)}) collective-permute-start(f32[8,128,128]{2,1,0:T(8,128)} %collective-permute-done.2), channel_id=1, source_target_pairs={{8,0},{16,8},{24,16},{32,24},{40,32},{48,40},{56,48},{64,56},{72,6... | collective-permute-start | bytes 1572872 | tf_op jit(solution)/shard_map/ppermute | solution.py:15
  115.7 13.2 %copy-start.4 = (f32[1024]{0:T(1024)S(1)}, f32[1024]{0:T(1024)}, u32[]{:S(2)}) copy-start(f32[1024]{0:T(1024)} %param.11) | copy-start | bytes 12292

commit v2 on v1

--- a/solution.py
+++ b/solution.py
@@ -46,6 +46,7 @@
         in_specs=[smem] * 3 + [pl.BlockSpec(memory_space=pltpu.HBM)],
         out_specs=[pl.BlockSpec(memory_space=pl.ANY)] * len(strides),
         scratch_shapes=[pltpu.SemaphoreType.DMA((len(strides),))],
+        compiler_params=pltpu.CompilerParams(vmem_limit_bytes=1024 * 1024),
         name="pick_rows",
     )(place, from_shard, from_slot, states)
 

time: 130 us -> 69.4 us (0.53)
  Pallas kernels: 68 us -> 4.42 us
  local copies, waits for them, and re-layouts: 1.31 us -> 5.01 us
    pallas_call x1, Pallas kernels: 65.5 us -> 1.92 us  [pick(): pl.pallas_call(functools.partial(pick_kernel, shards, live, strides), out...]
    unnamed x12 -> x16, local copies, waits for them, and re-layouts: 0.03 us -> 2.93 us
  transfers between devices with their start and end apart: 6 -> 6, of which waited for: 5 -> 4; matrix products, arithmetic and copies ran while one was open for 1% -> 3% of each run, Pallas kernels for 0% -> 0%
where the time goes in v2:
time: 69.4 us; the launch traced here: 69 us
  starting transfers between devices  33.3 us (48%)
  waiting for transfers between devices  14 us (20%)
  blocking collectives  10.4 us (15%)
  local copies, waits for them, and re-layouts  5.01 us (7%)
  Pallas kernels  4.42 us (6%)
  other arithmetic  1.04 us (1%)
  between operations  0.87 us (1%)
    ppermute x6, starting transfers between devices, shifted(): return lax.ppermute(block, axis, route)  33.3 us
    ppermute x6, waiting for transfers between devices, shifted(): return lax.ppermute(block, axis, route)  14 us
    all_to_all x1, blocking collectives, on_device(): lax.all_to_all(jnp.broadcast_to(mine[None], (group, 1, dim)), 'tensor', 0...  10.4 us
    unnamed x16, local copies, waits for them, and re-layouts  2.93 us
    pallas_call x1, Pallas kernels, run_steps(): pl.pallas_call(functools.partial(step_kernel, shards, live, strides), out...  2.5 us
    pallas_call x1, Pallas kernels, pick(): pl.pallas_call(functools.partial(pick_kernel, shards, live, strides), out...  1.92 us
  transfers between devices with their start and end apart: 6, of which 4 were waited for; matrix products, arithmetic and copies ran while one was open for 3% of the time, Pallas kernels for 0%

profile of v2, /device:TPU:1, one launch (start us, length us, event | category | flops | bytes accessed | tf_op | source)
XLA Modules:
  0.0 69.0 jit_solution(579299636645831682)
XLA Ops:
  0.7 1.6 %copy-done = f32[4,8,128,128]{3,2,1,0:T(8,128)S(1)} copy-done((f32[4,8,128,128]{3,2,1,0:T(8,128)S(1)}, f32[4,8,128,128]{3,2,1,0:T(8,128)}, u32[]{:S(2)}) %copy-start) | copy-done | bytes 2097176
  2.3 0.7 copy-done.2
  2.9 0.7 copy-done.4
  3.6 1.9 %pick_rows.1 = (f32[8,128,128]{2,1,0:T(8,128)}, f32[8,128,128]{2,1,0:T(8,128)}, f32[8,128,128]{2,1,0:T(8,128)}, f32[8,128,128]{2,1,0:T(8,128)}) custom-call(s32[1]{0:T(128)} %bitcast.place, s32[128]{0:T(128)S(1)} %copy-done.2, s32[128]{0:T(128)S(1)} %copy-done.4, f32[4,8,128,128]{3,2,1,0:T(8,128)S(1)} %copy-done), custom_call_target="tpu_custom_call" | custom-call | tf_op jit(solution)/shard_map/pick_rows/pallas_call | solution.py:43
  5.5 4.0 %collective-permute-start = (f32[8,128,128]{2,1,0:T(8,128)}, f32[8,128,128]{2,1,0:T(8,128)}, u32[]{:S(2)}, u32[]{:S(2)}) collective-permute-start(f32[8,128,128]{2,1,0:T(8,128)} %get-tuple-element.9), channel_id=1, source_target_pairs={{504,0},{0,8},{8,16},{16,24},{24,32},{32,40},{40,48},{48,56},{56,6... | collective-permute-start | bytes 1572872 | tf_op jit(solution)/shard_map/ppermute | solution.py:15
  9.5 12.1 %collective-permute-start.2 = (f32[8,128,128]{2,1,0:T(8,128)}, f32[8,128,128]{2,1,0:T(8,128)}, u32[]{:S(2)}, u32[]{:S(2)}) collective-permute-start(f32[8,128,128]{2,1,0:T(8,128)} %get-tuple-element.10), channel_id=1, source_target_pairs={{8,0},{16,8},{24,16},{32,24},{40,32},{48,40},{56,48},{64,56},{72,6... | collective-permute-start | bytes 1572872 | tf_op jit(solution)/shard_map/ppermute | solution.py:15
  21.6 1.9 %collective-permute-start.4 = (f32[8,128,128]{2,1,0:T(8,128)}, f32[8,128,128]{2,1,0:T(8,128)S(1)}, u32[]{:S(2)}, u32[]{:S(2)}) collective-permute-start(f32[8,128,128]{2,1,0:T(8,128)} %get-tuple-element.11), channel_id=1, source_target_pairs={{504,0},{0,8},{8,16},{16,24},{24,32},{32,40},{40,48},{48,56},{56,6... | collective-permute-start | bytes 1572872 | tf_op jit(solution)/shard_map/ppermute | solution.py:15
  23.5 6.7 %collective-permute-start.5 = (f32[8,128,128]{2,1,0:T(8,128)}, f32[8,128,128]{2,1,0:T(8,128)S(1)}, u32[]{:S(2)}, u32[]{:S(2)}) collective-permute-start(f32[8,128,128]{2,1,0:T(8,128)} %get-tuple-element.12), channel_id=1, source_target_pairs={{8,0},{16,8},{24,16},{32,24},{40,32},{48,40},{56,48},{64,56},{72,6... | collective-permute-start | bytes 1572872 | tf_op jit(solution)/shard_map/ppermute | solution.py:15
  30.4 0.1 copy.20
  30.6 0.8 %reshape.104 = f32[3,2,4,8,128]{4,3,2,1,0:T(8,128)S(1)} reshape(bf16[3,2,4,1024]{3,2,1,0:T(4,128)(2,1)} %param.9) | data formatting | bytes 147456 | tf_op jit(solution)/shard_map/transpose | solution.py:160
  31.5 0.1 reduce-precision_convert_fusion
  31.6 0.3 fusion.24
  31.9 0.2 broadcast_multiply_fusion
  32.1 1.9 %collective-permute-start.1 = (f32[8,128,128]{2,1,0:T(8,128)}, f32[8,128,128]{2,1,0:T(8,128)S(1)}, u32[]{:S(2)}, u32[]{:S(2)}) collective-permute-start(f32[8,128,128]{2,1,0:T(8,128)} %collective-permute-done), channel_id=1, source_target_pairs={{504,0},{0,8},{8,16},{16,24},{24,32},{32,40},{40,48},{48,56},{56,6... | collective-permute-start | bytes 1572872 | tf_op jit(solution)/shard_map/ppermute | solution.py:15
  34.1 6.7 %collective-permute-start.3 = (f32[8,128,128]{2,1,0:T(8,128)}, f32[8,128,128]{2,1,0:T(8,128)S(1)}, u32[]{:S(2)}, u32[]{:S(2)}) collective-permute-start(f32[8,128,128]{2,1,0:T(8,128)} %collective-permute-done.2), channel_id=1, source_target_pairs={{8,0},{16,8},{24,16},{32,24},{40,32},{48,40},{56,48},{64,56},{72,6... | collective-permute-start | bytes 1572872 | tf_op jit(solution)/shard_map/ppermute | solution.py:15
  41.0 1.8 %collective-permute-done.4.refs_2_ = f32[8,128,128]{2,1,0:T(8,128)S(1)} collective-permute-done((f32[8,128,128]{2,1,0:T(8,128)}, f32[8,128,128]{2,1,0:T(8,128)S(1)}, u32[]{:S(2)}, u32[]{:S(2)}) %collective-permute-start.4) | collective-permute-done | bytes 524320 | tf_op jit(solution)/shard_map/ppermute | solution.py:15
  42.8 1.0 %collective-permute-done.5.refs_3_ = f32[8,128,128]{2,1,0:T(8,128)S(1)} collective-permute-done((f32[8,128,128]{2,1,0:T(8,128)}, f32[8,128,128]{2,1,0:T(8,128)S(1)}, u32[]{:S(2)}, u32[]{:S(2)}) %collective-permute-start.5) | collective-permute-done | bytes 524320 | tf_op jit(solution)/shard_map/ppermute | solution.py:15
  43.7 10.3 %collective-permute-done.1.refs_0_ = f32[8,128,128]{2,1,0:T(8,128)S(1)} collective-permute-done((f32[8,128,128]{2,1,0:T(8,128)}, f32[8,128,128]{2,1,0:T(8,128)S(1)}, u32[]{:S(2)}, u32[]{:S(2)}) %collective-permute-start.1) | collective-permute-done | bytes 524320 | tf_op jit(solution)/shard_map/ppermute | solution.py:15
  54.0 1.0 %collective-permute-done.3.refs_1_ = f32[8,128,128]{2,1,0:T(8,128)S(1)} collective-permute-done((f32[8,128,128]{2,1,0:T(8,128)}, f32[8,128,128]{2,1,0:T(8,128)S(1)}, u32[]{:S(2)}, u32[]{:S(2)}) %collective-permute-start.3) | collective-permute-done | bytes 524320 | tf_op jit(solution)/shard_map/ppermute | solution.py:15
  55.1 2.5 %decode_steps.1 = (f32[2,8,128,128]{3,2,1,0:T(8,128)}, f32[2,8,8,128]{3,2,1,0:T(8,128)S(1)}, f32[2,8,128]{2,1,0:T(8,128)S(1)}) custom-call(s32[1]{0:T(128)} %bitcast.place, s32[128]{0:T(128)S(1)} %copy-done.3, s32[128]{0:T(128)S(1)} %copy-done.5, f32[4,8,128,128]{3,2,1,0:T(8,128)S(1)} %copy-done.1, f32[8,128,128]{2,1,0:T(8,128)S(1)} %collective-permute-done.1.refs_0_, ...), custom_call_target="tpu_custom_call" | custom-call | tf_op jit(solution)/shard_map/decode_steps/pallas_call | solution.py:126
  57.6 0.1 slice_reduce_fusion
  57.7 0.1 reshape_squeeze.4
  57.8 10.4 %all_to_all.5 = f32[8,1,128]{2,1,0:T(1,128)S(1)} all-to-all(f32[8,1,128]{2,1,0:T(1,128)S(1)} %broadcast_in_dim.8), channel_id=1, replica_groups=mesh['dp'=64,'tensor'=8] {'tensor'}, dimensions={0} | all-to-all | bytes 8192 | tf_op jit(solution)/shard_map/all_to_all | solution.py:199
  68.4 0.6 convert_element_type.46
  (35 shorter events, 1.0 us)
Async XLA Ops:
  0.6 54.4 %copy-start.5 = (s32[128]{0:T(128)S(1)}, s32[128]{0:T(128)}, u32[]{:S(2)}) copy-start(s32[128]{0:T(128)} %slot_ref.3) | copy-start | bytes 1540
  0.6 54.4 %copy-start.3 = (s32[128]{0:T(128)S(1)}, s32[128]{0:T(128)}, u32[]{:S(2)}) copy-start(s32[128]{0:T(128)} %shard_ref.3) | copy-start | bytes 1540
  0.7 29.6 %copy-start.7 = (f32[8]{0:T(128)S(1)}, f32[8]{0:T(128)}, u32[]{:S(2)}) copy-start(f32[8]{0:T(128)} %param.10) | copy-start | bytes 100
  0.7 1.6 %copy-start = (f32[4,8,128,128]{3,2,1,0:T(8,128)S(1)}, f32[4,8,128,128]{3,2,1,0:T(8,128)}, u32[]{:S(2)}) copy-start(f32[4,8,128,128]{3,2,1,0:T(8,128)} %states.3) | copy-start | bytes 6291460
  2.3 0.7 copy-start.2
  2.9 0.7 copy-start.4
  3.6 51.5 %copy-start.1 = (f32[4,8,128,128]{3,2,1,0:T(8,128)S(1)}, f32[4,8,128,128]{3,2,1,0:T(8,128)}, u32[]{:S(2)}) copy-start(f32[4,8,128,128]{3,2,1,0:T(8,128)} %states.3) | copy-start | bytes 6291460
  5.5 26.6 %collective-permute-start = (f32[8,128,128]{2,1,0:T(8,128)}, f32[8,128,128]{2,1,0:T(8,128)}, u32[]{:S(2)}, u32[]{:S(2)}) collective-permute-start(f32[8,128,128]{2,1,0:T(8,128)} %get-tuple-element.9), channel_id=1, source_target_pairs={{504,0},{0,8},{8,16},{16,24},{24,32},{32,40},{40,48},{48,56},{56,6... | collective-permute-start | bytes 1572872 | tf_op jit(solution)/shard_map/ppermute | solution.py:15
  9.5 24.6 %collective-permute-start.2 = (f32[8,128,128]{2,1,0:T(8,128)}, f32[8,128,128]{2,1,0:T(8,128)}, u32[]{:S(2)}, u32[]{:S(2)}) collective-permute-start(f32[8,128,128]{2,1,0:T(8,128)} %get-tuple-element.10), channel_id=1, source_target_pairs={{8,0},{16,8},{24,16},{32,24},{40,32},{48,40},{56,48},{64,56},{72,6... | collective-permute-start | bytes 1572872 | tf_op jit(solution)/shard_map/ppermute | solution.py:15
  21.6 21.2 %collective-permute-start.4 = (f32[8,128,128]{2,1,0:T(8,128)}, f32[8,128,128]{2,1,0:T(8,128)S(1)}, u32[]{:S(2)}, u32[]{:S(2)}) collective-permute-start(f32[8,128,128]{2,1,0:T(8,128)} %get-tuple-element.11), channel_id=1, source_target_pairs={{504,0},{0,8},{8,16},{16,24},{24,32},{32,40},{40,48},{48,56},{56,6... | collective-permute-start | bytes 1572872 | tf_op jit(solution)/shard_map/ppermute | solution.py:15
  23.5 20.2 %collective-permute-start.5 = (f32[8,128,128]{2,1,0:T(8,128)}, f32[8,128,128]{2,1,0:T(8,128)S(1)}, u32[]{:S(2)}, u32[]{:S(2)}) collective-permute-start(f32[8,128,128]{2,1,0:T(8,128)} %get-tuple-element.12), channel_id=1, source_target_pairs={{8,0},{16,8},{24,16},{32,24},{40,32},{48,40},{56,48},{64,56},{72,6... | collective-permute-start | bytes 1572872 | tf_op jit(solution)/shard_map/ppermute | solution.py:15
  32.1 21.9 %collective-permute-start.1 = (f32[8,128,128]{2,1,0:T(8,128)}, f32[8,128,128]{2,1,0:T(8,128)S(1)}, u32[]{:S(2)}, u32[]{:S(2)}) collective-permute-start(f32[8,128,128]{2,1,0:T(8,128)} %collective-permute-done), channel_id=1, source_target_pairs={{504,0},{0,8},{8,16},{16,24},{24,32},{32,40},{40,48},{48,56},{56,6... | collective-permute-start | bytes 1572872 | tf_op jit(solution)/shard_map/ppermute | solution.py:15
  34.1 20.9 %collective-permute-start.3 = (f32[8,128,128]{2,1,0:T(8,128)}, f32[8,128,128]{2,1,0:T(8,128)S(1)}, u32[]{:S(2)}, u32[]{:S(2)}) collective-permute-start(f32[8,128,128]{2,1,0:T(8,128)} %collective-permute-done.2), channel_id=1, source_target_pairs={{8,0},{16,8},{24,16},{32,24},{40,32},{48,40},{56,48},{64,56},{72,6... | collective-permute-start | bytes 1572872 | tf_op jit(solution)/shard_map/ppermute | solution.py:15
  55.0 13.2 %copy-start.6 = (f32[1024]{0:T(1024)S(1)}, f32[1024]{0:T(1024)}, u32[]{:S(2)}) copy-start(f32[1024]{0:T(1024)} %param.11) | copy-start | bytes 12292

commit v3 on v2

--- a/solution.py
+++ b/solution.py
@@ -9,10 +9,14 @@
 EPS = 1e-05
 
 
-def shifted(block, axis, distance):
+def swapped(block, axis, first):
     size = lax.axis_size(axis)
-    route = [((i - distance) % size, i) for i in range(size)]
-    return lax.ppermute(block, axis, route)
+    pairs = [((first + i) % size, (first + i + 1) % size) for i in range(0, size, 2)]
+    return lax.ppermute(block, axis, pairs + [(b, a) for a, b in pairs])
+
+
+def side_of(device):
+    return 2 * lax.rem(device, 2) - 1
 
 
 def split(x):
@@ -20,12 +24,20 @@
     return high.astype(jnp.bfloat16), (x - high).astype(jnp.bfloat16)
 
 
-def pick_kernel(shards, live, strides, place, shard_ref, slot_ref, states, *refs):
-    outs, sems = refs[:-1], refs[-1]
+def pick_kernel(shards, live, strides, place, shard_hbm, slot_hbm, states, *refs):
+    outs, (shard_ref, slot_ref, sems) = refs[: len(strides)], refs[len(strides) :]
     device = place[0]
+    plan = [
+        pltpu.make_async_copy(shard_hbm, shard_ref, sems.at[len(strides)]),
+        pltpu.make_async_copy(slot_hbm, slot_ref, sems.at[len(strides) + 1]),
+    ]
+    for copy in plan:
+        copy.start()
+    for copy in plan:
+        copy.wait()
     copies = []
     for n, stride in enumerate(strides):
-        target = lax.rem(device + stride + shards, shards)
+        target = lax.rem(device + stride * side_of(device) + shards, shards)
         slot = jnp.int32(0)
         for row in range(live):
             mine = shard_ref[target * live + row] == device
@@ -38,17 +50,25 @@
 
 
 def pick(place, from_shard, from_slot, states, shards, live, strides):
-    row = jax.ShapeDtypeStruct(states.shape[1:], states.dtype)
-    smem = pl.BlockSpec(memory_space=pltpu.SMEM)
+    row = pltpu.VMEM(states.shape[1:], states.dtype)
+    fixed = [
+        pltpu.with_memory_space_constraint(x, pltpu.HBM)
+        for x in (from_shard, from_slot, states)
+    ]
     return pl.pallas_call(
         functools.partial(pick_kernel, shards, live, strides),
         out_shape=[row] * len(strides),
-        in_specs=[smem] * 3 + [pl.BlockSpec(memory_space=pltpu.HBM)],
+        in_specs=[pl.BlockSpec(memory_space=pltpu.SMEM)]
+        + [pl.BlockSpec(memory_space=pltpu.HBM)] * 3,
         out_specs=[pl.BlockSpec(memory_space=pl.ANY)] * len(strides),
-        scratch_shapes=[pltpu.SemaphoreType.DMA((len(strides),))],
+        scratch_shapes=[
+            pltpu.SMEM(from_shard.shape, jnp.int32),
+            pltpu.SMEM(from_slot.shape, jnp.int32),
+            pltpu.SemaphoreType.DMA((len(strides) + 2,)),
+        ],
         compiler_params=pltpu.CompilerParams(vmem_limit_bytes=1024 * 1024),
         name="pick_rows",
-    )(place, from_shard, from_slot, states)
+    )(place, *fixed)
 
 
 def step_kernel(
@@ -75,7 +95,7 @@
 
         for k, stride in enumerate(strides):
 
-            @pl.when(gap == stride % shards)
+            @pl.when(gap == lax.rem(stride * side_of(device) + shards, shards))
             def _():
                 pltpu.make_async_copy(arrived[k].at[span], target, sem).start()
 
@@ -149,12 +169,12 @@
     heads, dim = states.shape[1], states.shape[2]
     features = heads * dim * lax.axis_size("tensor")
     place = lax.axis_index("dp").astype(jnp.int32).reshape(1)
+    rows = pick(place, from_shard, from_slot, states, shards, live, (-2, 2, -1, 1))
+    half_way_0, half_way_1 = swapped(rows[0], "dp", 0), swapped(rows[1], "dp", 1)
+    next_0, next_1 = swapped(rows[2], "dp", 0), swapped(rows[3], "dp", 1)
+    far_1, far_0 = swapped(half_way_0, "dp", 1), swapped(half_way_1, "dp", 0)
     strides = (2, -2, 1, -1)
-    rows = pick(place, from_shard, from_slot, states, shards, live, strides)
-    near_up, near_down = shifted(rows[0], "dp", 1), shifted(rows[1], "dp", -1)
-    up, down = shifted(rows[2], "dp", 1), shifted(rows[3], "dp", -1)
-    far_up, far_down = shifted(near_up, "dp", 1), shifted(near_down, "dp", -1)
-    arrived = [far_up, far_down, up, down]
+    arrived = [far_0, far_1, next_0, next_1]
 
     activity = projected.astype(jnp.float32)
     by_head = jnp.transpose(

time: 69.4 us -> 132 us (1.90)
  Pallas kernels: 4.42 us -> 68 us
  waiting for transfers between devices: 14 us -> 21 us
  starting transfers between devices: 33.3 us -> 28.8 us
  local copies, waits for them, and re-layouts: 5.01 us -> 1.31 us
    pallas_call x1, Pallas kernels: 1.92 us -> 65.5 us  [pick(): pl.pallas_call(functools.partial(pick_kernel, shards, live, strides), out...]
    ppermute x6, waiting for transfers between devices: 14 us -> 21 us  [swapped(): return lax.ppermute(block, axis, pairs + [(b, a) for a, b in pairs])]
    ppermute x6, starting transfers between devices: 33.3 us -> 28.8 us  [swapped(): return lax.ppermute(block, axis, pairs + [(b, a) for a, b in pairs])]
    unnamed x16 -> x12, local copies, waits for them, and re-layouts: 2.93 us -> 0.03 us
  transfers between devices with their start and end apart: 6 -> 6, of which waited for: 4 -> 4; matrix products, arithmetic and copies ran while one was open for 3% -> 1% of each run, Pallas kernels for 0% -> 0%
where the time goes in v3:
time: 132 us
  Pallas kernels  68 us (52%)
  starting transfers between devices  28.8 us (22%)
  waiting for transfers between devices  21 us (16%)
  blocking collectives  10.7 us (8%)
    pallas_call x1, Pallas kernels, pick(): pl.pallas_call(functools.partial(pick_kernel, shards, live, strides), out...  65.5 us
    ppermute x6, starting transfers between devices, swapped(): return lax.ppermute(block, axis, pairs + [(b, a) for a, b in pairs])  28.8 us
    ppermute x6, waiting for transfers between devices, swapped(): return lax.ppermute(block, axis, pairs + [(b, a) for a, b in pairs])  21 us
    all_to_all x1, blocking collectives, on_device(): lax.all_to_all(jnp.broadcast_to(mine[None], (group, 1, dim)), 'tensor', 0...  10.7 us
  transfers between devices with their start and end apart: 6, of which 4 were waited for; matrix products, arithmetic and copies ran while one was open for 1% of the time, Pallas kernels for 0%

profile of v3, /device:TPU:1, one launch (start us, length us, event | category | flops | bytes accessed | tf_op | source)
XLA Modules:
  0.0 131.8 jit_solution(8091280275050879497)
XLA Ops:
  0.7 65.5 %pick_rows.1 = (f32[8,128,128]{2,1,0:T(8,128)}, f32[8,128,128]{2,1,0:T(8,128)}, f32[8,128,128]{2,1,0:T(8,128)}, f32[8,128,128]{2,1,0:T(8,128)}) custom-call(s32[1]{0:T(128)} %bitcast.place, s32[128]{0:T(128)} %shard_ref.1, s32[128]{0:T(128)} %slot_ref.1, f32[4,8,128,128]{3,2,1,0:T(8,128)} %states.3), custom_call_target="tpu_custom_call" | custom-call | tf_op jit(solution)/shard_map/pick_rows/pallas_call | solution.py:58
  66.2 14.1 %collective-permute-start = (f32[8,128,128]{2,1,0:T(8,128)}, f32[8,128,128]{2,1,0:T(8,128)}, u32[]{:S(2)}, u32[]{:S(2)}) collective-permute-start(f32[8,128,128]{2,1,0:T(8,128)} %get-tuple-element.9), channel_id=1, source_target_pairs={{8,16},{24,32},{40,48},{56,64},{72,80},{88,96},{104,112},{120,128}... | collective-permute-start | bytes 1572872 | tf_op jit(solution)/shard_map/ppermute | solution.py:15
  80.3 1.9 %collective-permute-start.2 = (f32[8,128,128]{2,1,0:T(8,128)}, f32[8,128,128]{2,1,0:T(8,128)}, u32[]{:S(2)}, u32[]{:S(2)}) collective-permute-start(f32[8,128,128]{2,1,0:T(8,128)} %get-tuple-element.10), channel_id=1, source_target_pairs={{0,8},{16,24},{32,40},{48,56},{64,72},{80,88},{96,104},{112,120},{... | collective-permute-start | bytes 1572872 | tf_op jit(solution)/shard_map/ppermute | solution.py:15
  82.3 3.4 %collective-permute-start.4 = (f32[8,128,128]{2,1,0:T(8,128)}, f32[8,128,128]{2,1,0:T(8,128)S(1)}, u32[]{:S(2)}, u32[]{:S(2)}) collective-permute-start(f32[8,128,128]{2,1,0:T(8,128)} %get-tuple-element.11), channel_id=1, source_target_pairs={{0,8},{16,24},{32,40},{48,56},{64,72},{80,88},{96,104},{112,120},{... | collective-permute-start | bytes 1572872 | tf_op jit(solution)/shard_map/ppermute | solution.py:15
  85.6 1.9 %collective-permute-start.5 = (f32[8,128,128]{2,1,0:T(8,128)}, f32[8,128,128]{2,1,0:T(8,128)S(1)}, u32[]{:S(2)}, u32[]{:S(2)}) collective-permute-start(f32[8,128,128]{2,1,0:T(8,128)} %get-tuple-element.12), channel_id=1, source_target_pairs={{8,16},{24,32},{40,48},{56,64},{72,80},{88,96},{104,112},{120,128}... | collective-permute-start | bytes 1572872 | tf_op jit(solution)/shard_map/ppermute | solution.py:15
  87.7 0.1 copy.20
  87.8 0.1 copy.19
  88.0 0.1 reduce-precision_convert_fusion
  88.1 0.3 fusion.24
  88.5 0.2 broadcast_multiply_fusion
  88.7 3.6 %collective-permute-done = f32[8,128,128]{2,1,0:T(8,128)} collective-permute-done((f32[8,128,128]{2,1,0:T(8,128)}, f32[8,128,128]{2,1,0:T(8,128)}, u32[]{:S(2)}, u32[]{:S(2)}) %collective-permute-start) | collective-permute-done | bytes 524320 | tf_op jit(solution)/shard_map/ppermute | solution.py:15
  92.3 1.9 %collective-permute-start.1 = (f32[8,128,128]{2,1,0:T(8,128)}, f32[8,128,128]{2,1,0:T(8,128)S(1)}, u32[]{:S(2)}, u32[]{:S(2)}) collective-permute-start(f32[8,128,128]{2,1,0:T(8,128)} %collective-permute-done), channel_id=1, source_target_pairs={{0,8},{16,24},{32,40},{48,56},{64,72},{80,88},{96,104},{112,120},{... | collective-permute-start | bytes 1572872 | tf_op jit(solution)/shard_map/ppermute | solution.py:15
  94.2 0.8 collective-permute-done.2
  95.0 5.6 %collective-permute-start.3 = (f32[8,128,128]{2,1,0:T(8,128)}, f32[8,128,128]{2,1,0:T(8,128)S(1)}, u32[]{:S(2)}, u32[]{:S(2)}) collective-permute-start(f32[8,128,128]{2,1,0:T(8,128)} %collective-permute-done.2), channel_id=1, source_target_pairs={{8,16},{24,32},{40,48},{56,64},{72,80},{88,96},{104,112},{120,128}... | collective-permute-start | bytes 1572872 | tf_op jit(solution)/shard_map/ppermute | solution.py:15
  100.7 0.1 fusion.13
  100.8 5.3 %collective-permute-done.4.refs_2_ = f32[8,128,128]{2,1,0:T(8,128)S(1)} collective-permute-done((f32[8,128,128]{2,1,0:T(8,128)}, f32[8,128,128]{2,1,0:T(8,128)S(1)}, u32[]{:S(2)}, u32[]{:S(2)}) %collective-permute-start.4) | collective-permute-done | bytes 524320 | tf_op jit(solution)/shard_map/ppermute | solution.py:15
  106.2 11.2 %collective-permute-done.1.refs_0_ = f32[8,128,128]{2,1,0:T(8,128)S(1)} collective-permute-done((f32[8,128,128]{2,1,0:T(8,128)}, f32[8,128,128]{2,1,0:T(8,128)S(1)}, u32[]{:S(2)}, u32[]{:S(2)}) %collective-permute-start.1) | collective-permute-done | bytes 524320 | tf_op jit(solution)/shard_map/ppermute | solution.py:15
  117.5 2.5 %decode_steps.1 = (f32[2,8,128,128]{3,2,1,0:T(8,128)}, f32[2,8,8,128]{3,2,1,0:T(8,128)S(1)}, f32[2,8,128]{2,1,0:T(8,128)S(1)}) custom-call(s32[1]{0:T(128)} %bitcast.place, s32[128]{0:T(128)S(1)} %copy-done.1, s32[128]{0:T(128)S(1)} %copy-done.2, f32[4,8,128,128]{3,2,1,0:T(8,128)S(1)} %copy-done, f32[8,128,128]{2,1,0:T(8,128)S(1)} %collective-permute-done.1.refs_0_, ...), custom_call_target="tpu_custom_call" | custom-call | tf_op jit(solution)/shard_map/decode_steps/pallas_call | solution.py:146
  120.0 0.1 slice_reduce_fusion
  120.1 0.1 reshape_squeeze.4
  120.2 10.7 %all_to_all.5 = f32[8,1,128]{2,1,0:T(1,128)S(1)} all-to-all(f32[8,1,128]{2,1,0:T(1,128)S(1)} %broadcast_in_dim.8), channel_id=1, replica_groups=mesh['dp'=64,'tensor'=8] {'tensor'}, dimensions={0} | all-to-all | bytes 8192 | tf_op jit(solution)/shard_map/all_to_all | solution.py:219
  131.0 0.1 rsqrt.12
  131.0 0.1 fusion.22
  131.2 0.6 convert_element_type.46
  (31 shorter events, 0.7 us)
Async XLA Ops:
  0.6 116.8 %copy-start.2 = (s32[128]{0:T(128)S(1)}, s32[128]{0:T(128)}, u32[]{:S(2)}) copy-start(s32[128]{0:T(128)} %slot_ref.1) | copy-start | bytes 1540
  0.6 116.8 %copy-start.1 = (s32[128]{0:T(128)S(1)}, s32[128]{0:T(128)}, u32[]{:S(2)}) copy-start(s32[128]{0:T(128)} %shard_ref.1) | copy-start | bytes 1540
  0.7 116.8 %copy-start = (f32[4,8,128,128]{3,2,1,0:T(8,128)S(1)}, f32[4,8,128,128]{3,2,1,0:T(8,128)}, u32[]{:S(2)}) copy-start(f32[4,8,128,128]{3,2,1,0:T(8,128)} %states.3) | copy-start | bytes 6291460
  0.7 86.9 %copy-start.5 = (f32[8]{0:T(128)S(1)}, f32[8]{0:T(128)}, u32[]{:S(2)}) copy-start(f32[8]{0:T(128)} %param.10) | copy-start | bytes 100
  0.7 87.2 %copy-start.3 = (bf16[3,2,4,1024]{3,2,1,0:T(4,128)(2,1)S(1)}, bf16[3,2,4,1024]{3,2,1,0:T(4,128)(2,1)}, u32[]{:S(2)}) copy-start(bf16[3,2,4,1024]{3,2,1,0:T(4,128)(2,1)} %param.9) | copy-start | bytes 147460
  66.2 26.1 %collective-permute-start = (f32[8,128,128]{2,1,0:T(8,128)}, f32[8,128,128]{2,1,0:T(8,128)}, u32[]{:S(2)}, u32[]{:S(2)}) collective-permute-start(f32[8,128,128]{2,1,0:T(8,128)} %get-tuple-element.9), channel_id=1, source_target_pairs={{8,16},{24,32},{40,48},{56,64},{72,80},{88,96},{104,112},{120,128}... | collective-permute-start | bytes 1572872 | tf_op jit(solution)/shard_map/ppermute | solution.py:15
  80.3 14.7 %collective-permute-start.2 = (f32[8,128,128]{2,1,0:T(8,128)}, f32[8,128,128]{2,1,0:T(8,128)}, u32[]{:S(2)}, u32[]{:S(2)}) collective-permute-start(f32[8,128,128]{2,1,0:T(8,128)} %get-tuple-element.10), channel_id=1, source_target_pairs={{0,8},{16,24},{32,40},{48,56},{64,72},{80,88},{96,104},{112,120},{... | collective-permute-start | bytes 1572872 | tf_op jit(solution)/shard_map/ppermute | solution.py:15
  82.3 23.9 %collective-permute-start.4 = (f32[8,128,128]{2,1,0:T(8,128)}, f32[8,128,128]{2,1,0:T(8,128)S(1)}, u32[]{:S(2)}, u32[]{:S(2)}) collective-permute-start(f32[8,128,128]{2,1,0:T(8,128)} %get-tuple-element.11), channel_id=1, source_target_pairs={{0,8},{16,24},{32,40},{48,56},{64,72},{80,88},{96,104},{112,120},{... | collective-permute-start | bytes 1572872 | tf_op jit(solution)/shard_map/ppermute | solution.py:15
  85.6 20.5 %collective-permute-start.5 = (f32[8,128,128]{2,1,0:T(8,128)}, f32[8,128,128]{2,1,0:T(8,128)S(1)}, u32[]{:S(2)}, u32[]{:S(2)}) collective-permute-start(f32[8,128,128]{2,1,0:T(8,128)} %get-tuple-element.12), channel_id=1, source_target_pairs={{8,16},{24,32},{40,48},{56,64},{72,80},{88,96},{104,112},{120,128}... | collective-permute-start | bytes 1572872 | tf_op jit(solution)/shard_map/ppermute | solution.py:15
  92.3 25.1 %collective-permute-start.1 = (f32[8,128,128]{2,1,0:T(8,128)}, f32[8,128,128]{2,1,0:T(8,128)S(1)}, u32[]{:S(2)}, u32[]{:S(2)}) collective-permute-start(f32[8,128,128]{2,1,0:T(8,128)} %collective-permute-done), channel_id=1, source_target_pairs={{0,8},{16,24},{32,40},{48,56},{64,72},{80,88},{96,104},{112,120},{... | collective-permute-start | bytes 1572872 | tf_op jit(solution)/shard_map/ppermute | solution.py:15
  95.0 22.4 %collective-permute-start.3 = (f32[8,128,128]{2,1,0:T(8,128)}, f32[8,128,128]{2,1,0:T(8,128)S(1)}, u32[]{:S(2)}, u32[]{:S(2)}) collective-permute-start(f32[8,128,128]{2,1,0:T(8,128)} %collective-permute-done.2), channel_id=1, source_target_pairs={{8,16},{24,32},{40,48},{56,64},{72,80},{88,96},{104,112},{120,128}... | collective-permute-start | bytes 1572872 | tf_op jit(solution)/shard_map/ppermute | solution.py:15
  117.5 13.6 %copy-start.4 = (f32[1024]{0:T(1024)S(1)}, f32[1024]{0:T(1024)}, u32[]{:S(2)}) copy-start(f32[1024]{0:T(1024)} %param.11) | copy-start | bytes 12292

commit v4 on v3

--- a/solution.py
+++ b/solution.py
@@ -25,11 +25,12 @@
 
 
 def pick_kernel(shards, live, strides, place, shard_hbm, slot_hbm, states, *refs):
-    outs, (shard_ref, slot_ref, sems) = refs[: len(strides)], refs[len(strides) :]
+    n_rows = len(strides)
+    outs, (shard_ref, slot_ref, held, sems, sems_out) = refs[:n_rows], refs[n_rows:]
     device = place[0]
     plan = [
-        pltpu.make_async_copy(shard_hbm, shard_ref, sems.at[len(strides)]),
-        pltpu.make_async_copy(slot_hbm, slot_ref, sems.at[len(strides) + 1]),
+        pltpu.make_async_copy(shard_hbm, shard_ref, sems.at[n_rows]),
+        pltpu.make_async_copy(slot_hbm, slot_ref, sems.at[n_rows + 1]),
     ]
     for copy in plan:
         copy.start()
@@ -42,15 +43,21 @@
         for row in range(live):
             mine = shard_ref[target * live + row] == device
             slot = jnp.where(mine, slot_ref[target * live + row], slot)
-        copy = pltpu.make_async_copy(states.at[slot], outs[n], sems.at[n])
+        copy = pltpu.make_async_copy(states.at[slot], held.at[n], sems.at[n])
         copy.start()
         copies.append(copy)
-    for copy in copies:
+    copies_out = []
+    for n, copy in enumerate(copies):
         copy.wait()
+        copy_out = pltpu.make_async_copy(held.at[n], outs[n], sems_out.at[n])
+        copy_out.start()
+        copies_out.append(copy_out)
+    for copy_out in copies_out:
+        copy_out.wait()
 
 
 def pick(place, from_shard, from_slot, states, shards, live, strides):
-    row = pltpu.VMEM(states.shape[1:], states.dtype)
+    row = jax.ShapeDtypeStruct(states.shape[1:], states.dtype)
     fixed = [
         pltpu.with_memory_space_constraint(x, pltpu.HBM)
         for x in (from_shard, from_slot, states)
@@ -64,9 +71,11 @@
         scratch_shapes=[
             pltpu.SMEM(from_shard.shape, jnp.int32),
             pltpu.SMEM(from_slot.shape, jnp.int32),
+            pltpu.VMEM((len(strides),) + states.shape[1:], states.dtype),
             pltpu.SemaphoreType.DMA((len(strides) + 2,)),
+            pltpu.SemaphoreType.DMA((len(strides),)),
         ],
-        compiler_params=pltpu.CompilerParams(vmem_limit_bytes=1024 * 1024),
+        compiler_params=pltpu.CompilerParams(vmem_limit_bytes=4 * 1024 * 1024),
         name="pick_rows",
     )(place, *fixed)
 

time: 132 us -> 70.3 us (0.53)
  Pallas kernels: 68 us -> 6.23 us
    pallas_call x1, Pallas kernels: 65.5 us -> 3.71 us  [pick(): pl.pallas_call(functools.partial(pick_kernel, shards, live, strides), out...]
  transfers between devices with their start and end apart: 6 -> 6, of which waited for: 4 -> 4; matrix products, arithmetic and copies ran while one was open for 1% -> 2% of each run, Pallas kernels for 0% -> 0%
where the time goes in v4:
time: 70.3 us; the launch traced here: 69.9 us
  starting transfers between devices  28.8 us (41%)
  waiting for transfers between devices  21 us (30%)
  blocking collectives  10.7 us (15%)
  Pallas kernels  6.23 us (9%)
  local copies, waits for them, and re-layouts  1.31 us (2%)
  other arithmetic  1.04 us (1%)
  between operations  0.86 us (1%)
    ppermute x6, starting transfers between devices, swapped(): return lax.ppermute(block, axis, pairs + [(b, a) for a, b in pairs])  28.8 us
    ppermute x6, waiting for transfers between devices, swapped(): return lax.ppermute(block, axis, pairs + [(b, a) for a, b in pairs])  21 us
    all_to_all x1, blocking collectives, on_device(): lax.all_to_all(jnp.broadcast_to(mine[None], (group, 1, dim)), 'tensor', 0...  10.7 us
    pallas_call x1, Pallas kernels, pick(): pl.pallas_call(functools.partial(pick_kernel, shards, live, strides), out...  3.71 us
    pallas_call x1, Pallas kernels, run_steps(): pl.pallas_call(functools.partial(step_kernel, shards, live, strides), out...  2.52 us
  transfers between devices with their start and end apart: 6, of which 4 were waited for; matrix products, arithmetic and copies ran while one was open for 2% of the time, Pallas kernels for 0%

profile of v4, /device:TPU:1, one launch (start us, length us, event | category | flops | bytes accessed | tf_op | source)
XLA Modules:
  0.0 69.9 jit_solution(5608982453783989811)
XLA Ops:
  0.7 3.7 %pick_rows.1 = (f32[8,128,128]{2,1,0:T(8,128)}, f32[8,128,128]{2,1,0:T(8,128)}, f32[8,128,128]{2,1,0:T(8,128)}, f32[8,128,128]{2,1,0:T(8,128)}) custom-call(s32[1]{0:T(128)} %bitcast.place, s32[128]{0:T(128)} %shard_ref.1, s32[128]{0:T(128)} %slot_ref.1, f32[4,8,128,128]{3,2,1,0:T(8,128)} %states.3), custom_call_target="tpu_custom_call" | custom-call | tf_op jit(solution)/shard_map/pick_rows/pallas_call | solution.py:65
  4.4 14.1 %collective-permute-start = (f32[8,128,128]{2,1,0:T(8,128)}, f32[8,128,128]{2,1,0:T(8,128)}, u32[]{:S(2)}, u32[]{:S(2)}) collective-permute-start(f32[8,128,128]{2,1,0:T(8,128)} %get-tuple-element.9), channel_id=1, source_target_pairs={{8,16},{24,32},{40,48},{56,64},{72,80},{88,96},{104,112},{120,128}... | collective-permute-start | bytes 1572872 | tf_op jit(solution)/shard_map/ppermute | solution.py:15
  18.5 1.9 %collective-permute-start.2 = (f32[8,128,128]{2,1,0:T(8,128)}, f32[8,128,128]{2,1,0:T(8,128)}, u32[]{:S(2)}, u32[]{:S(2)}) collective-permute-start(f32[8,128,128]{2,1,0:T(8,128)} %get-tuple-element.10), channel_id=1, source_target_pairs={{0,8},{16,24},{32,40},{48,56},{64,72},{80,88},{96,104},{112,120},{... | collective-permute-start | bytes 1572872 | tf_op jit(solution)/shard_map/ppermute | solution.py:15
  20.5 3.4 %collective-permute-start.4 = (f32[8,128,128]{2,1,0:T(8,128)}, f32[8,128,128]{2,1,0:T(8,128)S(1)}, u32[]{:S(2)}, u32[]{:S(2)}) collective-permute-start(f32[8,128,128]{2,1,0:T(8,128)} %get-tuple-element.11), channel_id=1, source_target_pairs={{0,8},{16,24},{32,40},{48,56},{64,72},{80,88},{96,104},{112,120},{... | collective-permute-start | bytes 1572872 | tf_op jit(solution)/shard_map/ppermute | solution.py:15
  23.8 1.9 %collective-permute-start.5 = (f32[8,128,128]{2,1,0:T(8,128)}, f32[8,128,128]{2,1,0:T(8,128)S(1)}, u32[]{:S(2)}, u32[]{:S(2)}) collective-permute-start(f32[8,128,128]{2,1,0:T(8,128)} %get-tuple-element.12), channel_id=1, source_target_pairs={{8,16},{24,32},{40,48},{56,64},{72,80},{88,96},{104,112},{120,128}... | collective-permute-start | bytes 1572872 | tf_op jit(solution)/shard_map/ppermute | solution.py:15
  25.9 0.1 copy.20
  26.0 0.1 copy.19
  26.2 0.1 reduce-precision_convert_fusion
  26.3 0.3 fusion.24
  26.6 0.2 broadcast_multiply_fusion
  26.8 3.6 %collective-permute-done = f32[8,128,128]{2,1,0:T(8,128)} collective-permute-done((f32[8,128,128]{2,1,0:T(8,128)}, f32[8,128,128]{2,1,0:T(8,128)}, u32[]{:S(2)}, u32[]{:S(2)}) %collective-permute-start) | collective-permute-done | bytes 524320 | tf_op jit(solution)/shard_map/ppermute | solution.py:15
  30.5 1.9 %collective-permute-start.1 = (f32[8,128,128]{2,1,0:T(8,128)}, f32[8,128,128]{2,1,0:T(8,128)S(1)}, u32[]{:S(2)}, u32[]{:S(2)}) collective-permute-start(f32[8,128,128]{2,1,0:T(8,128)} %collective-permute-done), channel_id=1, source_target_pairs={{0,8},{16,24},{32,40},{48,56},{64,72},{80,88},{96,104},{112,120},{... | collective-permute-start | bytes 1572872 | tf_op jit(solution)/shard_map/ppermute | solution.py:15
  32.4 0.8 %collective-permute-done.2 = f32[8,128,128]{2,1,0:T(8,128)} collective-permute-done((f32[8,128,128]{2,1,0:T(8,128)}, f32[8,128,128]{2,1,0:T(8,128)}, u32[]{:S(2)}, u32[]{:S(2)}) %collective-permute-start.2) | collective-permute-done | bytes 524320 | tf_op jit(solution)/shard_map/ppermute | solution.py:15
  33.2 5.6 %collective-permute-start.3 = (f32[8,128,128]{2,1,0:T(8,128)}, f32[8,128,128]{2,1,0:T(8,128)S(1)}, u32[]{:S(2)}, u32[]{:S(2)}) collective-permute-start(f32[8,128,128]{2,1,0:T(8,128)} %collective-permute-done.2), channel_id=1, source_target_pairs={{8,16},{24,32},{40,48},{56,64},{72,80},{88,96},{104,112},{120,128}... | collective-permute-start | bytes 1572872 | tf_op jit(solution)/shard_map/ppermute | solution.py:15
  38.9 0.1 fusion.13
  39.0 5.3 %collective-permute-done.4.refs_2_ = f32[8,128,128]{2,1,0:T(8,128)S(1)} collective-permute-done((f32[8,128,128]{2,1,0:T(8,128)}, f32[8,128,128]{2,1,0:T(8,128)S(1)}, u32[]{:S(2)}, u32[]{:S(2)}) %collective-permute-start.4) | collective-permute-done | bytes 524320 | tf_op jit(solution)/shard_map/ppermute | solution.py:15
  44.3 11.2 %collective-permute-done.1.refs_0_ = f32[8,128,128]{2,1,0:T(8,128)S(1)} collective-permute-done((f32[8,128,128]{2,1,0:T(8,128)}, f32[8,128,128]{2,1,0:T(8,128)S(1)}, u32[]{:S(2)}, u32[]{:S(2)}) %collective-permute-start.1) | collective-permute-done | bytes 524320 | tf_op jit(solution)/shard_map/ppermute | solution.py:15
  55.7 2.5 %decode_steps.1 = (f32[2,8,128,128]{3,2,1,0:T(8,128)}, f32[2,8,8,128]{3,2,1,0:T(8,128)S(1)}, f32[2,8,128]{2,1,0:T(8,128)S(1)}) custom-call(s32[1]{0:T(128)} %bitcast.place, s32[128]{0:T(128)S(1)} %copy-done.1, s32[128]{0:T(128)S(1)} %copy-done.2, f32[4,8,128,128]{3,2,1,0:T(8,128)S(1)} %copy-done, f32[8,128,128]{2,1,0:T(8,128)S(1)} %collective-permute-done.1.refs_0_, ...), custom_call_target="tpu_custom_call" | custom-call | tf_op jit(solution)/shard_map/decode_steps/pallas_call | solution.py:155
  58.2 0.1 slice_reduce_fusion
  58.3 0.1 reshape_squeeze.4
  58.4 10.7 %all_to_all.5 = f32[8,1,128]{2,1,0:T(1,128)S(1)} all-to-all(f32[8,1,128]{2,1,0:T(1,128)S(1)} %broadcast_in_dim.8), channel_id=1, replica_groups=mesh['dp'=64,'tensor'=8] {'tensor'}, dimensions={0} | all-to-all | bytes 8192 | tf_op jit(solution)/shard_map/all_to_all | solution.py:228
  69.1 0.1 rsqrt.12
  69.2 0.1 fusion.22
  69.3 0.6 convert_element_type.46
  (31 shorter events, 0.7 us)
Async XLA Ops:
  0.6 55.0 %copy-start.2 = (s32[128]{0:T(128)S(1)}, s32[128]{0:T(128)}, u32[]{:S(2)}) copy-start(s32[128]{0:T(128)} %slot_ref.1) | copy-start | bytes 1540
  0.6 55.0 %copy-start.1 = (s32[128]{0:T(128)S(1)}, s32[128]{0:T(128)}, u32[]{:S(2)}) copy-start(s32[128]{0:T(128)} %shard_ref.1) | copy-start | bytes 1540
  0.7 55.0 %copy-start = (f32[4,8,128,128]{3,2,1,0:T(8,128)S(1)}, f32[4,8,128,128]{3,2,1,0:T(8,128)}, u32[]{:S(2)}) copy-start(f32[4,8,128,128]{3,2,1,0:T(8,128)} %states.3) | copy-start | bytes 6291460
  0.7 25.1 %copy-start.5 = (f32[8]{0:T(128)S(1)}, f32[8]{0:T(128)}, u32[]{:S(2)}) copy-start(f32[8]{0:T(128)} %param.10) | copy-start | bytes 100
  0.7 25.4 %copy-start.3 = (bf16[3,2,4,1024]{3,2,1,0:T(4,128)(2,1)S(1)}, bf16[3,2,4,1024]{3,2,1,0:T(4,128)(2,1)}, u32[]{:S(2)}) copy-start(bf16[3,2,4,1024]{3,2,1,0:T(4,128)(2,1)} %param.9) | copy-start | bytes 147460
  4.4 26.1 %collective-permute-start = (f32[8,128,128]{2,1,0:T(8,128)}, f32[8,128,128]{2,1,0:T(8,128)}, u32[]{:S(2)}, u32[]{:S(2)}) collective-permute-start(f32[8,128,128]{2,1,0:T(8,128)} %get-tuple-element.9), channel_id=1, source_target_pairs={{8,16},{24,32},{40,48},{56,64},{72,80},{88,96},{104,112},{120,128}... | collective-permute-start | bytes 1572872 | tf_op jit(solution)/shard_map/ppermute | solution.py:15
  18.5 14.7 %collective-permute-start.2 = (f32[8,128,128]{2,1,0:T(8,128)}, f32[8,128,128]{2,1,0:T(8,128)}, u32[]{:S(2)}, u32[]{:S(2)}) collective-permute-start(f32[8,128,128]{2,1,0:T(8,128)} %get-tuple-element.10), channel_id=1, source_target_pairs={{0,8},{16,24},{32,40},{48,56},{64,72},{80,88},{96,104},{112,120},{... | collective-permute-start | bytes 1572872 | tf_op jit(solution)/shard_map/ppermute | solution.py:15
  20.5 23.9 %collective-permute-start.4 = (f32[8,128,128]{2,1,0:T(8,128)}, f32[8,128,128]{2,1,0:T(8,128)S(1)}, u32[]{:S(2)}, u32[]{:S(2)}) collective-permute-start(f32[8,128,128]{2,1,0:T(8,128)} %get-tuple-element.11), channel_id=1, source_target_pairs={{0,8},{16,24},{32,40},{48,56},{64,72},{80,88},{96,104},{112,120},{... | collective-permute-start | bytes 1572872 | tf_op jit(solution)/shard_map/ppermute | solution.py:15
  23.8 20.5 %collective-permute-start.5 = (f32[8,128,128]{2,1,0:T(8,128)}, f32[8,128,128]{2,1,0:T(8,128)S(1)}, u32[]{:S(2)}, u32[]{:S(2)}) collective-permute-start(f32[8,128,128]{2,1,0:T(8,128)} %get-tuple-element.12), channel_id=1, source_target_pairs={{8,16},{24,32},{40,48},{56,64},{72,80},{88,96},{104,112},{120,128}... | collective-permute-start | bytes 1572872 | tf_op jit(solution)/shard_map/ppermute | solution.py:15
  30.5 25.1 %collective-permute-start.1 = (f32[8,128,128]{2,1,0:T(8,128)}, f32[8,128,128]{2,1,0:T(8,128)S(1)}, u32[]{:S(2)}, u32[]{:S(2)}) collective-permute-start(f32[8,128,128]{2,1,0:T(8,128)} %collective-permute-done), channel_id=1, source_target_pairs={{0,8},{16,24},{32,40},{48,56},{64,72},{80,88},{96,104},{112,120},{... | collective-permute-start | bytes 1572872 | tf_op jit(solution)/shard_map/ppermute | solution.py:15
  33.2 22.4 %collective-permute-start.3 = (f32[8,128,128]{2,1,0:T(8,128)}, f32[8,128,128]{2,1,0:T(8,128)S(1)}, u32[]{:S(2)}, u32[]{:S(2)}) collective-permute-start(f32[8,128,128]{2,1,0:T(8,128)} %collective-permute-done.2), channel_id=1, source_target_pairs={{8,16},{24,32},{40,48},{56,64},{72,80},{88,96},{104,112},{120,128}... | collective-permute-start | bytes 1572872 | tf_op jit(solution)/shard_map/ppermute | solution.py:15
  55.7 13.6 %copy-start.4 = (f32[1024]{0:T(1024)S(1)}, f32[1024]{0:T(1024)}, u32[]{:S(2)}) copy-start(f32[1024]{0:T(1024)} %param.11) | copy-start | bytes 12292

commit v5 on v0

v5 whole, which is shorter than its diff:
```python
import functools
import jax
import jax.numpy as jnp
from jax import lax
from jax.experimental import pallas as pl
from jax.experimental.pallas import tpu as pltpu
from jax.sharding import PartitionSpec as P

EPS = 1e-05
F32 = jnp.float32
BF16 = jnp.bfloat16
EARLY = 2
TILE = 8
MIB = 1024 * 1024


def swapped(block, axis, first):
    size = lax.axis_size(axis)
    pairs = [((first + i) % size, (first + i + 1) % size) for i in range(0, size, 2)]
    return lax.ppermute(block, axis, pairs + [(b, a) for a, b in pairs])


def side_of(device):
    return 2 * lax.rem(device, 2) - 1


def start_all(copies):
    for copy in copies:
        copy.start()


def wait_all(copies):
    for copy in copies:
        copy.wait()


def products(query, state):
    q_high = query.astype(BF16).astype(F32)
    both = jnp.concatenate([q_high, query - q_high], axis=0).astype(BF16)
    high = state.astype(BF16)
    low = (state - high.astype(F32)).astype(BF16)
    first = jnp.dot(both, high, preferred_element_type=F32)
    second = jnp.dot(both, low, preferred_element_type=F32)
    return first[:TILE] + first[TILE:] + second[:TILE]


def pick_kernel(shards, live, strides, place, shard_hbm, slot_hbm, query, states, *refs):
    n_rows = len(strides)
    outs = refs[:n_rows]
    shard_ref, slot_ref, held, tiles, sems, sems_out = refs[n_rows:]
    rows, dim = held.shape[1:]
    device = place[0]
    plan = [
        pltpu.make_async_copy(shard_hbm, shard_ref, sems.at[n_rows]),
        pltpu.make_async_copy(slot_hbm, slot_ref, sems.at[n_rows + 1]),
    ]
    start_all(plan)
    for head in range(rows // dim):
        tiles[head * TILE : (head + 1) * TILE] = query[:, head * dim : (head + 1) * dim]
    copies_out = [
        pltpu.make_async_copy(
            tiles, outs[n].at[rows : rows + tiles.shape[0]], sems_out.at[n_rows + n]
        )
        for n in range(2)
    ]
    start_all(copies_out)
    wait_all(plan)
    copies = []
    for n, stride in enumerate(strides):
        target = lax.rem(device + stride * side_of(device) + shards, shards)
        slot = jnp.int32(0)
        for row in range(live):
            mine = shard_ref[target * live + row] == device
            slot = jnp.where(mine, slot_ref[target * live + row], slot)
        copy = pltpu.make_async_copy(states.at[slot], held.at[n], sems.at[n])
        copy.start()
        copies.append(copy)
    for n, copy in enumerate(copies):
        copy.wait()
        copy_out = pltpu.make_async_copy(
            held.at[n], outs[n].at[0:rows], sems_out.at[n]
        )
        copy_out.start()
        copies_out.append(copy_out)
    wait_all(copies_out)


def pick(place, from_shard, from_slot, query, states, shards, live, strides):
    rows, dim = states.shape[1:]
    tile_rows = rows // dim * TILE
    fixed = [
        pltpu.with_memory_space_constraint(x, pltpu.HBM)
        for x in (from_shard, from_slot, states)
    ]
    hbm = pl.BlockSpec(memory_space=pltpu.HBM)
    return pl.pallas_call(
        functools.partial(pick_kernel, shards, live, strides),
        out_shape=[jax.ShapeDtypeStruct((rows + tile_rows, dim), F32)] * 2
        + [jax.ShapeDtypeStruct((rows, dim), F32)] * (len(strides) - 2),
        in_specs=[
            pl.BlockSpec(memory_space=pltpu.SMEM),
            hbm,
            hbm,
            pl.BlockSpec(memory_space=pltpu.VMEM),
            hbm,
        ],
        out_specs=[pl.BlockSpec(memory_space=pl.ANY)] * len(strides),
        scratch_shapes=[
            pltpu.SMEM(from_shard.shape, jnp.int32),
            pltpu.SMEM(from_slot.shape, jnp.int32),
            pltpu.VMEM((len(strides), rows, dim), F32),
            pltpu.VMEM((tile_rows, dim), F32),
            pltpu.SemaphoreType.DMA((len(strides) + 2,)),
            pltpu.SemaphoreType.DMA((len(strides) + 2,)),
        ],
        compiler_params=pltpu.CompilerParams(vmem_limit_bytes=6 * MIB),
        name="pick_rows",
    )(place, fixed[0], fixed[1], query, fixed[2])


def relay_kernel(from_1, from_0, lead_1, lead_0, rest_1, rest_0, held, made, sems, sems_out):
    dim = held.shape[2]
    heads = rest_0.shape[0] // dim + EARLY
    rows, early = heads * dim, EARLY * dim
    tile_rows = heads * TILE
    copies = [
        pltpu.make_async_copy(source, held.at[n], sems.at[n])
        for n, source in enumerate((from_0, from_1))
    ]
    start_all(copies)
    copies_out = []

    def send(source, target):
        copy = pltpu.make_async_copy(source, target, sems_out.at[len(copies_out)])
        copy.start()
        copies_out.append(copy)

    wait_all(copies)
    for n, (lead, rest) in enumerate(((lead_1, rest_1), (lead_0, rest_0))):
        send(held.at[n, early:rows], rest)
        send(held.at[n, 0:early], lead.at[tile_rows : tile_rows + early])
    for n, lead in enumerate((lead_1, lead_0)):
        for head in range(heads):
            query = held[1 - n, rows + head * TILE : rows + (head + 1) * TILE]
            state = held[n, head * dim : (head + 1) * dim]
            made[n, head * TILE : (head + 1) * TILE] = products(query, state)
        send(made.at[n], lead.at[0:tile_rows])
    wait_all(copies_out)


def relay(from_1, from_0, heads):
    dim = from_0.shape[1]
    lead = jax.ShapeDtypeStruct((heads * TILE + EARLY * dim, dim), F32)
    rest = jax.ShapeDtypeStruct(((heads - EARLY) * dim, dim), F32)
    anywhere = pl.BlockSpec(memory_space=pl.ANY)
    return pl.pallas_call(
        relay_kernel,
        out_shape=[lead, lead, rest, rest],
        in_specs=[anywhere] * 2,
        out_specs=[anywhere] * 4,
        scratch_shapes=[
            pltpu.VMEM((2,) + from_0.shape, F32),
            pltpu.VMEM((2, heads * TILE, dim), F32),
            pltpu.SemaphoreType.DMA((2,)),
            pltpu.SemaphoreType.DMA((6,)),
        ],
        compiler_params=pltpu.CompilerParams(vmem_limit_bytes=6 * MIB),
        name="relay_rows",
    )(from_1, from_0)


def gap_of(row, shards, live, place, shard_ref):
    device = place[0]
    return lax.rem(device - shard_ref[device * live + row] + shards, shards)


def at_stride(gap, stride, shards, place):
    return gap == lax.rem(stride * side_of(place[0]) + shards, shards)


def raw_kernel(
    shards, live, place, shard_ref, slot_ref, states, lead_1, lead_0, near_1, near_0,
    query, grown, base, raw, sums, held, made, sem_row, sem_tile,
):
    rows, dim = held.shape[1:]
    heads = rows // dim
    tile_rows = heads * TILE
    device = place[0]
    late = []
    for row in range(live):
        gap = gap_of(row, shards, live, place, shard_ref)
        slot = slot_ref[device * live + row]
        sources = [
            (gap == 0, states.at[slot]),
            (at_stride(gap, 1, shards, place), near_0),
            (at_stride(gap, -1, shards, place), near_1),
        ]
        for here, source in sources:

            @pl.when(here)
            def _():
                pltpu.make_async_copy(source, held.at[row], sem_row.at[row]).start()

        far_0 = at_stride(gap, 2, shards, place)
        far_1 = at_stride(gap, -2, shards, place)
        for here, lead in ((far_0, lead_0), (far_1, lead_1)):

            @pl.when(here)
            def _():
                pltpu.make_async_copy(
                    lead.at[0:tile_rows], made.at[row], sem_tile.at[row]
                ).start()

        late.append(jnp.logical_or(far_0, far_1))
    for row in range(live):

        @pl.when(late[row])
        def _():
            pltpu.make_async_copy(
                lead_0.at[0:tile_rows], made.at[row], sem_tile.at[row]
            ).wait()

        @pl.when(jnp.logical_not(late[row]))
        def _():
            pltpu.make_async_copy(near_0, held.at[row], sem_row.at[row]).wait()
            for head in range(heads):
                span = slice(head * dim, (head + 1) * dim)
                made[row, head * TILE : (head + 1) * TILE] = products(
                    query[:, span], held[row, span]
                )

    which = lax.rem(lax.broadcasted_iota(jnp.int32, (TILE, dim), 0), live)
    total = jnp.zeros((TILE, dim), F32)
    for head in range(heads):
        span = slice(head * dim, (head + 1) * dim)
        tile = made[0, head * TILE : (head + 1) * TILE]
        for row in range(1, live):
            other = made[row, head * TILE : (head + 1) * TILE]
            tile = jnp.where(which == row, other, tile)
        tile = tile * grown[:, span] + base[:, span]
        raw[:, span] = tile
        total = total + tile * tile
    total = jnp.broadcast_to(jnp.sum(total, axis=1, keepdims=True), (TILE, dim))
    for peer in range(sums.shape[0]):
        sums[peer] = total


def raw_of(place, from_shard, from_slot, states, arrived, small, shards, live, group):
    rows, dim = states.shape[1:]
    smem = pl.BlockSpec(memory_space=pltpu.SMEM)
    vmem = pl.BlockSpec(memory_space=pltpu.VMEM)
    anywhere = pl.BlockSpec(memory_space=pl.ANY)
    return pl.pallas_call(
        functools.partial(raw_kernel, shards, live),
        out_shape=[
            jax.ShapeDtypeStruct((TILE, rows), F32),
            jax.ShapeDtypeStruct((group, TILE, dim), F32),
        ],
        in_specs=[smem] * 3 + [anywhere] * (1 + len(arrived)) + [vmem] * len(small),
        out_specs=[vmem] * 2,
        scratch_shapes=[
            pltpu.VMEM((live, rows, dim), F32),
            pltpu.VMEM((live, rows // dim * TILE, dim), F32),
            pltpu.SemaphoreType.DMA((live,)),
            pltpu.SemaphoreType.DMA((live,)),
        ],
        compiler_params=pltpu.CompilerParams(vmem_limit_bytes=6 * MIB),
        cost_estimate=pl.CostEstimate(flops=10**12, bytes_accessed=MIB, transcendentals=0),
        name="raw_rows",
    )(place, from_shard, from_slot, states, *arrived, *small)


def final_kernel(
    shards, live, features, place, shard_ref, slot_ref, states, lead_1, lead_0,
    near_1, near_0, rest_1, rest_0, totals, raw, gated, keys, values, decay,
    attended, final, held, made, sem_in, sem_out,
):
    rows, dim = held.shape[1:]
    heads = rows // dim
    early, tile_rows = EARLY * dim, heads * TILE
    device = place[0]
    spans = (slice(0, early), slice(early, rows))
    for row in range(live):
        gap = gap_of(row, shards, live, place, shard_ref)
        slot = slot_ref[device * live + row]
        lead_span = slice(tile_rows, tile_rows + early)
        sources = [
            (gap == 0, [states.at[slot, span] for span in spans]),
            (at_stride(gap, 1, shards, place), [near_0.at[span] for span in spans]),
            (at_stride(gap, -1, shards, place), [near_1.at[span] for span in spans]),
            (at_stride(gap, 2, shards, place), [lead_0.at[lead_span], rest_0]),
            (at_stride(gap, -2, shards, place), [lead_1.at[lead_span], rest_1]),
        ]
        for here, parts in sources:

            @pl.when(here)
            def _():
                for part, source in enumerate(parts):
                    pltpu.make_async_copy(
                        source, held.at[row, spans[part]], sem_in.at[row, part]
                    ).start()

    total = totals[0]
    for peer in range(1, totals.shape[0]):
        total = total + totals[peer]
    scale = lax.rsqrt(total / features + EPS)
    for head in range(heads):
        span = slice(head * dim, (head + 1) * dim)
        tile = raw[:, span] * scale * gated[:, span]
        for step in range(attended.shape[0]):
            attended[step, :, span] = tile[step * live : (step + 1) * live].astype(BF16)
    copies_out = []
    for row in range(live):
        for part, span in enumerate(spans):
            pltpu.make_async_copy(
                near_0.at[span], held.at[row, span], sem_in.at[row, part]
            ).wait()
            for head in range(span.start // dim, span.stop // dim):
                block = slice(head * dim, (head + 1) * dim)
                outer = lax.dot_general(
                    keys[row, :, block],
                    values[row, :, block],
                    (((0,), (0,)), ((), ())),
                    preferred_element_type=F32,
                )
                made[row, block] = decay[:, block] * held[row, block] + outer
            copy = pltpu.make_async_copy(
                made.at[row, span], final.at[row, span], sem_out.at[row, part]
            )
            copy.start()
            copies_out.append(copy)
    wait_all(copies_out)


def final_of(
    place, from_shard, from_slot, states, arrived, small, shards, live, steps, features
):
    rows, dim = states.shape[1:]
    smem = pl.BlockSpec(memory_space=pltpu.SMEM)
    vmem = pl.BlockSpec(memory_space=pltpu.VMEM)
    anywhere = pl.BlockSpec(memory_space=pl.ANY)
    return pl.pallas_call(
        functools.partial(final_kernel, shards, live, features),
        out_shape=[
            jax.ShapeDtypeStruct((steps, live, rows), BF16),
            jax.ShapeDtypeStruct((live, rows, dim), F32),
        ],
        in_specs=[smem] * 3 + [anywhere] * (1 + len(arrived)) + [vmem] * len(small),
        out_specs=[vmem, anywhere],
        scratch_shapes=[
            pltpu.VMEM((live, rows, dim), F32),
            pltpu.VMEM((live, rows, dim), F32),
            pltpu.SemaphoreType.DMA((live, 2)),
            pltpu.SemaphoreType.DMA((live, 2)),
        ],
        compiler_params=pltpu.CompilerParams(vmem_limit_bytes=8 * MIB),
        name="final_rows",
    )(place, from_shard, from_slot, states, *arrived, *small)


def split(x):
    high = lax.reduce_precision(x, 8, 7)
    return high.astype(BF16), (x - high).astype(BF16)


def on_device(states, from_shard, from_slot, projected, decay_rate, norm_gain):
    shards, group = lax.axis_size("dp"), lax.axis_size("tensor")
    steps, live = projected.shape[:2]
    slots, heads, dim = states.shape[:3]
    width = heads * dim
    place = lax.axis_index("dp").astype(jnp.int32).reshape(1)
    states = states.reshape(slots, width, dim)
    activity = projected.astype(F32)

    def tile(x):
        flat = x.reshape(steps * live, width)
        return jnp.pad(flat, ((0, TILE - steps * live), (0, 0)))

    queries, keys, values = (jax.nn.silu(activity[:, :, i]) for i in range(3))
    query = tile(queries)

    rows = pick(
        place, from_shard, from_slot, query, states, shards, live, (-2, 2, -1, 1)
    )
    half_1, half_0 = swapped(rows[1], "dp", 1), swapped(rows[0], "dp", 0)
    near_1, near_0 = swapped(rows[3], "dp", 1), swapped(rows[2], "dp", 0)
    sent = relay(half_1, half_0, heads)
    lead_1, lead_0 = swapped(sent[0], "dp", 1), swapped(sent[1], "dp", 0)
    rest_1, rest_0 = swapped(sent[2], "dp", 1), swapped(sent[3], "dp", 0)

    retain = jnp.repeat(jnp.exp(-decay_rate), dim)
    power = [jnp.ones_like(retain)]
    for _ in range(steps):
        power.append(power[-1] * retain)
    base = []
    for t in range(steps):
        total = 0.0
        for u in range(t + 1):
            match = (queries[t] * keys[u]).reshape(live, heads, dim)
            match = jnp.broadcast_to(jnp.sum(match, axis=-1, keepdims=True), match.shape)
            total = total + power[t - u] * match.reshape(live, width) * values[u]
        base.append(total)
    base = tile(jnp.stack(base))
    by_step = (steps, live, width)
    grown = tile(jnp.broadcast_to(jnp.stack(power[1:])[:, None], by_step))
    gated = tile(jax.nn.sigmoid(activity[:, :, 3]) * norm_gain)
    faded = keys * jnp.stack(power[steps - 1 :: -1])[:, None]

    def stacked(*parts):
        whole = jnp.concatenate([jnp.swapaxes(part, 0, 1) for part in parts], axis=1)
        return jnp.pad(whole, ((0, 0), (0, 16 - whole.shape[1]), (0, 0)))

    k_high, k_low = split(faded)
    v_high, v_low = split(values)
    raw, sums = raw_of(
        place, from_shard, from_slot, states, (lead_1, lead_0, near_1, near_0),
        (query, grown, base), shards, live, group,
    )
    totals = lax.all_to_all(sums, "tensor", 0, 0)
    attended, final = final_of(
        place, from_shard, from_slot, states,
        (lead_1, lead_0, near_1, near_0, rest_1, rest_0),
        (
            totals,
            raw,
            gated,
            stacked(k_high, k_low, k_high),
            stacked(v_high, v_high, v_low),
            power[steps].reshape(1, width),
        ),
        shards, live, steps, width * group,
    )
    return attended, final.reshape(live, heads, dim, dim)


def solution(mesh):
    return jax.shard_map(
        on_device,
        mesh=mesh,
        in_specs=(
            P("dp", "tensor", None, None),
            P(),
            P(),
            P(None, "dp", None, "tensor"),
            P("tensor"),
            P("tensor"),
        ),
        out_specs=(P(None, "dp", "tensor"), P("dp", "tensor", None, None)),
        check_vma=False,
    )
```

time: 89.8 us -> 70 us (0.78)
  the two profiles are of different devices: /device:TPU:102 before, /device:TPU:1 now
where the time goes in v5:
time: 70 us; the launch traced here: 69.4 us
  starting transfers between devices  41.9 us (60%)
  Pallas kernels  11.8 us (17%)
  waiting for transfers between devices  9.07 us (13%)
  other arithmetic  4.68 us (7%)
  between operations  1.03 us (1%)
  local copies, waits for them, and re-layouts  0.96 us (1%)
    ppermute x8, starting transfers between devices, swapped(): return lax.ppermute(block, axis, pairs + [(b, a) for a, b in pairs])  34 us
    all_to_all x1, starting transfers between devices, on_device(): totals = lax.all_to_all(sums, 'tensor', 0, 0)  7.92 us
    all_to_all x1, waiting for transfers between devices, on_device(): totals = lax.all_to_all(sums, 'tensor', 0, 0)  4.57 us
    ppermute x8, waiting for transfers between devices, swapped(): return lax.ppermute(block, axis, pairs + [(b, a) for a, b in pairs])  4.5 us
    pallas_call x1, Pallas kernels, pick(): pl.pallas_call(functools.partial(pick_kernel, shards, live, strides), out...  3.99 us
    pallas_call x1, Pallas kernels, final_of(): pl.pallas_call(functools.partial(final_kernel, shards, live, features), o...  3.81 us
    pallas_call x1, Pallas kernels, raw_of(): pl.pallas_call(functools.partial(raw_kernel, shards, live), out_shape=[ja...  2.85 us
    transpose x3, other arithmetic, stacked(): jnp.swapaxes(part, 0, 1)  1.89 us
  transfers between devices with their start and end apart: 9, of which 4 were waited for; matrix products, arithmetic and copies ran while one was open for 6% of the time, Pallas kernels for 6%

profile of v5, /device:TPU:1, one launch (start us, length us, event | category | flops | bytes accessed | tf_op | source)
XLA Modules:
  0.0 69.4 jit_solution(9561582677497726657)
XLA Ops:
  0.7 0.8 %copy_convert_fusion = f32[3,2,4,1024]{3,0,1,2:T(4,128)S(1)} fusion(bf16[3,2,4,1024]{3,2,1,0:T(4,128)(2,1)} %param.9), kind=kLoop, calls=%fused_computation.17 | loop fusion | flops 24576 | bytes 147456 | tf_op jit(solution)/shard_map/convert_element_type | solution.py:373
  1.7 4.0 %pick_rows.1 = (f32[1088,128]{1,0:T(8,128)}, f32[1088,128]{1,0:T(8,128)}, f32[1024,128]{1,0:T(8,128)}, f32[1024,128]{1,0:T(8,128)}) custom-call(s32[1]{0:T(128)} %bitcast.place, s32[128]{0:T(128)} %shard_ref.3, s32[128]{0:T(128)} %slot_ref.3, f32[8,1024]{1,0:T(8,128)S(1)} %pad.20.query, f32[4,1024,128]{2,1,0:T(8,128)} %bitcast.57), custom_call_target="tpu_custom_call" | custom-call | tf_op jit(solution)/shard_map/pick_rows/pallas_call | solution.py:96
  5.7 14.3 %collective-permute-start = (f32[1088,128]{1,0:T(8,128)}, f32[1088,128]{1,0:T(8,128)S(1)}, u32[]{:S(2)}, u32[]{:S(2)}) collective-permute-start(f32[1088,128]{1,0:T(8,128)} %get-tuple-element.14), channel_id=1, source_target_pairs={{8,16},{24,32},{40,48},{56,64},{72,80},{88,96},{104,112},{120,128}... | collective-permute-start | bytes 1671176 | tf_op jit(solution)/shard_map/ppermute | solution.py:20
  20.0 1.9 %collective-permute-start.1 = (f32[1088,128]{1,0:T(8,128)}, f32[1088,128]{1,0:T(8,128)S(1)}, u32[]{:S(2)}, u32[]{:S(2)}) collective-permute-start(f32[1088,128]{1,0:T(8,128)} %get-tuple-element.15), channel_id=1, source_target_pairs={{0,8},{16,24},{32,40},{48,56},{64,72},{80,88},{96,104},{112,120},{... | collective-permute-start | bytes 1671176 | tf_op jit(solution)/shard_map/ppermute | solution.py:20
  21.9 2.7 %collective-permute-start.4 = (f32[1024,128]{1,0:T(8,128)}, f32[1024,128]{1,0:T(8,128)}, u32[]{:S(2)}, u32[]{:S(2)}) collective-permute-start(f32[1024,128]{1,0:T(8,128)} %get-tuple-element.18), channel_id=1, source_target_pairs={{8,16},{24,32},{40,48},{56,64},{72,80},{88,96},{104,112},{120,128}... | collective-permute-start | bytes 1572872 | tf_op jit(solution)/shard_map/ppermute | solution.py:20
  24.7 2.6 %collective-permute-start.5 = (f32[1024,128]{1,0:T(8,128)}, f32[1024,128]{1,0:T(8,128)}, u32[]{:S(2)}, u32[]{:S(2)}) collective-permute-start(f32[1024,128]{1,0:T(8,128)} %get-tuple-element.19), channel_id=1, source_target_pairs={{0,8},{16,24},{32,40},{48,56},{64,72},{80,88},{96,104},{112,120},{... | collective-permute-start | bytes 1572872 | tf_op jit(solution)/shard_map/ppermute | solution.py:20
  27.6 0.5 copy-done.1
  28.2 0.7 fusion.26
  28.9 0.2 fusion.3
  29.9 0.6 fusion.25
  30.7 0.6 broadcast_multiply_fusion
  31.3 1.3 %collective-permute-done.from_1 = f32[1088,128]{1,0:T(8,128)S(1)} collective-permute-done((f32[1088,128]{1,0:T(8,128)}, f32[1088,128]{1,0:T(8,128)S(1)}, u32[]{:S(2)}, u32[]{:S(2)}) %collective-permute-start) | collective-permute-done | bytes 557088 | tf_op jit(solution)/shard_map/ppermute | solution.py:20
  32.6 2.8 %collective-permute-done.1.from_0 = f32[1088,128]{1,0:T(8,128)S(1)} collective-permute-done((f32[1088,128]{1,0:T(8,128)}, f32[1088,128]{1,0:T(8,128)S(1)}, u32[]{:S(2)}, u32[]{:S(2)}) %collective-permute-start.1) | collective-permute-done | bytes 557088 | tf_op jit(solution)/shard_map/ppermute | solution.py:20
  35.4 1.2 %relay_rows.1 = (f32[320,128]{1,0:T(8,128)S(1)}, f32[320,128]{1,0:T(8,128)S(1)}, f32[768,128]{1,0:T(8,128)}, f32[768,128]{1,0:T(8,128)}) custom-call(f32[1088,128]{1,0:T(8,128)S(1)} %collective-permute-done.from_1, f32[1088,128]{1,0:T(8,128)S(1)} %collective-permute-done.1.from_0), custom_call_target="tpu_custom_call" | custom-call | tf_op jit(solution)/shard_map/relay_rows/pallas_call | solution.py:156
  36.6 3.5 %collective-permute-start.2 = (f32[320,128]{1,0:T(8,128)S(1)}, f32[320,128]{1,0:T(8,128)S(1)}, u32[]{:S(2)}, u32[]{:S(2)}) collective-permute-start(f32[320,128]{1,0:T(8,128)S(1)} %get-tuple-element.16), channel_id=1, source_target_pairs={{8,16},{24,32},{40,48},{56,64},{72,80},{88,96},{104,112},{120,128}... | collective-permute-start | bytes 491528 | tf_op jit(solution)/shard_map/ppermute | solution.py:20
  40.1 1.9 %collective-permute-start.3 = (f32[320,128]{1,0:T(8,128)S(1)}, f32[320,128]{1,0:T(8,128)S(1)}, u32[]{:S(2)}, u32[]{:S(2)}) collective-permute-start(f32[320,128]{1,0:T(8,128)S(1)} %get-tuple-element.17), channel_id=1, source_target_pairs={{0,8},{16,24},{32,40},{48,56},{64,72},{80,88},{96,104},{112,120},{... | collective-permute-start | bytes 491528 | tf_op jit(solution)/shard_map/ppermute | solution.py:20
  42.0 0.6 fusion.23
  42.6 5.1 %collective-permute-start.6 = (f32[768,128]{1,0:T(8,128)}, f32[768,128]{1,0:T(8,128)}, u32[]{:S(2)}, u32[]{:S(2)}) collective-permute-start(f32[768,128]{1,0:T(8,128)} %get-tuple-element.20), channel_id=1, source_target_pairs={{8,16},{24,32},{40,48},{56,64},{72,80},{88,96},{104,112},{120,128}... | collective-permute-start | bytes 1179656 | tf_op jit(solution)/shard_map/ppermute | solution.py:20
  47.7 1.9 %collective-permute-start.7 = (f32[768,128]{1,0:T(8,128)}, f32[768,128]{1,0:T(8,128)}, u32[]{:S(2)}, u32[]{:S(2)}) collective-permute-start(f32[768,128]{1,0:T(8,128)} %get-tuple-element.21), channel_id=1, source_target_pairs={{0,8},{16,24},{32,40},{48,56},{64,72},{80,88},{96,104},{112,120},{... | collective-permute-start | bytes 1179656 | tf_op jit(solution)/shard_map/ppermute | solution.py:20
  49.7 0.4 collective-permute-done.3.lead_0
  50.1 2.8 %raw_rows.1 = (f32[8,1024]{1,0:T(8,128)S(1)}, f32[8,8,128]{2,1,0:T(8,128)}) custom-call(s32[1]{0:T(128)} %bitcast.place, s32[128]{0:T(128)S(1)} %copy-done.3, s32[128]{0:T(128)S(1)} %copy-done.4, f32[4,1024,128]{2,1,0:T(8,128)S(1)} %bitcast.58, f32[320,128]{1,0:T(8,128)S(1)} %collective-permute-done.2.lead_1, f32[320,128]{1,0:T(8,128)S(1)} %collective-permute-done.3.lead_0, ...), custom_call_target="tpu_custom_call" | custom-call | flops 999999995904 | bytes 1048576 | tf_op jit(solution)/shard_map/raw_rows/pallas_call | solution.py:253
  53.0 7.9 %all-to-all-start = ((f32[8,8,128]{2,1,0:T(8,128)}), f32[8,8,128]{2,1,0:T(8,128)S(1)}, u32[]{:S(2)}, u32[]{:S(2)}) async-start(f32[8,8,128]{2,1,0:T(8,128)} %get-tuple-element.22), calls=%async_computation | async-start | bytes 65536 | tf_op jit(solution)/shard_map/all_to_all | solution.py:419
  61.0 4.6 %all-to-all-done.totals = f32[8,8,128]{2,1,0:T(8,128)S(1)} async-done(((f32[8,8,128]{2,1,0:T(8,128)}), f32[8,8,128]{2,1,0:T(8,128)S(1)}, u32[]{:S(2)}, u32[]{:S(2)}) %all-to-all-start) | async-done | bytes 32800 | tf_op jit(solution)/shard_map/all_to_all | solution.py:419
  65.6 3.8 %final_rows.1 = (bf16[3,2,1024]{2,1,0:T(2,128)(2,1)}, f32[2,1024,128]{2,1,0:T(8,128)}) custom-call(s32[1]{0:T(128)} %bitcast.place, s32[128]{0:T(128)S(1)} %copy-done.3, s32[128]{0:T(128)S(1)} %copy-done.4, f32[4,1024,128]{2,1,0:T(8,128)S(1)} %bitcast.59, f32[320,128]{1,0:T(8,128)S(1)} %collective-permute-done.2.lead_1, ...), custom_call_target="tpu_custom_call" | custom-call | tf_op jit(solution)/shard_map/final_rows/pallas_call | solution.py:342
  (58 shorter events, 1.6 us)
Async XLA Ops:
  0.6 26.6 %copy-start.11 = (f32[8]{0:T(128)S(1)}, f32[8]{0:T(128)}, u32[]{:S(2)}) copy-start(f32[8]{0:T(128)} %param.10) | copy-start | bytes 100
  0.6 30.0 %copy-start.10 = (f32[1024]{0:T(1024)S(1)}, f32[1024]{0:T(1024)}, u32[]{:S(2)}) copy-start(f32[1024]{0:T(1024)} %param.11) | copy-start | bytes 12292
  1.6 48.4 %copy-start = (f32[4,8,128,128]{3,2,1,0:T(8,128)S(1)}, f32[4,8,128,128]{3,2,1,0:T(8,128)}, u32[]{:S(2)}) copy-start(f32[4,8,128,128]{3,2,1,0:T(8,128)} %param.6) | copy-start | bytes 6291460
  1.7 48.4 %copy-start.3 = (s32[128]{0:T(128)S(1)}, s32[128]{0:T(128)}, u32[]{:S(2)}) copy-start(s32[128]{0:T(128)} %shard_ref.3) | copy-start | bytes 1540
  1.7 48.4 %copy-start.4 = (s32[128]{0:T(128)S(1)}, s32[128]{0:T(128)}, u32[]{:S(2)}) copy-start(s32[128]{0:T(128)} %slot_ref.3) | copy-start | bytes 1540
  5.7 26.9 %collective-permute-start = (f32[1088,128]{1,0:T(8,128)}, f32[1088,128]{1,0:T(8,128)S(1)}, u32[]{:S(2)}, u32[]{:S(2)}) collective-permute-start(f32[1088,128]{1,0:T(8,128)} %get-tuple-element.14), channel_id=1, source_target_pairs={{8,16},{24,32},{40,48},{56,64},{72,80},{88,96},{104,112},{120,128}... | collective-permute-start | bytes 1671176 | tf_op jit(solution)/shard_map/ppermute | solution.py:20
  20.0 15.4 %collective-permute-start.1 = (f32[1088,128]{1,0:T(8,128)}, f32[1088,128]{1,0:T(8,128)S(1)}, u32[]{:S(2)}, u32[]{:S(2)}) collective-permute-start(f32[1088,128]{1,0:T(8,128)} %get-tuple-element.15), channel_id=1, source_target_pairs={{0,8},{16,24},{32,40},{48,56},{64,72},{80,88},{96,104},{112,120},{... | collective-permute-start | bytes 1671176 | tf_op jit(solution)/shard_map/ppermute | solution.py:20
  21.9 25.8 %collective-permute-start.4 = (f32[1024,128]{1,0:T(8,128)}, f32[1024,128]{1,0:T(8,128)}, u32[]{:S(2)}, u32[]{:S(2)}) collective-permute-start(f32[1024,128]{1,0:T(8,128)} %get-tuple-element.18), channel_id=1, source_target_pairs={{8,16},{24,32},{40,48},{56,64},{72,80},{88,96},{104,112},{120,128}... | collective-permute-start | bytes 1572872 | tf_op jit(solution)/shard_map/ppermute | solution.py:20
  24.7 25.0 %collective-permute-start.5 = (f32[1024,128]{1,0:T(8,128)}, f32[1024,128]{1,0:T(8,128)}, u32[]{:S(2)}, u32[]{:S(2)}) collective-permute-start(f32[1024,128]{1,0:T(8,128)} %get-tuple-element.19), channel_id=1, source_target_pairs={{0,8},{16,24},{32,40},{48,56},{64,72},{80,88},{96,104},{112,120},{... | collective-permute-start | bytes 1572872 | tf_op jit(solution)/shard_map/ppermute | solution.py:20
  27.5 0.6 copy-start.1
  36.6 13.1 %collective-permute-start.2 = (f32[320,128]{1,0:T(8,128)S(1)}, f32[320,128]{1,0:T(8,128)S(1)}, u32[]{:S(2)}, u32[]{:S(2)}) collective-permute-start(f32[320,128]{1,0:T(8,128)S(1)} %get-tuple-element.16), channel_id=1, source_target_pairs={{8,16},{24,32},{40,48},{56,64},{72,80},{88,96},{104,112},{120,128}... | collective-permute-start | bytes 491528 | tf_op jit(solution)/shard_map/ppermute | solution.py:20
  40.1 9.9 %collective-permute-start.3 = (f32[320,128]{1,0:T(8,128)S(1)}, f32[320,128]{1,0:T(8,128)S(1)}, u32[]{:S(2)}, u32[]{:S(2)}) collective-permute-start(f32[320,128]{1,0:T(8,128)S(1)} %get-tuple-element.17), channel_id=1, source_target_pairs={{0,8},{16,24},{32,40},{48,56},{64,72},{80,88},{96,104},{112,120},{... | collective-permute-start | bytes 491528 | tf_op jit(solution)/shard_map/ppermute | solution.py:20
  42.6 23.0 %collective-permute-start.6 = (f32[768,128]{1,0:T(8,128)}, f32[768,128]{1,0:T(8,128)}, u32[]{:S(2)}, u32[]{:S(2)}) collective-permute-start(f32[768,128]{1,0:T(8,128)} %get-tuple-element.20), channel_id=1, source_target_pairs={{8,16},{24,32},{40,48},{56,64},{72,80},{88,96},{104,112},{120,128}... | collective-permute-start | bytes 1179656 | tf_op jit(solution)/shard_map/ppermute | solution.py:20
  47.7 17.9 %collective-permute-start.7 = (f32[768,128]{1,0:T(8,128)}, f32[768,128]{1,0:T(8,128)}, u32[]{:S(2)}, u32[]{:S(2)}) collective-permute-start(f32[768,128]{1,0:T(8,128)} %get-tuple-element.21), channel_id=1, source_target_pairs={{0,8},{16,24},{32,40},{48,56},{64,72},{80,88},{96,104},{112,120},{... | collective-permute-start | bytes 1179656 | tf_op jit(solution)/shard_map/ppermute | solution.py:20
  50.1 10.8 %copy-start.6 = (bf16[2,3,1024]{2,1,0:T(4,128)(2,1)S(1)}, bf16[2,3,1024]{2,1,0:T(4,128)(2,1)}, u32[]{:S(2)}) copy-start(bf16[2,3,1024]{2,1,0:T(4,128)(2,1)} %fusion.23) | copy-start | bytes 36868
  50.1 10.8 %copy-start.7 = (bf16[2,3,1024]{2,1,0:T(4,128)(2,1)S(1)}, bf16[2,3,1024]{2,1,0:T(4,128)(2,1)}, u32[]{:S(2)}) copy-start(bf16[2,3,1024]{2,1,0:T(4,128)(2,1)} %fusion.25) | copy-start | bytes 36868
  50.1 10.8 %copy-start.8 = (bf16[2,3,1024]{2,1,0:T(4,128)(2,1)S(1)}, bf16[2,3,1024]{2,1,0:T(4,128)(2,1)}, u32[]{:S(2)}) copy-start(bf16[2,3,1024]{2,1,0:T(4,128)(2,1)} %get-tuple-element.26) | copy-start | bytes 36868
  50.1 10.8 %copy-start.9 = (bf16[2,3,1024]{2,1,0:T(4,128)(2,1)S(1)}, bf16[2,3,1024]{2,1,0:T(4,128)(2,1)}, u32[]{:S(2)}) copy-start(bf16[2,3,1024]{2,1,0:T(4,128)(2,1)} %get-tuple-element.33) | copy-start | bytes 36868
  50.1 10.9 %copy-start.5 = (f32[6,1024]{1,0:T(8,128)S(1)}, f32[6,1024]{1,0:T(8,128)}, u32[]{:S(2)}) copy-start(f32[6,1024]{1,0:T(8,128)} %broadcast_multiply_fusion) | copy-start | bytes 73732
  50.1 15.5 %copy-start.2 = (f32[1,1024]{1,0:T(1,128)S(1)}, f32[1,1024]{1,0:T(1,128)}, u32[]{:S(2)}) copy-start(f32[1,1024]{1,0:T(1,128)} %copy-done.1) | copy-start | bytes 12292
  53.0 12.6 %all-to-all-start = ((f32[8,8,128]{2,1,0:T(8,128)}), f32[8,8,128]{2,1,0:T(8,128)S(1)}, u32[]{:S(2)}, u32[]{:S(2)}) async-start(f32[8,8,128]{2,1,0:T(8,128)} %get-tuple-element.22), calls=%async_computation | async-start | bytes 65536 | tf_op jit(solution)/shard_map/all_to_all | solution.py:419

commit v6 on v0

v6 whole, which is shorter than its diff:
```python
import functools
import jax
import jax.numpy as jnp
from jax import lax
from jax.experimental import pallas as pl
from jax.experimental.pallas import tpu as pltpu
from jax.sharding import PartitionSpec as P

EPS = 1e-05
F32 = jnp.float32
BF16 = jnp.bfloat16
EARLY = 2
TILE = 8
MIB = 1024 * 1024
SMEM = pl.BlockSpec(memory_space=pltpu.SMEM)
VMEM = pl.BlockSpec(memory_space=pltpu.VMEM)
HBM = pl.BlockSpec(memory_space=pltpu.HBM)


def swapped(block, axis, first):
    size = lax.axis_size(axis)
    pairs = [((first + i) % size, (first + i + 1) % size) for i in range(0, size, 2)]
    return lax.ppermute(block, axis, pairs + [(b, a) for a, b in pairs])


def side_of(device):
    return 2 * lax.rem(device, 2) - 1


def start_all(copies):
    for copy in copies:
        copy.start()


def wait_all(copies):
    for copy in copies:
        copy.wait()


def in_hbm(*arrays):
    return [pltpu.with_memory_space_constraint(x, pltpu.HBM) for x in arrays]


def products(query, state):
    q_high = query.astype(BF16).astype(F32)
    both = jnp.concatenate([q_high, query - q_high], axis=0).astype(BF16)
    high = state.astype(BF16)
    low = (state - high.astype(F32)).astype(BF16)
    first = jnp.dot(both, high, preferred_element_type=F32)
    second = jnp.dot(both, low, preferred_element_type=F32)
    return first[:TILE] + first[TILE:] + second[:TILE]


def pick_kernel(shards, live, strides, place, shard_hbm, slot_hbm, projected, states, *refs):
    n_rows = len(strides)
    outs = refs[:n_rows]
    shard_ref, slot_ref, inputs, sems = refs[n_rows:]
    rows, dim = outs[-1].shape
    device = place[0]
    plan = [
        pltpu.make_async_copy(shard_hbm, shard_ref, sems.at[n_rows]),
        pltpu.make_async_copy(slot_hbm, slot_ref, sems.at[n_rows + 1]),
    ]
    load = pltpu.make_async_copy(projected, inputs, sems.at[n_rows + 2])
    start_all(plan)
    load.start()
    wait_all(plan)
    copies = []
    for n, stride in enumerate(strides):
        target = lax.rem(device + stride * side_of(device) + shards, shards)
        slot = jnp.int32(0)
        for row in range(live):
            mine = shard_ref[target * live + row] == device
            slot = jnp.where(mine, slot_ref[target * live + row], slot)
        copies.append(
            pltpu.make_async_copy(states.at[slot], outs[n].at[0:rows], sems.at[n])
        )
    start_all(copies)
    load.wait()
    tile_rows = rows // dim * TILE
    for n in range(2):
        outs[n][rows : rows + tile_rows] = jnp.zeros((tile_rows, dim), F32)
    for step in range(inputs.shape[0]):
        for row in range(live):
            query = jax.nn.silu(inputs[step, row].astype(F32))[0:1]
            for head in range(rows // dim):
                at = rows + head * TILE + step * live + row
                part = query[:, head * dim : (head + 1) * dim]
                for n in range(2):
                    outs[n][at : at + 1] = part
    wait_all(copies)


def pick(place, from_shard, from_slot, projected, states, shards, live, strides):
    rows, dim = states.shape[1:]
    tile_rows = rows // dim * TILE
    return pl.pallas_call(
        functools.partial(pick_kernel, shards, live, strides),
        out_shape=[jax.ShapeDtypeStruct((rows + tile_rows, dim), F32)] * 2
        + [jax.ShapeDtypeStruct((rows, dim), F32)] * (len(strides) - 2),
        in_specs=[SMEM] + [HBM] * 4,
        out_specs=[VMEM] * len(strides),
        scratch_shapes=[
            pltpu.SMEM(from_shard.shape, jnp.int32),
            pltpu.SMEM(from_slot.shape, jnp.int32),
            pltpu.VMEM(projected.shape, projected.dtype),
            pltpu.SemaphoreType.DMA((len(strides) + 3,)),
        ],
        compiler_params=pltpu.CompilerParams(vmem_limit_bytes=6 * MIB),
        name="pick_rows",
    )(place, *in_hbm(from_shard, from_slot, projected, states))


def relay_kernel(from_1, from_0, _, lead_1, lead_0, rest_1, rest_0):
    dim = from_1.shape[1]
    heads = rest_0.shape[0] // dim + EARLY
    rows, early = heads * dim, EARLY * dim
    tile_rows = heads * TILE
    for source, other, lead, rest in (
        (from_0, from_1, lead_1, rest_1),
        (from_1, from_0, lead_0, rest_0),
    ):
        for head in range(heads):
            part = slice(head * TILE, (head + 1) * TILE)
            query = other[rows + head * TILE : rows + (head + 1) * TILE]
            state = source[head * dim : (head + 1) * dim]
            lead[part] = products(query, state)
            if head < EARLY:
                lead[tile_rows + head * dim : tile_rows + (head + 1) * dim] = state
            else:
                rest[(head - EARLY) * dim : (head - EARLY + 1) * dim] = state


def relay(from_1, from_0, after, heads):
    dim = from_0.shape[1]
    lead = jax.ShapeDtypeStruct((heads * TILE + EARLY * dim, dim), F32)
    rest = jax.ShapeDtypeStruct(((heads - EARLY) * dim, dim), F32)
    return pl.pallas_call(
        relay_kernel,
        out_shape=[lead, lead, rest, rest],
        in_specs=[VMEM] * 3,
        out_specs=[VMEM] * 4,
        compiler_params=pltpu.CompilerParams(vmem_limit_bytes=6 * MIB),
        name="relay_rows",
    )(from_1, from_0, after)


def gap_of(row, shards, live, place, shard_ref):
    device = place[0]
    return lax.rem(device - shard_ref[device * live + row] + shards, shards)


def at_stride(gap, stride, shards, place):
    return gap == lax.rem(stride * side_of(place[0]) + shards, shards)


def prepare_kernel(
    live, place, slot_ref, projected, rate, gain, states,
    query, grown, base, gated, decay, made, here, outer, parts, sems,
):
    rows, dim = here.shape[1:]
    heads = rows // dim
    steps = projected.shape[0]
    copies = [
        pltpu.make_async_copy(
            states.at[slot_ref[place[0] * live + row]], here.at[row], sems.at[row]
        )
        for row in range(live)
    ]
    start_all(copies)
    parts[...] = jnp.zeros_like(parts)
    for step in range(steps):
        for row in range(live):
            block = projected[step, row].astype(F32)
            at = step * live + row
            for n in range(parts.shape[0]):
                parts[n, at : at + 1] = block[n : n + 1]
    queries, keys, values = (jax.nn.silu(parts[n]) for n in range(3))
    index = lax.broadcasted_iota(jnp.int32, queries.shape, 0)
    step_of = (index // live).astype(F32)
    rates = jnp.broadcast_to(rate[...], queries.shape)
    query[...] = queries
    gated[...] = jax.nn.sigmoid(parts[3]) * gain[...]
    grown[...] = jnp.exp(-rates * (step_of + 1.0))
    decay[...] = jnp.exp(-steps * rate[...])
    faded = keys * jnp.exp(-rates * jnp.maximum(steps - 1.0 - step_of, 0.0))
    later = lambda x, count: jnp.concatenate(
        [jnp.zeros((count, rows), F32), x[: TILE - count]], axis=0
    )
    total = jnp.zeros_like(queries)
    for lag in range(steps):
        key = later(keys, lag * live) if lag else keys
        value = later(values, lag * live) if lag else values
        product = queries * key
        match = jnp.concatenate(
            [
                jnp.broadcast_to(
                    jnp.sum(
                        product[:, head * dim : (head + 1) * dim], axis=1, keepdims=True
                    ),
                    (TILE, dim),
                )
                for head in range(heads)
            ],
            axis=1,
        )
        total = total + jnp.exp(-rates * float(lag)) * match * value
    base[...] = total

    def halves(x):
        high = x.astype(BF16).astype(F32)
        return high, x - high

    nothing = jnp.zeros_like(queries)
    v_high, v_low = halves(values)
    right = jnp.concatenate([v_high, v_high, v_low, nothing], axis=0).astype(BF16)
    for row in range(live):
        k_high, k_low = halves(jnp.where(lax.rem(index, live) == row, faded, 0.0))
        left = jnp.concatenate([k_high, k_low, k_high, nothing], axis=0).astype(BF16)
        for head in range(heads):
            span = slice(head * dim, (head + 1) * dim)
            outer[row, span] = lax.dot_general(
                left[:, span],
                right[:, span],
                (((0,), (0,)), ((), ())),
                preferred_element_type=F32,
            )
    wait_all(copies)
    for row in range(live):
        for head in range(heads):
            span = slice(head * dim, (head + 1) * dim)
            made[row, head * TILE : (head + 1) * TILE] = products(
                queries[:, span], here[row, span]
            )


def prepare(place, from_slot, projected, rate, gain, states, live):
    rows, dim = states.shape[1:]
    tile = jax.ShapeDtypeStruct((TILE, rows), F32)
    whole = jax.ShapeDtypeStruct((live, rows, dim), F32)
    return pl.pallas_call(
        functools.partial(prepare_kernel, live),
        out_shape=[tile] * 4
        + [
            jax.ShapeDtypeStruct((1, rows), F32),
            jax.ShapeDtypeStruct((live, rows // dim * TILE, dim), F32),
            whole,
            whole,
        ],
        in_specs=[SMEM] * 2 + [VMEM] * 3 + [HBM],
        out_specs=[VMEM] * 8,
        scratch_shapes=[
            pltpu.VMEM((projected.shape[2], TILE, rows), F32),
            pltpu.SemaphoreType.DMA((live,)),
        ],
        compiler_params=pltpu.CompilerParams(vmem_limit_bytes=6 * MIB),
        name="prepare_rows",
    )(place, from_slot, projected, rate, gain, *in_hbm(states))


def diagonal(dim):
    row = lax.broadcasted_iota(jnp.int32, (TILE, dim), 0)
    return row == lax.broadcasted_iota(jnp.int32, (TILE, dim), 1)


def raw_kernel(
    shards, live, place, shard_ref, lead_1, lead_0, near_1, near_0,
    local, query, grown, base, raw, sums, made,
):
    rows, dim = near_0.shape
    heads = rows // dim
    tile_rows = heads * TILE
    for row in range(live):
        made[row] = local[row]
    for n, near in enumerate((near_1, near_0)):
        for head in range(heads):
            span = slice(head * dim, (head + 1) * dim)
            made[live + n, head * TILE : (head + 1) * TILE] = products(
                query[:, span], near[span]
            )
    for n, lead in enumerate((lead_1, lead_0)):
        made[live + 2 + n] = lead[0:tile_rows]
    picks = []
    for row in range(live):
        gap = gap_of(row, shards, live, place, shard_ref)
        index = jnp.int32(row)
        for n, stride in enumerate((-1, 1, -2, 2)):
            index = jnp.where(at_stride(gap, stride, shards, place), live + n, index)
        picks.append(index)
    which = lax.rem(lax.broadcasted_iota(jnp.int32, (TILE, dim), 0), live)
    total = jnp.zeros((TILE, dim), F32)
    for head in range(heads):
        span = slice(head * dim, (head + 1) * dim)
        part = slice(head * TILE, (head + 1) * TILE)
        tile = made[picks[0], part]
        for row in range(1, live):
            tile = jnp.where(which == row, made[picks[row], part], tile)
        tile = tile * grown[:, span] + base[:, span]
        raw[:, span] = tile
        total = total + tile * tile
    total = jnp.broadcast_to(jnp.sum(total, axis=1, keepdims=True), (TILE, dim))
    total = jnp.sum(jnp.where(diagonal(dim), total, 0.0), axis=0, keepdims=True)
    for peer in range(sums.shape[0]):
        sums[peer] = total


def raw_of(place, from_shard, arrived, small, shards, live, group):
    rows, dim = arrived[-1].shape
    return pl.pallas_call(
        functools.partial(raw_kernel, shards, live),
        out_shape=[
            jax.ShapeDtypeStruct((TILE, rows), F32),
            jax.ShapeDtypeStruct((group, 1, dim), F32),
        ],
        in_specs=[SMEM] * 2 + [VMEM] * (len(arrived) + len(small)),
        out_specs=[VMEM] * 2,
        scratch_shapes=[pltpu.VMEM((live + 4, rows // dim * TILE, dim), F32)],
        compiler_params=pltpu.CompilerParams(vmem_limit_bytes=6 * MIB),
        cost_estimate=pl.CostEstimate(flops=10**12, bytes_accessed=MIB, transcendentals=0),
        name="raw_rows",
    )(place, from_shard, *arrived, *small)


def final_kernel(
    shards, live, place, shard_ref, here, near_1, near_0, lead_1, lead_0,
    rest_1, rest_0, outer, decay, final, made, sems,
):
    rows, dim = here.shape[1:]
    heads = rows // dim
    tile_rows = heads * TILE
    copies = []
    for row in range(live):
        gap = gap_of(row, shards, live, place, shard_ref)

        def at(ref, head):
            return lambda: ref[head * dim : (head + 1) * dim]

        def relayed(lead, rest, head):
            if head < EARLY:
                start = tile_rows + head * dim
                return lambda: lead[start : start + dim]
            return at(rest, head - EARLY)

        for half in range(2):
            span = range(half * heads // 2, (half + 1) * heads // 2)
            sources = [
                (gap == 0, [at(here.at[row], head) for head in span]),
                (at_stride(gap, 1, shards, place), [at(near_0, head) for head in span]),
                (at_stride(gap, -1, shards, place), [at(near_1, head) for head in span]),
                (
                    at_stride(gap, 2, shards, place),
                    [relayed(lead_0, rest_0, head) for head in span],
                ),
                (
                    at_stride(gap, -2, shards, place),
                    [relayed(lead_1, rest_1, head) for head in span],
                ),
            ]
            for found, states in sources:

                @pl.when(found)
                def _():
                    for head, state in zip(span, states):
                        block = slice(head * dim, (head + 1) * dim)
                        made[row, block] = decay[:, block] * state() + outer[row, block]

            block = slice(span.start * dim, span.stop * dim)
            copy = pltpu.make_async_copy(
                made.at[row, block], final.at[row, block], sems.at[row, half]
            )
            copy.start()
            copies.append(copy)
    wait_all(copies)


def final_of(place, from_shard, sources, shards, live):
    rows, dim = sources[0].shape[1:]
    return pl.pallas_call(
        functools.partial(final_kernel, shards, live),
        out_shape=jax.ShapeDtypeStruct((live, rows, dim), F32),
        in_specs=[SMEM] * 2 + [VMEM] * len(sources),
        out_specs=pl.BlockSpec(memory_space=pl.ANY),
        scratch_shapes=[
            pltpu.VMEM((live, rows, dim), F32),
            pltpu.SemaphoreType.DMA((live, 2)),
        ],
        compiler_params=pltpu.CompilerParams(vmem_limit_bytes=9 * MIB),
        name="final_rows",
    )(place, from_shard, *sources)


def attend_kernel(live, features, totals, raw, gated, attended):
    dim = totals.shape[2]
    total = totals[0]
    for peer in range(1, totals.shape[0]):
        total = total + totals[peer]
    total = jnp.where(diagonal(dim), jnp.broadcast_to(total, (TILE, dim)), 0.0)
    total = jnp.sum(total, axis=1, keepdims=True)
    scale = jnp.broadcast_to(lax.rsqrt(total / features + EPS), raw.shape)
    tile = raw[...] * scale * gated[...]
    for step in range(attended.shape[0]):
        attended[step] = tile[step * live : (step + 1) * live].astype(BF16)


def attend(totals, raw, gated, live, steps, features):
    return pl.pallas_call(
        functools.partial(attend_kernel, live, features),
        out_shape=jax.ShapeDtypeStruct((steps, live, raw.shape[1]), BF16),
        in_specs=[VMEM] * 3,
        out_specs=VMEM,
        compiler_params=pltpu.CompilerParams(vmem_limit_bytes=4 * MIB),
        name="attend_rows",
    )(totals, raw, gated)


def on_device(states, from_shard, from_slot, projected, decay_rate, norm_gain):
    shards, group = lax.axis_size("dp"), lax.axis_size("tensor")
    steps, live = projected.shape[:2]
    slots, heads, dim = states.shape[:3]
    width = heads * dim
    place = lax.axis_index("dp").astype(jnp.int32).reshape(1)
    states = states.reshape(slots, width, dim)

    rate = jnp.repeat(decay_rate, dim).reshape(1, width)
    gain = norm_gain.reshape(1, width)
    query, grown, base, gated, decay, local, here, outer = prepare(
        place, from_slot, projected, rate, gain, states, live
    )

    rows = pick(
        place, from_shard, from_slot, projected, states, shards, live, (-2, 2, -1, 1)
    )
    half_1, half_0 = swapped(rows[1], "dp", 1), swapped(rows[0], "dp", 0)
    near_1, near_0 = swapped(rows[3], "dp", 1), swapped(rows[2], "dp", 0)
    sent = relay(half_1, half_0, decay, heads)
    lead_1, lead_0 = swapped(sent[0], "dp", 1), swapped(sent[1], "dp", 0)
    rest_1, rest_0 = swapped(sent[2], "dp", 1), swapped(sent[3], "dp", 0)

    raw, sums = raw_of(
        place, from_shard, (lead_1, lead_0, near_1, near_0),
        (local, query, grown, base), shards, live, group,
    )
    totals = lax.all_to_all(sums, "tensor", 0, 0)
    final = final_of(
        place, from_shard,
        (here, near_1, near_0, lead_1, lead_0, rest_1, rest_0, outer, decay),
        shards, live,
    )
    attended = attend(totals, raw, gated, live, steps, width * group)
    return attended, final.reshape(live, heads, dim, dim)


def solution(mesh):
    return jax.shard_map(
        on_device,
        mesh=mesh,
        in_specs=(
            P("dp", "tensor", None, None),
            P(),
            P(),
            P(None, "dp", None, "tensor"),
            P("tensor"),
            P("tensor"),
        ),
        out_specs=(P(None, "dp", "tensor"), P("dp", "tensor", None, None)),
        check_vma=False,
    )
```

time: 89.8 us -> 63 us (0.70)
  the two profiles are of different devices: /device:TPU:102 before, /device:TPU:1 now
where the time goes in v6:
time: 63 us; the launch traced here: 62.5 us
  starting transfers between devices  33.8 us (54%)
  blocking collectives  11.5 us (18%)
  Pallas kernels  9.73 us (15%)
  waiting for transfers between devices  6.56 us (10%)
  between operations  0.81 us (1%)
    ppermute x8, starting transfers between devices, swapped(): return lax.ppermute(block, axis, pairs + [(b, a) for a, b in pairs])  33.8 us
    all_to_all x1, blocking collectives, on_device(): totals = lax.all_to_all(sums, 'tensor', 0, 0)  11.5 us
    ppermute x8, waiting for transfers between devices, swapped(): return lax.ppermute(block, axis, pairs + [(b, a) for a, b in pairs])  6.56 us
    pallas_call x1, Pallas kernels, prepare(): pl.pallas_call(functools.partial(prepare_kernel, live), out_shape=[tile]...  2.45 us
    pallas_call x1, Pallas kernels, pick(): pl.pallas_call(functools.partial(pick_kernel, shards, live, strides), out...  2.4 us
    pallas_call x1, Pallas kernels, final_of(): pl.pallas_call(functools.partial(final_kernel, shards, live), out_shape=j...  2.19 us
  transfers between devices with their start and end apart: 8, of which 3 were waited for; matrix products, arithmetic and copies ran while one was open for 0% of the time, Pallas kernels for 8%

profile of v6, /device:TPU:1, one launch (start us, length us, event | category | flops | bytes accessed | tf_op | source)
XLA Modules:
  0.0 62.5 jit_solution(10034119305626659444)
XLA Ops:
  0.7 2.4 %pick_rows.1 = (f32[1088,128]{1,0:T(8,128)S(1)}, f32[1088,128]{1,0:T(8,128)S(1)}, f32[1024,128]{1,0:T(8,128)S(1)}, f32[1024,128]{1,0:T(8,128)S(1)}) custom-call(s32[1]{0:T(128)} %bitcast.place, s32[128]{0:T(128)} %shard_ref.3, s32[128]{0:T(128)} %slot_ref.1, bf16[3,2,4,1024]{3,2,1,0:T(4,128)(2,1)} %projected.3, f32[4,1024,128]{2,1,0:T(8,128)} %bitcast.7), custom_call_target="tpu_custom_call" | custom-call | tf_op jit(solution)/shard_map/pick_rows/pallas_call | solution.py:97
  3.1 0.0 copy-start.4
  3.1 14.2 %collective-permute-start = (f32[1088,128]{1,0:T(8,128)S(1)}, f32[1088,128]{1,0:T(8,128)S(1)}, u32[]{:S(2)}, u32[]{:S(2)}) collective-permute-start(f32[1088,128]{1,0:T(8,128)S(1)} %get-tuple-element.20), channel_id=1, source_target_pairs={{8,16},{24,32},{40,48},{56,64},{72,80},{88,96},{104,112},{120,128}... | collective-permute-start | bytes 1671176 | tf_op jit(solution)/shard_map/ppermute | solution.py:23
  17.3 1.9 %collective-permute-start.1 = (f32[1088,128]{1,0:T(8,128)S(1)}, f32[1088,128]{1,0:T(8,128)S(1)}, u32[]{:S(2)}, u32[]{:S(2)}) collective-permute-start(f32[1088,128]{1,0:T(8,128)S(1)} %get-tuple-element.21), channel_id=1, source_target_pairs={{0,8},{16,24},{32,40},{48,56},{64,72},{80,88},{96,104},{112,120},{... | collective-permute-start | bytes 1671176 | tf_op jit(solution)/shard_map/ppermute | solution.py:23
  19.2 2.7 %collective-permute-start.4 = (f32[1024,128]{1,0:T(8,128)S(1)}, f32[1024,128]{1,0:T(8,128)S(1)}, u32[]{:S(2)}, u32[]{:S(2)}) collective-permute-start(f32[1024,128]{1,0:T(8,128)S(1)} %get-tuple-element.25), channel_id=1, source_target_pairs={{8,16},{24,32},{40,48},{56,64},{72,80},{88,96},{104,112},{120,128}... | collective-permute-start | bytes 1572872 | tf_op jit(solution)/shard_map/ppermute | solution.py:23
  21.9 2.6 %collective-permute-start.5 = (f32[1024,128]{1,0:T(8,128)S(1)}, f32[1024,128]{1,0:T(8,128)S(1)}, u32[]{:S(2)}, u32[]{:S(2)}) collective-permute-start(f32[1024,128]{1,0:T(8,128)S(1)} %get-tuple-element.26), channel_id=1, source_target_pairs={{0,8},{16,24},{32,40},{48,56},{64,72},{80,88},{96,104},{112,120},{... | collective-permute-start | bytes 1572872 | tf_op jit(solution)/shard_map/ppermute | solution.py:23
  24.5 0.1 broadcast_in_dim.3
  24.6 2.5 %prepare_rows.1 = (f32[8,1024]{1,0:T(8,128)S(1)}, f32[8,1024]{1,0:T(8,128)S(1)}, f32[8,1024]{1,0:T(8,128)S(1)}, f32[8,1024]{1,0:T(8,128)S(1)}, f32[1,1024]{1,0:T...) custom-call(s32[1]{0:T(128)} %bitcast.place, s32[128]{0:T(128)S(1)} %copy-done.5, ...), custom_call_target="tpu_custom_call" | custom-call | tf_op jit(solution)/shard_map/prepare_rows/pallas_call | solution.py:241
  27.0 2.6 %collective-permute-done.from_1 = f32[1088,128]{1,0:T(8,128)S(1)} collective-permute-done((f32[1088,128]{1,0:T(8,128)S(1)}, f32[1088,128]{1,0:T(8,128)S(1)}, u32[]{:S(2)}, u32[]{:S(2)}) %collective-permute-start) | collective-permute-done | bytes 557088 | tf_op jit(solution)/shard_map/ppermute | solution.py:23
  29.6 2.7 %collective-permute-done.1.from_0 = f32[1088,128]{1,0:T(8,128)S(1)} collective-permute-done((f32[1088,128]{1,0:T(8,128)S(1)}, f32[1088,128]{1,0:T(8,128)S(1)}, u32[]{:S(2)}, u32[]{:S(2)}) %collective-permute-start.1) | collective-permute-done | bytes 557088 | tf_op jit(solution)/shard_map/ppermute | solution.py:23
  32.3 1.0 %relay_rows.1 = (f32[320,128]{1,0:T(8,128)S(1)}, f32[320,128]{1,0:T(8,128)S(1)}, f32[768,128]{1,0:T(8,128)}, f32[768,128]{1,0:T(8,128)}) custom-call(f32[1088,128]{1,0:T(8,128)S(1)} %collective-permute-done.from_1, f32[1088,128]{1,0:T(8,128)S(1)} %collective-permute-done.1.from_0, f32[1,1024]{1,0:T(1,128)S(1)} %get-tuple-element.22._.decay), custom_call_target="tpu_custom_call" | custom-call | tf_op jit(solution)/shard_map/relay_rows/pallas_call | solution.py:138
  33.3 3.6 %collective-permute-start.2 = (f32[320,128]{1,0:T(8,128)S(1)}, f32[320,128]{1,0:T(8,128)S(1)}, u32[]{:S(2)}, u32[]{:S(2)}) collective-permute-start(f32[320,128]{1,0:T(8,128)S(1)} %get-tuple-element.23), channel_id=1, source_target_pairs={{8,16},{24,32},{40,48},{56,64},{72,80},{88,96},{104,112},{120,128}... | collective-permute-start | bytes 491528 | tf_op jit(solution)/shard_map/ppermute | solution.py:23
  36.9 1.9 %collective-permute-start.3 = (f32[320,128]{1,0:T(8,128)S(1)}, f32[320,128]{1,0:T(8,128)S(1)}, u32[]{:S(2)}, u32[]{:S(2)}) collective-permute-start(f32[320,128]{1,0:T(8,128)S(1)} %get-tuple-element.24), channel_id=1, source_target_pairs={{0,8},{16,24},{32,40},{48,56},{64,72},{80,88},{96,104},{112,120},{... | collective-permute-start | bytes 491528 | tf_op jit(solution)/shard_map/ppermute | solution.py:23
  38.9 5.0 %collective-permute-start.6 = (f32[768,128]{1,0:T(8,128)}, f32[768,128]{1,0:T(8,128)}, u32[]{:S(2)}, u32[]{:S(2)}) collective-permute-start(f32[768,128]{1,0:T(8,128)} %get-tuple-element.35), channel_id=1, source_target_pairs={{8,16},{24,32},{40,48},{56,64},{72,80},{88,96},{104,112},{120,128}... | collective-permute-start | bytes 1179656 | tf_op jit(solution)/shard_map/ppermute | solution.py:23
  43.9 0.0 collective-permute-done.4.near_1
  43.9 1.9 %collective-permute-start.7 = (f32[768,128]{1,0:T(8,128)}, f32[768,128]{1,0:T(8,128)}, u32[]{:S(2)}, u32[]{:S(2)}) collective-permute-start(f32[768,128]{1,0:T(8,128)} %get-tuple-element.36), channel_id=1, source_target_pairs={{0,8},{16,24},{32,40},{48,56},{64,72},{80,88},{96,104},{112,120},{... | collective-permute-start | bytes 1179656 | tf_op jit(solution)/shard_map/ppermute | solution.py:23
  45.8 0.0 collective-permute-done.5.near_0
  45.8 0.0 collective-permute-done.2.lead_1
  45.8 1.3 %collective-permute-done.3.lead_0 = f32[320,128]{1,0:T(8,128)S(1)} collective-permute-done((f32[320,128]{1,0:T(8,128)S(1)}, f32[320,128]{1,0:T(8,128)S(1)}, u32[]{:S(2)}, u32[]{:S(2)}) %collective-permute-start.3) | collective-permute-done | bytes 163872 | tf_op jit(solution)/shard_map/ppermute | solution.py:23
  47.1 1.0 %raw_rows.1 = (f32[8,1024]{1,0:T(8,128)S(1)}, f32[8,1,128]{2,1,0:T(1,128)S(1)}) custom-call(s32[1]{0:T(128)} %bitcast.place, s32[128]{0:T(128)S(1)} %copy-done.4, f32[320,128]{1,0:T(8,128)S(1)} %collective-permute-done.2.lead_1, f32[320,128]{1,0:T(8,128)S(1)} %collective-permute-done.3.lead_0, f32[1024,128]{1,0:T(8,128)S(1)} %collective-permute-done.4.near_1, ...), custom_call_target="tpu_custom_call" | custom-call | flops 999999995904 | bytes 1048576 | tf_op jit(solution)/shard_map/raw_rows/pallas_call | solution.py:309
  48.1 11.5 %all_to_all.5.totals = f32[8,1,128]{2,1,0:T(1,128)S(1)} all-to-all(f32[8,1,128]{2,1,0:T(1,128)S(1)} %get-tuple-element.31), channel_id=1, replica_groups=mesh['dp'=64,'tensor'=8] {'tensor'}, dimensions={0} | all-to-all | bytes 8192 | tf_op jit(solution)/shard_map/all_to_all | solution.py:443
  59.6 0.7 %attend_rows.1 = bf16[3,2,1024]{2,1,0:T(2,128)(2,1)} custom-call(f32[8,1,128]{2,1,0:T(1,128)S(1)} %all_to_all.5.totals, f32[8,1024]{1,0:T(8,128)S(1)} %get-tuple-element.32.raw, f32[8,1024]{1,0:T(8,128)S(1)} %get-tuple-element.33.gated), custom_call_target="tpu_custom_call" | custom-call | tf_op jit(solution)/shard_map/attend_rows/pallas_call | solution.py:406
  60.3 0.0 collective-permute-done.6.rest_1
  60.3 2.2 %final_rows.1 = f32[2,1024,128]{2,1,0:T(8,128)} custom-call(s32[1]{0:T(128)} %bitcast.place, s32[128]{0:T(128)S(1)} %copy-done.4, f32[2,1024,128]{2,1,0:T(8,128)S(1)} %get-tuple-element.34.here, f32[1024,128]{1,0:T(8,128)S(1)} %collective-permute-done.4.near_1, f32[1024,128]{1,0:T(8,128)S(1)} %collective-permute-done.5.near_0, ...), custom_call_target="tpu_custom_call" | custom-call | tf_op jit(solution)/shard_map/final_rows/pallas_call | solution.py:378
  (14 shorter events, 0.0 us)
Async XLA Ops:
  0.6 23.9 %copy-start = (bf16[3,2,4,1024]{3,2,1,0:T(4,128)(2,1)S(1)}, bf16[3,2,4,1024]{3,2,1,0:T(4,128)(2,1)}, u32[]{:S(2)}) copy-start(bf16[3,2,4,1024]{3,2,1,0:T(4,128)(2,1)} %projected.3) | copy-start | bytes 147460
  0.6 23.9 %copy-start.5 = (s32[128]{0:T(128)S(1)}, s32[128]{0:T(128)}, u32[]{:S(2)}) copy-start(s32[128]{0:T(128)} %slot_ref.1) | copy-start | bytes 1540
  0.7 23.9 %copy-start.3 = (f32[1024]{0:T(1024)S(1)}, f32[1024]{0:T(1024)}, u32[]{:S(2)}) copy-start(f32[1024]{0:T(1024)} %param.11) | copy-start | bytes 12292
  0.7 23.8 %copy-start.6 = (f32[8]{0:T(128)S(1)}, f32[8]{0:T(128)}, u32[]{:S(2)}) copy-start(f32[8]{0:T(128)} %param.10) | copy-start | bytes 100
  3.1 44.0 %copy-start.4 = (s32[128]{0:T(128)S(1)}, s32[128]{0:T(128)}, u32[]{:S(2)}) copy-start(s32[128]{0:T(128)} %shard_ref.3) | copy-start | bytes 1540
  3.1 26.5 %collective-permute-start = (f32[1088,128]{1,0:T(8,128)S(1)}, f32[1088,128]{1,0:T(8,128)S(1)}, u32[]{:S(2)}, u32[]{:S(2)}) collective-permute-start(f32[1088,128]{1,0:T(8,128)S(1)} %get-tuple-element.20), channel_id=1, source_target_pairs={{8,16},{24,32},{40,48},{56,64},{72,80},{88,96},{104,112},{120,128}... | collective-permute-start | bytes 1671176 | tf_op jit(solution)/shard_map/ppermute | solution.py:23
  17.3 15.1 %collective-permute-start.1 = (f32[1088,128]{1,0:T(8,128)S(1)}, f32[1088,128]{1,0:T(8,128)S(1)}, u32[]{:S(2)}, u32[]{:S(2)}) collective-permute-start(f32[1088,128]{1,0:T(8,128)S(1)} %get-tuple-element.21), channel_id=1, source_target_pairs={{0,8},{16,24},{32,40},{48,56},{64,72},{80,88},{96,104},{112,120},{... | collective-permute-start | bytes 1671176 | tf_op jit(solution)/shard_map/ppermute | solution.py:23
  19.2 24.7 %collective-permute-start.4 = (f32[1024,128]{1,0:T(8,128)S(1)}, f32[1024,128]{1,0:T(8,128)S(1)}, u32[]{:S(2)}, u32[]{:S(2)}) collective-permute-start(f32[1024,128]{1,0:T(8,128)S(1)} %get-tuple-element.25), channel_id=1, source_target_pairs={{8,16},{24,32},{40,48},{56,64},{72,80},{88,96},{104,112},{120,128}... | collective-permute-start | bytes 1572872 | tf_op jit(solution)/shard_map/ppermute | solution.py:23
  21.9 23.9 %collective-permute-start.5 = (f32[1024,128]{1,0:T(8,128)S(1)}, f32[1024,128]{1,0:T(8,128)S(1)}, u32[]{:S(2)}, u32[]{:S(2)}) collective-permute-start(f32[1024,128]{1,0:T(8,128)S(1)} %get-tuple-element.26), channel_id=1, source_target_pairs={{0,8},{16,24},{32,40},{48,56},{64,72},{80,88},{96,104},{112,120},{... | collective-permute-start | bytes 1572872 | tf_op jit(solution)/shard_map/ppermute | solution.py:23
  27.0 20.0 %copy-start.1 = (f32[1,1024]{1,0:T(1,128)}, f32[1,1024]{1,0:T(1,128)S(1)}, u32[]{:S(2)}) copy-start(f32[1,1024]{1,0:T(1,128)S(1)} %get-tuple-element.22._.decay) | copy-start | bytes 12292
  33.3 12.5 %collective-permute-start.2 = (f32[320,128]{1,0:T(8,128)S(1)}, f32[320,128]{1,0:T(8,128)S(1)}, u32[]{:S(2)}, u32[]{:S(2)}) collective-permute-start(f32[320,128]{1,0:T(8,128)S(1)} %get-tuple-element.23), channel_id=1, source_target_pairs={{8,16},{24,32},{40,48},{56,64},{72,80},{88,96},{104,112},{120,128}... | collective-permute-start | bytes 491528 | tf_op jit(solution)/shard_map/ppermute | solution.py:23
  36.9 10.1 %collective-permute-start.3 = (f32[320,128]{1,0:T(8,128)S(1)}, f32[320,128]{1,0:T(8,128)S(1)}, u32[]{:S(2)}, u32[]{:S(2)}) collective-permute-start(f32[320,128]{1,0:T(8,128)S(1)} %get-tuple-element.24), channel_id=1, source_target_pairs={{0,8},{16,24},{32,40},{48,56},{64,72},{80,88},{96,104},{112,120},{... | collective-permute-start | bytes 491528 | tf_op jit(solution)/shard_map/ppermute | solution.py:23
  38.9 21.4 %collective-permute-start.6 = (f32[768,128]{1,0:T(8,128)}, f32[768,128]{1,0:T(8,128)}, u32[]{:S(2)}, u32[]{:S(2)}) collective-permute-start(f32[768,128]{1,0:T(8,128)} %get-tuple-element.35), channel_id=1, source_target_pairs={{8,16},{24,32},{40,48},{56,64},{72,80},{88,96},{104,112},{120,128}... | collective-permute-start | bytes 1179656 | tf_op jit(solution)/shard_map/ppermute | solution.py:23
  43.9 16.4 %collective-permute-start.7 = (f32[768,128]{1,0:T(8,128)}, f32[768,128]{1,0:T(8,128)}, u32[]{:S(2)}, u32[]{:S(2)}) collective-permute-start(f32[768,128]{1,0:T(8,128)} %get-tuple-element.36), channel_id=1, source_target_pairs={{0,8},{16,24},{32,40},{48,56},{64,72},{80,88},{96,104},{112,120},{... | collective-permute-start | bytes 1179656 | tf_op jit(solution)/shard_map/ppermute | solution.py:23
  47.1 13.2 %copy-start.2 = (f32[1,1024]{1,0:T(1,128)S(1)}, f32[1,1024]{1,0:T(1,128)}, u32[]{:S(2)}) copy-start(f32[1,1024]{1,0:T(1,128)} %copy-done.1) | copy-start | bytes 12292

commit v7 on v6

--- a/solution.py
+++ b/solution.py
@@ -264,8 +264,8 @@
 
 
 def raw_kernel(
-    shards, live, place, shard_ref, lead_1, lead_0, near_1, near_0,
-    local, query, grown, base, raw, sums, made,
+    shards, live, place, shard_ref, lead_1, lead_0, near_0, near_1,
+    local, query, grown, base, raw, sums, made, tiles, sem,
 ):
     rows, dim = near_0.shape
     heads = rows // dim
@@ -301,7 +301,10 @@
     total = jnp.broadcast_to(jnp.sum(total, axis=1, keepdims=True), (TILE, dim))
     total = jnp.sum(jnp.where(diagonal(dim), total, 0.0), axis=0, keepdims=True)
     for peer in range(sums.shape[0]):
-        sums[peer] = total
+        tiles[peer] = total
+    copy = pltpu.make_async_copy(tiles, sums, sem)
+    copy.start()
+    copy.wait()
 
 
 def raw_of(place, from_shard, arrived, small, shards, live, group):
@@ -313,8 +316,12 @@
             jax.ShapeDtypeStruct((group, 1, dim), F32),
         ],
         in_specs=[SMEM] * 2 + [VMEM] * (len(arrived) + len(small)),
-        out_specs=[VMEM] * 2,
-        scratch_shapes=[pltpu.VMEM((live + 4, rows // dim * TILE, dim), F32)],
+        out_specs=[VMEM, HBM],
+        scratch_shapes=[
+            pltpu.VMEM((live + 4, rows // dim * TILE, dim), F32),
+            pltpu.VMEM((group, 1, dim), F32),
+            pltpu.SemaphoreType.DMA(()),
+        ],
         compiler_params=pltpu.CompilerParams(vmem_limit_bytes=6 * MIB),
         cost_estimate=pl.CostEstimate(flops=10**12, bytes_accessed=MIB, transcendentals=0),
         name="raw_rows",
@@ -322,10 +329,11 @@
 
 
 def final_kernel(
-    shards, live, place, shard_ref, here, near_1, near_0, lead_1, lead_0,
-    rest_1, rest_0, outer, decay, final, made, sems,
+    shards, live, place, shard_ref, here, lead_1, lead_0, near_0, near_1,
+    rest_0, rest_1, outer, decay, final, token, made, sems,
 ):
     rows, dim = here.shape[1:]
+    token[...] = jnp.zeros_like(token)
     heads = rows // dim
     tile_rows = heads * TILE
     copies = []
@@ -377,19 +385,23 @@
     rows, dim = sources[0].shape[1:]
     return pl.pallas_call(
         functools.partial(final_kernel, shards, live),
-        out_shape=jax.ShapeDtypeStruct((live, rows, dim), F32),
+        out_shape=[
+            jax.ShapeDtypeStruct((live, rows, dim), F32),
+            jax.ShapeDtypeStruct((TILE, dim), F32),
+        ],
         in_specs=[SMEM] * 2 + [VMEM] * len(sources),
-        out_specs=pl.BlockSpec(memory_space=pl.ANY),
+        out_specs=[pl.BlockSpec(memory_space=pl.ANY), VMEM],
         scratch_shapes=[
             pltpu.VMEM((live, rows, dim), F32),
             pltpu.SemaphoreType.DMA((live, 2)),
         ],
         compiler_params=pltpu.CompilerParams(vmem_limit_bytes=9 * MIB),
+        cost_estimate=pl.CostEstimate(flops=10**10, bytes_accessed=MIB, transcendentals=0),
         name="final_rows",
     )(place, from_shard, *sources)
 
 
-def attend_kernel(live, features, totals, raw, gated, attended):
+def attend_kernel(live, features, totals, raw, gated, _, attended):
     dim = totals.shape[2]
     total = totals[0]
     for peer in range(1, totals.shape[0]):
@@ -402,15 +414,15 @@
         attended[step] = tile[step * live : (step + 1) * live].astype(BF16)
 
 
-def attend(totals, raw, gated, live, steps, features):
+def attend(totals, raw, gated, after, live, steps, features):
     return pl.pallas_call(
         functools.partial(attend_kernel, live, features),
         out_shape=jax.ShapeDtypeStruct((steps, live, raw.shape[1]), BF16),
-        in_specs=[VMEM] * 3,
+        in_specs=[VMEM] * 4,
         out_specs=VMEM,
         compiler_params=pltpu.CompilerParams(vmem_limit_bytes=4 * MIB),
         name="attend_rows",
-    )(totals, raw, gated)
+    )(totals, raw, gated, after)
 
 
 def on_device(states, from_shard, from_slot, projected, decay_rate, norm_gain):
@@ -437,16 +449,16 @@
     rest_1, rest_0 = swapped(sent[2], "dp", 1), swapped(sent[3], "dp", 0)
 
     raw, sums = raw_of(
-        place, from_shard, (lead_1, lead_0, near_1, near_0),
+        place, from_shard, (lead_1, lead_0, near_0, near_1),
         (local, query, grown, base), shards, live, group,
     )
     totals = lax.all_to_all(sums, "tensor", 0, 0)
-    final = final_of(
+    final, token = final_of(
         place, from_shard,
-        (here, near_1, near_0, lead_1, lead_0, rest_1, rest_0, outer, decay),
+        (here, lead_1, lead_0, near_0, near_1, rest_0, rest_1, outer, decay),
         shards, live,
     )
-    attended = attend(totals, raw, gated, live, steps, width * group)
+    attended = attend(totals, raw, gated, token, live, steps, width * group)
     return attended, final.reshape(live, heads, dim, dim)
 
 

time: 63 us -> 63.7 us (1.011)
  blocking collectives: 11.5 us -> 0 us
  starting transfers between devices: 33.8 us -> 43 us
  waiting for transfers between devices: 6.56 us -> 7.98 us
  local copies, waits for them, and re-layouts: 0.1 us -> 1.01 us
  Pallas kernels: 9.73 us -> 10.4 us
    all_to_all x1 -> x0, blocking collectives: 11.5 us -> none  [on_device(): totals = lax.all_to_all(sums, 'tensor', 0, 0)]
    all_to_all x0 -> x1, starting transfers between devices: none -> 8.93 us  [on_device(): totals = lax.all_to_all(sums, 'tensor', 0, 0)]
    all_to_all x0 -> x1, waiting for transfers between devices: none -> 1.38 us  [on_device(): totals = lax.all_to_all(sums, 'tensor', 0, 0)]
    unnamed x14 -> x18, local copies, waits for them, and re-layouts: 0.03 us -> 0.94 us
  transfers between devices with their start and end apart: 8 -> 9, of which waited for: 3 -> 4; matrix products, arithmetic and copies ran while one was open for 0% -> 0% of each run, Pallas kernels for 8% -> 11%
where the time goes in v7:
time: 63.7 us; the launch traced here: 63.2 us
  starting transfers between devices  43 us (68%)
  Pallas kernels  10.4 us (16%)
  waiting for transfers between devices  7.98 us (13%)
  local copies, waits for them, and re-layouts  1.01 us (2%)
  between operations  0.87 us (1%)
    ppermute x8, starting transfers between devices, swapped(): return lax.ppermute(block, axis, pairs + [(b, a) for a, b in pairs])  34.1 us
    all_to_all x1, starting transfers between devices, on_device(): totals = lax.all_to_all(sums, 'tensor', 0, 0)  8.93 us
    ppermute x8, waiting for transfers between devices, swapped(): return lax.ppermute(block, axis, pairs + [(b, a) for a, b in pairs])  6.6 us
    pallas_call x1, Pallas kernels, prepare(): pl.pallas_call(functools.partial(prepare_kernel, live), out_shape=[tile]...  2.45 us
    pallas_call x1, Pallas kernels, pick(): pl.pallas_call(functools.partial(pick_kernel, shards, live, strides), out...  2.4 us
    pallas_call x1, Pallas kernels, final_of(): pl.pallas_call(functools.partial(final_kernel, shards, live), out_shape=[...  2.18 us
    pallas_call x1, Pallas kernels, raw_of(): pl.pallas_call(functools.partial(raw_kernel, shards, live), out_shape=[ja...  1.63 us
    all_to_all x1, waiting for transfers between devices, on_device(): totals = lax.all_to_all(sums, 'tensor', 0, 0)  1.38 us
  transfers between devices with their start and end apart: 9, of which 4 were waited for; matrix products, arithmetic and copies ran while one was open for 0% of the time, Pallas kernels for 11%

profile of v7, /device:TPU:1, one launch (start us, length us, event | category | flops | bytes accessed | tf_op | source)
XLA Modules:
  0.0 63.2 jit_solution(15526792249135741120)
XLA Ops:
  0.7 2.4 %pick_rows.1 = (f32[1088,128]{1,0:T(8,128)S(1)}, f32[1088,128]{1,0:T(8,128)S(1)}, f32[1024,128]{1,0:T(8,128)S(1)}, f32[1024,128]{1,0:T(8,128)S(1)}) custom-call(s32[1]{0:T(128)} %bitcast.place, s32[128]{0:T(128)} %shard_ref.3, s32[128]{0:T(128)} %slot_ref.1, bf16[3,2,4,1024]{3,2,1,0:T(4,128)(2,1)} %projected.3, f32[4,1024,128]{2,1,0:T(8,128)} %bitcast.7), custom_call_target="tpu_custom_call" | custom-call | tf_op jit(solution)/shard_map/pick_rows/pallas_call | solution.py:97
  3.1 0.0 copy-start.5
  3.1 14.3 %collective-permute-start = (f32[1088,128]{1,0:T(8,128)S(1)}, f32[1088,128]{1,0:T(8,128)S(1)}, u32[]{:S(2)}, u32[]{:S(2)}) collective-permute-start(f32[1088,128]{1,0:T(8,128)S(1)} %get-tuple-element.22), channel_id=1, source_target_pairs={{8,16},{24,32},{40,48},{56,64},{72,80},{88,96},{104,112},{120,128}... | collective-permute-start | bytes 1671176 | tf_op jit(solution)/shard_map/ppermute | solution.py:23
  17.4 1.9 %collective-permute-start.1 = (f32[1088,128]{1,0:T(8,128)S(1)}, f32[1088,128]{1,0:T(8,128)S(1)}, u32[]{:S(2)}, u32[]{:S(2)}) collective-permute-start(f32[1088,128]{1,0:T(8,128)S(1)} %get-tuple-element.23), channel_id=1, source_target_pairs={{0,8},{16,24},{32,40},{48,56},{64,72},{80,88},{96,104},{112,120},{... | collective-permute-start | bytes 1671176 | tf_op jit(solution)/shard_map/ppermute | solution.py:23
  19.3 3.4 %collective-permute-start.4 = (f32[1024,128]{1,0:T(8,128)S(1)}, f32[1024,128]{1,0:T(8,128)S(1)}, u32[]{:S(2)}, u32[]{:S(2)}) collective-permute-start(f32[1024,128]{1,0:T(8,128)S(1)} %get-tuple-element.27), channel_id=1, source_target_pairs={{0,8},{16,24},{32,40},{48,56},{64,72},{80,88},{96,104},{112,120},{... | collective-permute-start | bytes 1572872 | tf_op jit(solution)/shard_map/ppermute | solution.py:23
  22.7 1.9 %collective-permute-start.5 = (f32[1024,128]{1,0:T(8,128)S(1)}, f32[1024,128]{1,0:T(8,128)S(1)}, u32[]{:S(2)}, u32[]{:S(2)}) collective-permute-start(f32[1024,128]{1,0:T(8,128)S(1)} %get-tuple-element.28), channel_id=1, source_target_pairs={{8,16},{24,32},{40,48},{56,64},{72,80},{88,96},{104,112},{120,128}... | collective-permute-start | bytes 1572872 | tf_op jit(solution)/shard_map/ppermute | solution.py:23
  24.6 0.1 broadcast_in_dim.3
  24.7 2.5 %prepare_rows.1 = (f32[8,1024]{1,0:T(8,128)S(1)}, f32[8,1024]{1,0:T(8,128)S(1)}, f32[8,1024]{1,0:T(8,128)S(1)}, f32[8,1024]{1,0:T(8,128)S(1)}, f32[1,1024]{1,0:T...) custom-call(s32[1]{0:T(128)} %bitcast.place, s32[128]{0:T(128)S(1)} %copy-done.4, ...), custom_call_target="tpu_custom_call" | custom-call | tf_op jit(solution)/shard_map/prepare_rows/pallas_call | solution.py:241
  27.2 2.6 %collective-permute-done.from_1 = f32[1088,128]{1,0:T(8,128)S(1)} collective-permute-done((f32[1088,128]{1,0:T(8,128)S(1)}, f32[1088,128]{1,0:T(8,128)S(1)}, u32[]{:S(2)}, u32[]{:S(2)}) %collective-permute-start) | collective-permute-done | bytes 557088 | tf_op jit(solution)/shard_map/ppermute | solution.py:23
  29.7 2.7 %collective-permute-done.1.from_0 = f32[1088,128]{1,0:T(8,128)S(1)} collective-permute-done((f32[1088,128]{1,0:T(8,128)S(1)}, f32[1088,128]{1,0:T(8,128)S(1)}, u32[]{:S(2)}, u32[]{:S(2)}) %collective-permute-start.1) | collective-permute-done | bytes 557088 | tf_op jit(solution)/shard_map/ppermute | solution.py:23
  32.5 1.0 %relay_rows.1 = (f32[320,128]{1,0:T(8,128)S(1)}, f32[320,128]{1,0:T(8,128)S(1)}, f32[768,128]{1,0:T(8,128)}, f32[768,128]{1,0:T(8,128)}) custom-call(f32[1088,128]{1,0:T(8,128)S(1)} %collective-permute-done.from_1, f32[1088,128]{1,0:T(8,128)S(1)} %collective-permute-done.1.from_0, f32[1,1024]{1,0:T(1,128)S(1)} %get-tuple-element.24._.decay), custom_call_target="tpu_custom_call" | custom-call | tf_op jit(solution)/shard_map/relay_rows/pallas_call | solution.py:138
  33.5 3.6 %collective-permute-start.2 = (f32[320,128]{1,0:T(8,128)S(1)}, f32[320,128]{1,0:T(8,128)S(1)}, u32[]{:S(2)}, u32[]{:S(2)}) collective-permute-start(f32[320,128]{1,0:T(8,128)S(1)} %get-tuple-element.25), channel_id=1, source_target_pairs={{8,16},{24,32},{40,48},{56,64},{72,80},{88,96},{104,112},{120,128}... | collective-permute-start | bytes 491528 | tf_op jit(solution)/shard_map/ppermute | solution.py:23
  37.1 1.9 %collective-permute-start.3 = (f32[320,128]{1,0:T(8,128)S(1)}, f32[320,128]{1,0:T(8,128)S(1)}, u32[]{:S(2)}, u32[]{:S(2)}) collective-permute-start(f32[320,128]{1,0:T(8,128)S(1)} %get-tuple-element.26), channel_id=1, source_target_pairs={{0,8},{16,24},{32,40},{48,56},{64,72},{80,88},{96,104},{112,120},{... | collective-permute-start | bytes 491528 | tf_op jit(solution)/shard_map/ppermute | solution.py:23
  39.0 3.4 %collective-permute-start.6 = (f32[768,128]{1,0:T(8,128)}, f32[768,128]{1,0:T(8,128)}, u32[]{:S(2)}, u32[]{:S(2)}) collective-permute-start(f32[768,128]{1,0:T(8,128)} %get-tuple-element.37), channel_id=1, source_target_pairs={{0,8},{16,24},{32,40},{48,56},{64,72},{80,88},{96,104},{112,120},{... | collective-permute-start | bytes 1179656 | tf_op jit(solution)/shard_map/ppermute | solution.py:23
  42.4 1.3 %collective-permute-done.4.near_0 = f32[1024,128]{1,0:T(8,128)S(1)} collective-permute-done((f32[1024,128]{1,0:T(8,128)S(1)}, f32[1024,128]{1,0:T(8,128)S(1)}, u32[]{:S(2)}, u32[]{:S(2)}) %collective-permute-start.4) | collective-permute-done | bytes 524320 | tf_op jit(solution)/shard_map/ppermute | solution.py:23
  43.7 3.7 %collective-permute-start.7 = (f32[768,128]{1,0:T(8,128)}, f32[768,128]{1,0:T(8,128)}, u32[]{:S(2)}, u32[]{:S(2)}) collective-permute-start(f32[768,128]{1,0:T(8,128)} %get-tuple-element.38), channel_id=1, source_target_pairs={{8,16},{24,32},{40,48},{56,64},{72,80},{88,96},{104,112},{120,128}... | collective-permute-start | bytes 1179656 | tf_op jit(solution)/shard_map/ppermute | solution.py:23
  47.4 0.0 collective-permute-done.5.near_1
  47.5 1.6 %raw_rows.1 = (f32[8,1024]{1,0:T(8,128)S(1)}, f32[8,1,128]{2,1,0:T(1,128)}) custom-call(s32[1]{0:T(128)} %bitcast.place, s32[128]{0:T(128)S(1)} %copy-done.5, f32[320,128]{1,0:T(8,128)S(1)} %collective-permute-done.2.lead_1, f32[320,128]{1,0:T(8,128)S(1)} %collective-permute-done.3.lead_0, f32[1024,128]{1,0:T(8,128)S(1)} %collective-permute-done.4.near_0, ...), custom_call_target="tpu_custom_call" | custom-call | flops 999999995904 | bytes 1048576 | tf_op jit(solution)/shard_map/raw_rows/pallas_call | solution.py:312
  49.1 8.9 %all-to-all-start = ((f32[8,1,128]{2,1,0:T(1,128)}), f32[8,1,128]{2,1,0:T(1,128)S(1)}, u32[]{:S(2)}, u32[]{:S(2)}) async-start(f32[8,1,128]{2,1,0:T(1,128)} %get-tuple-element.33), calls=%async_computation | async-start | bytes 8192 | tf_op jit(solution)/shard_map/all_to_all | solution.py:455
  58.0 0.0 collective-permute-done.6.rest_0
  58.1 0.9 %copy-done.7 = f32[320,128]{1,0:T(8,128)S(1)} copy-done((f32[320,128]{1,0:T(8,128)S(1)}, f32[320,128]{1,0:T(8,128)}, u32[]{:S(2)}) %copy-start.7) | copy-done | bytes 163864
  59.0 2.2 %final_rows.1 = (f32[2,1024,128]{2,1,0:T(8,128)}, f32[8,128]{1,0:T(8,128)S(1)}) custom-call(s32[1]{0:T(128)} %bitcast.place, s32[128]{0:T(128)S(1)} %copy-done.5, f32[2,1024,128]{2,1,0:T(8,128)S(1)} %get-tuple-element.36.here, f32[320,128]{1,0:T(8,128)S(1)} %collective-permute-done.2.lead_1, f32[320,128]{1,0:T(8,128)S(1)} %copy-done.7, ...), custom_call_target="tpu_custom_call" | custom-call | flops 10000000000 | bytes 1048576 | tf_op jit(solution)/shard_map/final_rows/pallas_call | solution.py:386
  61.2 1.4 %all-to-all-done.totals = f32[8,1,128]{2,1,0:T(1,128)S(1)} async-done(((f32[8,1,128]{2,1,0:T(1,128)}), f32[8,1,128]{2,1,0:T(1,128)S(1)}, u32[]{:S(2)}, u32[]{:S(2)}) %all-to-all-start) | async-done | bytes 4128 | tf_op jit(solution)/shard_map/all_to_all | solution.py:455
  62.5 0.7 %attend_rows.1 = bf16[3,2,1024]{2,1,0:T(2,128)(2,1)} custom-call(f32[8,1,128]{2,1,0:T(1,128)S(1)} %all-to-all-done.totals, f32[8,1024]{1,0:T(8,128)S(1)} %get-tuple-element.34.raw, f32[8,1024]{1,0:T(8,128)S(1)} %get-tuple-element.35.gated, f32[8,128]{1,0:T(8,128)S(1)} %get-tuple-element.40._), custom_call_target="tpu_custom_call" | custom-call | tf_op jit(solution)/shard_map/attend_rows/pallas_call | solution.py:418
  (19 shorter events, 0.0 us)
Async XLA Ops:
  0.6 24.1 %copy-start = (bf16[3,2,4,1024]{3,2,1,0:T(4,128)(2,1)S(1)}, bf16[3,2,4,1024]{3,2,1,0:T(4,128)(2,1)}, u32[]{:S(2)}) copy-start(bf16[3,2,4,1024]{3,2,1,0:T(4,128)(2,1)} %projected.3) | copy-start | bytes 147460
  0.6 24.1 %copy-start.4 = (s32[128]{0:T(128)S(1)}, s32[128]{0:T(128)}, u32[]{:S(2)}) copy-start(s32[128]{0:T(128)} %slot_ref.1) | copy-start | bytes 1540
  0.7 24.1 %copy-start.1 = (f32[1024]{0:T(1024)S(1)}, f32[1024]{0:T(1024)}, u32[]{:S(2)}) copy-start(f32[1024]{0:T(1024)} %param.11) | copy-start | bytes 12292
  0.7 24.0 %copy-start.8 = (f32[8]{0:T(128)S(1)}, f32[8]{0:T(128)}, u32[]{:S(2)}) copy-start(f32[8]{0:T(128)} %param.10) | copy-start | bytes 100
  3.1 44.4 %copy-start.5 = (s32[128]{0:T(128)S(1)}, s32[128]{0:T(128)}, u32[]{:S(2)}) copy-start(s32[128]{0:T(128)} %shard_ref.3) | copy-start | bytes 1540
  3.1 26.6 %collective-permute-start = (f32[1088,128]{1,0:T(8,128)S(1)}, f32[1088,128]{1,0:T(8,128)S(1)}, u32[]{:S(2)}, u32[]{:S(2)}) collective-permute-start(f32[1088,128]{1,0:T(8,128)S(1)} %get-tuple-element.22), channel_id=1, source_target_pairs={{8,16},{24,32},{40,48},{56,64},{72,80},{88,96},{104,112},{120,128}... | collective-permute-start | bytes 1671176 | tf_op jit(solution)/shard_map/ppermute | solution.py:23
  17.4 15.1 %collective-permute-start.1 = (f32[1088,128]{1,0:T(8,128)S(1)}, f32[1088,128]{1,0:T(8,128)S(1)}, u32[]{:S(2)}, u32[]{:S(2)}) collective-permute-start(f32[1088,128]{1,0:T(8,128)S(1)} %get-tuple-element.23), channel_id=1, source_target_pairs={{0,8},{16,24},{32,40},{48,56},{64,72},{80,88},{96,104},{112,120},{... | collective-permute-start | bytes 1671176 | tf_op jit(solution)/shard_map/ppermute | solution.py:23
  19.3 24.4 %collective-permute-start.4 = (f32[1024,128]{1,0:T(8,128)S(1)}, f32[1024,128]{1,0:T(8,128)S(1)}, u32[]{:S(2)}, u32[]{:S(2)}) collective-permute-start(f32[1024,128]{1,0:T(8,128)S(1)} %get-tuple-element.27), channel_id=1, source_target_pairs={{0,8},{16,24},{32,40},{48,56},{64,72},{80,88},{96,104},{112,120},{... | collective-permute-start | bytes 1572872 | tf_op jit(solution)/shard_map/ppermute | solution.py:23
  22.7 24.7 %collective-permute-start.5 = (f32[1024,128]{1,0:T(8,128)S(1)}, f32[1024,128]{1,0:T(8,128)S(1)}, u32[]{:S(2)}, u32[]{:S(2)}) collective-permute-start(f32[1024,128]{1,0:T(8,128)S(1)} %get-tuple-element.28), channel_id=1, source_target_pairs={{8,16},{24,32},{40,48},{56,64},{72,80},{88,96},{104,112},{120,128}... | collective-permute-start | bytes 1572872 | tf_op jit(solution)/shard_map/ppermute | solution.py:23
  27.2 20.3 %copy-start.2 = (f32[1,1024]{1,0:T(1,128)}, f32[1,1024]{1,0:T(1,128)S(1)}, u32[]{:S(2)}) copy-start(f32[1,1024]{1,0:T(1,128)S(1)} %get-tuple-element.24._.decay) | copy-start | bytes 12292
  33.5 13.9 %collective-permute-start.2 = (f32[320,128]{1,0:T(8,128)S(1)}, f32[320,128]{1,0:T(8,128)S(1)}, u32[]{:S(2)}, u32[]{:S(2)}) collective-permute-start(f32[320,128]{1,0:T(8,128)S(1)} %get-tuple-element.25), channel_id=1, source_target_pairs={{8,16},{24,32},{40,48},{56,64},{72,80},{88,96},{104,112},{120,128}... | collective-permute-start | bytes 491528 | tf_op jit(solution)/shard_map/ppermute | solution.py:23
  37.1 10.3 %collective-permute-start.3 = (f32[320,128]{1,0:T(8,128)S(1)}, f32[320,128]{1,0:T(8,128)S(1)}, u32[]{:S(2)}, u32[]{:S(2)}) collective-permute-start(f32[320,128]{1,0:T(8,128)S(1)} %get-tuple-element.26), channel_id=1, source_target_pairs={{0,8},{16,24},{32,40},{48,56},{64,72},{80,88},{96,104},{112,120},{... | collective-permute-start | bytes 491528 | tf_op jit(solution)/shard_map/ppermute | solution.py:23
  39.0 19.0 %collective-permute-start.6 = (f32[768,128]{1,0:T(8,128)}, f32[768,128]{1,0:T(8,128)}, u32[]{:S(2)}, u32[]{:S(2)}) collective-permute-start(f32[768,128]{1,0:T(8,128)} %get-tuple-element.37), channel_id=1, source_target_pairs={{0,8},{16,24},{32,40},{48,56},{64,72},{80,88},{96,104},{112,120},{... | collective-permute-start | bytes 1179656 | tf_op jit(solution)/shard_map/ppermute | solution.py:23
  43.7 14.3 %collective-permute-start.7 = (f32[768,128]{1,0:T(8,128)}, f32[768,128]{1,0:T(8,128)}, u32[]{:S(2)}, u32[]{:S(2)}) collective-permute-start(f32[768,128]{1,0:T(8,128)} %get-tuple-element.38), channel_id=1, source_target_pairs={{8,16},{24,32},{40,48},{56,64},{72,80},{88,96},{104,112},{120,128}... | collective-permute-start | bytes 1179656 | tf_op jit(solution)/shard_map/ppermute | solution.py:23
  47.4 1.7 %copy-start.6 = (f32[320,128]{1,0:T(8,128)}, f32[320,128]{1,0:T(8,128)S(1)}, u32[]{:S(2)}) copy-start(f32[320,128]{1,0:T(8,128)S(1)} %collective-permute-done.3.lead_0) | copy-start | bytes 491524
  47.5 10.6 %copy-start.3 = (f32[1,1024]{1,0:T(1,128)S(1)}, f32[1,1024]{1,0:T(1,128)}, u32[]{:S(2)}) copy-start(f32[1,1024]{1,0:T(1,128)} %copy-done.2) | copy-start | bytes 12292
  49.1 13.4 %all-to-all-start = ((f32[8,1,128]{2,1,0:T(1,128)}), f32[8,1,128]{2,1,0:T(1,128)S(1)}, u32[]{:S(2)}, u32[]{:S(2)}) async-start(f32[8,1,128]{2,1,0:T(1,128)} %get-tuple-element.33), calls=%async_computation | async-start | bytes 8192 | tf_op jit(solution)/shard_map/all_to_all | solution.py:455
  58.1 0.9 %copy-start.7 = (f32[320,128]{1,0:T(8,128)S(1)}, f32[320,128]{1,0:T(8,128)}, u32[]{:S(2)}) copy-start(f32[320,128]{1,0:T(8,128)} %copy-done.6) | copy-start | bytes 491524

commit v8 on v7

--- a/solution.py
+++ b/solution.py
@@ -9,7 +9,7 @@
 EPS = 1e-05
 F32 = jnp.float32
 BF16 = jnp.bfloat16
-EARLY = 2
+EARLY = 3
 TILE = 8
 MIB = 1024 * 1024
 SMEM = pl.BlockSpec(memory_space=pltpu.SMEM)
@@ -111,7 +111,7 @@
     )(place, *in_hbm(from_shard, from_slot, projected, states))
 
 
-def relay_kernel(from_1, from_0, _, lead_1, lead_0, rest_1, rest_0):
+def relay_kernel(from_0, from_1, _, lead_1, lead_0, rest_1, rest_0):
     dim = from_1.shape[1]
     heads = rest_0.shape[0] // dim + EARLY
     rows, early = heads * dim, EARLY * dim
@@ -131,7 +131,7 @@
                 rest[(head - EARLY) * dim : (head - EARLY + 1) * dim] = state
 
 
-def relay(from_1, from_0, after, heads):
+def relay(from_0, from_1, after, heads):
     dim = from_0.shape[1]
     lead = jax.ShapeDtypeStruct((heads * TILE + EARLY * dim, dim), F32)
     rest = jax.ShapeDtypeStruct(((heads - EARLY) * dim, dim), F32)
@@ -142,7 +142,7 @@
         out_specs=[VMEM] * 4,
         compiler_params=pltpu.CompilerParams(vmem_limit_bytes=6 * MIB),
         name="relay_rows",
-    )(from_1, from_0, after)
+    )(from_0, from_1, after)
 
 
 def gap_of(row, shards, live, place, shard_ref):
@@ -264,7 +264,7 @@
 
 
 def raw_kernel(
-    shards, live, place, shard_ref, lead_1, lead_0, near_0, near_1,
+    shards, live, place, shard_ref, lead_0, lead_1, near_1, near_0,
     local, query, grown, base, raw, sums, made, tiles, sem,
 ):
     rows, dim = near_0.shape
@@ -329,48 +329,61 @@
 
 
 def final_kernel(
-    shards, live, place, shard_ref, here, lead_1, lead_0, near_0, near_1,
-    rest_0, rest_1, outer, decay, final, token, made, sems,
+    shards, live, place, shard_ref, here, lead_0, lead_1, near_1, near_0,
+    rest_1, rest_0, outer, decay, final, token, held, made, sems_in, sems,
 ):
     rows, dim = here.shape[1:]
+    heads = rows // dim
+    early, tile_rows = EARLY * dim, heads * TILE
     token[...] = jnp.zeros_like(token)
-    heads = rows // dim
-    tile_rows = heads * TILE
+
+    def loads(row, lead, rest):
+        return [
+            pltpu.make_async_copy(
+                lead.at[tile_rows : tile_rows + early],
+                held.at[row, 0:early],
+                sems_in.at[row, 0],
+            ),
+            pltpu.make_async_copy(rest, held.at[row, early:rows], sems_in.at[row, 1]),
+        ]
+
+    cases = []
+    for row in range(live):
+        gap = gap_of(row, shards, live, place, shard_ref)
+        far_0 = at_stride(gap, 2, shards, place)
+        far_1 = at_stride(gap, -2, shards, place)
+        for found, lead, rest in ((far_0, lead_0, rest_0), (far_1, lead_1, rest_1)):
+
+            @pl.when(found)
+            def _():
+                start_all(loads(row, lead, rest))
+
+        cases.append(
+            [
+                (gap == 0, here.at[row]),
+                (at_stride(gap, 1, shards, place), near_0),
+                (at_stride(gap, -1, shards, place), near_1),
+                (jnp.logical_or(far_0, far_1), held.at[row]),
+            ]
+        )
     copies = []
     for row in range(live):
-        gap = gap_of(row, shards, live, place, shard_ref)
-
-        def at(ref, head):
-            return lambda: ref[head * dim : (head + 1) * dim]
-
-        def relayed(lead, rest, head):
-            if head < EARLY:
-                start = tile_rows + head * dim
-                return lambda: lead[start : start + dim]
-            return at(rest, head - EARLY)
+
+        @pl.when(cases[row][3][0])
+        def _():
+            wait_all(loads(row, lead_0, rest_0))
 
         for half in range(2):
             span = range(half * heads // 2, (half + 1) * heads // 2)
-            sources = [
-                (gap == 0, [at(here.at[row], head) for head in span]),
-                (at_stride(gap, 1, shards, place), [at(near_0, head) for head in span]),
-                (at_stride(gap, -1, shards, place), [at(near_1, head) for head in span]),
-                (
-                    at_stride(gap, 2, shards, place),
-                    [relayed(lead_0, rest_0, head) for head in span],
-                ),
-                (
-                    at_stride(gap, -2, shards, place),
-                    [relayed(lead_1, rest_1, head) for head in span],
-                ),
-            ]
-            for found, states in sources:
+            for found, source in cases[row]:
 
                 @pl.when(found)
                 def _():
-                    for head, state in zip(span, states):
+                    for head in span:
                         block = slice(head * dim, (head + 1) * dim)
-                        made[row, block] = decay[:, block] * state() + outer[row, block]
+                        made[row, block] = (
+                            decay[:, block] * source[block] + outer[row, block]
+                        )
 
             block = slice(span.start * dim, span.stop * dim)
             copy = pltpu.make_async_copy(
@@ -381,24 +394,26 @@
     wait_all(copies)
 
 
-def final_of(place, from_shard, sources, shards, live):
-    rows, dim = sources[0].shape[1:]
+def final_of(place, from_shard, here, lead, near, rest, small, shards, live):
+    rows, dim = here.shape[1:]
     return pl.pallas_call(
         functools.partial(final_kernel, shards, live),
         out_shape=[
             jax.ShapeDtypeStruct((live, rows, dim), F32),
             jax.ShapeDtypeStruct((TILE, dim), F32),
         ],
-        in_specs=[SMEM] * 2 + [VMEM] * len(sources),
+        in_specs=[SMEM] * 2 + [VMEM] + [HBM] * 2 + [VMEM] * 2 + [HBM] * 2 + [VMEM] * 2,
         out_specs=[pl.BlockSpec(memory_space=pl.ANY), VMEM],
         scratch_shapes=[
             pltpu.VMEM((live, rows, dim), F32),
+            pltpu.VMEM((live, rows, dim), F32),
             pltpu.SemaphoreType.DMA((live, 2)),
-        ],
-        compiler_params=pltpu.CompilerParams(vmem_limit_bytes=9 * MIB),
+            pltpu.SemaphoreType.DMA((live, 2)),
+        ],
+        compiler_params=pltpu.CompilerParams(vmem_limit_bytes=8 * MIB),
         cost_estimate=pl.CostEstimate(flops=10**10, bytes_accessed=MIB, transcendentals=0),
         name="final_rows",
-    )(place, from_shard, *sources)
+    )(place, from_shard, here, *in_hbm(*lead), *near, *in_hbm(*rest), *small)
 
 
 def attend_kernel(live, features, totals, raw, gated, _, attended):
@@ -444,19 +459,18 @@
     )
     half_1, half_0 = swapped(rows[1], "dp", 1), swapped(rows[0], "dp", 0)
     near_1, near_0 = swapped(rows[3], "dp", 1), swapped(rows[2], "dp", 0)
-    sent = relay(half_1, half_0, decay, heads)
+    sent = relay(half_0, half_1, decay, heads)
     lead_1, lead_0 = swapped(sent[0], "dp", 1), swapped(sent[1], "dp", 0)
     rest_1, rest_0 = swapped(sent[2], "dp", 1), swapped(sent[3], "dp", 0)
 
     raw, sums = raw_of(
-        place, from_shard, (lead_1, lead_0, near_0, near_1),
+        place, from_shard, (lead_0, lead_1, near_1, near_0),
         (local, query, grown, base), shards, live, group,
     )
     totals = lax.all_to_all(sums, "tensor", 0, 0)
     final, token = final_of(
-        place, from_shard,
-        (here, lead_1, lead_0, near_0, near_1, rest_0, rest_1, outer, decay),
-        shards, live,
+        place, from_shard, here, (lead_0, lead_1), (near_1, near_0), (rest_1, rest_0),
+        (outer, decay), shards, live,
     )
     attended = attend(totals, raw, gated, token, live, steps, width * group)
     return attended, final.reshape(live, heads, dim, dim)

time: 63.7 us -> 62.5 us (0.981)
  starting transfers between devices: 43 us -> 40.6 us
  waiting for transfers between devices: 7.98 us -> 9.54 us
  local copies, waits for them, and re-layouts: 1.01 us -> 0.11 us
    ppermute x8, starting transfers between devices: 34.1 us -> 32.9 us  [swapped(): return lax.ppermute(block, axis, pairs + [(b, a) for a, b in pairs])]
    all_to_all x1, starting transfers between devices: 8.93 us -> 7.76 us  [on_device(): totals = lax.all_to_all(sums, 'tensor', 0, 0)]
    ppermute x8, waiting for transfers between devices: 6.6 us -> 7.76 us  [swapped(): return lax.ppermute(block, axis, pairs + [(b, a) for a, b in pairs])]
    unnamed x18, local copies, waits for them, and re-layouts: 0.94 us -> 0.04 us
  transfers between devices with their start and end apart: 9 -> 9, of which waited for: 4 -> 3; matrix products, arithmetic and copies ran while one was open for 0% -> 0% of each run, Pallas kernels for 11% -> 12%
where the time goes in v8:
time: 62.5 us; the launch traced here: 62 us
  starting transfers between devices  40.6 us (65%)
  Pallas kernels  10.8 us (17%)
  waiting for transfers between devices  9.54 us (15%)
  between operations  0.86 us (1%)
    ppermute x8, starting transfers between devices, swapped(): return lax.ppermute(block, axis, pairs + [(b, a) for a, b in pairs])  32.9 us
    ppermute x8, waiting for transfers between devices, swapped(): return lax.ppermute(block, axis, pairs + [(b, a) for a, b in pairs])  7.76 us
    all_to_all x1, starting transfers between devices, on_device(): totals = lax.all_to_all(sums, 'tensor', 0, 0)  7.76 us
    pallas_call x1, Pallas kernels, final_of(): pl.pallas_call(functools.partial(final_kernel, shards, live), out_shape=[...  2.7 us
    pallas_call x1, Pallas kernels, prepare(): pl.pallas_call(functools.partial(prepare_kernel, live), out_shape=[tile]...  2.45 us
    pallas_call x1, Pallas kernels, pick(): pl.pallas_call(functools.partial(pick_kernel, shards, live, strides), out...  2.4 us
    all_to_all x1, waiting for transfers between devices, on_device(): totals = lax.all_to_all(sums, 'tensor', 0, 0)  1.77 us
    pallas_call x1, Pallas kernels, raw_of(): pl.pallas_call(functools.partial(raw_kernel, shards, live), out_shape=[ja...  1.63 us
  transfers between devices with their start and end apart: 9, of which 3 were waited for; matrix products, arithmetic and copies ran while one was open for 0% of the time, Pallas kernels for 12%

profile of v8, /device:TPU:1, one launch (start us, length us, event | category | flops | bytes accessed | tf_op | source)
XLA Modules:
  0.0 62.0 jit_solution(14352801050578361073)
XLA Ops:
  0.7 2.4 %pick_rows.1 = (f32[1088,128]{1,0:T(8,128)S(1)}, f32[1088,128]{1,0:T(8,128)S(1)}, f32[1024,128]{1,0:T(8,128)S(1)}, f32[1024,128]{1,0:T(8,128)S(1)}) custom-call(s32[1]{0:T(128)} %bitcast.place, s32[128]{0:T(128)} %shard_ref.3, s32[128]{0:T(128)} %slot_ref.1, bf16[3,2,4,1024]{3,2,1,0:T(4,128)(2,1)} %projected.3, f32[4,1024,128]{2,1,0:T(8,128)} %bitcast.7), custom_call_target="tpu_custom_call" | custom-call | tf_op jit(solution)/shard_map/pick_rows/pallas_call | solution.py:97
  3.1 0.0 copy-start.5
  3.1 3.9 %collective-permute-start = (f32[1088,128]{1,0:T(8,128)S(1)}, f32[1088,128]{1,0:T(8,128)S(1)}, u32[]{:S(2)}, u32[]{:S(2)}) collective-permute-start(f32[1088,128]{1,0:T(8,128)S(1)} %get-tuple-element.22), channel_id=1, source_target_pairs={{0,8},{16,24},{32,40},{48,56},{64,72},{80,88},{96,104},{112,120},{... | collective-permute-start | bytes 1671176 | tf_op jit(solution)/shard_map/ppermute | solution.py:23
  7.1 12.7 %collective-permute-start.1 = (f32[1088,128]{1,0:T(8,128)S(1)}, f32[1088,128]{1,0:T(8,128)S(1)}, u32[]{:S(2)}, u32[]{:S(2)}) collective-permute-start(f32[1088,128]{1,0:T(8,128)S(1)} %get-tuple-element.23), channel_id=1, source_target_pairs={{8,16},{24,32},{40,48},{56,64},{72,80},{88,96},{104,112},{120,128}... | collective-permute-start | bytes 1671176 | tf_op jit(solution)/shard_map/ppermute | solution.py:23
  19.7 1.9 %collective-permute-start.4 = (f32[1024,128]{1,0:T(8,128)S(1)}, f32[1024,128]{1,0:T(8,128)S(1)}, u32[]{:S(2)}, u32[]{:S(2)}) collective-permute-start(f32[1024,128]{1,0:T(8,128)S(1)} %get-tuple-element.27), channel_id=1, source_target_pairs={{8,16},{24,32},{40,48},{56,64},{72,80},{88,96},{104,112},{120,128}... | collective-permute-start | bytes 1572872 | tf_op jit(solution)/shard_map/ppermute | solution.py:23
  21.6 1.9 %collective-permute-start.5 = (f32[1024,128]{1,0:T(8,128)S(1)}, f32[1024,128]{1,0:T(8,128)S(1)}, u32[]{:S(2)}, u32[]{:S(2)}) collective-permute-start(f32[1024,128]{1,0:T(8,128)S(1)} %get-tuple-element.28), channel_id=1, source_target_pairs={{0,8},{16,24},{32,40},{48,56},{64,72},{80,88},{96,104},{112,120},{... | collective-permute-start | bytes 1572872 | tf_op jit(solution)/shard_map/ppermute | solution.py:23
  23.6 0.1 broadcast_in_dim.3
  23.7 2.4 %prepare_rows.1 = (f32[8,1024]{1,0:T(8,128)S(1)}, f32[8,1024]{1,0:T(8,128)S(1)}, f32[8,1024]{1,0:T(8,128)S(1)}, f32[8,1024]{1,0:T(8,128)S(1)}, f32[1,1024]{1,0:T...) custom-call(s32[1]{0:T(128)} %bitcast.place, s32[128]{0:T(128)S(1)} %copy-done.4, ...), custom_call_target="tpu_custom_call" | custom-call | tf_op jit(solution)/shard_map/prepare_rows/pallas_call | solution.py:241
  26.1 0.0 collective-permute-done.from_0
  26.1 5.6 %collective-permute-done.1.from_1 = f32[1088,128]{1,0:T(8,128)S(1)} collective-permute-done((f32[1088,128]{1,0:T(8,128)S(1)}, f32[1088,128]{1,0:T(8,128)S(1)}, u32[]{:S(2)}, u32[]{:S(2)}) %collective-permute-start.1) | collective-permute-done | bytes 557088 | tf_op jit(solution)/shard_map/ppermute | solution.py:23
  31.7 1.0 %relay_rows.1 = (f32[448,128]{1,0:T(8,128)S(1)}, f32[448,128]{1,0:T(8,128)S(1)}, f32[640,128]{1,0:T(8,128)}, f32[640,128]{1,0:T(8,128)}) custom-call(f32[1088,128]{1,0:T(8,128)S(1)} %collective-permute-done.from_0, f32[1088,128]{1,0:T(8,128)S(1)} %collective-permute-done.1.from_1, f32[1,1024]{1,0:T(1,128)S(1)} %get-tuple-element.24._.decay), custom_call_target="tpu_custom_call" | custom-call | tf_op jit(solution)/shard_map/relay_rows/pallas_call | solution.py:138
  32.7 1.9 %collective-permute-start.2 = (f32[448,128]{1,0:T(8,128)S(1)}, f32[448,128]{1,0:T(8,128)S(1)}, u32[]{:S(2)}, u32[]{:S(2)}) collective-permute-start(f32[448,128]{1,0:T(8,128)S(1)} %get-tuple-element.25), channel_id=1, source_target_pairs={{0,8},{16,24},{32,40},{48,56},{64,72},{80,88},{96,104},{112,120},{... | collective-permute-start | bytes 688136 | tf_op jit(solution)/shard_map/ppermute | solution.py:23
  34.6 6.4 %collective-permute-start.3 = (f32[448,128]{1,0:T(8,128)S(1)}, f32[448,128]{1,0:T(8,128)S(1)}, u32[]{:S(2)}, u32[]{:S(2)}) collective-permute-start(f32[448,128]{1,0:T(8,128)S(1)} %get-tuple-element.26), channel_id=1, source_target_pairs={{8,16},{24,32},{40,48},{56,64},{72,80},{88,96},{104,112},{120,128}... | collective-permute-start | bytes 688136 | tf_op jit(solution)/shard_map/ppermute | solution.py:23
  41.0 2.2 %collective-permute-start.6 = (f32[640,128]{1,0:T(8,128)}, f32[640,128]{1,0:T(8,128)}, u32[]{:S(2)}, u32[]{:S(2)}) collective-permute-start(f32[640,128]{1,0:T(8,128)} %get-tuple-element.37), channel_id=1, source_target_pairs={{8,16},{24,32},{40,48},{56,64},{72,80},{88,96},{104,112},{120,128}... | collective-permute-start | bytes 983048 | tf_op jit(solution)/shard_map/ppermute | solution.py:23
  43.2 0.0 collective-permute-done.4.near_1
  43.2 1.9 %collective-permute-start.7 = (f32[640,128]{1,0:T(8,128)}, f32[640,128]{1,0:T(8,128)}, u32[]{:S(2)}, u32[]{:S(2)}) collective-permute-start(f32[640,128]{1,0:T(8,128)} %get-tuple-element.38), channel_id=1, source_target_pairs={{0,8},{16,24},{32,40},{48,56},{64,72},{80,88},{96,104},{112,120},{... | collective-permute-start | bytes 983048 | tf_op jit(solution)/shard_map/ppermute | solution.py:23
  45.2 0.0 collective-permute-done.5.near_0
  45.2 2.2 %collective-permute-done.3.lead_1 = f32[448,128]{1,0:T(8,128)S(1)} collective-permute-done((f32[448,128]{1,0:T(8,128)S(1)}, f32[448,128]{1,0:T(8,128)S(1)}, u32[]{:S(2)}, u32[]{:S(2)}) %collective-permute-start.3) | collective-permute-done | bytes 229408 | tf_op jit(solution)/shard_map/ppermute | solution.py:23
  47.4 1.6 %raw_rows.1 = (f32[8,1024]{1,0:T(8,128)S(1)}, f32[8,1,128]{2,1,0:T(1,128)}) custom-call(s32[1]{0:T(128)} %bitcast.place, s32[128]{0:T(128)S(1)} %copy-done.5, f32[448,128]{1,0:T(8,128)S(1)} %collective-permute-done.2.lead_0, f32[448,128]{1,0:T(8,128)S(1)} %collective-permute-done.3.lead_1, f32[1024,128]{1,0:T(8,128)S(1)} %collective-permute-done.4.near_1, ...), custom_call_target="tpu_custom_call" | custom-call | flops 999999995904 | bytes 1048576 | tf_op jit(solution)/shard_map/raw_rows/pallas_call | solution.py:312
  49.0 7.8 %all-to-all-start = ((f32[8,1,128]{2,1,0:T(1,128)}), f32[8,1,128]{2,1,0:T(1,128)S(1)}, u32[]{:S(2)}, u32[]{:S(2)}) async-start(f32[8,1,128]{2,1,0:T(1,128)} %get-tuple-element.33), calls=%async_computation | async-start | bytes 8192 | tf_op jit(solution)/shard_map/all_to_all | solution.py:470
  56.8 0.0 collective-permute-done.7.rest_0
  56.8 2.7 %final_rows.1 = (f32[2,1024,128]{2,1,0:T(8,128)}, f32[8,128]{1,0:T(8,128)S(1)}) custom-call(s32[1]{0:T(128)} %bitcast.place, s32[128]{0:T(128)S(1)} %copy-done.5, f32[2,1024,128]{2,1,0:T(8,128)S(1)} %get-tuple-element.36.here, f32[448,128]{1,0:T(8,128)} %copy-done.6, f32[448,128]{1,0:T(8,128)} %copy-done.7, f32[1024,128]{1,0:T(8,128)S(1)} %collective-permute-done.4.near_1, ...), custom_call_target="tpu_custom_call" | custom-call | flops 10000000000 | bytes 1048576 | tf_op jit(solution)/shard_map/final_rows/pallas_call | solution.py:399
  59.5 1.8 %all-to-all-done.totals = f32[8,1,128]{2,1,0:T(1,128)S(1)} async-done(((f32[8,1,128]{2,1,0:T(1,128)}), f32[8,1,128]{2,1,0:T(1,128)S(1)}, u32[]{:S(2)}, u32[]{:S(2)}) %all-to-all-start) | async-done | bytes 4128 | tf_op jit(solution)/shard_map/all_to_all | solution.py:470
  61.3 0.7 %attend_rows.1 = bf16[3,2,1024]{2,1,0:T(2,128)(2,1)} custom-call(f32[8,1,128]{2,1,0:T(1,128)S(1)} %all-to-all-done.totals, f32[8,1024]{1,0:T(8,128)S(1)} %get-tuple-element.34.raw, f32[8,1024]{1,0:T(8,128)S(1)} %get-tuple-element.35.gated, f32[8,128]{1,0:T(8,128)S(1)} %get-tuple-element.40._), custom_call_target="tpu_custom_call" | custom-call | tf_op jit(solution)/shard_map/attend_rows/pallas_call | solution.py:433
  (19 shorter events, 0.0 us)
Async XLA Ops:
  0.6 23.0 %copy-start = (bf16[3,2,4,1024]{3,2,1,0:T(4,128)(2,1)S(1)}, bf16[3,2,4,1024]{3,2,1,0:T(4,128)(2,1)}, u32[]{:S(2)}) copy-start(bf16[3,2,4,1024]{3,2,1,0:T(4,128)(2,1)} %projected.3) | copy-start | bytes 147460
  0.6 23.0 %copy-start.4 = (s32[128]{0:T(128)S(1)}, s32[128]{0:T(128)}, u32[]{:S(2)}) copy-start(s32[128]{0:T(128)} %slot_ref.1) | copy-start | bytes 1540
  0.7 23.0 %copy-start.1 = (f32[1024]{0:T(1024)S(1)}, f32[1024]{0:T(1024)}, u32[]{:S(2)}) copy-start(f32[1024]{0:T(1024)} %param.11) | copy-start | bytes 12292
  0.7 22.9 %copy-start.8 = (f32[8]{0:T(128)S(1)}, f32[8]{0:T(128)}, u32[]{:S(2)}) copy-start(f32[8]{0:T(128)} %param.10) | copy-start | bytes 100
  3.1 44.3 %copy-start.5 = (s32[128]{0:T(128)S(1)}, s32[128]{0:T(128)}, u32[]{:S(2)}) copy-start(s32[128]{0:T(128)} %shard_ref.3) | copy-start | bytes 1540
  3.1 23.0 %collective-permute-start = (f32[1088,128]{1,0:T(8,128)S(1)}, f32[1088,128]{1,0:T(8,128)S(1)}, u32[]{:S(2)}, u32[]{:S(2)}) collective-permute-start(f32[1088,128]{1,0:T(8,128)S(1)} %get-tuple-element.22), channel_id=1, source_target_pairs={{0,8},{16,24},{32,40},{48,56},{64,72},{80,88},{96,104},{112,120},{... | collective-permute-start | bytes 1671176 | tf_op jit(solution)/shard_map/ppermute | solution.py:23
  7.1 24.7 %collective-permute-start.1 = (f32[1088,128]{1,0:T(8,128)S(1)}, f32[1088,128]{1,0:T(8,128)S(1)}, u32[]{:S(2)}, u32[]{:S(2)}) collective-permute-start(f32[1088,128]{1,0:T(8,128)S(1)} %get-tuple-element.23), channel_id=1, source_target_pairs={{8,16},{24,32},{40,48},{56,64},{72,80},{88,96},{104,112},{120,128}... | collective-permute-start | bytes 1671176 | tf_op jit(solution)/shard_map/ppermute | solution.py:23
  19.7 23.5 %collective-permute-start.4 = (f32[1024,128]{1,0:T(8,128)S(1)}, f32[1024,128]{1,0:T(8,128)S(1)}, u32[]{:S(2)}, u32[]{:S(2)}) collective-permute-start(f32[1024,128]{1,0:T(8,128)S(1)} %get-tuple-element.27), channel_id=1, source_target_pairs={{8,16},{24,32},{40,48},{56,64},{72,80},{88,96},{104,112},{120,128}... | collective-permute-start | bytes 1572872 | tf_op jit(solution)/shard_map/ppermute | solution.py:23
  21.6 23.5 %collective-permute-start.5 = (f32[1024,128]{1,0:T(8,128)S(1)}, f32[1024,128]{1,0:T(8,128)S(1)}, u32[]{:S(2)}, u32[]{:S(2)}) collective-permute-start(f32[1024,128]{1,0:T(8,128)S(1)} %get-tuple-element.28), channel_id=1, source_target_pairs={{0,8},{16,24},{32,40},{48,56},{64,72},{80,88},{96,104},{112,120},{... | collective-permute-start | bytes 1572872 | tf_op jit(solution)/shard_map/ppermute | solution.py:23
  26.1 21.2 %copy-start.2 = (f32[1,1024]{1,0:T(1,128)}, f32[1,1024]{1,0:T(1,128)S(1)}, u32[]{:S(2)}) copy-start(f32[1,1024]{1,0:T(1,128)S(1)} %get-tuple-element.24._.decay) | copy-start | bytes 12292
  32.7 12.5 %collective-permute-start.2 = (f32[448,128]{1,0:T(8,128)S(1)}, f32[448,128]{1,0:T(8,128)S(1)}, u32[]{:S(2)}, u32[]{:S(2)}) collective-permute-start(f32[448,128]{1,0:T(8,128)S(1)} %get-tuple-element.25), channel_id=1, source_target_pairs={{0,8},{16,24},{32,40},{48,56},{64,72},{80,88},{96,104},{112,120},{... | collective-permute-start | bytes 688136 | tf_op jit(solution)/shard_map/ppermute | solution.py:23
  34.6 12.7 %collective-permute-start.3 = (f32[448,128]{1,0:T(8,128)S(1)}, f32[448,128]{1,0:T(8,128)S(1)}, u32[]{:S(2)}, u32[]{:S(2)}) collective-permute-start(f32[448,128]{1,0:T(8,128)S(1)} %get-tuple-element.26), channel_id=1, source_target_pairs={{8,16},{24,32},{40,48},{56,64},{72,80},{88,96},{104,112},{120,128}... | collective-permute-start | bytes 688136 | tf_op jit(solution)/shard_map/ppermute | solution.py:23
  41.0 15.8 %collective-permute-start.6 = (f32[640,128]{1,0:T(8,128)}, f32[640,128]{1,0:T(8,128)}, u32[]{:S(2)}, u32[]{:S(2)}) collective-permute-start(f32[640,128]{1,0:T(8,128)} %get-tuple-element.37), channel_id=1, source_target_pairs={{8,16},{24,32},{40,48},{56,64},{72,80},{88,96},{104,112},{120,128}... | collective-permute-start | bytes 983048 | tf_op jit(solution)/shard_map/ppermute | solution.py:23
  43.2 13.5 %collective-permute-start.7 = (f32[640,128]{1,0:T(8,128)}, f32[640,128]{1,0:T(8,128)}, u32[]{:S(2)}, u32[]{:S(2)}) collective-permute-start(f32[640,128]{1,0:T(8,128)} %get-tuple-element.38), channel_id=1, source_target_pairs={{0,8},{16,24},{32,40},{48,56},{64,72},{80,88},{96,104},{112,120},{... | collective-permute-start | bytes 983048 | tf_op jit(solution)/shard_map/ppermute | solution.py:23
  45.2 3.8 %copy-start.6 = (f32[448,128]{1,0:T(8,128)}, f32[448,128]{1,0:T(8,128)S(1)}, u32[]{:S(2)}) copy-start(f32[448,128]{1,0:T(8,128)S(1)} %collective-permute-done.2.lead_0) | copy-start | bytes 688132
  47.4 1.7 %copy-start.7 = (f32[448,128]{1,0:T(8,128)}, f32[448,128]{1,0:T(8,128)S(1)}, u32[]{:S(2)}) copy-start(f32[448,128]{1,0:T(8,128)S(1)} %collective-permute-done.3.lead_1) | copy-start | bytes 688132
  47.4 9.4 %copy-start.3 = (f32[1,1024]{1,0:T(1,128)S(1)}, f32[1,1024]{1,0:T(1,128)}, u32[]{:S(2)}) copy-start(f32[1,1024]{1,0:T(1,128)} %copy-done.2) | copy-start | bytes 12292
  49.0 12.3 %all-to-all-start = ((f32[8,1,128]{2,1,0:T(1,128)}), f32[8,1,128]{2,1,0:T(1,128)S(1)}, u32[]{:S(2)}, u32[]{:S(2)}) async-start(f32[8,1,128]{2,1,0:T(1,128)} %get-tuple-element.33), calls=%async_computation | async-start | bytes 8192 | tf_op jit(solution)/shard_map/all_to_all | solution.py:470

commit v9 on v8

--- a/solution.py
+++ b/solution.py
@@ -9,7 +9,7 @@
 EPS = 1e-05
 F32 = jnp.float32
 BF16 = jnp.bfloat16
-EARLY = 3
+EARLY = 1
 TILE = 8
 MIB = 1024 * 1024
 SMEM = pl.BlockSpec(memory_space=pltpu.SMEM)
@@ -17,14 +17,18 @@
 HBM = pl.BlockSpec(memory_space=pltpu.HBM)
 
 
-def swapped(block, axis, first):
-    size = lax.axis_size(axis)
-    pairs = [((first + i) % size, (first + i + 1) % size) for i in range(0, size, 2)]
-    return lax.ppermute(block, axis, pairs + [(b, a) for a, b in pairs])
-
-
-def side_of(device):
-    return 2 * lax.rem(device, 2) - 1
+def swapped(block, first):
+    shards, group = lax.axis_size("dp"), lax.axis_size("tensor")
+    route = []
+    for i in range(0, shards, 2):
+        for j in range(group):
+            low = (first + j % 2 + i) % shards
+            high = (low + 1) % shards
+            route += [
+                (low * group + j, high * group + j),
+                (high * group + j, low * group + j),
+            ]
+    return lax.ppermute(block, ("dp", "tensor"), route)
 
 
 def start_all(copies):
@@ -67,7 +71,7 @@
     wait_all(plan)
     copies = []
     for n, stride in enumerate(strides):
-        target = lax.rem(device + stride * side_of(device) + shards, shards)
+        target = lax.rem(device + stride * place[1] + shards, shards)
         slot = jnp.int32(0)
         for row in range(live):
             mine = shard_ref[target * live + row] == device
@@ -151,7 +155,7 @@
 
 
 def at_stride(gap, stride, shards, place):
-    return gap == lax.rem(stride * side_of(place[0]) + shards, shards)
+    return gap == lax.rem(stride * place[1] + shards, shards)
 
 
 def prepare_kernel(
@@ -445,7 +449,9 @@
     steps, live = projected.shape[:2]
     slots, heads, dim = states.shape[:3]
     width = heads * dim
-    place = lax.axis_index("dp").astype(jnp.int32).reshape(1)
+    shard = lax.axis_index("dp").astype(jnp.int32)
+    side = 2 * ((shard ^ lax.axis_index("tensor").astype(jnp.int32)) & 1) - 1
+    place = jnp.stack([shard, side])
     states = states.reshape(slots, width, dim)
 
     rate = jnp.repeat(decay_rate, dim).reshape(1, width)
@@ -457,11 +463,11 @@
     rows = pick(
         place, from_shard, from_slot, projected, states, shards, live, (-2, 2, -1, 1)
     )
-    half_1, half_0 = swapped(rows[1], "dp", 1), swapped(rows[0], "dp", 0)
-    near_1, near_0 = swapped(rows[3], "dp", 1), swapped(rows[2], "dp", 0)
+    half_1, half_0 = swapped(rows[1], 1), swapped(rows[0], 0)
+    near_1, near_0 = swapped(rows[3], 1), swapped(rows[2], 0)
     sent = relay(half_0, half_1, decay, heads)
-    lead_1, lead_0 = swapped(sent[0], "dp", 1), swapped(sent[1], "dp", 0)
-    rest_1, rest_0 = swapped(sent[2], "dp", 1), swapped(sent[3], "dp", 0)
+    lead_1, lead_0 = swapped(sent[0], 1), swapped(sent[1], 0)
+    rest_1, rest_0 = swapped(sent[2], 1), swapped(sent[3], 0)
 
     raw, sums = raw_of(
         place, from_shard, (lead_0, lead_1, near_1, near_0),

time: 62.5 us -> 62.6 us (level)
  the two profiles are of different devices: /device:TPU:1 before, /device:TPU:24 now
where the time goes in v9:
time: 62.6 us; the launch traced here: 62.1 us
  starting transfers between devices  38.2 us (61%)
  Pallas kernels  11.5 us (18%)
  waiting for transfers between devices  11.4 us (18%)
  between operations  0.9 us (1%)
    ppermute x8, starting transfers between devices, swapped(): return lax.ppermute(block, ('dp', 'tensor'), route)  33.5 us
    ppermute x8, waiting for transfers between devices, swapped(): return lax.ppermute(block, ('dp', 'tensor'), route)  11.4 us
    all_to_all x1, starting transfers between devices, on_device(): totals = lax.all_to_all(sums, 'tensor', 0, 0)  4.7 us
    pallas_call x1, Pallas kernels, pick(): pl.pallas_call(functools.partial(pick_kernel, shards, live, strides), out...  2.96 us
    pallas_call x1, Pallas kernels, final_of(): pl.pallas_call(functools.partial(final_kernel, shards, live), out_shape=[...  2.7 us
    pallas_call x1, Pallas kernels, prepare(): pl.pallas_call(functools.partial(prepare_kernel, live), out_shape=[tile]...  2.45 us
    pallas_call x1, Pallas kernels, raw_of(): pl.pallas_call(functools.partial(raw_kernel, shards, live), out_shape=[ja...  1.63 us
  transfers between devices with their start and end apart: 9, of which 2 were waited for; matrix products, arithmetic and copies ran while one was open for 0% of the time, Pallas kernels for 13%

profile of v9, /device:TPU:24, one launch (start us, length us, event | category | flops | bytes accessed | tf_op | source)
XLA Modules:
  0.0 62.1 jit_solution(16667630228181573954)
XLA Ops:
  0.6 0.0 copy-start
  0.6 0.0 copy-start.4
  0.7 0.1 pad_add_fusion.place
  0.8 3.0 %pick_rows.1 = (f32[1088,128]{1,0:T(8,128)S(1)}, f32[1088,128]{1,0:T(8,128)S(1)}, f32[1024,128]{1,0:T(8,128)S(1)}, f32[1024,128]{1,0:T(8,128)S(1)}) custom-call(s32[2]{0:T(128)S(1)} %pad_add_fusion.place, s32[128]{0:T(128)} %shard_ref.3, s32[128]{0:T(128)} %slot_ref.1, bf16[3,2,4,1024]{3,2,1,0:T(4,128)(2,1)} %projected.3, f32[4,1024,128]{2,1,0:T(8,128)} %bitcast.8), custom_call_target="tpu_custom_call" | custom-call | tf_op jit(solution)/shard_map/pick_rows/pallas_call | solution.py:101
  3.7 0.0 copy-start.5
  3.7 3.2 %collective-permute-start = (f32[1088,128]{1,0:T(8,128)S(1)}, f32[1088,128]{1,0:T(8,128)S(1)}, u32[]{:S(2)}, u32[]{:S(2)}) collective-permute-start(f32[1088,128]{1,0:T(8,128)S(1)} %get-tuple-element.22), channel_id=1, source_target_pairs={{0,8},{8,0},{9,17},{17,9},{2,10},{10,2},{11,19},{19,11},{4,12},{12... | collective-permute-start | bytes 1671176 | tf_op jit(solution)/shard_map/ppermute | solution.py:31
  7.0 12.9 %collective-permute-start.1 = (f32[1088,128]{1,0:T(8,128)S(1)}, f32[1088,128]{1,0:T(8,128)S(1)}, u32[]{:S(2)}, u32[]{:S(2)}) collective-permute-start(f32[1088,128]{1,0:T(8,128)S(1)} %get-tuple-element.23), channel_id=1, source_target_pairs={{8,16},{16,8},{17,25},{25,17},{10,18},{18,10},{19,27},{27,19},{12,... | collective-permute-start | bytes 1671176 | tf_op jit(solution)/shard_map/ppermute | solution.py:31
  19.9 1.9 %collective-permute-start.4 = (f32[1024,128]{1,0:T(8,128)S(1)}, f32[1024,128]{1,0:T(8,128)S(1)}, u32[]{:S(2)}, u32[]{:S(2)}) collective-permute-start(f32[1024,128]{1,0:T(8,128)S(1)} %get-tuple-element.27), channel_id=1, source_target_pairs={{8,16},{16,8},{17,25},{25,17},{10,18},{18,10},{19,27},{27,19},{12,... | collective-permute-start | bytes 1572872 | tf_op jit(solution)/shard_map/ppermute | solution.py:31
  21.9 1.9 %collective-permute-start.5 = (f32[1024,128]{1,0:T(8,128)S(1)}, f32[1024,128]{1,0:T(8,128)S(1)}, u32[]{:S(2)}, u32[]{:S(2)}) collective-permute-start(f32[1024,128]{1,0:T(8,128)S(1)} %get-tuple-element.28), channel_id=1, source_target_pairs={{0,8},{8,0},{9,17},{17,9},{2,10},{10,2},{11,19},{19,11},{4,12},{12... | collective-permute-start | bytes 1572872 | tf_op jit(solution)/shard_map/ppermute | solution.py:31
  23.8 0.1 broadcast_in_dim.3
  23.9 2.5 %prepare_rows.1 = (f32[8,1024]{1,0:T(8,128)S(1)}, f32[8,1024]{1,0:T(8,128)S(1)}, f32[8,1024]{1,0:T(8,128)S(1)}, f32[8,1024]{1,0:T(8,128)S(1)}, f32[1,1024]{1,0:T...) custom-call(s32[2]{0:T(128)S(1)} %pad_add_fusion.place, ...), custom_call_target="tpu_custom_call" | custom-call | tf_op jit(solution)/shard_map/prepare_rows/pallas_call | solution.py:245
  26.4 0.0 collective-permute-done.from_0
  26.4 6.6 %collective-permute-done.1.from_1 = f32[1088,128]{1,0:T(8,128)S(1)} collective-permute-done((f32[1088,128]{1,0:T(8,128)S(1)}, f32[1088,128]{1,0:T(8,128)S(1)}, u32[]{:S(2)}, u32[]{:S(2)}) %collective-permute-start.1) | collective-permute-done | bytes 557088 | tf_op jit(solution)/shard_map/ppermute | solution.py:31
  33.0 1.0 %relay_rows.1 = (f32[192,128]{1,0:T(8,128)S(1)}, f32[192,128]{1,0:T(8,128)S(1)}, f32[896,128]{1,0:T(8,128)}, f32[896,128]{1,0:T(8,128)}) custom-call(f32[1088,128]{1,0:T(8,128)S(1)} %collective-permute-done.from_0, f32[1088,128]{1,0:T(8,128)S(1)} %collective-permute-done.1.from_1, f32[1,1024]{1,0:T(1,128)S(1)} %get-tuple-element.24._.decay), custom_call_target="tpu_custom_call" | custom-call | tf_op jit(solution)/shard_map/relay_rows/pallas_call | solution.py:142
  34.0 1.9 %collective-permute-start.2 = (f32[192,128]{1,0:T(8,128)S(1)}, f32[192,128]{1,0:T(8,128)S(1)}, u32[]{:S(2)}, u32[]{:S(2)}) collective-permute-start(f32[192,128]{1,0:T(8,128)S(1)} %get-tuple-element.25), channel_id=1, source_target_pairs={{0,8},{8,0},{9,17},{17,9},{2,10},{10,2},{11,19},{19,11},{4,12},{12... | collective-permute-start | bytes 294920 | tf_op jit(solution)/shard_map/ppermute | solution.py:31
  35.9 7.7 %collective-permute-start.3 = (f32[192,128]{1,0:T(8,128)S(1)}, f32[192,128]{1,0:T(8,128)S(1)}, u32[]{:S(2)}, u32[]{:S(2)}) collective-permute-start(f32[192,128]{1,0:T(8,128)S(1)} %get-tuple-element.26), channel_id=1, source_target_pairs={{8,16},{16,8},{17,25},{25,17},{10,18},{18,10},{19,27},{27,19},{12,... | collective-permute-start | bytes 294920 | tf_op jit(solution)/shard_map/ppermute | solution.py:31
  43.7 1.9 %collective-permute-start.6 = (f32[896,128]{1,0:T(8,128)}, f32[896,128]{1,0:T(8,128)}, u32[]{:S(2)}, u32[]{:S(2)}) collective-permute-start(f32[896,128]{1,0:T(8,128)} %get-tuple-element.37), channel_id=1, source_target_pairs={{8,16},{16,8},{17,25},{25,17},{10,18},{18,10},{19,27},{27,19},{12,... | collective-permute-start | bytes 1376264 | tf_op jit(solution)/shard_map/ppermute | solution.py:31
  45.6 0.0 collective-permute-done.4.near_1
  45.6 1.9 %collective-permute-start.7 = (f32[896,128]{1,0:T(8,128)}, f32[896,128]{1,0:T(8,128)}, u32[]{:S(2)}, u32[]{:S(2)}) collective-permute-start(f32[896,128]{1,0:T(8,128)} %get-tuple-element.38), channel_id=1, source_target_pairs={{0,8},{8,0},{9,17},{17,9},{2,10},{10,2},{11,19},{19,11},{4,12},{12... | collective-permute-start | bytes 1376264 | tf_op jit(solution)/shard_map/ppermute | solution.py:31
  47.6 1.6 %raw_rows.1 = (f32[8,1024]{1,0:T(8,128)S(1)}, f32[8,1,128]{2,1,0:T(1,128)}) custom-call(s32[2]{0:T(128)S(1)} %pad_add_fusion.place, s32[128]{0:T(128)S(1)} %copy-done.5, f32[192,128]{1,0:T(8,128)S(1)} %collective-permute-done.2.lead_0, f32[192,128]{1,0:T(8,128)S(1)} %collective-permute-done.3.lead_1, f32[1024,128]{1,0:T(8,128)S(1)} %collective-permute-done.4.near_1, ...), custom_call_target="tpu_custom_call" | custom-call | flops 999999995904 | bytes 1048576 | tf_op jit(solution)/shard_map/raw_rows/pallas_call | solution.py:316
  49.3 4.7 %all-to-all-start = ((f32[8,1,128]{2,1,0:T(1,128)}), f32[8,1,128]{2,1,0:T(1,128)S(1)}, u32[]{:S(2)}, u32[]{:S(2)}) async-start(f32[8,1,128]{2,1,0:T(1,128)} %get-tuple-element.33), calls=%async_computation | async-start | bytes 8192 | tf_op jit(solution)/shard_map/all_to_all | solution.py:476
  54.0 4.7 %collective-permute-done.6.rest_1 = f32[896,128]{1,0:T(8,128)} collective-permute-done((f32[896,128]{1,0:T(8,128)}, f32[896,128]{1,0:T(8,128)}, u32[]{:S(2)}, u32[]{:S(2)}) %collective-permute-start.6) | collective-permute-done | bytes 458784 | tf_op jit(solution)/shard_map/ppermute | solution.py:31
  58.7 2.7 %final_rows.1 = (f32[2,1024,128]{2,1,0:T(8,128)}, f32[8,128]{1,0:T(8,128)S(1)}) custom-call(s32[2]{0:T(128)S(1)} %pad_add_fusion.place, s32[128]{0:T(128)S(1)} %copy-done.5, f32[2,1024,128]{2,1,0:T(8,128)S(1)} %get-tuple-element.36.here, f32[192,128]{1,0:T(8,128)} %copy-done.6, f32[192,128]{1,0:T(8,128)} %copy-done.7, ...), custom_call_target="tpu_custom_call" | custom-call | flops 10000000000 | bytes 1048576 | tf_op jit(solution)/shard_map/final_rows/pallas_call | solution.py:403
  61.4 0.7 %attend_rows.1 = bf16[3,2,1024]{2,1,0:T(2,128)(2,1)} custom-call(f32[8,1,128]{2,1,0:T(1,128)S(1)} %all-to-all-done.totals, f32[8,1024]{1,0:T(8,128)S(1)} %get-tuple-element.34.raw, f32[8,1024]{1,0:T(8,128)S(1)} %get-tuple-element.35.gated, f32[8,128]{1,0:T(8,128)S(1)} %get-tuple-element.40._), custom_call_target="tpu_custom_call" | custom-call | tf_op jit(solution)/shard_map/attend_rows/pallas_call | solution.py:437
  (20 shorter events, 0.0 us)
Async XLA Ops:
  0.6 23.2 %copy-start = (bf16[3,2,4,1024]{3,2,1,0:T(4,128)(2,1)S(1)}, bf16[3,2,4,1024]{3,2,1,0:T(4,128)(2,1)}, u32[]{:S(2)}) copy-start(bf16[3,2,4,1024]{3,2,1,0:T(4,128)(2,1)} %projected.3) | copy-start | bytes 147460
  0.6 23.2 %copy-start.4 = (s32[128]{0:T(128)S(1)}, s32[128]{0:T(128)}, u32[]{:S(2)}) copy-start(s32[128]{0:T(128)} %slot_ref.1) | copy-start | bytes 1540
  0.7 23.2 %copy-start.1 = (f32[1024]{0:T(1024)S(1)}, f32[1024]{0:T(1024)}, u32[]{:S(2)}) copy-start(f32[1024]{0:T(1024)} %param.11) | copy-start | bytes 12292
  0.7 23.1 %copy-start.8 = (f32[8]{0:T(128)S(1)}, f32[8]{0:T(128)}, u32[]{:S(2)}) copy-start(f32[8]{0:T(128)} %param.10) | copy-start | bytes 100
  3.7 43.9 %copy-start.5 = (s32[128]{0:T(128)S(1)}, s32[128]{0:T(128)}, u32[]{:S(2)}) copy-start(s32[128]{0:T(128)} %shard_ref.3) | copy-start | bytes 1540
  3.7 22.6 %collective-permute-start = (f32[1088,128]{1,0:T(8,128)S(1)}, f32[1088,128]{1,0:T(8,128)S(1)}, u32[]{:S(2)}, u32[]{:S(2)}) collective-permute-start(f32[1088,128]{1,0:T(8,128)S(1)} %get-tuple-element.22), channel_id=1, source_target_pairs={{0,8},{8,0},{9,17},{17,9},{2,10},{10,2},{11,19},{19,11},{4,12},{12... | collective-permute-start | bytes 1671176 | tf_op jit(solution)/shard_map/ppermute | solution.py:31
  7.0 26.0 %collective-permute-start.1 = (f32[1088,128]{1,0:T(8,128)S(1)}, f32[1088,128]{1,0:T(8,128)S(1)}, u32[]{:S(2)}, u32[]{:S(2)}) collective-permute-start(f32[1088,128]{1,0:T(8,128)S(1)} %get-tuple-element.23), channel_id=1, source_target_pairs={{8,16},{16,8},{17,25},{25,17},{10,18},{18,10},{19,27},{27,19},{12,... | collective-permute-start | bytes 1671176 | tf_op jit(solution)/shard_map/ppermute | solution.py:31
  19.9 25.7 %collective-permute-start.4 = (f32[1024,128]{1,0:T(8,128)S(1)}, f32[1024,128]{1,0:T(8,128)S(1)}, u32[]{:S(2)}, u32[]{:S(2)}) collective-permute-start(f32[1024,128]{1,0:T(8,128)S(1)} %get-tuple-element.27), channel_id=1, source_target_pairs={{8,16},{16,8},{17,25},{25,17},{10,18},{18,10},{19,27},{27,19},{12,... | collective-permute-start | bytes 1572872 | tf_op jit(solution)/shard_map/ppermute | solution.py:31
  21.9 25.7 %collective-permute-start.5 = (f32[1024,128]{1,0:T(8,128)S(1)}, f32[1024,128]{1,0:T(8,128)S(1)}, u32[]{:S(2)}, u32[]{:S(2)}) collective-permute-start(f32[1024,128]{1,0:T(8,128)S(1)} %get-tuple-element.28), channel_id=1, source_target_pairs={{0,8},{8,0},{9,17},{17,9},{2,10},{10,2},{11,19},{19,11},{4,12},{12... | collective-permute-start | bytes 1572872 | tf_op jit(solution)/shard_map/ppermute | solution.py:31
  26.3 21.2 %copy-start.2 = (f32[1,1024]{1,0:T(1,128)}, f32[1,1024]{1,0:T(1,128)S(1)}, u32[]{:S(2)}) copy-start(f32[1,1024]{1,0:T(1,128)S(1)} %get-tuple-element.24._.decay) | copy-start | bytes 12292
  34.0 13.5 %collective-permute-start.2 = (f32[192,128]{1,0:T(8,128)S(1)}, f32[192,128]{1,0:T(8,128)S(1)}, u32[]{:S(2)}, u32[]{:S(2)}) collective-permute-start(f32[192,128]{1,0:T(8,128)S(1)} %get-tuple-element.25), channel_id=1, source_target_pairs={{0,8},{8,0},{9,17},{17,9},{2,10},{10,2},{11,19},{19,11},{4,12},{12... | collective-permute-start | bytes 294920 | tf_op jit(solution)/shard_map/ppermute | solution.py:31
  35.9 11.6 %collective-permute-start.3 = (f32[192,128]{1,0:T(8,128)S(1)}, f32[192,128]{1,0:T(8,128)S(1)}, u32[]{:S(2)}, u32[]{:S(2)}) collective-permute-start(f32[192,128]{1,0:T(8,128)S(1)} %get-tuple-element.26), channel_id=1, source_target_pairs={{8,16},{16,8},{17,25},{25,17},{10,18},{18,10},{19,27},{27,19},{12,... | collective-permute-start | bytes 294920 | tf_op jit(solution)/shard_map/ppermute | solution.py:31
  43.7 15.0 %collective-permute-start.6 = (f32[896,128]{1,0:T(8,128)}, f32[896,128]{1,0:T(8,128)}, u32[]{:S(2)}, u32[]{:S(2)}) collective-permute-start(f32[896,128]{1,0:T(8,128)} %get-tuple-element.37), channel_id=1, source_target_pairs={{8,16},{16,8},{17,25},{25,17},{10,18},{18,10},{19,27},{27,19},{12,... | collective-permute-start | bytes 1376264 | tf_op jit(solution)/shard_map/ppermute | solution.py:31
  45.6 13.1 %collective-permute-start.7 = (f32[896,128]{1,0:T(8,128)}, f32[896,128]{1,0:T(8,128)}, u32[]{:S(2)}, u32[]{:S(2)}) collective-permute-start(f32[896,128]{1,0:T(8,128)} %get-tuple-element.38), channel_id=1, source_target_pairs={{0,8},{8,0},{9,17},{17,9},{2,10},{10,2},{11,19},{19,11},{4,12},{12... | collective-permute-start | bytes 1376264 | tf_op jit(solution)/shard_map/ppermute | solution.py:31
  47.5 1.7 %copy-start.6 = (f32[192,128]{1,0:T(8,128)}, f32[192,128]{1,0:T(8,128)S(1)}, u32[]{:S(2)}) copy-start(f32[192,128]{1,0:T(8,128)S(1)} %collective-permute-done.2.lead_0) | copy-start | bytes 294916
  47.6 1.7 %copy-start.7 = (f32[192,128]{1,0:T(8,128)}, f32[192,128]{1,0:T(8,128)S(1)}, u32[]{:S(2)}) copy-start(f32[192,128]{1,0:T(8,128)S(1)} %collective-permute-done.3.lead_1) | copy-start | bytes 294916
  47.6 11.1 %copy-start.3 = (f32[1,1024]{1,0:T(1,128)S(1)}, f32[1,1024]{1,0:T(1,128)}, u32[]{:S(2)}) copy-start(f32[1,1024]{1,0:T(1,128)} %copy-done.2) | copy-start | bytes 12292
  49.3 12.2 %all-to-all-start = ((f32[8,1,128]{2,1,0:T(1,128)}), f32[8,1,128]{2,1,0:T(1,128)S(1)}, u32[]{:S(2)}, u32[]{:S(2)}) async-start(f32[8,1,128]{2,1,0:T(1,128)} %get-tuple-element.33), calls=%async_computation | async-start | bytes 8192 | tf_op jit(solution)/shard_map/all_to_all | solution.py:476

commit v10 on v9

--- a/solution.py
+++ b/solution.py
@@ -9,7 +9,7 @@
 EPS = 1e-05
 F32 = jnp.float32
 BF16 = jnp.bfloat16
-EARLY = 1
+EARLY = 3
 TILE = 8
 MIB = 1024 * 1024
 SMEM = pl.BlockSpec(memory_space=pltpu.SMEM)
@@ -31,6 +31,11 @@
     return lax.ppermute(block, ("dp", "tensor"), route)
 
 
+def spot(place, group):
+    shard = lax.div(place[0], group)
+    return shard, 2 * ((shard ^ lax.rem(place[0], group)) & 1) - 1
+
+
 def start_all(copies):
     for copy in copies:
         copy.start()
@@ -55,12 +60,13 @@
     return first[:TILE] + first[TILE:] + second[:TILE]
 
 
-def pick_kernel(shards, live, strides, place, shard_hbm, slot_hbm, projected, states, *refs):
+def pick_kernel(shards, live, group, strides, place, shard_hbm, slot_hbm, projected, states, *refs):
     n_rows = len(strides)
     outs = refs[:n_rows]
-    shard_ref, slot_ref, inputs, sems = refs[n_rows:]
-    rows, dim = outs[-1].shape
-    device = place[0]
+    token, shard_ref, slot_ref, inputs, sems = refs[n_rows:]
+    dim = outs[0].shape[1]
+    rows = states.shape[1]
+    device, side = spot(place, group)
     plan = [
         pltpu.make_async_copy(shard_hbm, shard_ref, sems.at[n_rows]),
         pltpu.make_async_copy(slot_hbm, slot_ref, sems.at[n_rows + 1]),
@@ -71,18 +77,15 @@
     wait_all(plan)
     copies = []
     for n, stride in enumerate(strides):
-        target = lax.rem(device + stride * place[1] + shards, shards)
-        slot = jnp.int32(0)
-        for row in range(live):
-            mine = shard_ref[target * live + row] == device
-            slot = jnp.where(mine, slot_ref[target * live + row], slot)
+        slot = slot_for(stride, shards, live, device, side, shard_ref, slot_ref)
         copies.append(
             pltpu.make_async_copy(states.at[slot], outs[n].at[0:rows], sems.at[n])
         )
     start_all(copies)
+    token[...] = jnp.zeros_like(token)
     load.wait()
     tile_rows = rows // dim * TILE
-    for n in range(2):
+    for n in range(n_rows):
         outs[n][rows : rows + tile_rows] = jnp.zeros((tile_rows, dim), F32)
     for step in range(inputs.shape[0]):
         for row in range(live):
@@ -90,27 +93,27 @@
             for head in range(rows // dim):
                 at = rows + head * TILE + step * live + row
                 part = query[:, head * dim : (head + 1) * dim]
-                for n in range(2):
+                for n in range(n_rows):
                     outs[n][at : at + 1] = part
     wait_all(copies)
 
 
-def pick(place, from_shard, from_slot, projected, states, shards, live, strides):
+def pick(place, from_shard, from_slot, projected, states, shards, live, group, strides):
     rows, dim = states.shape[1:]
     tile_rows = rows // dim * TILE
     return pl.pallas_call(
-        functools.partial(pick_kernel, shards, live, strides),
-        out_shape=[jax.ShapeDtypeStruct((rows + tile_rows, dim), F32)] * 2
-        + [jax.ShapeDtypeStruct((rows, dim), F32)] * (len(strides) - 2),
+        functools.partial(pick_kernel, shards, live, group, strides),
+        out_shape=[jax.ShapeDtypeStruct((rows + tile_rows, dim), F32)] * len(strides)
+        + [jax.ShapeDtypeStruct((TILE, dim), F32)],
         in_specs=[SMEM] + [HBM] * 4,
-        out_specs=[VMEM] * len(strides),
+        out_specs=[VMEM] * (len(strides) + 1),
         scratch_shapes=[
             pltpu.SMEM(from_shard.shape, jnp.int32),
             pltpu.SMEM(from_slot.shape, jnp.int32),
             pltpu.VMEM(projected.shape, projected.dtype),
             pltpu.SemaphoreType.DMA((len(strides) + 3,)),
         ],
-        compiler_params=pltpu.CompilerParams(vmem_limit_bytes=6 * MIB),
+        compiler_params=pltpu.CompilerParams(vmem_limit_bytes=4 * MIB),
         name="pick_rows",
     )(place, *in_hbm(from_shard, from_slot, projected, states))
 
@@ -149,29 +152,45 @@
     )(from_0, from_1, after)
 
 
-def gap_of(row, shards, live, place, shard_ref):
-    device = place[0]
+def gap_of(row, shards, live, device, shard_ref):
     return lax.rem(device - shard_ref[device * live + row] + shards, shards)
 
 
-def at_stride(gap, stride, shards, place):
-    return gap == lax.rem(stride * place[1] + shards, shards)
+def at_stride(gap, stride, shards, side):
+    return gap == lax.rem(stride * side + shards, shards)
+
+
+def slot_for(stride, shards, live, device, side, shard_ref, slot_ref):
+    target = lax.rem(device + stride * side + shards, shards)
+    slot = jnp.int32(0)
+    for row in range(live):
+        mine = shard_ref[target * live + row] == device
+        slot = jnp.where(mine, slot_ref[target * live + row], slot)
+    return slot
 
 
 def prepare_kernel(
-    live, place, slot_ref, projected, rate, gain, states,
-    query, grown, base, gated, decay, made, here, outer, parts, sems,
+    shards, live, group, strides, place, shard_ref, slot_ref, projected, rate, gain, _, states,
+    query, grown, base, gated, decay, made, here, outer, token, *refs,
 ):
+    outs, (parts, sems) = refs[:-2], refs[-2:]
+    token[...] = jnp.zeros_like(token)
     rows, dim = here.shape[1:]
     heads = rows // dim
     steps = projected.shape[0]
+    device, side = spot(place, group)
     copies = [
         pltpu.make_async_copy(
-            states.at[slot_ref[place[0] * live + row]], here.at[row], sems.at[row]
+            states.at[slot_ref[device * live + row]], here.at[row], sems.at[row]
         )
         for row in range(live)
     ]
     start_all(copies)
+    sends = []
+    for n, stride in enumerate(strides):
+        slot = slot_for(stride, shards, live, device, side, shard_ref, slot_ref)
+        sends.append(pltpu.make_async_copy(states.at[slot], outs[n], sems.at[live + n]))
+    start_all(sends)
     parts[...] = jnp.zeros_like(parts)
     for step in range(steps):
         for row in range(live):
@@ -236,30 +255,35 @@
             made[row, head * TILE : (head + 1) * TILE] = products(
                 queries[:, span], here[row, span]
             )
-
-
-def prepare(place, from_slot, projected, rate, gain, states, live):
+    wait_all(sends)
+
+
+def prepare(
+    place, from_shard, from_slot, projected, rate, gain, after, states, shards, live, group, strides
+):
     rows, dim = states.shape[1:]
     tile = jax.ShapeDtypeStruct((TILE, rows), F32)
     whole = jax.ShapeDtypeStruct((live, rows, dim), F32)
     return pl.pallas_call(
-        functools.partial(prepare_kernel, live),
+        functools.partial(prepare_kernel, shards, live, group, strides),
         out_shape=[tile] * 4
         + [
             jax.ShapeDtypeStruct((1, rows), F32),
             jax.ShapeDtypeStruct((live, rows // dim * TILE, dim), F32),
             whole,
             whole,
-        ],
-        in_specs=[SMEM] * 2 + [VMEM] * 3 + [HBM],
-        out_specs=[VMEM] * 8,
+            jax.ShapeDtypeStruct((TILE, dim), F32),
+        ]
+        + [jax.ShapeDtypeStruct((rows, dim), F32)] * len(strides),
+        in_specs=[SMEM] * 3 + [VMEM] * 4 + [HBM],
+        out_specs=[VMEM] * (9 + len(strides)),
         scratch_shapes=[
             pltpu.VMEM((projected.shape[2], TILE, rows), F32),
-            pltpu.SemaphoreType.DMA((live,)),
+            pltpu.SemaphoreType.DMA((live + len(strides),)),
         ],
-        compiler_params=pltpu.CompilerParams(vmem_limit_bytes=6 * MIB),
+        compiler_params=pltpu.CompilerParams(vmem_limit_bytes=8 * MIB),
         name="prepare_rows",
-    )(place, from_slot, projected, rate, gain, *in_hbm(states))
+    )(place, from_shard, from_slot, projected, rate, gain, after, *in_hbm(states))
 
 
 def diagonal(dim):
@@ -268,7 +292,7 @@
 
 
 def raw_kernel(
-    shards, live, place, shard_ref, lead_0, lead_1, near_1, near_0,
+    shards, live, group, place, shard_ref, lead_0, lead_1, near_1, near_0,
     local, query, grown, base, raw, sums, made, tiles, sem,
 ):
     rows, dim = near_0.shape
@@ -285,11 +309,12 @@
     for n, lead in enumerate((lead_1, lead_0)):
         made[live + 2 + n] = lead[0:tile_rows]
     picks = []
-    for row in range(live):
-        gap = gap_of(row, shards, live, place, shard_ref)
+    device, side = spot(place, group)
+    for row in range(live):
+        gap = gap_of(row, shards, live, device, shard_ref)
         index = jnp.int32(row)
         for n, stride in enumerate((-1, 1, -2, 2)):
-            index = jnp.where(at_stride(gap, stride, shards, place), live + n, index)
+            index = jnp.where(at_stride(gap, stride, shards, side), live + n, index)
         picks.append(index)
     which = lax.rem(lax.broadcasted_iota(jnp.int32, (TILE, dim), 0), live)
     total = jnp.zeros((TILE, dim), F32)
@@ -314,7 +339,7 @@
 def raw_of(place, from_shard, arrived, small, shards, live, group):
     rows, dim = arrived[-1].shape
     return pl.pallas_call(
-        functools.partial(raw_kernel, shards, live),
+        functools.partial(raw_kernel, shards, live, group),
         out_shape=[
             jax.ShapeDtypeStruct((TILE, rows), F32),
             jax.ShapeDtypeStruct((group, 1, dim), F32),
@@ -333,12 +358,13 @@
 
 
 def final_kernel(
-    shards, live, place, shard_ref, here, lead_0, lead_1, near_1, near_0,
+    shards, live, group, place, shard_ref, here, lead_0, lead_1, near_1, near_0,
     rest_1, rest_0, outer, decay, final, token, held, made, sems_in, sems,
 ):
     rows, dim = here.shape[1:]
     heads = rows // dim
     early, tile_rows = EARLY * dim, heads * TILE
+    device, side = spot(place, group)
     token[...] = jnp.zeros_like(token)
 
     def loads(row, lead, rest):
@@ -353,9 +379,9 @@
 
     cases = []
     for row in range(live):
-        gap = gap_of(row, shards, live, place, shard_ref)
-        far_0 = at_stride(gap, 2, shards, place)
-        far_1 = at_stride(gap, -2, shards, place)
+        gap = gap_of(row, shards, live, device, shard_ref)
+        far_0 = at_stride(gap, 2, shards, side)
+        far_1 = at_stride(gap, -2, shards, side)
         for found, lead, rest in ((far_0, lead_0, rest_0), (far_1, lead_1, rest_1)):
 
             @pl.when(found)
@@ -365,8 +391,8 @@
         cases.append(
             [
                 (gap == 0, here.at[row]),
-                (at_stride(gap, 1, shards, place), near_0),
-                (at_stride(gap, -1, shards, place), near_1),
+                (at_stride(gap, 1, shards, side), near_0),
+                (at_stride(gap, -1, shards, side), near_1),
                 (jnp.logical_or(far_0, far_1), held.at[row]),
             ]
         )
@@ -398,10 +424,10 @@
     wait_all(copies)
 
 
-def final_of(place, from_shard, here, lead, near, rest, small, shards, live):
+def final_of(place, from_shard, here, lead, near, rest, small, shards, live, group):
     rows, dim = here.shape[1:]
     return pl.pallas_call(
-        functools.partial(final_kernel, shards, live),
+        functools.partial(final_kernel, shards, live, group),
         out_shape=[
             jax.ShapeDtypeStruct((live, rows, dim), F32),
             jax.ShapeDtypeStruct((TILE, dim), F32),
@@ -449,23 +475,21 @@
     steps, live = projected.shape[:2]
     slots, heads, dim = states.shape[:3]
     width = heads * dim
-    shard = lax.axis_index("dp").astype(jnp.int32)
-    side = 2 * ((shard ^ lax.axis_index("tensor").astype(jnp.int32)) & 1) - 1
-    place = jnp.stack([shard, side])
+    place = lax.axis_index(("dp", "tensor")).astype(jnp.int32).reshape(1)
     states = states.reshape(slots, width, dim)
 
+    row_0, row_1, after = pick(
+        place, from_shard, from_slot, projected, states, shards, live, group, (-2, 2)
+    )
+    half_1, half_0 = swapped(row_1, 1), swapped(row_0, 0)
     rate = jnp.repeat(decay_rate, dim).reshape(1, width)
     gain = norm_gain.reshape(1, width)
-    query, grown, base, gated, decay, local, here, outer = prepare(
-        place, from_slot, projected, rate, gain, states, live
+    query, grown, base, gated, decay, local, here, outer, token, row_0, row_1 = prepare(
+        place, from_shard, from_slot, projected, rate, gain, after, states, shards, live,
+        group, (-1, 1),
     )
-
-    rows = pick(
-        place, from_shard, from_slot, projected, states, shards, live, (-2, 2, -1, 1)
-    )
-    half_1, half_0 = swapped(rows[1], 1), swapped(rows[0], 0)
-    near_1, near_0 = swapped(rows[3], 1), swapped(rows[2], 0)
-    sent = relay(half_0, half_1, decay, heads)
+    near_1, near_0 = swapped(row_1, 1), swapped(row_0, 0)
+    sent = relay(half_0, half_1, token, heads)
     lead_1, lead_0 = swapped(sent[0], 1), swapped(sent[1], 0)
     rest_1, rest_0 = swapped(sent[2], 1), swapped(sent[3], 0)
 
@@ -476,7 +500,7 @@
     totals = lax.all_to_all(sums, "tensor", 0, 0)
     final, token = final_of(
         place, from_shard, here, (lead_0, lead_1), (near_1, near_0), (rest_1, rest_0),
-        (outer, decay), shards, live,
+        (outer, decay), shards, live, group,
     )
     attended = attend(totals, raw, gated, token, live, steps, width * group)
     return attended, final.reshape(live, heads, dim, dim)

time: 62.6 us -> 59.7 us (0.954)
  the two profiles are of different devices: /device:TPU:24 before, /device:TPU:1 now
where the time goes in v10:
time: 59.7 us; the launch traced here: 59.3 us
  starting transfers between devices  42.2 us (71%)
  Pallas kernels  9.29 us (16%)
  waiting for transfers between devices  6.8 us (11%)
  between operations  0.83 us (1%)
    ppermute x8, starting transfers between devices, swapped(): return lax.ppermute(block, ('dp', 'tensor'), route)  36.2 us
    all_to_all x1, starting transfers between devices, on_device(): totals = lax.all_to_all(sums, 'tensor', 0, 0)  6.02 us
    ppermute x8, waiting for transfers between devices, swapped(): return lax.ppermute(block, ('dp', 'tensor'), route)  3.96 us
    all_to_all x1, waiting for transfers between devices, on_device(): totals = lax.all_to_all(sums, 'tensor', 0, 0)  2.84 us
    pallas_call x1, Pallas kernels, prepare(): pl.pallas_call(functools.partial(prepare_kernel, shards, live, group, str...  2.29 us
    pallas_call x1, Pallas kernels, pick(): pl.pallas_call(functools.partial(pick_kernel, shards, live, group, stride...  2.06 us
    pallas_call x1, Pallas kernels, final_of(): pl.pallas_call(functools.partial(final_kernel, shards, live, group), out_...  1.65 us
    pallas_call x1, Pallas kernels, raw_of(): pl.pallas_call(functools.partial(raw_kernel, shards, live, group), out_sh...  1.63 us
  transfers between devices with their start and end apart: 9, of which 3 were waited for; matrix products, arithmetic and copies ran while one was open for 0% of the time, Pallas kernels for 11%

profile of v10, /device:TPU:1, one launch (start us, length us, event | category | flops | bytes accessed | tf_op | source)
XLA Modules:
  0.0 59.3 jit_solution(9248727825875166658)
XLA Ops:
  0.7 2.1 %pick_rows.1 = (f32[1088,128]{1,0:T(8,128)S(1)}, f32[1088,128]{1,0:T(8,128)S(1)}, f32[8,128]{1,0:T(8,128)S(1)}) custom-call(s32[1]{0:T(128)} %bitcast.place, s32[128]{0:T(128)} %shard_ref.5, s32[128]{0:T(128)} %slot_ref.1, bf16[3,2,4,1024]{3,2,1,0:T(4,128)(2,1)} %projected.3, f32[4,1024,128]{2,1,0:T(8,128)} %bitcast.7), custom_call_target="tpu_custom_call" | custom-call | tf_op jit(solution)/shard_map/pick_rows/pallas_call | solution.py:104
  2.8 14.1 %collective-permute-start = (f32[1088,128]{1,0:T(8,128)S(1)}, f32[1088,128]{1,0:T(8,128)S(1)}, u32[]{:S(2)}, u32[]{:S(2)}) collective-permute-start(f32[1088,128]{1,0:T(8,128)S(1)} %get-tuple-element.24), channel_id=1, source_target_pairs={{0,8},{8,0},{9,17},{17,9},{2,10},{10,2},{11,19},{19,11},{4,12},{12... | collective-permute-start | bytes 1671176 | tf_op jit(solution)/shard_map/ppermute | solution.py:31
  16.9 1.9 %collective-permute-start.1 = (f32[1088,128]{1,0:T(8,128)S(1)}, f32[1088,128]{1,0:T(8,128)S(1)}, u32[]{:S(2)}, u32[]{:S(2)}) collective-permute-start(f32[1088,128]{1,0:T(8,128)S(1)} %get-tuple-element.25), channel_id=1, source_target_pairs={{8,16},{16,8},{17,25},{25,17},{10,18},{18,10},{19,27},{27,19},{12,... | collective-permute-start | bytes 1671176 | tf_op jit(solution)/shard_map/ppermute | solution.py:31
  18.8 0.1 broadcast_in_dim.3
  18.9 2.3 %prepare_rows.1 = (f32[8,1024]{1,0:T(8,128)S(1)}, f32[8,1024]{1,0:T(8,128)S(1)}, f32[8,1024]{1,0:T(8,128)S(1)}, f32[8,1024]{1,0:T(8,128)S(1)}, f32[1,1024]{1,0:T...) custom-call(s32[1]{0:T(128)} %bitcast.place, ...), custom_call_target="tpu_custom_call" | custom-call | tf_op jit(solution)/shard_map/prepare_rows/pallas_call | solution.py:267
  21.2 3.4 %collective-permute-start.4 = (f32[1024,128]{1,0:T(8,128)S(1)}, f32[1024,128]{1,0:T(8,128)S(1)}, u32[]{:S(2)}, u32[]{:S(2)}) collective-permute-start(f32[1024,128]{1,0:T(8,128)S(1)} %get-tuple-element.30), channel_id=1, source_target_pairs={{8,16},{16,8},{17,25},{25,17},{10,18},{18,10},{19,27},{27,19},{12,... | collective-permute-start | bytes 1572872 | tf_op jit(solution)/shard_map/ppermute | solution.py:31
  24.6 1.9 %collective-permute-start.5 = (f32[1024,128]{1,0:T(8,128)S(1)}, f32[1024,128]{1,0:T(8,128)S(1)}, u32[]{:S(2)}, u32[]{:S(2)}) collective-permute-start(f32[1024,128]{1,0:T(8,128)S(1)} %get-tuple-element.31), channel_id=1, source_target_pairs={{0,8},{8,0},{9,17},{17,9},{2,10},{10,2},{11,19},{19,11},{4,12},{12... | collective-permute-start | bytes 1572872 | tf_op jit(solution)/shard_map/ppermute | solution.py:31
  26.5 0.0 collective-permute-done.from_0
  26.5 0.9 %collective-permute-done.1.from_1 = f32[1088,128]{1,0:T(8,128)S(1)} collective-permute-done((f32[1088,128]{1,0:T(8,128)S(1)}, f32[1088,128]{1,0:T(8,128)S(1)}, u32[]{:S(2)}, u32[]{:S(2)}) %collective-permute-start.1) | collective-permute-done | bytes 557088 | tf_op jit(solution)/shard_map/ppermute | solution.py:31
  27.5 1.0 %relay_rows.1 = (f32[448,128]{1,0:T(8,128)S(1)}, f32[448,128]{1,0:T(8,128)S(1)}, f32[640,128]{1,0:T(8,128)}, f32[640,128]{1,0:T(8,128)}) custom-call(f32[1088,128]{1,0:T(8,128)S(1)} %collective-permute-done.from_0, f32[1088,128]{1,0:T(8,128)S(1)} %collective-permute-done.1.from_1, f32[8,128]{1,0:T(8,128)S(1)} %get-tuple-element.27._), custom_call_target="tpu_custom_call" | custom-call | tf_op jit(solution)/shard_map/relay_rows/pallas_call | solution.py:145
  28.4 7.1 %collective-permute-start.2 = (f32[448,128]{1,0:T(8,128)S(1)}, f32[448,128]{1,0:T(8,128)S(1)}, u32[]{:S(2)}, u32[]{:S(2)}) collective-permute-start(f32[448,128]{1,0:T(8,128)S(1)} %get-tuple-element.28), channel_id=1, source_target_pairs={{0,8},{8,0},{9,17},{17,9},{2,10},{10,2},{11,19},{19,11},{4,12},{12... | collective-permute-start | bytes 688136 | tf_op jit(solution)/shard_map/ppermute | solution.py:31
  35.5 1.9 %collective-permute-start.3 = (f32[448,128]{1,0:T(8,128)S(1)}, f32[448,128]{1,0:T(8,128)S(1)}, u32[]{:S(2)}, u32[]{:S(2)}) collective-permute-start(f32[448,128]{1,0:T(8,128)S(1)} %get-tuple-element.29), channel_id=1, source_target_pairs={{8,16},{16,8},{17,25},{25,17},{10,18},{18,10},{19,27},{27,19},{12,... | collective-permute-start | bytes 688136 | tf_op jit(solution)/shard_map/ppermute | solution.py:31
  37.5 3.4 %collective-permute-start.6 = (f32[640,128]{1,0:T(8,128)}, f32[640,128]{1,0:T(8,128)}, u32[]{:S(2)}, u32[]{:S(2)}) collective-permute-start(f32[640,128]{1,0:T(8,128)} %get-tuple-element.40), channel_id=1, source_target_pairs={{8,16},{16,8},{17,25},{25,17},{10,18},{18,10},{19,27},{27,19},{12,... | collective-permute-start | bytes 983048 | tf_op jit(solution)/shard_map/ppermute | solution.py:31
  40.8 0.0 collective-permute-done.4.near_1
  40.9 2.5 %collective-permute-start.7 = (f32[640,128]{1,0:T(8,128)}, f32[640,128]{1,0:T(8,128)}, u32[]{:S(2)}, u32[]{:S(2)}) collective-permute-start(f32[640,128]{1,0:T(8,128)} %get-tuple-element.41), channel_id=1, source_target_pairs={{0,8},{8,0},{9,17},{17,9},{2,10},{10,2},{11,19},{19,11},{4,12},{12... | collective-permute-start | bytes 983048 | tf_op jit(solution)/shard_map/ppermute | solution.py:31
  43.4 0.0 collective-permute-done.5.near_0
  43.4 3.0 %collective-permute-done.2.lead_0 = f32[448,128]{1,0:T(8,128)S(1)} collective-permute-done((f32[448,128]{1,0:T(8,128)S(1)}, f32[448,128]{1,0:T(8,128)S(1)}, u32[]{:S(2)}, u32[]{:S(2)}) %collective-permute-start.2) | collective-permute-done | bytes 229408 | tf_op jit(solution)/shard_map/ppermute | solution.py:31
  46.4 0.0 collective-permute-done.3.lead_1
  46.4 1.6 %raw_rows.1 = (f32[8,1024]{1,0:T(8,128)S(1)}, f32[8,1,128]{2,1,0:T(1,128)}) custom-call(s32[1]{0:T(128)} %bitcast.place, s32[128]{0:T(128)S(1)} %copy-done.3, f32[448,128]{1,0:T(8,128)S(1)} %collective-permute-done.2.lead_0, f32[448,128]{1,0:T(8,128)S(1)} %collective-permute-done.3.lead_1, f32[1024,128]{1,0:T(8,128)S(1)} %collective-permute-done.4.near_1, ...), custom_call_target="tpu_custom_call" | custom-call | flops 999999995904 | bytes 1048576 | tf_op jit(solution)/shard_map/raw_rows/pallas_call | solution.py:341
  48.0 6.0 %all-to-all-start = ((f32[8,1,128]{2,1,0:T(1,128)}), f32[8,1,128]{2,1,0:T(1,128)S(1)}, u32[]{:S(2)}, u32[]{:S(2)}) async-start(f32[8,1,128]{2,1,0:T(1,128)} %get-tuple-element.36), calls=%async_computation | async-start | bytes 8192 | tf_op jit(solution)/shard_map/all_to_all | solution.py:500
  54.1 0.0 collective-permute-done.6.rest_1
  54.1 1.6 %final_rows.1 = (f32[2,1024,128]{2,1,0:T(8,128)}, f32[8,128]{1,0:T(8,128)S(1)}) custom-call(s32[1]{0:T(128)} %bitcast.place, s32[128]{0:T(128)S(1)} %copy-done.3, f32[2,1024,128]{2,1,0:T(8,128)S(1)} %get-tuple-element.39.here, f32[448,128]{1,0:T(8,128)} %copy-done.4, f32[448,128]{1,0:T(8,128)} %copy-done.5, f32[1024,128]{1,0:T(8,128)S(1)} %collective-permute-done.4.near_1, ...), custom_call_target="tpu_custom_call" | custom-call | flops 10000000000 | bytes 1048576 | tf_op jit(solution)/shard_map/final_rows/pallas_call | solution.py:429
  55.7 2.8 %all-to-all-done.totals = f32[8,1,128]{2,1,0:T(1,128)S(1)} async-done(((f32[8,1,128]{2,1,0:T(1,128)}), f32[8,1,128]{2,1,0:T(1,128)S(1)}, u32[]{:S(2)}, u32[]{:S(2)}) %all-to-all-start) | async-done | bytes 4128 | tf_op jit(solution)/shard_map/all_to_all | solution.py:500
  58.6 0.7 %attend_rows.1 = bf16[3,2,1024]{2,1,0:T(2,128)(2,1)} custom-call(f32[8,1,128]{2,1,0:T(1,128)S(1)} %all-to-all-done.totals, f32[8,1024]{1,0:T(8,128)S(1)} %get-tuple-element.37.raw, f32[8,1024]{1,0:T(8,128)S(1)} %get-tuple-element.38.gated, f32[8,128]{1,0:T(8,128)S(1)} %get-tuple-element.44._), custom_call_target="tpu_custom_call" | custom-call | tf_op jit(solution)/shard_map/attend_rows/pallas_call | solution.py:463
  (15 shorter events, 0.0 us)
Async XLA Ops:
  0.6 18.3 %copy-start.3 = (s32[128]{0:T(128)S(1)}, s32[128]{0:T(128)}, u32[]{:S(2)}) copy-start(s32[128]{0:T(128)} %shard_ref.5) | copy-start | bytes 1540
  0.6 18.3 %copy-start = (bf16[3,2,4,1024]{3,2,1,0:T(4,128)(2,1)S(1)}, bf16[3,2,4,1024]{3,2,1,0:T(4,128)(2,1)}, u32[]{:S(2)}) copy-start(bf16[3,2,4,1024]{3,2,1,0:T(4,128)(2,1)} %projected.3) | copy-start | bytes 147460
  0.7 18.3 %copy-start.2 = (s32[128]{0:T(128)S(1)}, s32[128]{0:T(128)}, u32[]{:S(2)}) copy-start(s32[128]{0:T(128)} %slot_ref.1) | copy-start | bytes 1540
  0.7 18.3 %copy-start.1 = (f32[1024]{0:T(1024)S(1)}, f32[1024]{0:T(1024)}, u32[]{:S(2)}) copy-start(f32[1024]{0:T(1024)} %param.11) | copy-start | bytes 12292
  0.7 18.2 %copy-start.6 = (f32[8]{0:T(128)S(1)}, f32[8]{0:T(128)}, u32[]{:S(2)}) copy-start(f32[8]{0:T(128)} %param.10) | copy-start | bytes 100
  2.8 23.8 %collective-permute-start = (f32[1088,128]{1,0:T(8,128)S(1)}, f32[1088,128]{1,0:T(8,128)S(1)}, u32[]{:S(2)}, u32[]{:S(2)}) collective-permute-start(f32[1088,128]{1,0:T(8,128)S(1)} %get-tuple-element.24), channel_id=1, source_target_pairs={{0,8},{8,0},{9,17},{17,9},{2,10},{10,2},{11,19},{19,11},{4,12},{12... | collective-permute-start | bytes 1671176 | tf_op jit(solution)/shard_map/ppermute | solution.py:31
  16.9 10.6 %collective-permute-start.1 = (f32[1088,128]{1,0:T(8,128)S(1)}, f32[1088,128]{1,0:T(8,128)S(1)}, u32[]{:S(2)}, u32[]{:S(2)}) collective-permute-start(f32[1088,128]{1,0:T(8,128)S(1)} %get-tuple-element.25), channel_id=1, source_target_pairs={{8,16},{16,8},{17,25},{25,17},{10,18},{18,10},{19,27},{27,19},{12,... | collective-permute-start | bytes 1671176 | tf_op jit(solution)/shard_map/ppermute | solution.py:31
  21.2 19.6 %collective-permute-start.4 = (f32[1024,128]{1,0:T(8,128)S(1)}, f32[1024,128]{1,0:T(8,128)S(1)}, u32[]{:S(2)}, u32[]{:S(2)}) collective-permute-start(f32[1024,128]{1,0:T(8,128)S(1)} %get-tuple-element.30), channel_id=1, source_target_pairs={{8,16},{16,8},{17,25},{25,17},{10,18},{18,10},{19,27},{27,19},{12,... | collective-permute-start | bytes 1572872 | tf_op jit(solution)/shard_map/ppermute | solution.py:31
  24.6 18.8 %collective-permute-start.5 = (f32[1024,128]{1,0:T(8,128)S(1)}, f32[1024,128]{1,0:T(8,128)S(1)}, u32[]{:S(2)}, u32[]{:S(2)}) collective-permute-start(f32[1024,128]{1,0:T(8,128)S(1)} %get-tuple-element.31), channel_id=1, source_target_pairs={{0,8},{8,0},{9,17},{17,9},{2,10},{10,2},{11,19},{19,11},{4,12},{12... | collective-permute-start | bytes 1572872 | tf_op jit(solution)/shard_map/ppermute | solution.py:31
  28.4 17.9 %collective-permute-start.2 = (f32[448,128]{1,0:T(8,128)S(1)}, f32[448,128]{1,0:T(8,128)S(1)}, u32[]{:S(2)}, u32[]{:S(2)}) collective-permute-start(f32[448,128]{1,0:T(8,128)S(1)} %get-tuple-element.28), channel_id=1, source_target_pairs={{0,8},{8,0},{9,17},{17,9},{2,10},{10,2},{11,19},{19,11},{4,12},{12... | collective-permute-start | bytes 688136 | tf_op jit(solution)/shard_map/ppermute | solution.py:31
  35.5 10.8 %collective-permute-start.3 = (f32[448,128]{1,0:T(8,128)S(1)}, f32[448,128]{1,0:T(8,128)S(1)}, u32[]{:S(2)}, u32[]{:S(2)}) collective-permute-start(f32[448,128]{1,0:T(8,128)S(1)} %get-tuple-element.29), channel_id=1, source_target_pairs={{8,16},{16,8},{17,25},{25,17},{10,18},{18,10},{19,27},{27,19},{12,... | collective-permute-start | bytes 688136 | tf_op jit(solution)/shard_map/ppermute | solution.py:31
  37.5 16.6 %collective-permute-start.6 = (f32[640,128]{1,0:T(8,128)}, f32[640,128]{1,0:T(8,128)}, u32[]{:S(2)}, u32[]{:S(2)}) collective-permute-start(f32[640,128]{1,0:T(8,128)} %get-tuple-element.40), channel_id=1, source_target_pairs={{8,16},{16,8},{17,25},{25,17},{10,18},{18,10},{19,27},{27,19},{12,... | collective-permute-start | bytes 983048 | tf_op jit(solution)/shard_map/ppermute | solution.py:31
  40.9 13.2 %collective-permute-start.7 = (f32[640,128]{1,0:T(8,128)}, f32[640,128]{1,0:T(8,128)}, u32[]{:S(2)}, u32[]{:S(2)}) collective-permute-start(f32[640,128]{1,0:T(8,128)} %get-tuple-element.41), channel_id=1, source_target_pairs={{0,8},{8,0},{9,17},{17,9},{2,10},{10,2},{11,19},{19,11},{4,12},{12... | collective-permute-start | bytes 983048 | tf_op jit(solution)/shard_map/ppermute | solution.py:31
  46.4 1.6 %copy-start.4 = (f32[448,128]{1,0:T(8,128)}, f32[448,128]{1,0:T(8,128)S(1)}, u32[]{:S(2)}) copy-start(f32[448,128]{1,0:T(8,128)S(1)} %collective-permute-done.2.lead_0) | copy-start | bytes 688132
  46.4 1.7 %copy-start.5 = (f32[448,128]{1,0:T(8,128)}, f32[448,128]{1,0:T(8,128)S(1)}, u32[]{:S(2)}) copy-start(f32[448,128]{1,0:T(8,128)S(1)} %collective-permute-done.3.lead_1) | copy-start | bytes 688132
  48.0 10.5 %all-to-all-start = ((f32[8,1,128]{2,1,0:T(1,128)}), f32[8,1,128]{2,1,0:T(1,128)S(1)}, u32[]{:S(2)}, u32[]{:S(2)}) async-start(f32[8,1,128]{2,1,0:T(1,128)} %get-tuple-element.36), calls=%async_computation | async-start | bytes 8192 | tf_op jit(solution)/shard_map/all_to_all | solution.py:500

commit v11 on v10

--- a/solution.py
+++ b/solution.py
@@ -63,30 +63,21 @@
 def pick_kernel(shards, live, group, strides, place, shard_hbm, slot_hbm, projected, states, *refs):
     n_rows = len(strides)
     outs = refs[:n_rows]
-    token, shard_ref, slot_ref, inputs, sems = refs[n_rows:]
+    staged, shard_ref, slot_ref, inputs, sems = refs[n_rows:]
     dim = outs[0].shape[1]
     rows = states.shape[1]
     device, side = spot(place, group)
-    plan = [
-        pltpu.make_async_copy(shard_hbm, shard_ref, sems.at[n_rows]),
-        pltpu.make_async_copy(slot_hbm, slot_ref, sems.at[n_rows + 1]),
+    copies = [
+        pltpu.make_async_copy(shard_hbm, shard_ref, sems.at[0]),
+        pltpu.make_async_copy(slot_hbm, slot_ref, sems.at[1]),
+        pltpu.make_async_copy(projected, inputs, sems.at[2]),
+        pltpu.make_async_copy(states, staged, sems.at[3]),
     ]
-    load = pltpu.make_async_copy(projected, inputs, sems.at[n_rows + 2])
-    start_all(plan)
-    load.start()
-    wait_all(plan)
-    copies = []
-    for n, stride in enumerate(strides):
-        slot = slot_for(stride, shards, live, device, side, shard_ref, slot_ref)
-        copies.append(
-            pltpu.make_async_copy(states.at[slot], outs[n].at[0:rows], sems.at[n])
-        )
     start_all(copies)
-    token[...] = jnp.zeros_like(token)
-    load.wait()
     tile_rows = rows // dim * TILE
     for n in range(n_rows):
         outs[n][rows : rows + tile_rows] = jnp.zeros((tile_rows, dim), F32)
+    copies[2].wait()
     for step in range(inputs.shape[0]):
         for row in range(live):
             query = jax.nn.silu(inputs[step, row].astype(F32))[0:1]
@@ -95,7 +86,14 @@
                 part = query[:, head * dim : (head + 1) * dim]
                 for n in range(n_rows):
                     outs[n][at : at + 1] = part
-    wait_all(copies)
+    wait_all(copies[:2])
+    slots = [
+        slot_for(stride, shards, live, device, side, shard_ref, slot_ref)
+        for stride in strides
+    ]
+    copies[3].wait()
+    for n, slot in enumerate(slots):
+        outs[n][0:rows] = staged[slot]
 
 
 def pick(place, from_shard, from_slot, projected, states, shards, live, group, strides):
@@ -104,16 +102,16 @@
     return pl.pallas_call(
         functools.partial(pick_kernel, shards, live, group, strides),
         out_shape=[jax.ShapeDtypeStruct((rows + tile_rows, dim), F32)] * len(strides)
-        + [jax.ShapeDtypeStruct((TILE, dim), F32)],
+        + [jax.ShapeDtypeStruct(states.shape, F32)],
         in_specs=[SMEM] + [HBM] * 4,
         out_specs=[VMEM] * (len(strides) + 1),
         scratch_shapes=[
             pltpu.SMEM(from_shard.shape, jnp.int32),
             pltpu.SMEM(from_slot.shape, jnp.int32),
             pltpu.VMEM(projected.shape, projected.dtype),
-            pltpu.SemaphoreType.DMA((len(strides) + 3,)),
+            pltpu.SemaphoreType.DMA((4,)),
         ],
-        compiler_params=pltpu.CompilerParams(vmem_limit_bytes=4 * MIB),
+        compiler_params=pltpu.CompilerParams(vmem_limit_bytes=6 * MIB),
         name="pick_rows",
     )(place, *in_hbm(from_shard, from_slot, projected, states))
 
@@ -170,27 +168,20 @@
 
 
 def prepare_kernel(
-    shards, live, group, strides, place, shard_ref, slot_ref, projected, rate, gain, _, states,
+    shards, live, group, strides, place, shard_ref, slot_ref, projected, rate, gain, states,
     query, grown, base, gated, decay, made, here, outer, token, *refs,
 ):
-    outs, (parts, sems) = refs[:-2], refs[-2:]
+    outs, parts = refs[:-1], refs[-1]
     token[...] = jnp.zeros_like(token)
     rows, dim = here.shape[1:]
     heads = rows // dim
     steps = projected.shape[0]
     device, side = spot(place, group)
-    copies = [
-        pltpu.make_async_copy(
-            states.at[slot_ref[device * live + row]], here.at[row], sems.at[row]
-        )
-        for row in range(live)
-    ]
-    start_all(copies)
-    sends = []
     for n, stride in enumerate(strides):
         slot = slot_for(stride, shards, live, device, side, shard_ref, slot_ref)
-        sends.append(pltpu.make_async_copy(states.at[slot], outs[n], sems.at[live + n]))
-    start_all(sends)
+        outs[n][...] = states[slot]
+    for row in range(live):
+        here[row] = states[slot_ref[device * live + row]]
     parts[...] = jnp.zeros_like(parts)
     for step in range(steps):
         for row in range(live):
@@ -248,18 +239,16 @@
                 (((0,), (0,)), ((), ())),
                 preferred_element_type=F32,
             )
-    wait_all(copies)
     for row in range(live):
         for head in range(heads):
             span = slice(head * dim, (head + 1) * dim)
             made[row, head * TILE : (head + 1) * TILE] = products(
                 queries[:, span], here[row, span]
             )
-    wait_all(sends)
 
 
 def prepare(
-    place, from_shard, from_slot, projected, rate, gain, after, states, shards, live, group, strides
+    place, from_shard, from_slot, projected, rate, gain, states, shards, live, group, strides
 ):
     rows, dim = states.shape[1:]
     tile = jax.ShapeDtypeStruct((TILE, rows), F32)
@@ -275,15 +264,12 @@
             jax.ShapeDtypeStruct((TILE, dim), F32),
         ]
         + [jax.ShapeDtypeStruct((rows, dim), F32)] * len(strides),
-        in_specs=[SMEM] * 3 + [VMEM] * 4 + [HBM],
+        in_specs=[SMEM] * 3 + [VMEM] * 4,
         out_specs=[VMEM] * (9 + len(strides)),
-        scratch_shapes=[
-            pltpu.VMEM((projected.shape[2], TILE, rows), F32),
-            pltpu.SemaphoreType.DMA((live + len(strides),)),
-        ],
+        scratch_shapes=[pltpu.VMEM((projected.shape[2], TILE, rows), F32)],
         compiler_params=pltpu.CompilerParams(vmem_limit_bytes=8 * MIB),
         name="prepare_rows",
-    )(place, from_shard, from_slot, projected, rate, gain, after, *in_hbm(states))
+    )(place, from_shard, from_slot, projected, rate, gain, states)
 
 
 def diagonal(dim):
@@ -478,14 +464,14 @@
     place = lax.axis_index(("dp", "tensor")).astype(jnp.int32).reshape(1)
     states = states.reshape(slots, width, dim)
 
-    row_0, row_1, after = pick(
+    row_0, row_1, staged = pick(
         place, from_shard, from_slot, projected, states, shards, live, group, (-2, 2)
     )
     half_1, half_0 = swapped(row_1, 1), swapped(row_0, 0)
     rate = jnp.repeat(decay_rate, dim).reshape(1, width)
     gain = norm_gain.reshape(1, width)
     query, grown, base, gated, decay, local, here, outer, token, row_0, row_1 = prepare(
-        place, from_shard, from_slot, projected, rate, gain, after, states, shards, live,
+        place, from_shard, from_slot, projected, rate, gain, staged, shards, live,
         group, (-1, 1),
     )
     near_1, near_0 = swapped(row_1, 1), swapped(row_0, 0)

time: 59.7 us -> 60.3 us (1.010)
  starting transfers between devices: 42.2 us -> 46.1 us
  waiting for transfers between devices: 6.8 us -> 3.82 us
    all_to_all x1, starting transfers between devices: 6.02 us -> 8.84 us  [on_device(): totals = lax.all_to_all(sums, 'tensor', 0, 0)]
    ppermute x8, waiting for transfers between devices: 3.96 us -> 2.04 us  [swapped(): return lax.ppermute(block, ('dp', 'tensor'), route)]
    ppermute x8, starting transfers between devices: 36.2 us -> 37.3 us  [swapped(): return lax.ppermute(block, ('dp', 'tensor'), route)]
    pallas_call x1, Pallas kernels: 2.29 us -> 1.23 us  [prepare(): pl.pallas_call(functools.partial(prepare_kernel, shards, live, group, str...]
    pallas_call x1, Pallas kernels: 1.65 us -> 2.7 us  [final_of(): pl.pallas_call(functools.partial(final_kernel, shards, live, group), out_...]
    all_to_all x1, waiting for transfers between devices: 2.84 us -> 1.78 us  [on_device(): totals = lax.all_to_all(sums, 'tensor', 0, 0)]
where the time goes in v11:
time: 60.3 us; the launch traced here: 59.9 us
  starting transfers between devices  46.1 us (76%)
  Pallas kernels  8.98 us (15%)
  waiting for transfers between devices  3.82 us (6%)
  between operations  0.85 us (1%)
    ppermute x8, starting transfers between devices, swapped(): return lax.ppermute(block, ('dp', 'tensor'), route)  37.3 us
    all_to_all x1, starting transfers between devices, on_device(): totals = lax.all_to_all(sums, 'tensor', 0, 0)  8.84 us
    pallas_call x1, Pallas kernels, final_of(): pl.pallas_call(functools.partial(final_kernel, shards, live, group), out_...  2.7 us
    ppermute x8, waiting for transfers between devices, swapped(): return lax.ppermute(block, ('dp', 'tensor'), route)  2.04 us
    all_to_all x1, waiting for transfers between devices, on_device(): totals = lax.all_to_all(sums, 'tensor', 0, 0)  1.78 us
    pallas_call x1, Pallas kernels, pick(): pl.pallas_call(functools.partial(pick_kernel, shards, live, group, stride...  1.75 us
    pallas_call x1, Pallas kernels, raw_of(): pl.pallas_call(functools.partial(raw_kernel, shards, live, group), out_sh...  1.62 us
    pallas_call x1, Pallas kernels, prepare(): pl.pallas_call(functools.partial(prepare_kernel, shards, live, group, str...  1.23 us
  transfers between devices with their start and end apart: 9, of which 3 were waited for; matrix products, arithmetic and copies ran while one was open for 0% of the time, Pallas kernels for 11%

profile of v11, /device:TPU:1, one launch (start us, length us, event | category | flops | bytes accessed | tf_op | source)
XLA Modules:
  0.0 59.9 jit_solution(6725629995610765121)
XLA Ops:
  0.7 1.8 %pick_rows.1 = (f32[1088,128]{1,0:T(8,128)S(1)}, f32[1088,128]{1,0:T(8,128)S(1)}, f32[4,1024,128]{2,1,0:T(8,128)S(1)}) custom-call(s32[1]{0:T(128)} %bitcast.place, s32[128]{0:T(128)} %shard_ref.5, s32[128]{0:T(128)} %slot_ref.1, bf16[3,2,4,1024]{3,2,1,0:T(4,128)(2,1)} %projected.3, f32[4,1024,128]{2,1,0:T(8,128)} %bitcast.7), custom_call_target="tpu_custom_call" | custom-call | tf_op jit(solution)/shard_map/pick_rows/pallas_call | solution.py:102
  2.4 14.1 %collective-permute-start = (f32[1088,128]{1,0:T(8,128)S(1)}, f32[1088,128]{1,0:T(8,128)S(1)}, u32[]{:S(2)}, u32[]{:S(2)}) collective-permute-start(f32[1088,128]{1,0:T(8,128)S(1)} %get-tuple-element.24), channel_id=1, source_target_pairs={{0,8},{8,0},{9,17},{17,9},{2,10},{10,2},{11,19},{19,11},{4,12},{12... | collective-permute-start | bytes 1671176 | tf_op jit(solution)/shard_map/ppermute | solution.py:31
  16.6 1.9 %collective-permute-start.1 = (f32[1088,128]{1,0:T(8,128)S(1)}, f32[1088,128]{1,0:T(8,128)S(1)}, u32[]{:S(2)}, u32[]{:S(2)}) collective-permute-start(f32[1088,128]{1,0:T(8,128)S(1)} %get-tuple-element.25), channel_id=1, source_target_pairs={{8,16},{16,8},{17,25},{25,17},{10,18},{18,10},{19,27},{27,19},{12,... | collective-permute-start | bytes 1671176 | tf_op jit(solution)/shard_map/ppermute | solution.py:31
  18.5 0.1 broadcast_in_dim.3
  18.6 1.2 %prepare_rows.1 = (f32[8,1024]{1,0:T(8,128)S(1)}, f32[8,1024]{1,0:T(8,128)S(1)}, f32[8,1024]{1,0:T(8,128)S(1)}, f32[8,1024]{1,0:T(8,128)S(1)}, f32[1,1024]{1,0:T...) custom-call(s32[1]{0:T(128)} %bitcast.place, ...), custom_call_target="tpu_custom_call" | custom-call | tf_op jit(solution)/shard_map/prepare_rows/pallas_call | solution.py:256
  19.9 3.4 %collective-permute-start.4 = (f32[1024,128]{1,0:T(8,128)S(1)}, f32[1024,128]{1,0:T(8,128)S(1)}, u32[]{:S(2)}, u32[]{:S(2)}) collective-permute-start(f32[1024,128]{1,0:T(8,128)S(1)} %get-tuple-element.30), channel_id=1, source_target_pairs={{8,16},{16,8},{17,25},{25,17},{10,18},{18,10},{19,27},{27,19},{12,... | collective-permute-start | bytes 1572872 | tf_op jit(solution)/shard_map/ppermute | solution.py:31
  23.2 1.9 %collective-permute-start.5 = (f32[1024,128]{1,0:T(8,128)S(1)}, f32[1024,128]{1,0:T(8,128)S(1)}, u32[]{:S(2)}, u32[]{:S(2)}) collective-permute-start(f32[1024,128]{1,0:T(8,128)S(1)} %get-tuple-element.31), channel_id=1, source_target_pairs={{0,8},{8,0},{9,17},{17,9},{2,10},{10,2},{11,19},{19,11},{4,12},{12... | collective-permute-start | bytes 1572872 | tf_op jit(solution)/shard_map/ppermute | solution.py:31
  25.2 1.0 %collective-permute-done.from_0 = f32[1088,128]{1,0:T(8,128)S(1)} collective-permute-done((f32[1088,128]{1,0:T(8,128)S(1)}, f32[1088,128]{1,0:T(8,128)S(1)}, u32[]{:S(2)}, u32[]{:S(2)}) %collective-permute-start) | collective-permute-done | bytes 557088 | tf_op jit(solution)/shard_map/ppermute | solution.py:31
  26.1 1.1 %collective-permute-done.1.from_1 = f32[1088,128]{1,0:T(8,128)S(1)} collective-permute-done((f32[1088,128]{1,0:T(8,128)S(1)}, f32[1088,128]{1,0:T(8,128)S(1)}, u32[]{:S(2)}, u32[]{:S(2)}) %collective-permute-start.1) | collective-permute-done | bytes 557088 | tf_op jit(solution)/shard_map/ppermute | solution.py:31
  27.2 1.0 %relay_rows.1 = (f32[448,128]{1,0:T(8,128)S(1)}, f32[448,128]{1,0:T(8,128)S(1)}, f32[640,128]{1,0:T(8,128)}, f32[640,128]{1,0:T(8,128)}) custom-call(f32[1088,128]{1,0:T(8,128)S(1)} %collective-permute-done.from_0, f32[1088,128]{1,0:T(8,128)S(1)} %collective-permute-done.1.from_1, f32[8,128]{1,0:T(8,128)S(1)} %get-tuple-element.27._), custom_call_target="tpu_custom_call" | custom-call | tf_op jit(solution)/shard_map/relay_rows/pallas_call | solution.py:143
  28.2 7.1 %collective-permute-start.2 = (f32[448,128]{1,0:T(8,128)S(1)}, f32[448,128]{1,0:T(8,128)S(1)}, u32[]{:S(2)}, u32[]{:S(2)}) collective-permute-start(f32[448,128]{1,0:T(8,128)S(1)} %get-tuple-element.28), channel_id=1, source_target_pairs={{0,8},{8,0},{9,17},{17,9},{2,10},{10,2},{11,19},{19,11},{4,12},{12... | collective-permute-start | bytes 688136 | tf_op jit(solution)/shard_map/ppermute | solution.py:31
  35.2 1.9 %collective-permute-start.3 = (f32[448,128]{1,0:T(8,128)S(1)}, f32[448,128]{1,0:T(8,128)S(1)}, u32[]{:S(2)}, u32[]{:S(2)}) collective-permute-start(f32[448,128]{1,0:T(8,128)S(1)} %get-tuple-element.29), channel_id=1, source_target_pairs={{8,16},{16,8},{17,25},{25,17},{10,18},{18,10},{19,27},{27,19},{12,... | collective-permute-start | bytes 688136 | tf_op jit(solution)/shard_map/ppermute | solution.py:31
  37.2 3.4 %collective-permute-start.6 = (f32[640,128]{1,0:T(8,128)}, f32[640,128]{1,0:T(8,128)}, u32[]{:S(2)}, u32[]{:S(2)}) collective-permute-start(f32[640,128]{1,0:T(8,128)} %get-tuple-element.40), channel_id=1, source_target_pairs={{8,16},{16,8},{17,25},{25,17},{10,18},{18,10},{19,27},{27,19},{12,... | collective-permute-start | bytes 983048 | tf_op jit(solution)/shard_map/ppermute | solution.py:31
  40.5 0.0 collective-permute-done.4.near_1
  40.6 3.6 %collective-permute-start.7 = (f32[640,128]{1,0:T(8,128)}, f32[640,128]{1,0:T(8,128)}, u32[]{:S(2)}, u32[]{:S(2)}) collective-permute-start(f32[640,128]{1,0:T(8,128)} %get-tuple-element.41), channel_id=1, source_target_pairs={{0,8},{8,0},{9,17},{17,9},{2,10},{10,2},{11,19},{19,11},{4,12},{12... | collective-permute-start | bytes 983048 | tf_op jit(solution)/shard_map/ppermute | solution.py:31
  44.1 0.0 collective-permute-done.5.near_0
  44.1 0.0 collective-permute-done.2.lead_0
  44.2 0.0 collective-permute-done.3.lead_1
  44.2 1.6 %raw_rows.1 = (f32[8,1024]{1,0:T(8,128)S(1)}, f32[8,1,128]{2,1,0:T(1,128)}) custom-call(s32[1]{0:T(128)} %bitcast.place, s32[128]{0:T(128)S(1)} %copy-done.3, f32[448,128]{1,0:T(8,128)S(1)} %collective-permute-done.2.lead_0, f32[448,128]{1,0:T(8,128)S(1)} %collective-permute-done.3.lead_1, f32[1024,128]{1,0:T(8,128)S(1)} %collective-permute-done.4.near_1, ...), custom_call_target="tpu_custom_call" | custom-call | flops 999999995904 | bytes 1048576 | tf_op jit(solution)/shard_map/raw_rows/pallas_call | solution.py:327
  45.8 8.8 %all-to-all-start = ((f32[8,1,128]{2,1,0:T(1,128)}), f32[8,1,128]{2,1,0:T(1,128)S(1)}, u32[]{:S(2)}, u32[]{:S(2)}) async-start(f32[8,1,128]{2,1,0:T(1,128)} %get-tuple-element.36), calls=%async_computation | async-start | bytes 8192 | tf_op jit(solution)/shard_map/all_to_all | solution.py:486
  54.7 0.0 collective-permute-done.6.rest_1
  54.7 2.7 %final_rows.1 = (f32[2,1024,128]{2,1,0:T(8,128)}, f32[8,128]{1,0:T(8,128)S(1)}) custom-call(s32[1]{0:T(128)} %bitcast.place, s32[128]{0:T(128)S(1)} %copy-done.3, f32[2,1024,128]{2,1,0:T(8,128)S(1)} %get-tuple-element.39.here, f32[448,128]{1,0:T(8,128)} %copy-done.4, f32[448,128]{1,0:T(8,128)} %copy-done.5, f32[1024,128]{1,0:T(8,128)S(1)} %collective-permute-done.4.near_1, ...), custom_call_target="tpu_custom_call" | custom-call | flops 10000000000 | bytes 1048576 | tf_op jit(solution)/shard_map/final_rows/pallas_call | solution.py:415
  57.4 1.8 %all-to-all-done.totals = f32[8,1,128]{2,1,0:T(1,128)S(1)} async-done(((f32[8,1,128]{2,1,0:T(1,128)}), f32[8,1,128]{2,1,0:T(1,128)S(1)}, u32[]{:S(2)}, u32[]{:S(2)}) %all-to-all-start) | async-done | bytes 4128 | tf_op jit(solution)/shard_map/all_to_all | solution.py:486
  59.2 0.7 %attend_rows.1 = bf16[3,2,1024]{2,1,0:T(2,128)(2,1)} custom-call(f32[8,1,128]{2,1,0:T(1,128)S(1)} %all-to-all-done.totals, f32[8,1024]{1,0:T(8,128)S(1)} %get-tuple-element.37.raw, f32[8,1024]{1,0:T(8,128)S(1)} %get-tuple-element.38.gated, f32[8,128]{1,0:T(8,128)S(1)} %get-tuple-element.44._), custom_call_target="tpu_custom_call" | custom-call | tf_op jit(solution)/shard_map/attend_rows/pallas_call | solution.py:449
  (15 shorter events, 0.0 us)
Async XLA Ops:
  0.6 18.0 %copy-start.3 = (s32[128]{0:T(128)S(1)}, s32[128]{0:T(128)}, u32[]{:S(2)}) copy-start(s32[128]{0:T(128)} %shard_ref.5) | copy-start | bytes 1540
  0.6 18.0 %copy-start = (bf16[3,2,4,1024]{3,2,1,0:T(4,128)(2,1)S(1)}, bf16[3,2,4,1024]{3,2,1,0:T(4,128)(2,1)}, u32[]{:S(2)}) copy-start(bf16[3,2,4,1024]{3,2,1,0:T(4,128)(2,1)} %projected.3) | copy-start | bytes 147460
  0.7 18.0 %copy-start.2 = (s32[128]{0:T(128)S(1)}, s32[128]{0:T(128)}, u32[]{:S(2)}) copy-start(s32[128]{0:T(128)} %slot_ref.1) | copy-start | bytes 1540
  0.7 18.0 %copy-start.1 = (f32[1024]{0:T(1024)S(1)}, f32[1024]{0:T(1024)}, u32[]{:S(2)}) copy-start(f32[1024]{0:T(1024)} %param.11) | copy-start | bytes 12292
  0.7 17.9 %copy-start.6 = (f32[8]{0:T(128)S(1)}, f32[8]{0:T(128)}, u32[]{:S(2)}) copy-start(f32[8]{0:T(128)} %param.10) | copy-start | bytes 100
  2.4 23.7 %collective-permute-start = (f32[1088,128]{1,0:T(8,128)S(1)}, f32[1088,128]{1,0:T(8,128)S(1)}, u32[]{:S(2)}, u32[]{:S(2)}) collective-permute-start(f32[1088,128]{1,0:T(8,128)S(1)} %get-tuple-element.24), channel_id=1, source_target_pairs={{0,8},{8,0},{9,17},{17,9},{2,10},{10,2},{11,19},{19,11},{4,12},{12... | collective-permute-start | bytes 1671176 | tf_op jit(solution)/shard_map/ppermute | solution.py:31
  16.6 10.6 %collective-permute-start.1 = (f32[1088,128]{1,0:T(8,128)S(1)}, f32[1088,128]{1,0:T(8,128)S(1)}, u32[]{:S(2)}, u32[]{:S(2)}) collective-permute-start(f32[1088,128]{1,0:T(8,128)S(1)} %get-tuple-element.25), channel_id=1, source_target_pairs={{8,16},{16,8},{17,25},{25,17},{10,18},{18,10},{19,27},{27,19},{12,... | collective-permute-start | bytes 1671176 | tf_op jit(solution)/shard_map/ppermute | solution.py:31
  19.9 20.7 %collective-permute-start.4 = (f32[1024,128]{1,0:T(8,128)S(1)}, f32[1024,128]{1,0:T(8,128)S(1)}, u32[]{:S(2)}, u32[]{:S(2)}) collective-permute-start(f32[1024,128]{1,0:T(8,128)S(1)} %get-tuple-element.30), channel_id=1, source_target_pairs={{8,16},{16,8},{17,25},{25,17},{10,18},{18,10},{19,27},{27,19},{12,... | collective-permute-start | bytes 1572872 | tf_op jit(solution)/shard_map/ppermute | solution.py:31
  23.2 20.9 %collective-permute-start.5 = (f32[1024,128]{1,0:T(8,128)S(1)}, f32[1024,128]{1,0:T(8,128)S(1)}, u32[]{:S(2)}, u32[]{:S(2)}) collective-permute-start(f32[1024,128]{1,0:T(8,128)S(1)} %get-tuple-element.31), channel_id=1, source_target_pairs={{0,8},{8,0},{9,17},{17,9},{2,10},{10,2},{11,19},{19,11},{4,12},{12... | collective-permute-start | bytes 1572872 | tf_op jit(solution)/shard_map/ppermute | solution.py:31
  28.2 16.0 %collective-permute-start.2 = (f32[448,128]{1,0:T(8,128)S(1)}, f32[448,128]{1,0:T(8,128)S(1)}, u32[]{:S(2)}, u32[]{:S(2)}) collective-permute-start(f32[448,128]{1,0:T(8,128)S(1)} %get-tuple-element.28), channel_id=1, source_target_pairs={{0,8},{8,0},{9,17},{17,9},{2,10},{10,2},{11,19},{19,11},{4,12},{12... | collective-permute-start | bytes 688136 | tf_op jit(solution)/shard_map/ppermute | solution.py:31
  35.2 8.9 %collective-permute-start.3 = (f32[448,128]{1,0:T(8,128)S(1)}, f32[448,128]{1,0:T(8,128)S(1)}, u32[]{:S(2)}, u32[]{:S(2)}) collective-permute-start(f32[448,128]{1,0:T(8,128)S(1)} %get-tuple-element.29), channel_id=1, source_target_pairs={{8,16},{16,8},{17,25},{25,17},{10,18},{18,10},{19,27},{27,19},{12,... | collective-permute-start | bytes 688136 | tf_op jit(solution)/shard_map/ppermute | solution.py:31
  37.2 17.5 %collective-permute-start.6 = (f32[640,128]{1,0:T(8,128)}, f32[640,128]{1,0:T(8,128)}, u32[]{:S(2)}, u32[]{:S(2)}) collective-permute-start(f32[640,128]{1,0:T(8,128)} %get-tuple-element.40), channel_id=1, source_target_pairs={{8,16},{16,8},{17,25},{25,17},{10,18},{18,10},{19,27},{27,19},{12,... | collective-permute-start | bytes 983048 | tf_op jit(solution)/shard_map/ppermute | solution.py:31
  40.6 14.1 %collective-permute-start.7 = (f32[640,128]{1,0:T(8,128)}, f32[640,128]{1,0:T(8,128)}, u32[]{:S(2)}, u32[]{:S(2)}) collective-permute-start(f32[640,128]{1,0:T(8,128)} %get-tuple-element.41), channel_id=1, source_target_pairs={{0,8},{8,0},{9,17},{17,9},{2,10},{10,2},{11,19},{19,11},{4,12},{12... | collective-permute-start | bytes 983048 | tf_op jit(solution)/shard_map/ppermute | solution.py:31
  44.2 1.7 %copy-start.4 = (f32[448,128]{1,0:T(8,128)}, f32[448,128]{1,0:T(8,128)S(1)}, u32[]{:S(2)}) copy-start(f32[448,128]{1,0:T(8,128)S(1)} %collective-permute-done.2.lead_0) | copy-start | bytes 688132
  44.2 1.7 %copy-start.5 = (f32[448,128]{1,0:T(8,128)}, f32[448,128]{1,0:T(8,128)S(1)}, u32[]{:S(2)}) copy-start(f32[448,128]{1,0:T(8,128)S(1)} %collective-permute-done.3.lead_1) | copy-start | bytes 688132
  45.8 13.3 %all-to-all-start = ((f32[8,1,128]{2,1,0:T(1,128)}), f32[8,1,128]{2,1,0:T(1,128)S(1)}, u32[]{:S(2)}, u32[]{:S(2)}) async-start(f32[8,1,128]{2,1,0:T(1,128)} %get-tuple-element.36), calls=%async_computation | async-start | bytes 8192 | tf_op jit(solution)/shard_map/all_to_all | solution.py:486

commit v12 on v11

--- a/solution.py
+++ b/solution.py
@@ -61,9 +61,10 @@
 
 
 def pick_kernel(shards, live, group, strides, place, shard_hbm, slot_hbm, projected, states, *refs):
-    n_rows = len(strides)
-    outs = refs[:n_rows]
-    staged, shard_ref, slot_ref, inputs, sems = refs[n_rows:]
+    n_rows = 2
+    outs = refs[: len(strides)]
+    refs = refs[len(strides) :]
+    staged, shard_ref, slot_ref, inputs, sems = refs
     dim = outs[0].shape[1]
     rows = states.shape[1]
     device, side = spot(place, group)
@@ -101,7 +102,8 @@
     tile_rows = rows // dim * TILE
     return pl.pallas_call(
         functools.partial(pick_kernel, shards, live, group, strides),
-        out_shape=[jax.ShapeDtypeStruct((rows + tile_rows, dim), F32)] * len(strides)
+        out_shape=[jax.ShapeDtypeStruct((rows + tile_rows, dim), F32)] * 2
+        + [jax.ShapeDtypeStruct((rows, dim), F32)] * (len(strides) - 2)
         + [jax.ShapeDtypeStruct(states.shape, F32)],
         in_specs=[SMEM] + [HBM] * 4,
         out_specs=[VMEM] * (len(strides) + 1),
@@ -168,7 +170,7 @@
 
 
 def prepare_kernel(
-    shards, live, group, strides, place, shard_ref, slot_ref, projected, rate, gain, states,
+    shards, live, group, strides, place, shard_ref, slot_ref, projected, rate, gain, _, states,
     query, grown, base, gated, decay, made, here, outer, token, *refs,
 ):
     outs, parts = refs[:-1], refs[-1]
@@ -248,7 +250,7 @@
 
 
 def prepare(
-    place, from_shard, from_slot, projected, rate, gain, states, shards, live, group, strides
+    place, from_shard, from_slot, projected, rate, gain, after, states, shards, live, group, strides
 ):
     rows, dim = states.shape[1:]
     tile = jax.ShapeDtypeStruct((TILE, rows), F32)
@@ -264,12 +266,12 @@
             jax.ShapeDtypeStruct((TILE, dim), F32),
         ]
         + [jax.ShapeDtypeStruct((rows, dim), F32)] * len(strides),
-        in_specs=[SMEM] * 3 + [VMEM] * 4,
+        in_specs=[SMEM] * 3 + [VMEM] * 5,
         out_specs=[VMEM] * (9 + len(strides)),
         scratch_shapes=[pltpu.VMEM((projected.shape[2], TILE, rows), F32)],
         compiler_params=pltpu.CompilerParams(vmem_limit_bytes=8 * MIB),
         name="prepare_rows",
-    )(place, from_shard, from_slot, projected, rate, gain, states)
+    )(place, from_shard, from_slot, projected, rate, gain, after, states)
 
 
 def diagonal(dim):
@@ -464,17 +466,17 @@
     place = lax.axis_index(("dp", "tensor")).astype(jnp.int32).reshape(1)
     states = states.reshape(slots, width, dim)
 
-    row_0, row_1, staged = pick(
-        place, from_shard, from_slot, projected, states, shards, live, group, (-2, 2)
+    row_0, row_1, next_1, staged = pick(
+        place, from_shard, from_slot, projected, states, shards, live, group, (-2, 2, 1)
     )
     half_1, half_0 = swapped(row_1, 1), swapped(row_0, 0)
     rate = jnp.repeat(decay_rate, dim).reshape(1, width)
     gain = norm_gain.reshape(1, width)
-    query, grown, base, gated, decay, local, here, outer, token, row_0, row_1 = prepare(
-        place, from_shard, from_slot, projected, rate, gain, staged, shards, live,
-        group, (-1, 1),
+    query, grown, base, gated, decay, local, here, outer, token, next_0 = prepare(
+        place, from_shard, from_slot, projected, rate, gain, half_0, staged, shards, live,
+        group, (-1,),
     )
-    near_1, near_0 = swapped(row_1, 1), swapped(row_0, 0)
+    near_1, near_0 = swapped(next_1, 1), swapped(next_0, 0)
     sent = relay(half_0, half_1, token, heads)
     lead_1, lead_0 = swapped(sent[0], 1), swapped(sent[1], 0)
     rest_1, rest_0 = swapped(sent[2], 1), swapped(sent[3], 0)

time: 60.3 us -> 60.6 us (level)
  waiting for transfers between devices: 3.82 us -> 7.06 us
  starting transfers between devices: 46.1 us -> 44.3 us
  Pallas kernels: 8.98 us -> 7.91 us
    ppermute x8, waiting for transfers between devices: 2.04 us -> 6.36 us  [swapped(): return lax.ppermute(block, ('dp', 'tensor'), route)]
    all_to_all x1, starting transfers between devices: 8.84 us -> 4.59 us  [on_device(): totals = lax.all_to_all(sums, 'tensor', 0, 0)]
    ppermute x8, starting transfers between devices: 37.3 us -> 39.7 us  [swapped(): return lax.ppermute(block, ('dp', 'tensor'), route)]
    all_to_all x1, waiting for transfers between devices: 1.78 us -> 0.7 us  [on_device(): totals = lax.all_to_all(sums, 'tensor', 0, 0)]
    pallas_call x1, Pallas kernels: 2.7 us -> 1.64 us  [final_of(): pl.pallas_call(functools.partial(final_kernel, shards, live, group), out_...]
  transfers between devices with their start and end apart: 9 -> 9, of which waited for: 3 -> 3; matrix products, arithmetic and copies ran while one was open for 0% -> 0% of each run, Pallas kernels for 11% -> 9%
where the time goes in v12:
time: 60.6 us; the launch traced here: 60.2 us
  starting transfers between devices  44.3 us (73%)
  Pallas kernels  7.91 us (13%)
  waiting for transfers between devices  7.06 us (12%)
  between operations  0.85 us (1%)
    ppermute x8, starting transfers between devices, swapped(): return lax.ppermute(block, ('dp', 'tensor'), route)  39.7 us
    ppermute x8, waiting for transfers between devices, swapped(): return lax.ppermute(block, ('dp', 'tensor'), route)  6.36 us
    all_to_all x1, starting transfers between devices, on_device(): totals = lax.all_to_all(sums, 'tensor', 0, 0)  4.59 us
    pallas_call x1, Pallas kernels, pick(): pl.pallas_call(functools.partial(pick_kernel, shards, live, group, stride...  1.79 us
    pallas_call x1, Pallas kernels, final_of(): pl.pallas_call(functools.partial(final_kernel, shards, live, group), out_...  1.64 us
    pallas_call x1, Pallas kernels, raw_of(): pl.pallas_call(functools.partial(raw_kernel, shards, live, group), out_sh...  1.63 us
  transfers between devices with their start and end apart: 9, of which 3 were waited for; matrix products, arithmetic and copies ran while one was open for 0% of the time, Pallas kernels for 9%

profile of v12, /device:TPU:1, one launch (start us, length us, event | category | flops | bytes accessed | tf_op | source)
XLA Modules:
  0.0 60.2 jit_solution(14436083365404170453)
XLA Ops:
  0.7 1.8 %pick_rows.1 = (f32[1088,128]{1,0:T(8,128)S(1)}, f32[1088,128]{1,0:T(8,128)S(1)}, f32[1024,128]{1,0:T(8,128)S(1)}, f32[4,1024,128]{2,1,0:T(8,128)S(1)}) custom-call(s32[1]{0:T(128)} %bitcast.place, s32[128]{0:T(128)} %shard_ref.5, s32[128]{0:T(128)} %slot_ref.1, bf16[3,2,4,1024]{3,2,1,0:T(4,128)(2,1)} %projected.3, f32[4,1024,128]{2,1,0:T(8,128)} %bitcast.7), custom_call_target="tpu_custom_call" | custom-call | tf_op jit(solution)/shard_map/pick_rows/pallas_call | solution.py:103
  2.5 14.1 %collective-permute-start = (f32[1088,128]{1,0:T(8,128)S(1)}, f32[1088,128]{1,0:T(8,128)S(1)}, u32[]{:S(2)}, u32[]{:S(2)}) collective-permute-start(f32[1088,128]{1,0:T(8,128)S(1)} %get-tuple-element.24), channel_id=1, source_target_pairs={{0,8},{8,0},{9,17},{17,9},{2,10},{10,2},{11,19},{19,11},{4,12},{12... | collective-permute-start | bytes 1671176 | tf_op jit(solution)/shard_map/ppermute | solution.py:31
  16.6 1.9 %collective-permute-start.1 = (f32[1088,128]{1,0:T(8,128)S(1)}, f32[1088,128]{1,0:T(8,128)S(1)}, u32[]{:S(2)}, u32[]{:S(2)}) collective-permute-start(f32[1088,128]{1,0:T(8,128)S(1)} %get-tuple-element.25), channel_id=1, source_target_pairs={{8,16},{16,8},{17,25},{25,17},{10,18},{18,10},{19,27},{27,19},{12,... | collective-permute-start | bytes 1671176 | tf_op jit(solution)/shard_map/ppermute | solution.py:31
  18.6 3.4 %collective-permute-start.4 = (f32[1024,128]{1,0:T(8,128)S(1)}, f32[1024,128]{1,0:T(8,128)S(1)}, u32[]{:S(2)}, u32[]{:S(2)}) collective-permute-start(f32[1024,128]{1,0:T(8,128)S(1)} %get-tuple-element.30), channel_id=1, source_target_pairs={{8,16},{16,8},{17,25},{25,17},{10,18},{18,10},{19,27},{27,19},{12,... | collective-permute-start | bytes 1572872 | tf_op jit(solution)/shard_map/ppermute | solution.py:31
  21.9 4.2 %collective-permute-done._.from_0 = f32[1088,128]{1,0:T(8,128)S(1)} collective-permute-done((f32[1088,128]{1,0:T(8,128)S(1)}, f32[1088,128]{1,0:T(8,128)S(1)}, u32[]{:S(2)}, u32[]{:S(2)}) %collective-permute-start) | collective-permute-done | bytes 557088 | tf_op jit(solution)/shard_map/ppermute | solution.py:31
  26.1 0.1 broadcast_in_dim.3
  26.2 1.2 %prepare_rows.1 = (f32[8,1024]{1,0:T(8,128)S(1)}, f32[8,1024]{1,0:T(8,128)S(1)}, f32[8,1024]{1,0:T(8,128)S(1)}, f32[8,1024]{1,0:T(8,128)S(1)}, f32[1,1024]{1,0:T...) custom-call(s32[1]{0:T(128)} %bitcast.place, ...), custom_call_target="tpu_custom_call" | custom-call | tf_op jit(solution)/shard_map/prepare_rows/pallas_call | solution.py:258
  27.4 6.4 %collective-permute-start.5 = (f32[1024,128]{1,0:T(8,128)S(1)}, f32[1024,128]{1,0:T(8,128)S(1)}, u32[]{:S(2)}, u32[]{:S(2)}) collective-permute-start(f32[1024,128]{1,0:T(8,128)S(1)} %get-tuple-element.31), channel_id=1, source_target_pairs={{0,8},{8,0},{9,17},{17,9},{2,10},{10,2},{11,19},{19,11},{4,12},{12... | collective-permute-start | bytes 1572872 | tf_op jit(solution)/shard_map/ppermute | solution.py:31
  33.8 0.0 collective-permute-done.1.from_1
  33.8 1.0 %relay_rows.1 = (f32[448,128]{1,0:T(8,128)S(1)}, f32[448,128]{1,0:T(8,128)S(1)}, f32[640,128]{1,0:T(8,128)}, f32[640,128]{1,0:T(8,128)}) custom-call(f32[1088,128]{1,0:T(8,128)S(1)} %collective-permute-done._.from_0, f32[1088,128]{1,0:T(8,128)S(1)} %collective-permute-done.1.from_1, f32[8,128]{1,0:T(8,128)S(1)} %get-tuple-element.27._), custom_call_target="tpu_custom_call" | custom-call | tf_op jit(solution)/shard_map/relay_rows/pallas_call | solution.py:145
  34.8 2.2 %collective-permute-start.2 = (f32[448,128]{1,0:T(8,128)S(1)}, f32[448,128]{1,0:T(8,128)S(1)}, u32[]{:S(2)}, u32[]{:S(2)}) collective-permute-start(f32[448,128]{1,0:T(8,128)S(1)} %get-tuple-element.28), channel_id=1, source_target_pairs={{0,8},{8,0},{9,17},{17,9},{2,10},{10,2},{11,19},{19,11},{4,12},{12... | collective-permute-start | bytes 688136 | tf_op jit(solution)/shard_map/ppermute | solution.py:31
  37.0 1.9 %collective-permute-start.3 = (f32[448,128]{1,0:T(8,128)S(1)}, f32[448,128]{1,0:T(8,128)S(1)}, u32[]{:S(2)}, u32[]{:S(2)}) collective-permute-start(f32[448,128]{1,0:T(8,128)S(1)} %get-tuple-element.29), channel_id=1, source_target_pairs={{8,16},{16,8},{17,25},{25,17},{10,18},{18,10},{19,27},{27,19},{12,... | collective-permute-start | bytes 688136 | tf_op jit(solution)/shard_map/ppermute | solution.py:31
  38.9 3.4 %collective-permute-start.6 = (f32[640,128]{1,0:T(8,128)}, f32[640,128]{1,0:T(8,128)}, u32[]{:S(2)}, u32[]{:S(2)}) collective-permute-start(f32[640,128]{1,0:T(8,128)} %get-tuple-element.40), channel_id=1, source_target_pairs={{8,16},{16,8},{17,25},{25,17},{10,18},{18,10},{19,27},{27,19},{12,... | collective-permute-start | bytes 983048 | tf_op jit(solution)/shard_map/ppermute | solution.py:31
  42.3 0.0 collective-permute-done.4.near_1
  42.3 6.4 %collective-permute-start.7 = (f32[640,128]{1,0:T(8,128)}, f32[640,128]{1,0:T(8,128)}, u32[]{:S(2)}, u32[]{:S(2)}) collective-permute-start(f32[640,128]{1,0:T(8,128)} %get-tuple-element.41), channel_id=1, source_target_pairs={{0,8},{8,0},{9,17},{17,9},{2,10},{10,2},{11,19},{19,11},{4,12},{12... | collective-permute-start | bytes 983048 | tf_op jit(solution)/shard_map/ppermute | solution.py:31
  48.8 0.0 collective-permute-done.3.lead_1
  48.8 0.0 collective-permute-done.5.near_0
  48.8 1.6 %raw_rows.1 = (f32[8,1024]{1,0:T(8,128)S(1)}, f32[8,1,128]{2,1,0:T(1,128)}) custom-call(s32[1]{0:T(128)} %bitcast.place, s32[128]{0:T(128)S(1)} %copy-done.3, f32[448,128]{1,0:T(8,128)S(1)} %collective-permute-done.2.lead_0, f32[448,128]{1,0:T(8,128)S(1)} %collective-permute-done.3.lead_1, f32[1024,128]{1,0:T(8,128)S(1)} %collective-permute-done.4.near_1, ...), custom_call_target="tpu_custom_call" | custom-call | flops 999999995904 | bytes 1048576 | tf_op jit(solution)/shard_map/raw_rows/pallas_call | solution.py:329
  50.4 4.6 %all-to-all-start = ((f32[8,1,128]{2,1,0:T(1,128)}), f32[8,1,128]{2,1,0:T(1,128)S(1)}, u32[]{:S(2)}, u32[]{:S(2)}) async-start(f32[8,1,128]{2,1,0:T(1,128)} %get-tuple-element.36), calls=%async_computation | async-start | bytes 8192 | tf_op jit(solution)/shard_map/all_to_all | solution.py:488
  55.0 0.0 collective-permute-done.6.rest_1
  55.0 2.1 %collective-permute-done.7.rest_0 = f32[640,128]{1,0:T(8,128)} collective-permute-done((f32[640,128]{1,0:T(8,128)}, f32[640,128]{1,0:T(8,128)}, u32[]{:S(2)}, u32[]{:S(2)}) %collective-permute-start.7) | collective-permute-done | bytes 327712 | tf_op jit(solution)/shard_map/ppermute | solution.py:31
  57.2 1.6 %final_rows.1 = (f32[2,1024,128]{2,1,0:T(8,128)}, f32[8,128]{1,0:T(8,128)S(1)}) custom-call(s32[1]{0:T(128)} %bitcast.place, s32[128]{0:T(128)S(1)} %copy-done.3, f32[2,1024,128]{2,1,0:T(8,128)S(1)} %get-tuple-element.39.here, f32[448,128]{1,0:T(8,128)} %copy-done.4, f32[448,128]{1,0:T(8,128)} %copy-done.5, f32[1024,128]{1,0:T(8,128)S(1)} %collective-permute-done.4.near_1, ...), custom_call_target="tpu_custom_call" | custom-call | flops 10000000000 | bytes 1048576 | tf_op jit(solution)/shard_map/final_rows/pallas_call | solution.py:417
  58.8 0.7 %all-to-all-done.totals = f32[8,1,128]{2,1,0:T(1,128)S(1)} async-done(((f32[8,1,128]{2,1,0:T(1,128)}), f32[8,1,128]{2,1,0:T(1,128)S(1)}, u32[]{:S(2)}, u32[]{:S(2)}) %all-to-all-start) | async-done | bytes 4128 | tf_op jit(solution)/shard_map/all_to_all | solution.py:488
  59.5 0.7 %attend_rows.1 = bf16[3,2,1024]{2,1,0:T(2,128)(2,1)} custom-call(f32[8,1,128]{2,1,0:T(1,128)S(1)} %all-to-all-done.totals, f32[8,1024]{1,0:T(8,128)S(1)} %get-tuple-element.37.raw, f32[8,1024]{1,0:T(8,128)S(1)} %get-tuple-element.38.gated, f32[8,128]{1,0:T(8,128)S(1)} %get-tuple-element.44._), custom_call_target="tpu_custom_call" | custom-call | tf_op jit(solution)/shard_map/attend_rows/pallas_call | solution.py:451
  (15 shorter events, 0.0 us)
Async XLA Ops:
  0.6 25.6 %copy-start.3 = (s32[128]{0:T(128)S(1)}, s32[128]{0:T(128)}, u32[]{:S(2)}) copy-start(s32[128]{0:T(128)} %shard_ref.5) | copy-start | bytes 1540
  0.6 25.6 %copy-start = (bf16[3,2,4,1024]{3,2,1,0:T(4,128)(2,1)S(1)}, bf16[3,2,4,1024]{3,2,1,0:T(4,128)(2,1)}, u32[]{:S(2)}) copy-start(bf16[3,2,4,1024]{3,2,1,0:T(4,128)(2,1)} %projected.3) | copy-start | bytes 147460
  0.7 25.6 %copy-start.2 = (s32[128]{0:T(128)S(1)}, s32[128]{0:T(128)}, u32[]{:S(2)}) copy-start(s32[128]{0:T(128)} %slot_ref.1) | copy-start | bytes 1540
  0.7 25.6 %copy-start.1 = (f32[1024]{0:T(1024)S(1)}, f32[1024]{0:T(1024)}, u32[]{:S(2)}) copy-start(f32[1024]{0:T(1024)} %param.11) | copy-start | bytes 12292
  0.7 25.5 %copy-start.6 = (f32[8]{0:T(128)S(1)}, f32[8]{0:T(128)}, u32[]{:S(2)}) copy-start(f32[8]{0:T(128)} %param.10) | copy-start | bytes 100
  2.5 23.7 %collective-permute-start = (f32[1088,128]{1,0:T(8,128)S(1)}, f32[1088,128]{1,0:T(8,128)S(1)}, u32[]{:S(2)}, u32[]{:S(2)}) collective-permute-start(f32[1088,128]{1,0:T(8,128)S(1)} %get-tuple-element.24), channel_id=1, source_target_pairs={{0,8},{8,0},{9,17},{17,9},{2,10},{10,2},{11,19},{19,11},{4,12},{12... | collective-permute-start | bytes 1671176 | tf_op jit(solution)/shard_map/ppermute | solution.py:31
  16.6 17.2 %collective-permute-start.1 = (f32[1088,128]{1,0:T(8,128)S(1)}, f32[1088,128]{1,0:T(8,128)S(1)}, u32[]{:S(2)}, u32[]{:S(2)}) collective-permute-start(f32[1088,128]{1,0:T(8,128)S(1)} %get-tuple-element.25), channel_id=1, source_target_pairs={{8,16},{16,8},{17,25},{25,17},{10,18},{18,10},{19,27},{27,19},{12,... | collective-permute-start | bytes 1671176 | tf_op jit(solution)/shard_map/ppermute | solution.py:31
  18.6 23.7 %collective-permute-start.4 = (f32[1024,128]{1,0:T(8,128)S(1)}, f32[1024,128]{1,0:T(8,128)S(1)}, u32[]{:S(2)}, u32[]{:S(2)}) collective-permute-start(f32[1024,128]{1,0:T(8,128)S(1)} %get-tuple-element.30), channel_id=1, source_target_pairs={{8,16},{16,8},{17,25},{25,17},{10,18},{18,10},{19,27},{27,19},{12,... | collective-permute-start | bytes 1572872 | tf_op jit(solution)/shard_map/ppermute | solution.py:31
  27.4 21.4 %collective-permute-start.5 = (f32[1024,128]{1,0:T(8,128)S(1)}, f32[1024,128]{1,0:T(8,128)S(1)}, u32[]{:S(2)}, u32[]{:S(2)}) collective-permute-start(f32[1024,128]{1,0:T(8,128)S(1)} %get-tuple-element.31), channel_id=1, source_target_pairs={{0,8},{8,0},{9,17},{17,9},{2,10},{10,2},{11,19},{19,11},{4,12},{12... | collective-permute-start | bytes 1572872 | tf_op jit(solution)/shard_map/ppermute | solution.py:31
  34.8 13.9 %collective-permute-start.2 = (f32[448,128]{1,0:T(8,128)S(1)}, f32[448,128]{1,0:T(8,128)S(1)}, u32[]{:S(2)}, u32[]{:S(2)}) collective-permute-start(f32[448,128]{1,0:T(8,128)S(1)} %get-tuple-element.28), channel_id=1, source_target_pairs={{0,8},{8,0},{9,17},{17,9},{2,10},{10,2},{11,19},{19,11},{4,12},{12... | collective-permute-start | bytes 688136 | tf_op jit(solution)/shard_map/ppermute | solution.py:31
  37.0 11.7 %collective-permute-start.3 = (f32[448,128]{1,0:T(8,128)S(1)}, f32[448,128]{1,0:T(8,128)S(1)}, u32[]{:S(2)}, u32[]{:S(2)}) collective-permute-start(f32[448,128]{1,0:T(8,128)S(1)} %get-tuple-element.29), channel_id=1, source_target_pairs={{8,16},{16,8},{17,25},{25,17},{10,18},{18,10},{19,27},{27,19},{12,... | collective-permute-start | bytes 688136 | tf_op jit(solution)/shard_map/ppermute | solution.py:31
  38.9 16.1 %collective-permute-start.6 = (f32[640,128]{1,0:T(8,128)}, f32[640,128]{1,0:T(8,128)}, u32[]{:S(2)}, u32[]{:S(2)}) collective-permute-start(f32[640,128]{1,0:T(8,128)} %get-tuple-element.40), channel_id=1, source_target_pairs={{8,16},{16,8},{17,25},{25,17},{10,18},{18,10},{19,27},{27,19},{12,... | collective-permute-start | bytes 983048 | tf_op jit(solution)/shard_map/ppermute | solution.py:31
  42.3 14.9 %collective-permute-start.7 = (f32[640,128]{1,0:T(8,128)}, f32[640,128]{1,0:T(8,128)}, u32[]{:S(2)}, u32[]{:S(2)}) collective-permute-start(f32[640,128]{1,0:T(8,128)} %get-tuple-element.41), channel_id=1, source_target_pairs={{0,8},{8,0},{9,17},{17,9},{2,10},{10,2},{11,19},{19,11},{4,12},{12... | collective-permute-start | bytes 983048 | tf_op jit(solution)/shard_map/ppermute | solution.py:31
  48.7 1.7 %copy-start.4 = (f32[448,128]{1,0:T(8,128)}, f32[448,128]{1,0:T(8,128)S(1)}, u32[]{:S(2)}) copy-start(f32[448,128]{1,0:T(8,128)S(1)} %collective-permute-done.2.lead_0) | copy-start | bytes 688132
  48.8 1.7 %copy-start.5 = (f32[448,128]{1,0:T(8,128)}, f32[448,128]{1,0:T(8,128)S(1)}, u32[]{:S(2)}) copy-start(f32[448,128]{1,0:T(8,128)S(1)} %collective-permute-done.3.lead_1) | copy-start | bytes 688132
  50.4 9.1 %all-to-all-start = ((f32[8,1,128]{2,1,0:T(1,128)}), f32[8,1,128]{2,1,0:T(1,128)S(1)}, u32[]{:S(2)}, u32[]{:S(2)}) async-start(f32[8,1,128]{2,1,0:T(1,128)} %get-tuple-element.36), calls=%async_computation | async-start | bytes 8192 | tf_op jit(solution)/shard_map/all_to_all | solution.py:488

commit v13 on v12

--- a/solution.py
+++ b/solution.py
@@ -118,7 +118,7 @@
     )(place, *in_hbm(from_shard, from_slot, projected, states))
 
 
-def relay_kernel(from_0, from_1, _, lead_1, lead_0, rest_1, rest_0):
+def relay_kernel(from_0, from_1, near, lead_1, lead_0, rest_1, rest_0, next_row):
     dim = from_1.shape[1]
     heads = rest_0.shape[0] // dim + EARLY
     rows, early = heads * dim, EARLY * dim
@@ -136,20 +136,21 @@
                 lead[tile_rows + head * dim : tile_rows + (head + 1) * dim] = state
             else:
                 rest[(head - EARLY) * dim : (head - EARLY + 1) * dim] = state
-
-
-def relay(from_0, from_1, after, heads):
+    next_row[...] = near[...]
+
+
+def relay(from_0, from_1, near, heads):
     dim = from_0.shape[1]
     lead = jax.ShapeDtypeStruct((heads * TILE + EARLY * dim, dim), F32)
     rest = jax.ShapeDtypeStruct(((heads - EARLY) * dim, dim), F32)
     return pl.pallas_call(
         relay_kernel,
-        out_shape=[lead, lead, rest, rest],
+        out_shape=[lead, lead, rest, rest, jax.ShapeDtypeStruct(near.shape, F32)],
         in_specs=[VMEM] * 3,
-        out_specs=[VMEM] * 4,
+        out_specs=[VMEM] * 5,
         compiler_params=pltpu.CompilerParams(vmem_limit_bytes=6 * MIB),
         name="relay_rows",
-    )(from_0, from_1, after)
+    )(from_0, from_1, near)
 
 
 def gap_of(row, shards, live, device, shard_ref):
@@ -473,11 +474,11 @@
     rate = jnp.repeat(decay_rate, dim).reshape(1, width)
     gain = norm_gain.reshape(1, width)
     query, grown, base, gated, decay, local, here, outer, token, next_0 = prepare(
-        place, from_shard, from_slot, projected, rate, gain, half_0, staged, shards, live,
+        place, from_shard, from_slot, projected, rate, gain, row_0, staged, shards, live,
         group, (-1,),
     )
-    near_1, near_0 = swapped(next_1, 1), swapped(next_0, 0)
-    sent = relay(half_0, half_1, token, heads)
+    sent = relay(half_0, half_1, next_0, heads)
+    near_1, near_0 = swapped(next_1, 1), swapped(sent[4], 0)
     lead_1, lead_0 = swapped(sent[0], 1), swapped(sent[1], 0)
     rest_1, rest_0 = swapped(sent[2], 1), swapped(sent[3], 0)
 

time: 60.6 us -> 61.3 us (1.012)
  starting transfers between devices: 44.3 us -> 45 us
    ppermute x8, waiting for transfers between devices: 6.36 us -> 4.08 us  [swapped(): return lax.ppermute(block, ('dp', 'tensor'), route)]
    all_to_all x1, waiting for transfers between devices: 0.7 us -> 2.59 us  [on_device(): totals = lax.all_to_all(sums, 'tensor', 0, 0)]
    ppermute x8, starting transfers between devices: 39.7 us -> 40.4 us  [swapped(): return lax.ppermute(block, ('dp', 'tensor'), route)]
  transfers between devices with their start and end apart: 9 -> 9, of which waited for: 3 -> 4; matrix products, arithmetic and copies ran while one was open for 0% -> 0% of each run, Pallas kernels for 9% -> 10%
where the time goes in v13:
time: 61.3 us; the launch traced here: 60.9 us
  starting transfers between devices  45 us (73%)
  Pallas kernels  8.33 us (14%)
  waiting for transfers between devices  6.67 us (11%)
  between operations  0.85 us (1%)
    ppermute x8, starting transfers between devices, swapped(): return lax.ppermute(block, ('dp', 'tensor'), route)  40.4 us
    all_to_all x1, starting transfers between devices, on_device(): totals = lax.all_to_all(sums, 'tensor', 0, 0)  4.59 us
    ppermute x8, waiting for transfers between devices, swapped(): return lax.ppermute(block, ('dp', 'tensor'), route)  4.08 us
    all_to_all x1, waiting for transfers between devices, on_device(): totals = lax.all_to_all(sums, 'tensor', 0, 0)  2.59 us
    pallas_call x1, Pallas kernels, pick(): pl.pallas_call(functools.partial(pick_kernel, shards, live, group, stride...  1.77 us
    pallas_call x1, Pallas kernels, final_of(): pl.pallas_call(functools.partial(final_kernel, shards, live, group), out_...  1.64 us
    pallas_call x1, Pallas kernels, raw_of(): pl.pallas_call(functools.partial(raw_kernel, shards, live, group), out_sh...  1.63 us
    pallas_call x1, Pallas kernels, prepare(): pl.pallas_call(functools.partial(prepare_kernel, shards, live, group, str...  1.37 us
  transfers between devices with their start and end apart: 9, of which 4 were waited for; matrix products, arithmetic and copies ran while one was open for 0% of the time, Pallas kernels for 10%

profile of v13, /device:TPU:1, one launch (start us, length us, event | category | flops | bytes accessed | tf_op | source)
XLA Modules:
  0.0 60.9 jit_solution(4738549806893487852)
XLA Ops:
  0.7 1.8 %pick_rows.1 = (f32[1088,128]{1,0:T(8,128)S(1)}, f32[1088,128]{1,0:T(8,128)S(1)}, f32[1024,128]{1,0:T(8,128)S(1)}, f32[4,1024,128]{2,1,0:T(8,128)S(1)}) custom-call(s32[1]{0:T(128)} %bitcast.place, s32[128]{0:T(128)} %shard_ref.5, s32[128]{0:T(128)} %slot_ref.1, bf16[3,2,4,1024]{3,2,1,0:T(4,128)(2,1)} %projected.3, f32[4,1024,128]{2,1,0:T(8,128)} %bitcast.7), custom_call_target="tpu_custom_call" | custom-call | tf_op jit(solution)/shard_map/pick_rows/pallas_call | solution.py:103
  2.5 14.1 %collective-permute-start = (f32[1088,128]{1,0:T(8,128)S(1)}, f32[1088,128]{1,0:T(8,128)S(1)}, u32[]{:S(2)}, u32[]{:S(2)}) collective-permute-start(f32[1088,128]{1,0:T(8,128)S(1)} %get-tuple-element.24._), channel_id=1, source_target_pairs={{0,8},{8,0},{9,17},{17,9},{2,10},{10,2},{11,19},{19,11},{4,12},{12... | collective-permute-start | bytes 1671176 | tf_op jit(solution)/shard_map/ppermute | solution.py:31
  16.6 1.9 %collective-permute-start.1 = (f32[1088,128]{1,0:T(8,128)S(1)}, f32[1088,128]{1,0:T(8,128)S(1)}, u32[]{:S(2)}, u32[]{:S(2)}) collective-permute-start(f32[1088,128]{1,0:T(8,128)S(1)} %get-tuple-element.25), channel_id=1, source_target_pairs={{8,16},{16,8},{17,25},{25,17},{10,18},{18,10},{19,27},{27,19},{12,... | collective-permute-start | bytes 1671176 | tf_op jit(solution)/shard_map/ppermute | solution.py:31
  18.6 3.4 %collective-permute-start.4 = (f32[1024,128]{1,0:T(8,128)S(1)}, f32[1024,128]{1,0:T(8,128)S(1)}, u32[]{:S(2)}, u32[]{:S(2)}) collective-permute-start(f32[1024,128]{1,0:T(8,128)S(1)} %get-tuple-element.30), channel_id=1, source_target_pairs={{8,16},{16,8},{17,25},{25,17},{10,18},{18,10},{19,27},{27,19},{12,... | collective-permute-start | bytes 1572872 | tf_op jit(solution)/shard_map/ppermute | solution.py:31
  21.9 0.1 broadcast_in_dim.3
  22.0 1.4 %prepare_rows.1 = (f32[8,1024]{1,0:T(8,128)S(1)}, f32[8,1024]{1,0:T(8,128)S(1)}, f32[8,1024]{1,0:T(8,128)S(1)}, f32[8,1024]{1,0:T(8,128)S(1)}, f32[1,1024]{1,0:T...) custom-call(s32[1]{0:T(128)} %bitcast.place, ...), custom_call_target="tpu_custom_call" | custom-call | tf_op jit(solution)/shard_map/prepare_rows/pallas_call | solution.py:259
  23.4 2.7 %collective-permute-done.from_0 = f32[1088,128]{1,0:T(8,128)S(1)} collective-permute-done((f32[1088,128]{1,0:T(8,128)S(1)}, f32[1088,128]{1,0:T(8,128)S(1)}, u32[]{:S(2)}, u32[]{:S(2)}) %collective-permute-start) | collective-permute-done | bytes 557088 | tf_op jit(solution)/shard_map/ppermute | solution.py:31
  26.1 1.1 %collective-permute-done.1.from_1 = f32[1088,128]{1,0:T(8,128)S(1)} collective-permute-done((f32[1088,128]{1,0:T(8,128)S(1)}, f32[1088,128]{1,0:T(8,128)S(1)}, u32[]{:S(2)}, u32[]{:S(2)}) %collective-permute-start.1) | collective-permute-done | bytes 557088 | tf_op jit(solution)/shard_map/ppermute | solution.py:31
  27.2 1.2 %relay_rows.1 = (f32[448,128]{1,0:T(8,128)S(1)}, f32[448,128]{1,0:T(8,128)S(1)}, f32[640,128]{1,0:T(8,128)}, f32[640,128]{1,0:T(8,128)}, f32[1024,128]{1,0:T(8,128)S(1)}) custom-call(f32[1088,128]{1,0:T(8,128)S(1)} %collective-permute-done.from_0, f32[1088,128]{1,0:T(8,128)S(1)} %collective-permute-done.1.from_1, f32[1024,128]{1,0:T(8,128)S(1)} %get-tuple-element.27.near), custom_call_target="tpu_custom_call" | custom-call | tf_op jit(solution)/shard_map/relay_rows/pallas_call | solution.py:146
  28.4 7.1 %collective-permute-start.5 = (f32[1024,128]{1,0:T(8,128)S(1)}, f32[1024,128]{1,0:T(8,128)S(1)}, u32[]{:S(2)}, u32[]{:S(2)}) collective-permute-start(f32[1024,128]{1,0:T(8,128)S(1)} %get-tuple-element.31), channel_id=1, source_target_pairs={{0,8},{8,0},{9,17},{17,9},{2,10},{10,2},{11,19},{19,11},{4,12},{12... | collective-permute-start | bytes 1572872 | tf_op jit(solution)/shard_map/ppermute | solution.py:31
  35.5 1.9 %collective-permute-start.2 = (f32[448,128]{1,0:T(8,128)S(1)}, f32[448,128]{1,0:T(8,128)S(1)}, u32[]{:S(2)}, u32[]{:S(2)}) collective-permute-start(f32[448,128]{1,0:T(8,128)S(1)} %get-tuple-element.28), channel_id=1, source_target_pairs={{0,8},{8,0},{9,17},{17,9},{2,10},{10,2},{11,19},{19,11},{4,12},{12... | collective-permute-start | bytes 688136 | tf_op jit(solution)/shard_map/ppermute | solution.py:31
  37.4 1.9 %collective-permute-start.3 = (f32[448,128]{1,0:T(8,128)S(1)}, f32[448,128]{1,0:T(8,128)S(1)}, u32[]{:S(2)}, u32[]{:S(2)}) collective-permute-start(f32[448,128]{1,0:T(8,128)S(1)} %get-tuple-element.29), channel_id=1, source_target_pairs={{8,16},{16,8},{17,25},{25,17},{10,18},{18,10},{19,27},{27,19},{12,... | collective-permute-start | bytes 688136 | tf_op jit(solution)/shard_map/ppermute | solution.py:31
  39.4 3.4 %collective-permute-start.6 = (f32[640,128]{1,0:T(8,128)}, f32[640,128]{1,0:T(8,128)}, u32[]{:S(2)}, u32[]{:S(2)}) collective-permute-start(f32[640,128]{1,0:T(8,128)} %get-tuple-element.40), channel_id=1, source_target_pairs={{8,16},{16,8},{17,25},{25,17},{10,18},{18,10},{19,27},{27,19},{12,... | collective-permute-start | bytes 983048 | tf_op jit(solution)/shard_map/ppermute | solution.py:31
  42.7 0.0 collective-permute-done.4.near_1
  42.7 6.7 %collective-permute-start.7 = (f32[640,128]{1,0:T(8,128)}, f32[640,128]{1,0:T(8,128)}, u32[]{:S(2)}, u32[]{:S(2)}) collective-permute-start(f32[640,128]{1,0:T(8,128)} %get-tuple-element.41), channel_id=1, source_target_pairs={{0,8},{8,0},{9,17},{17,9},{2,10},{10,2},{11,19},{19,11},{4,12},{12... | collective-permute-start | bytes 983048 | tf_op jit(solution)/shard_map/ppermute | solution.py:31
  49.4 0.0 collective-permute-done.2.lead_0
  49.5 0.0 collective-permute-done.3.lead_1
  49.5 1.6 %raw_rows.1 = (f32[8,1024]{1,0:T(8,128)S(1)}, f32[8,1,128]{2,1,0:T(1,128)}) custom-call(s32[1]{0:T(128)} %bitcast.place, s32[128]{0:T(128)S(1)} %copy-done.3, f32[448,128]{1,0:T(8,128)S(1)} %collective-permute-done.2.lead_0, f32[448,128]{1,0:T(8,128)S(1)} %collective-permute-done.3.lead_1, f32[1024,128]{1,0:T(8,128)S(1)} %collective-permute-done.4.near_1, ...), custom_call_target="tpu_custom_call" | custom-call | flops 999999995904 | bytes 1048576 | tf_op jit(solution)/shard_map/raw_rows/pallas_call | solution.py:330
  51.1 4.6 %all-to-all-start = ((f32[8,1,128]{2,1,0:T(1,128)}), f32[8,1,128]{2,1,0:T(1,128)S(1)}, u32[]{:S(2)}, u32[]{:S(2)}) async-start(f32[8,1,128]{2,1,0:T(1,128)} %get-tuple-element.36), calls=%async_computation | async-start | bytes 8192 | tf_op jit(solution)/shard_map/all_to_all | solution.py:489
  55.7 0.0 collective-permute-done.6.rest_1
  55.7 0.3 collective-permute-done.7.rest_0
  56.0 1.6 %final_rows.1 = (f32[2,1024,128]{2,1,0:T(8,128)}, f32[8,128]{1,0:T(8,128)S(1)}) custom-call(s32[1]{0:T(128)} %bitcast.place, s32[128]{0:T(128)S(1)} %copy-done.3, f32[2,1024,128]{2,1,0:T(8,128)S(1)} %get-tuple-element.39.here, f32[448,128]{1,0:T(8,128)} %copy-done.4, f32[448,128]{1,0:T(8,128)} %copy-done.5, f32[1024,128]{1,0:T(8,128)S(1)} %collective-permute-done.4.near_1, ...), custom_call_target="tpu_custom_call" | custom-call | flops 10000000000 | bytes 1048576 | tf_op jit(solution)/shard_map/final_rows/pallas_call | solution.py:418
  57.6 2.6 %all-to-all-done.totals = f32[8,1,128]{2,1,0:T(1,128)S(1)} async-done(((f32[8,1,128]{2,1,0:T(1,128)}), f32[8,1,128]{2,1,0:T(1,128)S(1)}, u32[]{:S(2)}, u32[]{:S(2)}) %all-to-all-start) | async-done | bytes 4128 | tf_op jit(solution)/shard_map/all_to_all | solution.py:489
  60.2 0.7 %attend_rows.1 = bf16[3,2,1024]{2,1,0:T(2,128)(2,1)} custom-call(f32[8,1,128]{2,1,0:T(1,128)S(1)} %all-to-all-done.totals, f32[8,1024]{1,0:T(8,128)S(1)} %get-tuple-element.37.raw, f32[8,1024]{1,0:T(8,128)S(1)} %get-tuple-element.38.gated, f32[8,128]{1,0:T(8,128)S(1)} %get-tuple-element.44._), custom_call_target="tpu_custom_call" | custom-call | tf_op jit(solution)/shard_map/attend_rows/pallas_call | solution.py:452
  (15 shorter events, 0.0 us)
Async XLA Ops:
  0.6 21.4 %copy-start.3 = (s32[128]{0:T(128)S(1)}, s32[128]{0:T(128)}, u32[]{:S(2)}) copy-start(s32[128]{0:T(128)} %shard_ref.5) | copy-start | bytes 1540
  0.6 21.4 %copy-start.2 = (s32[128]{0:T(128)S(1)}, s32[128]{0:T(128)}, u32[]{:S(2)}) copy-start(s32[128]{0:T(128)} %slot_ref.1) | copy-start | bytes 1540
  0.7 21.4 %copy-start = (bf16[3,2,4,1024]{3,2,1,0:T(4,128)(2,1)S(1)}, bf16[3,2,4,1024]{3,2,1,0:T(4,128)(2,1)}, u32[]{:S(2)}) copy-start(bf16[3,2,4,1024]{3,2,1,0:T(4,128)(2,1)} %projected.3) | copy-start | bytes 147460
  0.7 21.3 %copy-start.6 = (f32[8]{0:T(128)S(1)}, f32[8]{0:T(128)}, u32[]{:S(2)}) copy-start(f32[8]{0:T(128)} %param.10) | copy-start | bytes 100
  0.7 21.3 %copy-start.1 = (f32[1024]{0:T(1024)S(1)}, f32[1024]{0:T(1024)}, u32[]{:S(2)}) copy-start(f32[1024]{0:T(1024)} %param.11) | copy-start | bytes 12292
  2.5 23.7 %collective-permute-start = (f32[1088,128]{1,0:T(8,128)S(1)}, f32[1088,128]{1,0:T(8,128)S(1)}, u32[]{:S(2)}, u32[]{:S(2)}) collective-permute-start(f32[1088,128]{1,0:T(8,128)S(1)} %get-tuple-element.24._), channel_id=1, source_target_pairs={{0,8},{8,0},{9,17},{17,9},{2,10},{10,2},{11,19},{19,11},{4,12},{12... | collective-permute-start | bytes 1671176 | tf_op jit(solution)/shard_map/ppermute | solution.py:31
  16.6 10.6 %collective-permute-start.1 = (f32[1088,128]{1,0:T(8,128)S(1)}, f32[1088,128]{1,0:T(8,128)S(1)}, u32[]{:S(2)}, u32[]{:S(2)}) collective-permute-start(f32[1088,128]{1,0:T(8,128)S(1)} %get-tuple-element.25), channel_id=1, source_target_pairs={{8,16},{16,8},{17,25},{25,17},{10,18},{18,10},{19,27},{27,19},{12,... | collective-permute-start | bytes 1671176 | tf_op jit(solution)/shard_map/ppermute | solution.py:31
  18.6 24.2 %collective-permute-start.4 = (f32[1024,128]{1,0:T(8,128)S(1)}, f32[1024,128]{1,0:T(8,128)S(1)}, u32[]{:S(2)}, u32[]{:S(2)}) collective-permute-start(f32[1024,128]{1,0:T(8,128)S(1)} %get-tuple-element.30), channel_id=1, source_target_pairs={{8,16},{16,8},{17,25},{25,17},{10,18},{18,10},{19,27},{27,19},{12,... | collective-permute-start | bytes 1572872 | tf_op jit(solution)/shard_map/ppermute | solution.py:31
  28.4 21.1 %collective-permute-start.5 = (f32[1024,128]{1,0:T(8,128)S(1)}, f32[1024,128]{1,0:T(8,128)S(1)}, u32[]{:S(2)}, u32[]{:S(2)}) collective-permute-start(f32[1024,128]{1,0:T(8,128)S(1)} %get-tuple-element.31), channel_id=1, source_target_pairs={{0,8},{8,0},{9,17},{17,9},{2,10},{10,2},{11,19},{19,11},{4,12},{12... | collective-permute-start | bytes 1572872 | tf_op jit(solution)/shard_map/ppermute | solution.py:31
  35.5 13.9 %collective-permute-start.2 = (f32[448,128]{1,0:T(8,128)S(1)}, f32[448,128]{1,0:T(8,128)S(1)}, u32[]{:S(2)}, u32[]{:S(2)}) collective-permute-start(f32[448,128]{1,0:T(8,128)S(1)} %get-tuple-element.28), channel_id=1, source_target_pairs={{0,8},{8,0},{9,17},{17,9},{2,10},{10,2},{11,19},{19,11},{4,12},{12... | collective-permute-start | bytes 688136 | tf_op jit(solution)/shard_map/ppermute | solution.py:31
  37.4 12.0 %collective-permute-start.3 = (f32[448,128]{1,0:T(8,128)S(1)}, f32[448,128]{1,0:T(8,128)S(1)}, u32[]{:S(2)}, u32[]{:S(2)}) collective-permute-start(f32[448,128]{1,0:T(8,128)S(1)} %get-tuple-element.29), channel_id=1, source_target_pairs={{8,16},{16,8},{17,25},{25,17},{10,18},{18,10},{19,27},{27,19},{12,... | collective-permute-start | bytes 688136 | tf_op jit(solution)/shard_map/ppermute | solution.py:31
  39.4 16.4 %collective-permute-start.6 = (f32[640,128]{1,0:T(8,128)}, f32[640,128]{1,0:T(8,128)}, u32[]{:S(2)}, u32[]{:S(2)}) collective-permute-start(f32[640,128]{1,0:T(8,128)} %get-tuple-element.40), channel_id=1, source_target_pairs={{8,16},{16,8},{17,25},{25,17},{10,18},{18,10},{19,27},{27,19},{12,... | collective-permute-start | bytes 983048 | tf_op jit(solution)/shard_map/ppermute | solution.py:31
  42.7 13.3 %collective-permute-start.7 = (f32[640,128]{1,0:T(8,128)}, f32[640,128]{1,0:T(8,128)}, u32[]{:S(2)}, u32[]{:S(2)}) collective-permute-start(f32[640,128]{1,0:T(8,128)} %get-tuple-element.41), channel_id=1, source_target_pairs={{0,8},{8,0},{9,17},{17,9},{2,10},{10,2},{11,19},{19,11},{4,12},{12... | collective-permute-start | bytes 983048 | tf_op jit(solution)/shard_map/ppermute | solution.py:31
  49.4 1.7 %copy-start.4 = (f32[448,128]{1,0:T(8,128)}, f32[448,128]{1,0:T(8,128)S(1)}, u32[]{:S(2)}) copy-start(f32[448,128]{1,0:T(8,128)S(1)} %collective-permute-done.2.lead_0) | copy-start | bytes 688132
  49.5 1.7 %copy-start.5 = (f32[448,128]{1,0:T(8,128)}, f32[448,128]{1,0:T(8,128)S(1)}, u32[]{:S(2)}) copy-start(f32[448,128]{1,0:T(8,128)S(1)} %collective-permute-done.3.lead_1) | copy-start | bytes 688132
  51.1 9.1 %all-to-all-start = ((f32[8,1,128]{2,1,0:T(1,128)}), f32[8,1,128]{2,1,0:T(1,128)S(1)}, u32[]{:S(2)}, u32[]{:S(2)}) async-start(f32[8,1,128]{2,1,0:T(1,128)} %get-tuple-element.36), calls=%async_computation | async-start | bytes 8192 | tf_op jit(solution)/shard_map/all_to_all | solution.py:489

commit v14 on v11

--- a/solution.py
+++ b/solution.py
@@ -9,7 +9,7 @@
 EPS = 1e-05
 F32 = jnp.float32
 BF16 = jnp.bfloat16
-EARLY = 3
+EARLY = 2
 TILE = 8
 MIB = 1024 * 1024
 SMEM = pl.BlockSpec(memory_space=pltpu.SMEM)

time: 60.3 us -> 59 us (0.978)
  starting transfers between devices: 46.1 us -> 44.9 us
  waiting for transfers between devices: 3.82 us -> 4.88 us
  Pallas kernels: 8.98 us -> 7.94 us
    all_to_all x1, starting transfers between devices: 8.84 us -> 7.58 us  [on_device(): totals = lax.all_to_all(sums, 'tensor', 0, 0)]
    pallas_call x1, Pallas kernels: 2.7 us -> 1.64 us  [final_of(): pl.pallas_call(functools.partial(final_kernel, shards, live, group), out_...]
  transfers between devices with their start and end apart: 9 -> 9, of which waited for: 3 -> 4; matrix products, arithmetic and copies ran while one was open for 0% -> 0% of each run, Pallas kernels for 11% -> 9%
where the time goes in v14:
time: 59 us; the launch traced here: 58.6 us
  starting transfers between devices  44.9 us (76%)
  Pallas kernels  7.94 us (13%)
  waiting for transfers between devices  4.88 us (8%)
  between operations  0.85 us (1%)
    ppermute x8, starting transfers between devices, swapped(): return lax.ppermute(block, ('dp', 'tensor'), route)  37.3 us
    all_to_all x1, starting transfers between devices, on_device(): totals = lax.all_to_all(sums, 'tensor', 0, 0)  7.58 us
    ppermute x8, waiting for transfers between devices, swapped(): return lax.ppermute(block, ('dp', 'tensor'), route)  2.52 us
    all_to_all x1, waiting for transfers between devices, on_device(): totals = lax.all_to_all(sums, 'tensor', 0, 0)  2.36 us
    pallas_call x1, Pallas kernels, pick(): pl.pallas_call(functools.partial(pick_kernel, shards, live, group, stride...  1.75 us
    pallas_call x1, Pallas kernels, final_of(): pl.pallas_call(functools.partial(final_kernel, shards, live, group), out_...  1.64 us
    pallas_call x1, Pallas kernels, raw_of(): pl.pallas_call(functools.partial(raw_kernel, shards, live, group), out_sh...  1.63 us
    pallas_call x1, Pallas kernels, prepare(): pl.pallas_call(functools.partial(prepare_kernel, shards, live, group, str...  1.23 us
  transfers between devices with their start and end apart: 9, of which 4 were waited for; matrix products, arithmetic and copies ran while one was open for 0% of the time, Pallas kernels for 9%

profile of v14, /device:TPU:1, one launch (start us, length us, event | category | flops | bytes accessed | tf_op | source)
XLA Modules:
  0.0 58.6 jit_solution(2237383151936074588)
XLA Ops:
  0.7 1.8 %pick_rows.1 = (f32[1088,128]{1,0:T(8,128)S(1)}, f32[1088,128]{1,0:T(8,128)S(1)}, f32[4,1024,128]{2,1,0:T(8,128)S(1)}) custom-call(s32[1]{0:T(128)} %bitcast.place, s32[128]{0:T(128)} %shard_ref.5, s32[128]{0:T(128)} %slot_ref.1, bf16[3,2,4,1024]{3,2,1,0:T(4,128)(2,1)} %projected.3, f32[4,1024,128]{2,1,0:T(8,128)} %bitcast.7), custom_call_target="tpu_custom_call" | custom-call | tf_op jit(solution)/shard_map/pick_rows/pallas_call | solution.py:102
  2.4 14.1 %collective-permute-start = (f32[1088,128]{1,0:T(8,128)S(1)}, f32[1088,128]{1,0:T(8,128)S(1)}, u32[]{:S(2)}, u32[]{:S(2)}) collective-permute-start(f32[1088,128]{1,0:T(8,128)S(1)} %get-tuple-element.24), channel_id=1, source_target_pairs={{0,8},{8,0},{9,17},{17,9},{2,10},{10,2},{11,19},{19,11},{4,12},{12... | collective-permute-start | bytes 1671176 | tf_op jit(solution)/shard_map/ppermute | solution.py:31
  16.6 1.9 %collective-permute-start.1 = (f32[1088,128]{1,0:T(8,128)S(1)}, f32[1088,128]{1,0:T(8,128)S(1)}, u32[]{:S(2)}, u32[]{:S(2)}) collective-permute-start(f32[1088,128]{1,0:T(8,128)S(1)} %get-tuple-element.25), channel_id=1, source_target_pairs={{8,16},{16,8},{17,25},{25,17},{10,18},{18,10},{19,27},{27,19},{12,... | collective-permute-start | bytes 1671176 | tf_op jit(solution)/shard_map/ppermute | solution.py:31
  18.5 0.1 broadcast_in_dim.3
  18.6 1.2 %prepare_rows.1 = (f32[8,1024]{1,0:T(8,128)S(1)}, f32[8,1024]{1,0:T(8,128)S(1)}, f32[8,1024]{1,0:T(8,128)S(1)}, f32[8,1024]{1,0:T(8,128)S(1)}, f32[1,1024]{1,0:T...) custom-call(s32[1]{0:T(128)} %bitcast.place, ...), custom_call_target="tpu_custom_call" | custom-call | tf_op jit(solution)/shard_map/prepare_rows/pallas_call | solution.py:256
  19.9 3.4 %collective-permute-start.4 = (f32[1024,128]{1,0:T(8,128)S(1)}, f32[1024,128]{1,0:T(8,128)S(1)}, u32[]{:S(2)}, u32[]{:S(2)}) collective-permute-start(f32[1024,128]{1,0:T(8,128)S(1)} %get-tuple-element.30), channel_id=1, source_target_pairs={{8,16},{16,8},{17,25},{25,17},{10,18},{18,10},{19,27},{27,19},{12,... | collective-permute-start | bytes 1572872 | tf_op jit(solution)/shard_map/ppermute | solution.py:31
  23.2 1.9 %collective-permute-start.5 = (f32[1024,128]{1,0:T(8,128)S(1)}, f32[1024,128]{1,0:T(8,128)S(1)}, u32[]{:S(2)}, u32[]{:S(2)}) collective-permute-start(f32[1024,128]{1,0:T(8,128)S(1)} %get-tuple-element.31), channel_id=1, source_target_pairs={{0,8},{8,0},{9,17},{17,9},{2,10},{10,2},{11,19},{19,11},{4,12},{12... | collective-permute-start | bytes 1572872 | tf_op jit(solution)/shard_map/ppermute | solution.py:31
  25.2 1.0 %collective-permute-done.from_0 = f32[1088,128]{1,0:T(8,128)S(1)} collective-permute-done((f32[1088,128]{1,0:T(8,128)S(1)}, f32[1088,128]{1,0:T(8,128)S(1)}, u32[]{:S(2)}, u32[]{:S(2)}) %collective-permute-start) | collective-permute-done | bytes 557088 | tf_op jit(solution)/shard_map/ppermute | solution.py:31
  26.1 1.1 %collective-permute-done.1.from_1 = f32[1088,128]{1,0:T(8,128)S(1)} collective-permute-done((f32[1088,128]{1,0:T(8,128)S(1)}, f32[1088,128]{1,0:T(8,128)S(1)}, u32[]{:S(2)}, u32[]{:S(2)}) %collective-permute-start.1) | collective-permute-done | bytes 557088 | tf_op jit(solution)/shard_map/ppermute | solution.py:31
  27.2 1.0 %relay_rows.1 = (f32[320,128]{1,0:T(8,128)S(1)}, f32[320,128]{1,0:T(8,128)S(1)}, f32[768,128]{1,0:T(8,128)}, f32[768,128]{1,0:T(8,128)}) custom-call(f32[1088,128]{1,0:T(8,128)S(1)} %collective-permute-done.from_0, f32[1088,128]{1,0:T(8,128)S(1)} %collective-permute-done.1.from_1, f32[8,128]{1,0:T(8,128)S(1)} %get-tuple-element.27._), custom_call_target="tpu_custom_call" | custom-call | tf_op jit(solution)/shard_map/relay_rows/pallas_call | solution.py:143
  28.2 7.1 %collective-permute-start.2 = (f32[320,128]{1,0:T(8,128)S(1)}, f32[320,128]{1,0:T(8,128)S(1)}, u32[]{:S(2)}, u32[]{:S(2)}) collective-permute-start(f32[320,128]{1,0:T(8,128)S(1)} %get-tuple-element.28), channel_id=1, source_target_pairs={{0,8},{8,0},{9,17},{17,9},{2,10},{10,2},{11,19},{19,11},{4,12},{12... | collective-permute-start | bytes 491528 | tf_op jit(solution)/shard_map/ppermute | solution.py:31
  35.3 1.9 %collective-permute-start.3 = (f32[320,128]{1,0:T(8,128)S(1)}, f32[320,128]{1,0:T(8,128)S(1)}, u32[]{:S(2)}, u32[]{:S(2)}) collective-permute-start(f32[320,128]{1,0:T(8,128)S(1)} %get-tuple-element.29), channel_id=1, source_target_pairs={{8,16},{16,8},{17,25},{25,17},{10,18},{18,10},{19,27},{27,19},{12,... | collective-permute-start | bytes 491528 | tf_op jit(solution)/shard_map/ppermute | solution.py:31
  37.2 3.4 %collective-permute-start.6 = (f32[768,128]{1,0:T(8,128)}, f32[768,128]{1,0:T(8,128)}, u32[]{:S(2)}, u32[]{:S(2)}) collective-permute-start(f32[768,128]{1,0:T(8,128)} %get-tuple-element.40), channel_id=1, source_target_pairs={{8,16},{16,8},{17,25},{25,17},{10,18},{18,10},{19,27},{27,19},{12,... | collective-permute-start | bytes 1179656 | tf_op jit(solution)/shard_map/ppermute | solution.py:31
  40.6 0.0 collective-permute-done.4.near_1
  40.6 3.6 %collective-permute-start.7 = (f32[768,128]{1,0:T(8,128)}, f32[768,128]{1,0:T(8,128)}, u32[]{:S(2)}, u32[]{:S(2)}) collective-permute-start(f32[768,128]{1,0:T(8,128)} %get-tuple-element.41), channel_id=1, source_target_pairs={{0,8},{8,0},{9,17},{17,9},{2,10},{10,2},{11,19},{19,11},{4,12},{12... | collective-permute-start | bytes 1179656 | tf_op jit(solution)/shard_map/ppermute | solution.py:31
  44.1 0.0 collective-permute-done.5.near_0
  44.1 0.0 collective-permute-done.2.lead_0
  44.2 0.0 collective-permute-done.3.lead_1
  44.2 1.6 %raw_rows.1 = (f32[8,1024]{1,0:T(8,128)S(1)}, f32[8,1,128]{2,1,0:T(1,128)}) custom-call(s32[1]{0:T(128)} %bitcast.place, s32[128]{0:T(128)S(1)} %copy-done.3, f32[320,128]{1,0:T(8,128)S(1)} %collective-permute-done.2.lead_0, f32[320,128]{1,0:T(8,128)S(1)} %collective-permute-done.3.lead_1, f32[1024,128]{1,0:T(8,128)S(1)} %collective-permute-done.4.near_1, ...), custom_call_target="tpu_custom_call" | custom-call | flops 999999995904 | bytes 1048576 | tf_op jit(solution)/shard_map/raw_rows/pallas_call | solution.py:327
  45.8 7.6 %all-to-all-start = ((f32[8,1,128]{2,1,0:T(1,128)}), f32[8,1,128]{2,1,0:T(1,128)S(1)}, u32[]{:S(2)}, u32[]{:S(2)}) async-start(f32[8,1,128]{2,1,0:T(1,128)} %get-tuple-element.36), calls=%async_computation | async-start | bytes 8192 | tf_op jit(solution)/shard_map/all_to_all | solution.py:486
  53.4 0.5 collective-permute-done.7.rest_0
  53.9 1.6 %final_rows.1 = (f32[2,1024,128]{2,1,0:T(8,128)}, f32[8,128]{1,0:T(8,128)S(1)}) custom-call(s32[1]{0:T(128)} %bitcast.place, s32[128]{0:T(128)S(1)} %copy-done.3, f32[2,1024,128]{2,1,0:T(8,128)S(1)} %get-tuple-element.39.here, f32[320,128]{1,0:T(8,128)} %copy-done.4, f32[320,128]{1,0:T(8,128)} %copy-done.5, f32[1024,128]{1,0:T(8,128)S(1)} %collective-permute-done.4.near_1, ...), custom_call_target="tpu_custom_call" | custom-call | flops 10000000000 | bytes 1048576 | tf_op jit(solution)/shard_map/final_rows/pallas_call | solution.py:415
  55.6 2.4 %all-to-all-done.totals = f32[8,1,128]{2,1,0:T(1,128)S(1)} async-done(((f32[8,1,128]{2,1,0:T(1,128)}), f32[8,1,128]{2,1,0:T(1,128)S(1)}, u32[]{:S(2)}, u32[]{:S(2)}) %all-to-all-start) | async-done | bytes 4128 | tf_op jit(solution)/shard_map/all_to_all | solution.py:486
  57.9 0.7 %attend_rows.1 = bf16[3,2,1024]{2,1,0:T(2,128)(2,1)} custom-call(f32[8,1,128]{2,1,0:T(1,128)S(1)} %all-to-all-done.totals, f32[8,1024]{1,0:T(8,128)S(1)} %get-tuple-element.37.raw, f32[8,1024]{1,0:T(8,128)S(1)} %get-tuple-element.38.gated, f32[8,128]{1,0:T(8,128)S(1)} %get-tuple-element.44._), custom_call_target="tpu_custom_call" | custom-call | tf_op jit(solution)/shard_map/attend_rows/pallas_call | solution.py:449
  (15 shorter events, 0.0 us)
Async XLA Ops:
  0.6 18.0 %copy-start.3 = (s32[128]{0:T(128)S(1)}, s32[128]{0:T(128)}, u32[]{:S(2)}) copy-start(s32[128]{0:T(128)} %shard_ref.5) | copy-start | bytes 1540
  0.6 18.0 %copy-start = (bf16[3,2,4,1024]{3,2,1,0:T(4,128)(2,1)S(1)}, bf16[3,2,4,1024]{3,2,1,0:T(4,128)(2,1)}, u32[]{:S(2)}) copy-start(bf16[3,2,4,1024]{3,2,1,0:T(4,128)(2,1)} %projected.3) | copy-start | bytes 147460
  0.7 18.0 %copy-start.2 = (s32[128]{0:T(128)S(1)}, s32[128]{0:T(128)}, u32[]{:S(2)}) copy-start(s32[128]{0:T(128)} %slot_ref.1) | copy-start | bytes 1540
  0.7 18.0 %copy-start.1 = (f32[1024]{0:T(1024)S(1)}, f32[1024]{0:T(1024)}, u32[]{:S(2)}) copy-start(f32[1024]{0:T(1024)} %param.11) | copy-start | bytes 12292
  0.7 17.9 %copy-start.6 = (f32[8]{0:T(128)S(1)}, f32[8]{0:T(128)}, u32[]{:S(2)}) copy-start(f32[8]{0:T(128)} %param.10) | copy-start | bytes 100
  2.4 23.7 %collective-permute-start = (f32[1088,128]{1,0:T(8,128)S(1)}, f32[1088,128]{1,0:T(8,128)S(1)}, u32[]{:S(2)}, u32[]{:S(2)}) collective-permute-start(f32[1088,128]{1,0:T(8,128)S(1)} %get-tuple-element.24), channel_id=1, source_target_pairs={{0,8},{8,0},{9,17},{17,9},{2,10},{10,2},{11,19},{19,11},{4,12},{12... | collective-permute-start | bytes 1671176 | tf_op jit(solution)/shard_map/ppermute | solution.py:31
  16.6 10.6 %collective-permute-start.1 = (f32[1088,128]{1,0:T(8,128)S(1)}, f32[1088,128]{1,0:T(8,128)S(1)}, u32[]{:S(2)}, u32[]{:S(2)}) collective-permute-start(f32[1088,128]{1,0:T(8,128)S(1)} %get-tuple-element.25), channel_id=1, source_target_pairs={{8,16},{16,8},{17,25},{25,17},{10,18},{18,10},{19,27},{27,19},{12,... | collective-permute-start | bytes 1671176 | tf_op jit(solution)/shard_map/ppermute | solution.py:31
  19.9 20.7 %collective-permute-start.4 = (f32[1024,128]{1,0:T(8,128)S(1)}, f32[1024,128]{1,0:T(8,128)S(1)}, u32[]{:S(2)}, u32[]{:S(2)}) collective-permute-start(f32[1024,128]{1,0:T(8,128)S(1)} %get-tuple-element.30), channel_id=1, source_target_pairs={{8,16},{16,8},{17,25},{25,17},{10,18},{18,10},{19,27},{27,19},{12,... | collective-permute-start | bytes 1572872 | tf_op jit(solution)/shard_map/ppermute | solution.py:31
  23.2 20.9 %collective-permute-start.5 = (f32[1024,128]{1,0:T(8,128)S(1)}, f32[1024,128]{1,0:T(8,128)S(1)}, u32[]{:S(2)}, u32[]{:S(2)}) collective-permute-start(f32[1024,128]{1,0:T(8,128)S(1)} %get-tuple-element.31), channel_id=1, source_target_pairs={{0,8},{8,0},{9,17},{17,9},{2,10},{10,2},{11,19},{19,11},{4,12},{12... | collective-permute-start | bytes 1572872 | tf_op jit(solution)/shard_map/ppermute | solution.py:31
  28.2 16.0 %collective-permute-start.2 = (f32[320,128]{1,0:T(8,128)S(1)}, f32[320,128]{1,0:T(8,128)S(1)}, u32[]{:S(2)}, u32[]{:S(2)}) collective-permute-start(f32[320,128]{1,0:T(8,128)S(1)} %get-tuple-element.28), channel_id=1, source_target_pairs={{0,8},{8,0},{9,17},{17,9},{2,10},{10,2},{11,19},{19,11},{4,12},{12... | collective-permute-start | bytes 491528 | tf_op jit(solution)/shard_map/ppermute | solution.py:31
  35.3 8.9 %collective-permute-start.3 = (f32[320,128]{1,0:T(8,128)S(1)}, f32[320,128]{1,0:T(8,128)S(1)}, u32[]{:S(2)}, u32[]{:S(2)}) collective-permute-start(f32[320,128]{1,0:T(8,128)S(1)} %get-tuple-element.29), channel_id=1, source_target_pairs={{8,16},{16,8},{17,25},{25,17},{10,18},{18,10},{19,27},{27,19},{12,... | collective-permute-start | bytes 491528 | tf_op jit(solution)/shard_map/ppermute | solution.py:31
  37.2 16.2 %collective-permute-start.6 = (f32[768,128]{1,0:T(8,128)}, f32[768,128]{1,0:T(8,128)}, u32[]{:S(2)}, u32[]{:S(2)}) collective-permute-start(f32[768,128]{1,0:T(8,128)} %get-tuple-element.40), channel_id=1, source_target_pairs={{8,16},{16,8},{17,25},{25,17},{10,18},{18,10},{19,27},{27,19},{12,... | collective-permute-start | bytes 1179656 | tf_op jit(solution)/shard_map/ppermute | solution.py:31
  40.6 13.3 %collective-permute-start.7 = (f32[768,128]{1,0:T(8,128)}, f32[768,128]{1,0:T(8,128)}, u32[]{:S(2)}, u32[]{:S(2)}) collective-permute-start(f32[768,128]{1,0:T(8,128)} %get-tuple-element.41), channel_id=1, source_target_pairs={{0,8},{8,0},{9,17},{17,9},{2,10},{10,2},{11,19},{19,11},{4,12},{12... | collective-permute-start | bytes 1179656 | tf_op jit(solution)/shard_map/ppermute | solution.py:31
  44.2 1.7 %copy-start.4 = (f32[320,128]{1,0:T(8,128)}, f32[320,128]{1,0:T(8,128)S(1)}, u32[]{:S(2)}) copy-start(f32[320,128]{1,0:T(8,128)S(1)} %collective-permute-done.2.lead_0) | copy-start | bytes 491524
  44.2 1.7 %copy-start.5 = (f32[320,128]{1,0:T(8,128)}, f32[320,128]{1,0:T(8,128)S(1)}, u32[]{:S(2)}) copy-start(f32[320,128]{1,0:T(8,128)S(1)} %collective-permute-done.3.lead_1) | copy-start | bytes 491524
  45.8 12.1 %all-to-all-start = ((f32[8,1,128]{2,1,0:T(1,128)}), f32[8,1,128]{2,1,0:T(1,128)S(1)}, u32[]{:S(2)}, u32[]{:S(2)}) async-start(f32[8,1,128]{2,1,0:T(1,128)} %get-tuple-element.36), calls=%async_computation | async-start | bytes 8192 | tf_op jit(solution)/shard_map/all_to_all | solution.py:486

commit v15 on v14

--- a/solution.py
+++ b/solution.py
@@ -63,7 +63,7 @@
 def pick_kernel(shards, live, group, strides, place, shard_hbm, slot_hbm, projected, states, *refs):
     n_rows = len(strides)
     outs = refs[:n_rows]
-    staged, shard_ref, slot_ref, inputs, sems = refs[n_rows:]
+    shard_ref, slot_ref, inputs, staged, sems = refs[n_rows:]
     dim = outs[0].shape[1]
     rows = states.shape[1]
     device, side = spot(place, group)
@@ -101,14 +101,14 @@
     tile_rows = rows // dim * TILE
     return pl.pallas_call(
         functools.partial(pick_kernel, shards, live, group, strides),
-        out_shape=[jax.ShapeDtypeStruct((rows + tile_rows, dim), F32)] * len(strides)
-        + [jax.ShapeDtypeStruct(states.shape, F32)],
+        out_shape=[jax.ShapeDtypeStruct((rows + tile_rows, dim), F32)] * len(strides),
         in_specs=[SMEM] + [HBM] * 4,
-        out_specs=[VMEM] * (len(strides) + 1),
+        out_specs=[VMEM] * len(strides),
         scratch_shapes=[
             pltpu.SMEM(from_shard.shape, jnp.int32),
             pltpu.SMEM(from_slot.shape, jnp.int32),
             pltpu.VMEM(projected.shape, projected.dtype),
+            pltpu.VMEM(states.shape, F32),
             pltpu.SemaphoreType.DMA((4,)),
         ],
         compiler_params=pltpu.CompilerParams(vmem_limit_bytes=6 * MIB),
@@ -168,20 +168,27 @@
 
 
 def prepare_kernel(
-    shards, live, group, strides, place, shard_ref, slot_ref, projected, rate, gain, states,
+    shards, live, group, strides, place, shard_ref, slot_ref, projected, rate, gain, _, states,
     query, grown, base, gated, decay, made, here, outer, token, *refs,
 ):
-    outs, parts = refs[:-1], refs[-1]
+    outs, (parts, sems) = refs[:-2], refs[-2:]
     token[...] = jnp.zeros_like(token)
     rows, dim = here.shape[1:]
     heads = rows // dim
     steps = projected.shape[0]
     device, side = spot(place, group)
+    copies = [
+        pltpu.make_async_copy(
+            states.at[slot_ref[device * live + row]], here.at[row], sems.at[row]
+        )
+        for row in range(live)
+    ]
+    start_all(copies)
+    sends = []
     for n, stride in enumerate(strides):
         slot = slot_for(stride, shards, live, device, side, shard_ref, slot_ref)
-        outs[n][...] = states[slot]
-    for row in range(live):
-        here[row] = states[slot_ref[device * live + row]]
+        sends.append(pltpu.make_async_copy(states.at[slot], outs[n], sems.at[live + n]))
+    start_all(sends)
     parts[...] = jnp.zeros_like(parts)
     for step in range(steps):
         for row in range(live):
@@ -239,16 +246,18 @@
                 (((0,), (0,)), ((), ())),
                 preferred_element_type=F32,
             )
+    wait_all(copies)
     for row in range(live):
         for head in range(heads):
             span = slice(head * dim, (head + 1) * dim)
             made[row, head * TILE : (head + 1) * TILE] = products(
                 queries[:, span], here[row, span]
             )
+    wait_all(sends)
 
 
 def prepare(
-    place, from_shard, from_slot, projected, rate, gain, states, shards, live, group, strides
+    place, from_shard, from_slot, projected, rate, gain, after, states, shards, live, group, strides
 ):
     rows, dim = states.shape[1:]
     tile = jax.ShapeDtypeStruct((TILE, rows), F32)
@@ -264,12 +273,15 @@
             jax.ShapeDtypeStruct((TILE, dim), F32),
         ]
         + [jax.ShapeDtypeStruct((rows, dim), F32)] * len(strides),
-        in_specs=[SMEM] * 3 + [VMEM] * 4,
+        in_specs=[SMEM] * 3 + [VMEM] * 4 + [HBM],
         out_specs=[VMEM] * (9 + len(strides)),
-        scratch_shapes=[pltpu.VMEM((projected.shape[2], TILE, rows), F32)],
+        scratch_shapes=[
+            pltpu.VMEM((projected.shape[2], TILE, rows), F32),
+            pltpu.SemaphoreType.DMA((live + len(strides),)),
+        ],
         compiler_params=pltpu.CompilerParams(vmem_limit_bytes=8 * MIB),
         name="prepare_rows",
-    )(place, from_shard, from_slot, projected, rate, gain, states)
+    )(place, from_shard, from_slot, projected, rate, gain, after, *in_hbm(states))
 
 
 def diagonal(dim):
@@ -464,14 +476,14 @@
     place = lax.axis_index(("dp", "tensor")).astype(jnp.int32).reshape(1)
     states = states.reshape(slots, width, dim)
 
-    row_0, row_1, staged = pick(
+    row_0, row_1 = pick(
         place, from_shard, from_slot, projected, states, shards, live, group, (-2, 2)
     )
     half_1, half_0 = swapped(row_1, 1), swapped(row_0, 0)
     rate = jnp.repeat(decay_rate, dim).reshape(1, width)
     gain = norm_gain.reshape(1, width)
     query, grown, base, gated, decay, local, here, outer, token, row_0, row_1 = prepare(
-        place, from_shard, from_slot, projected, rate, gain, staged, shards, live,
+        place, from_shard, from_slot, projected, rate, gain, row_1, states, shards, live,
         group, (-1, 1),
     )
     near_1, near_0 = swapped(row_1, 1), swapped(row_0, 0)

time: 59 us -> 59.5 us (level); the launches traced: 58.6 us -> 58.4 us
  starting transfers between devices: 44.9 us -> 42.3 us
  Pallas kernels: 7.94 us -> 10.1 us
    ppermute x8, waiting for transfers between devices: 2.52 us -> 5.15 us  [swapped(): return lax.ppermute(block, ('dp', 'tensor'), route)]
    all_to_all x1, waiting for transfers between devices: 2.36 us -> 0.01 us  [on_device(): totals = lax.all_to_all(sums, 'tensor', 0, 0)]
    all_to_all x1, starting transfers between devices: 7.58 us -> 6.06 us  [on_device(): totals = lax.all_to_all(sums, 'tensor', 0, 0)]
    ppermute x8, starting transfers between devices: 37.3 us -> 36.2 us  [swapped(): return lax.ppermute(block, ('dp', 'tensor'), route)]
    pallas_call x1, Pallas kernels: 1.23 us -> 2.29 us  [prepare(): pl.pallas_call(functools.partial(prepare_kernel, shards, live, group, str...]
    pallas_call x1, Pallas kernels: 1.64 us -> 2.7 us  [final_of(): pl.pallas_call(functools.partial(final_kernel, shards, live, group), out_...]
  transfers between devices with their start and end apart: 9 -> 9, of which waited for: 4 -> 3; matrix products, arithmetic and copies ran while one was open for 0% -> 0% of each run, Pallas kernels for 9% -> 13%
where the time goes in v15:
time: 59.5 us; the launch traced here: 58.4 us
  starting transfers between devices  42.3 us (71%)
  Pallas kernels  10.1 us (17%)
  waiting for transfers between devices  5.15 us (9%)
  between operations  0.84 us (1%)
    ppermute x8, starting transfers between devices, swapped(): return lax.ppermute(block, ('dp', 'tensor'), route)  36.2 us
    all_to_all x1, starting transfers between devices, on_device(): totals = lax.all_to_all(sums, 'tensor', 0, 0)  6.06 us
    ppermute x8, waiting for transfers between devices, swapped(): return lax.ppermute(block, ('dp', 'tensor'), route)  5.15 us
    pallas_call x1, Pallas kernels, final_of(): pl.pallas_call(functools.partial(final_kernel, shards, live, group), out_...  2.7 us
    pallas_call x1, Pallas kernels, prepare(): pl.pallas_call(functools.partial(prepare_kernel, shards, live, group, str...  2.29 us
    pallas_call x1, Pallas kernels, pick(): pl.pallas_call(functools.partial(pick_kernel, shards, live, group, stride...  1.75 us
    pallas_call x1, Pallas kernels, raw_of(): pl.pallas_call(functools.partial(raw_kernel, shards, live, group), out_sh...  1.62 us
  transfers between devices with their start and end apart: 9, of which 3 were waited for; matrix products, arithmetic and copies ran while one was open for 0% of the time, Pallas kernels for 13%

profile of v15, /device:TPU:1, one launch (start us, length us, event | category | flops | bytes accessed | tf_op | source)
XLA Modules:
  0.0 58.4 jit_solution(2521979865321553717)
XLA Ops:
  0.7 1.8 %pick_rows.1 = (f32[1088,128]{1,0:T(8,128)S(1)}, f32[1088,128]{1,0:T(8,128)S(1)}) custom-call(s32[1]{0:T(128)} %bitcast.place, s32[128]{0:T(128)} %shard_ref.5, s32[128]{0:T(128)} %slot_ref.1, bf16[3,2,4,1024]{3,2,1,0:T(4,128)(2,1)} %projected.3, f32[4,1024,128]{2,1,0:T(8,128)} %bitcast.7), custom_call_target="tpu_custom_call" | custom-call | tf_op jit(solution)/shard_map/pick_rows/pallas_call | solution.py:102
  2.4 14.1 %collective-permute-start = (f32[1088,128]{1,0:T(8,128)S(1)}, f32[1088,128]{1,0:T(8,128)S(1)}, u32[]{:S(2)}, u32[]{:S(2)}) collective-permute-start(f32[1088,128]{1,0:T(8,128)S(1)} %get-tuple-element.23), channel_id=1, source_target_pairs={{0,8},{8,0},{9,17},{17,9},{2,10},{10,2},{11,19},{19,11},{4,12},{12... | collective-permute-start | bytes 1671176 | tf_op jit(solution)/shard_map/ppermute | solution.py:31
  16.6 1.9 %collective-permute-start.1 = (f32[1088,128]{1,0:T(8,128)S(1)}, f32[1088,128]{1,0:T(8,128)S(1)}, u32[]{:S(2)}, u32[]{:S(2)}) collective-permute-start(f32[1088,128]{1,0:T(8,128)S(1)} %get-tuple-element.24._), channel_id=1, source_target_pairs={{8,16},{16,8},{17,25},{25,17},{10,18},{18,10},{19,27},{27,19},{12,... | collective-permute-start | bytes 1671176 | tf_op jit(solution)/shard_map/ppermute | solution.py:31
  18.5 0.1 broadcast_in_dim.3
  18.6 2.3 %prepare_rows.1 = (f32[8,1024]{1,0:T(8,128)S(1)}, f32[8,1024]{1,0:T(8,128)S(1)}, f32[8,1024]{1,0:T(8,128)S(1)}, f32[8,1024]{1,0:T(8,128)S(1)}, f32[1,1024]{1,0:T...) custom-call(s32[1]{0:T(128)} %bitcast.place, ...), custom_call_target="tpu_custom_call" | custom-call | tf_op jit(solution)/shard_map/prepare_rows/pallas_call | solution.py:265
  20.9 3.4 %collective-permute-start.4 = (f32[1024,128]{1,0:T(8,128)S(1)}, f32[1024,128]{1,0:T(8,128)S(1)}, u32[]{:S(2)}, u32[]{:S(2)}) collective-permute-start(f32[1024,128]{1,0:T(8,128)S(1)} %get-tuple-element.28), channel_id=1, source_target_pairs={{8,16},{16,8},{17,25},{25,17},{10,18},{18,10},{19,27},{27,19},{12,... | collective-permute-start | bytes 1572872 | tf_op jit(solution)/shard_map/ppermute | solution.py:31
  24.3 1.9 %collective-permute-start.5 = (f32[1024,128]{1,0:T(8,128)S(1)}, f32[1024,128]{1,0:T(8,128)S(1)}, u32[]{:S(2)}, u32[]{:S(2)}) collective-permute-start(f32[1024,128]{1,0:T(8,128)S(1)} %get-tuple-element.29), channel_id=1, source_target_pairs={{0,8},{8,0},{9,17},{17,9},{2,10},{10,2},{11,19},{19,11},{4,12},{12... | collective-permute-start | bytes 1572872 | tf_op jit(solution)/shard_map/ppermute | solution.py:31
  26.2 0.9 %collective-permute-done.1.from_1 = f32[1088,128]{1,0:T(8,128)S(1)} collective-permute-done((f32[1088,128]{1,0:T(8,128)S(1)}, f32[1088,128]{1,0:T(8,128)S(1)}, u32[]{:S(2)}, u32[]{:S(2)}) %collective-permute-start.1) | collective-permute-done | bytes 557088 | tf_op jit(solution)/shard_map/ppermute | solution.py:31
  27.2 1.0 %relay_rows.1 = (f32[320,128]{1,0:T(8,128)S(1)}, f32[320,128]{1,0:T(8,128)S(1)}, f32[768,128]{1,0:T(8,128)}, f32[768,128]{1,0:T(8,128)}) custom-call(f32[1088,128]{1,0:T(8,128)S(1)} %collective-permute-done.from_0, f32[1088,128]{1,0:T(8,128)S(1)} %collective-permute-done.1.from_1, f32[8,128]{1,0:T(8,128)S(1)} %get-tuple-element.25._), custom_call_target="tpu_custom_call" | custom-call | tf_op jit(solution)/shard_map/relay_rows/pallas_call | solution.py:143
  28.2 7.1 %collective-permute-start.2 = (f32[320,128]{1,0:T(8,128)S(1)}, f32[320,128]{1,0:T(8,128)S(1)}, u32[]{:S(2)}, u32[]{:S(2)}) collective-permute-start(f32[320,128]{1,0:T(8,128)S(1)} %get-tuple-element.26), channel_id=1, source_target_pairs={{0,8},{8,0},{9,17},{17,9},{2,10},{10,2},{11,19},{19,11},{4,12},{12... | collective-permute-start | bytes 491528 | tf_op jit(solution)/shard_map/ppermute | solution.py:31
  35.3 1.9 %collective-permute-start.3 = (f32[320,128]{1,0:T(8,128)S(1)}, f32[320,128]{1,0:T(8,128)S(1)}, u32[]{:S(2)}, u32[]{:S(2)}) collective-permute-start(f32[320,128]{1,0:T(8,128)S(1)} %get-tuple-element.27), channel_id=1, source_target_pairs={{8,16},{16,8},{17,25},{25,17},{10,18},{18,10},{19,27},{27,19},{12,... | collective-permute-start | bytes 491528 | tf_op jit(solution)/shard_map/ppermute | solution.py:31
  37.2 3.4 %collective-permute-start.6 = (f32[768,128]{1,0:T(8,128)}, f32[768,128]{1,0:T(8,128)}, u32[]{:S(2)}, u32[]{:S(2)}) collective-permute-start(f32[768,128]{1,0:T(8,128)} %get-tuple-element.38), channel_id=1, source_target_pairs={{8,16},{16,8},{17,25},{25,17},{10,18},{18,10},{19,27},{27,19},{12,... | collective-permute-start | bytes 1179656 | tf_op jit(solution)/shard_map/ppermute | solution.py:31
  40.6 0.0 collective-permute-done.4.near_1
  40.6 2.5 %collective-permute-start.7 = (f32[768,128]{1,0:T(8,128)}, f32[768,128]{1,0:T(8,128)}, u32[]{:S(2)}, u32[]{:S(2)}) collective-permute-start(f32[768,128]{1,0:T(8,128)} %get-tuple-element.39), channel_id=1, source_target_pairs={{0,8},{8,0},{9,17},{17,9},{2,10},{10,2},{11,19},{19,11},{4,12},{12... | collective-permute-start | bytes 1179656 | tf_op jit(solution)/shard_map/ppermute | solution.py:31
  43.1 0.0 collective-permute-done.5.near_0
  43.1 1.6 %collective-permute-done.2.lead_0 = f32[320,128]{1,0:T(8,128)S(1)} collective-permute-done((f32[320,128]{1,0:T(8,128)S(1)}, f32[320,128]{1,0:T(8,128)S(1)}, u32[]{:S(2)}, u32[]{:S(2)}) %collective-permute-start.2) | collective-permute-done | bytes 163872 | tf_op jit(solution)/shard_map/ppermute | solution.py:31
  44.6 0.0 collective-permute-done.3.lead_1
  44.6 1.6 %raw_rows.1 = (f32[8,1024]{1,0:T(8,128)S(1)}, f32[8,1,128]{2,1,0:T(1,128)}) custom-call(s32[1]{0:T(128)} %bitcast.place, s32[128]{0:T(128)S(1)} %copy-done.3, f32[320,128]{1,0:T(8,128)S(1)} %collective-permute-done.2.lead_0, f32[320,128]{1,0:T(8,128)S(1)} %collective-permute-done.3.lead_1, f32[1024,128]{1,0:T(8,128)S(1)} %collective-permute-done.4.near_1, ...), custom_call_target="tpu_custom_call" | custom-call | flops 999999995904 | bytes 1048576 | tf_op jit(solution)/shard_map/raw_rows/pallas_call | solution.py:339
  46.3 6.1 %all-to-all-start = ((f32[8,1,128]{2,1,0:T(1,128)}), f32[8,1,128]{2,1,0:T(1,128)S(1)}, u32[]{:S(2)}, u32[]{:S(2)}) async-start(f32[8,1,128]{2,1,0:T(1,128)} %get-tuple-element.34), calls=%async_computation | async-start | bytes 8192 | tf_op jit(solution)/shard_map/all_to_all | solution.py:498
  52.4 0.0 collective-permute-done.6.rest_1
  52.4 2.6 %collective-permute-done.7.rest_0 = f32[768,128]{1,0:T(8,128)} collective-permute-done((f32[768,128]{1,0:T(8,128)}, f32[768,128]{1,0:T(8,128)}, u32[]{:S(2)}, u32[]{:S(2)}) %collective-permute-start.7) | collective-permute-done | bytes 393248 | tf_op jit(solution)/shard_map/ppermute | solution.py:31
  55.0 2.7 %final_rows.1 = (f32[2,1024,128]{2,1,0:T(8,128)}, f32[8,128]{1,0:T(8,128)S(1)}) custom-call(s32[1]{0:T(128)} %bitcast.place, s32[128]{0:T(128)S(1)} %copy-done.3, f32[2,1024,128]{2,1,0:T(8,128)S(1)} %get-tuple-element.37.here, f32[320,128]{1,0:T(8,128)} %copy-done.4, f32[320,128]{1,0:T(8,128)} %copy-done.5, f32[1024,128]{1,0:T(8,128)S(1)} %collective-permute-done.4.near_1, ...), custom_call_target="tpu_custom_call" | custom-call | flops 10000000000 | bytes 1048576 | tf_op jit(solution)/shard_map/final_rows/pallas_call | solution.py:427
  57.7 0.0 all-to-all-done.totals
  57.7 0.7 %attend_rows.1 = bf16[3,2,1024]{2,1,0:T(2,128)(2,1)} custom-call(f32[8,1,128]{2,1,0:T(1,128)S(1)} %all-to-all-done.totals, f32[8,1024]{1,0:T(8,128)S(1)} %get-tuple-element.35.raw, f32[8,1024]{1,0:T(8,128)S(1)} %get-tuple-element.36.gated, f32[8,128]{1,0:T(8,128)S(1)} %get-tuple-element.42._), custom_call_target="tpu_custom_call" | custom-call | tf_op jit(solution)/shard_map/attend_rows/pallas_call | solution.py:461
  (15 shorter events, 0.0 us)
Async XLA Ops:
  0.6 18.0 %copy-start.3 = (s32[128]{0:T(128)S(1)}, s32[128]{0:T(128)}, u32[]{:S(2)}) copy-start(s32[128]{0:T(128)} %shard_ref.5) | copy-start | bytes 1540
  0.6 18.0 %copy-start = (bf16[3,2,4,1024]{3,2,1,0:T(4,128)(2,1)S(1)}, bf16[3,2,4,1024]{3,2,1,0:T(4,128)(2,1)}, u32[]{:S(2)}) copy-start(bf16[3,2,4,1024]{3,2,1,0:T(4,128)(2,1)} %projected.3) | copy-start | bytes 147460
  0.7 18.0 %copy-start.2 = (s32[128]{0:T(128)S(1)}, s32[128]{0:T(128)}, u32[]{:S(2)}) copy-start(s32[128]{0:T(128)} %slot_ref.1) | copy-start | bytes 1540
  0.7 18.0 %copy-start.1 = (f32[1024]{0:T(1024)S(1)}, f32[1024]{0:T(1024)}, u32[]{:S(2)}) copy-start(f32[1024]{0:T(1024)} %param.11) | copy-start | bytes 12292
  0.7 17.9 %copy-start.6 = (f32[8]{0:T(128)S(1)}, f32[8]{0:T(128)}, u32[]{:S(2)}) copy-start(f32[8]{0:T(128)} %param.10) | copy-start | bytes 100
  2.4 23.8 %collective-permute-start = (f32[1088,128]{1,0:T(8,128)S(1)}, f32[1088,128]{1,0:T(8,128)S(1)}, u32[]{:S(2)}, u32[]{:S(2)}) collective-permute-start(f32[1088,128]{1,0:T(8,128)S(1)} %get-tuple-element.23), channel_id=1, source_target_pairs={{0,8},{8,0},{9,17},{17,9},{2,10},{10,2},{11,19},{19,11},{4,12},{12... | collective-permute-start | bytes 1671176 | tf_op jit(solution)/shard_map/ppermute | solution.py:31
  16.6 10.6 %collective-permute-start.1 = (f32[1088,128]{1,0:T(8,128)S(1)}, f32[1088,128]{1,0:T(8,128)S(1)}, u32[]{:S(2)}, u32[]{:S(2)}) collective-permute-start(f32[1088,128]{1,0:T(8,128)S(1)} %get-tuple-element.24._), channel_id=1, source_target_pairs={{8,16},{16,8},{17,25},{25,17},{10,18},{18,10},{19,27},{27,19},{12,... | collective-permute-start | bytes 1671176 | tf_op jit(solution)/shard_map/ppermute | solution.py:31
  20.9 19.6 %collective-permute-start.4 = (f32[1024,128]{1,0:T(8,128)S(1)}, f32[1024,128]{1,0:T(8,128)S(1)}, u32[]{:S(2)}, u32[]{:S(2)}) collective-permute-start(f32[1024,128]{1,0:T(8,128)S(1)} %get-tuple-element.28), channel_id=1, source_target_pairs={{8,16},{16,8},{17,25},{25,17},{10,18},{18,10},{19,27},{27,19},{12,... | collective-permute-start | bytes 1572872 | tf_op jit(solution)/shard_map/ppermute | solution.py:31
  24.3 18.8 %collective-permute-start.5 = (f32[1024,128]{1,0:T(8,128)S(1)}, f32[1024,128]{1,0:T(8,128)S(1)}, u32[]{:S(2)}, u32[]{:S(2)}) collective-permute-start(f32[1024,128]{1,0:T(8,128)S(1)} %get-tuple-element.29), channel_id=1, source_target_pairs={{0,8},{8,0},{9,17},{17,9},{2,10},{10,2},{11,19},{19,11},{4,12},{12... | collective-permute-start | bytes 1572872 | tf_op jit(solution)/shard_map/ppermute | solution.py:31
  28.2 16.5 %collective-permute-start.2 = (f32[320,128]{1,0:T(8,128)S(1)}, f32[320,128]{1,0:T(8,128)S(1)}, u32[]{:S(2)}, u32[]{:S(2)}) collective-permute-start(f32[320,128]{1,0:T(8,128)S(1)} %get-tuple-element.26), channel_id=1, source_target_pairs={{0,8},{8,0},{9,17},{17,9},{2,10},{10,2},{11,19},{19,11},{4,12},{12... | collective-permute-start | bytes 491528 | tf_op jit(solution)/shard_map/ppermute | solution.py:31
  35.3 9.4 %collective-permute-start.3 = (f32[320,128]{1,0:T(8,128)S(1)}, f32[320,128]{1,0:T(8,128)S(1)}, u32[]{:S(2)}, u32[]{:S(2)}) collective-permute-start(f32[320,128]{1,0:T(8,128)S(1)} %get-tuple-element.27), channel_id=1, source_target_pairs={{8,16},{16,8},{17,25},{25,17},{10,18},{18,10},{19,27},{27,19},{12,... | collective-permute-start | bytes 491528 | tf_op jit(solution)/shard_map/ppermute | solution.py:31
  37.2 15.2 %collective-permute-start.6 = (f32[768,128]{1,0:T(8,128)}, f32[768,128]{1,0:T(8,128)}, u32[]{:S(2)}, u32[]{:S(2)}) collective-permute-start(f32[768,128]{1,0:T(8,128)} %get-tuple-element.38), channel_id=1, source_target_pairs={{8,16},{16,8},{17,25},{25,17},{10,18},{18,10},{19,27},{27,19},{12,... | collective-permute-start | bytes 1179656 | tf_op jit(solution)/shard_map/ppermute | solution.py:31
  40.6 14.4 %collective-permute-start.7 = (f32[768,128]{1,0:T(8,128)}, f32[768,128]{1,0:T(8,128)}, u32[]{:S(2)}, u32[]{:S(2)}) collective-permute-start(f32[768,128]{1,0:T(8,128)} %get-tuple-element.39), channel_id=1, source_target_pairs={{0,8},{8,0},{9,17},{17,9},{2,10},{10,2},{11,19},{19,11},{4,12},{12... | collective-permute-start | bytes 1179656 | tf_op jit(solution)/shard_map/ppermute | solution.py:31
  44.6 1.6 %copy-start.4 = (f32[320,128]{1,0:T(8,128)}, f32[320,128]{1,0:T(8,128)S(1)}, u32[]{:S(2)}) copy-start(f32[320,128]{1,0:T(8,128)S(1)} %collective-permute-done.2.lead_0) | copy-start | bytes 491524
  44.6 1.6 %copy-start.5 = (f32[320,128]{1,0:T(8,128)}, f32[320,128]{1,0:T(8,128)S(1)}, u32[]{:S(2)}) copy-start(f32[320,128]{1,0:T(8,128)S(1)} %collective-permute-done.3.lead_1) | copy-start | bytes 491524
  46.3 11.4 %all-to-all-start = ((f32[8,1,128]{2,1,0:T(1,128)}), f32[8,1,128]{2,1,0:T(1,128)S(1)}, u32[]{:S(2)}, u32[]{:S(2)}) async-start(f32[8,1,128]{2,1,0:T(1,128)} %get-tuple-element.34), calls=%async_computation | async-start | bytes 8192 | tf_op jit(solution)/shard_map/all_to_all | solution.py:498

commit v16 on v15

--- a/solution.py
+++ b/solution.py
@@ -9,7 +9,7 @@
 EPS = 1e-05
 F32 = jnp.float32
 BF16 = jnp.bfloat16
-EARLY = 2
+EARLY = 3
 TILE = 8
 MIB = 1024 * 1024
 SMEM = pl.BlockSpec(memory_space=pltpu.SMEM)

time: 59.5 us -> 59.4 us (level); the launches traced: 58.4 us -> 59 us
  waiting for transfers between devices: 5.15 us -> 6.79 us
  Pallas kernels: 10.1 us -> 8.99 us
    all_to_all x1, waiting for transfers between devices: 0.01 us -> 2.84 us  [on_device(): totals = lax.all_to_all(sums, 'tensor', 0, 0)]
    ppermute x8, waiting for transfers between devices: 5.15 us -> 3.95 us  [swapped(): return lax.ppermute(block, ('dp', 'tensor'), route)]
    pallas_call x1, Pallas kernels: 2.7 us -> 1.65 us  [final_of(): pl.pallas_call(functools.partial(final_kernel, shards, live, group), out_...]
  transfers between devices with their start and end apart: 9 -> 9, of which waited for: 3 -> 3; matrix products, arithmetic and copies ran while one was open for 0% -> 0% of each run, Pallas kernels for 13% -> 11%
where the time goes in v16:
time: 59.4 us; the launch traced here: 59 us
  starting transfers between devices  42.2 us (71%)
  Pallas kernels  8.99 us (15%)
  waiting for transfers between devices  6.79 us (11%)
  between operations  0.83 us (1%)
    ppermute x8, starting transfers between devices, swapped(): return lax.ppermute(block, ('dp', 'tensor'), route)  36.3 us
    all_to_all x1, starting transfers between devices, on_device(): totals = lax.all_to_all(sums, 'tensor', 0, 0)  5.99 us
    ppermute x8, waiting for transfers between devices, swapped(): return lax.ppermute(block, ('dp', 'tensor'), route)  3.95 us
    all_to_all x1, waiting for transfers between devices, on_device(): totals = lax.all_to_all(sums, 'tensor', 0, 0)  2.84 us
    pallas_call x1, Pallas kernels, prepare(): pl.pallas_call(functools.partial(prepare_kernel, shards, live, group, str...  2.29 us
    pallas_call x1, Pallas kernels, pick(): pl.pallas_call(functools.partial(pick_kernel, shards, live, group, stride...  1.75 us
    pallas_call x1, Pallas kernels, final_of(): pl.pallas_call(functools.partial(final_kernel, shards, live, group), out_...  1.65 us
    pallas_call x1, Pallas kernels, raw_of(): pl.pallas_call(functools.partial(raw_kernel, shards, live, group), out_sh...  1.63 us
  transfers between devices with their start and end apart: 9, of which 3 were waited for; matrix products, arithmetic and copies ran while one was open for 0% of the time, Pallas kernels for 11%

profile of v16, /device:TPU:1, one launch (start us, length us, event | category | flops | bytes accessed | tf_op | source)
XLA Modules:
  0.0 59.0 jit_solution(10457426570122873173)
XLA Ops:
  0.7 1.8 %pick_rows.1 = (f32[1088,128]{1,0:T(8,128)S(1)}, f32[1088,128]{1,0:T(8,128)S(1)}) custom-call(s32[1]{0:T(128)} %bitcast.place, s32[128]{0:T(128)} %shard_ref.5, s32[128]{0:T(128)} %slot_ref.1, bf16[3,2,4,1024]{3,2,1,0:T(4,128)(2,1)} %projected.3, f32[4,1024,128]{2,1,0:T(8,128)} %bitcast.7), custom_call_target="tpu_custom_call" | custom-call | tf_op jit(solution)/shard_map/pick_rows/pallas_call | solution.py:102
  2.4 14.1 %collective-permute-start = (f32[1088,128]{1,0:T(8,128)S(1)}, f32[1088,128]{1,0:T(8,128)S(1)}, u32[]{:S(2)}, u32[]{:S(2)}) collective-permute-start(f32[1088,128]{1,0:T(8,128)S(1)} %get-tuple-element.23), channel_id=1, source_target_pairs={{0,8},{8,0},{9,17},{17,9},{2,10},{10,2},{11,19},{19,11},{4,12},{12... | collective-permute-start | bytes 1671176 | tf_op jit(solution)/shard_map/ppermute | solution.py:31
  16.6 1.9 %collective-permute-start.1 = (f32[1088,128]{1,0:T(8,128)S(1)}, f32[1088,128]{1,0:T(8,128)S(1)}, u32[]{:S(2)}, u32[]{:S(2)}) collective-permute-start(f32[1088,128]{1,0:T(8,128)S(1)} %get-tuple-element.24._), channel_id=1, source_target_pairs={{8,16},{16,8},{17,25},{25,17},{10,18},{18,10},{19,27},{27,19},{12,... | collective-permute-start | bytes 1671176 | tf_op jit(solution)/shard_map/ppermute | solution.py:31
  18.5 0.1 broadcast_in_dim.3
  18.6 2.3 %prepare_rows.1 = (f32[8,1024]{1,0:T(8,128)S(1)}, f32[8,1024]{1,0:T(8,128)S(1)}, f32[8,1024]{1,0:T(8,128)S(1)}, f32[8,1024]{1,0:T(8,128)S(1)}, f32[1,1024]{1,0:T...) custom-call(s32[1]{0:T(128)} %bitcast.place, ...), custom_call_target="tpu_custom_call" | custom-call | tf_op jit(solution)/shard_map/prepare_rows/pallas_call | solution.py:265
  20.9 3.4 %collective-permute-start.4 = (f32[1024,128]{1,0:T(8,128)S(1)}, f32[1024,128]{1,0:T(8,128)S(1)}, u32[]{:S(2)}, u32[]{:S(2)}) collective-permute-start(f32[1024,128]{1,0:T(8,128)S(1)} %get-tuple-element.28), channel_id=1, source_target_pairs={{8,16},{16,8},{17,25},{25,17},{10,18},{18,10},{19,27},{27,19},{12,... | collective-permute-start | bytes 1572872 | tf_op jit(solution)/shard_map/ppermute | solution.py:31
  24.3 2.0 %collective-permute-start.5 = (f32[1024,128]{1,0:T(8,128)S(1)}, f32[1024,128]{1,0:T(8,128)S(1)}, u32[]{:S(2)}, u32[]{:S(2)}) collective-permute-start(f32[1024,128]{1,0:T(8,128)S(1)} %get-tuple-element.29), channel_id=1, source_target_pairs={{0,8},{8,0},{9,17},{17,9},{2,10},{10,2},{11,19},{19,11},{4,12},{12... | collective-permute-start | bytes 1572872 | tf_op jit(solution)/shard_map/ppermute | solution.py:31
  26.3 0.0 collective-permute-done.from_0
  26.3 0.9 %collective-permute-done.1.from_1 = f32[1088,128]{1,0:T(8,128)S(1)} collective-permute-done((f32[1088,128]{1,0:T(8,128)S(1)}, f32[1088,128]{1,0:T(8,128)S(1)}, u32[]{:S(2)}, u32[]{:S(2)}) %collective-permute-start.1) | collective-permute-done | bytes 557088 | tf_op jit(solution)/shard_map/ppermute | solution.py:31
  27.2 1.0 %relay_rows.1 = (f32[448,128]{1,0:T(8,128)S(1)}, f32[448,128]{1,0:T(8,128)S(1)}, f32[640,128]{1,0:T(8,128)}, f32[640,128]{1,0:T(8,128)}) custom-call(f32[1088,128]{1,0:T(8,128)S(1)} %collective-permute-done.from_0, f32[1088,128]{1,0:T(8,128)S(1)} %collective-permute-done.1.from_1, f32[8,128]{1,0:T(8,128)S(1)} %get-tuple-element.25._), custom_call_target="tpu_custom_call" | custom-call | tf_op jit(solution)/shard_map/relay_rows/pallas_call | solution.py:143
  28.2 7.1 %collective-permute-start.2 = (f32[448,128]{1,0:T(8,128)S(1)}, f32[448,128]{1,0:T(8,128)S(1)}, u32[]{:S(2)}, u32[]{:S(2)}) collective-permute-start(f32[448,128]{1,0:T(8,128)S(1)} %get-tuple-element.26), channel_id=1, source_target_pairs={{0,8},{8,0},{9,17},{17,9},{2,10},{10,2},{11,19},{19,11},{4,12},{12... | collective-permute-start | bytes 688136 | tf_op jit(solution)/shard_map/ppermute | solution.py:31
  35.2 1.9 %collective-permute-start.3 = (f32[448,128]{1,0:T(8,128)S(1)}, f32[448,128]{1,0:T(8,128)S(1)}, u32[]{:S(2)}, u32[]{:S(2)}) collective-permute-start(f32[448,128]{1,0:T(8,128)S(1)} %get-tuple-element.27), channel_id=1, source_target_pairs={{8,16},{16,8},{17,25},{25,17},{10,18},{18,10},{19,27},{27,19},{12,... | collective-permute-start | bytes 688136 | tf_op jit(solution)/shard_map/ppermute | solution.py:31
  37.2 3.4 %collective-permute-start.6 = (f32[640,128]{1,0:T(8,128)}, f32[640,128]{1,0:T(8,128)}, u32[]{:S(2)}, u32[]{:S(2)}) collective-permute-start(f32[640,128]{1,0:T(8,128)} %get-tuple-element.38), channel_id=1, source_target_pairs={{8,16},{16,8},{17,25},{25,17},{10,18},{18,10},{19,27},{27,19},{12,... | collective-permute-start | bytes 983048 | tf_op jit(solution)/shard_map/ppermute | solution.py:31
  40.5 0.0 collective-permute-done.4.near_1
  40.6 2.5 %collective-permute-start.7 = (f32[640,128]{1,0:T(8,128)}, f32[640,128]{1,0:T(8,128)}, u32[]{:S(2)}, u32[]{:S(2)}) collective-permute-start(f32[640,128]{1,0:T(8,128)} %get-tuple-element.39), channel_id=1, source_target_pairs={{0,8},{8,0},{9,17},{17,9},{2,10},{10,2},{11,19},{19,11},{4,12},{12... | collective-permute-start | bytes 983048 | tf_op jit(solution)/shard_map/ppermute | solution.py:31
  43.1 0.0 collective-permute-done.5.near_0
  43.1 3.0 %collective-permute-done.2.lead_0 = f32[448,128]{1,0:T(8,128)S(1)} collective-permute-done((f32[448,128]{1,0:T(8,128)S(1)}, f32[448,128]{1,0:T(8,128)S(1)}, u32[]{:S(2)}, u32[]{:S(2)}) %collective-permute-start.2) | collective-permute-done | bytes 229408 | tf_op jit(solution)/shard_map/ppermute | solution.py:31
  46.1 1.6 %raw_rows.1 = (f32[8,1024]{1,0:T(8,128)S(1)}, f32[8,1,128]{2,1,0:T(1,128)}) custom-call(s32[1]{0:T(128)} %bitcast.place, s32[128]{0:T(128)S(1)} %copy-done.3, f32[448,128]{1,0:T(8,128)S(1)} %collective-permute-done.2.lead_0, f32[448,128]{1,0:T(8,128)S(1)} %collective-permute-done.3.lead_1, f32[1024,128]{1,0:T(8,128)S(1)} %collective-permute-done.4.near_1, ...), custom_call_target="tpu_custom_call" | custom-call | flops 999999995904 | bytes 1048576 | tf_op jit(solution)/shard_map/raw_rows/pallas_call | solution.py:339
  47.8 6.0 %all-to-all-start = ((f32[8,1,128]{2,1,0:T(1,128)}), f32[8,1,128]{2,1,0:T(1,128)S(1)}, u32[]{:S(2)}, u32[]{:S(2)}) async-start(f32[8,1,128]{2,1,0:T(1,128)} %get-tuple-element.34), calls=%async_computation | async-start | bytes 8192 | tf_op jit(solution)/shard_map/all_to_all | solution.py:498
  53.8 0.0 collective-permute-done.6.rest_1
  53.8 0.0 collective-permute-done.7.rest_0
  53.8 1.6 %final_rows.1 = (f32[2,1024,128]{2,1,0:T(8,128)}, f32[8,128]{1,0:T(8,128)S(1)}) custom-call(s32[1]{0:T(128)} %bitcast.place, s32[128]{0:T(128)S(1)} %copy-done.3, f32[2,1024,128]{2,1,0:T(8,128)S(1)} %get-tuple-element.37.here, f32[448,128]{1,0:T(8,128)} %copy-done.4, f32[448,128]{1,0:T(8,128)} %copy-done.5, f32[1024,128]{1,0:T(8,128)S(1)} %collective-permute-done.4.near_1, ...), custom_call_target="tpu_custom_call" | custom-call | flops 10000000000 | bytes 1048576 | tf_op jit(solution)/shard_map/final_rows/pallas_call | solution.py:427
  55.4 2.8 %all-to-all-done.totals = f32[8,1,128]{2,1,0:T(1,128)S(1)} async-done(((f32[8,1,128]{2,1,0:T(1,128)}), f32[8,1,128]{2,1,0:T(1,128)S(1)}, u32[]{:S(2)}, u32[]{:S(2)}) %all-to-all-start) | async-done | bytes 4128 | tf_op jit(solution)/shard_map/all_to_all | solution.py:498
  58.3 0.7 %attend_rows.1 = bf16[3,2,1024]{2,1,0:T(2,128)(2,1)} custom-call(f32[8,1,128]{2,1,0:T(1,128)S(1)} %all-to-all-done.totals, f32[8,1024]{1,0:T(8,128)S(1)} %get-tuple-element.35.raw, f32[8,1024]{1,0:T(8,128)S(1)} %get-tuple-element.36.gated, f32[8,128]{1,0:T(8,128)S(1)} %get-tuple-element.42._), custom_call_target="tpu_custom_call" | custom-call | tf_op jit(solution)/shard_map/attend_rows/pallas_call | solution.py:461
  (15 shorter events, 0.0 us)
Async XLA Ops:
  0.6 18.0 %copy-start.3 = (s32[128]{0:T(128)S(1)}, s32[128]{0:T(128)}, u32[]{:S(2)}) copy-start(s32[128]{0:T(128)} %shard_ref.5) | copy-start | bytes 1540
  0.6 18.0 %copy-start = (bf16[3,2,4,1024]{3,2,1,0:T(4,128)(2,1)S(1)}, bf16[3,2,4,1024]{3,2,1,0:T(4,128)(2,1)}, u32[]{:S(2)}) copy-start(bf16[3,2,4,1024]{3,2,1,0:T(4,128)(2,1)} %projected.3) | copy-start | bytes 147460
  0.7 18.0 %copy-start.2 = (s32[128]{0:T(128)S(1)}, s32[128]{0:T(128)}, u32[]{:S(2)}) copy-start(s32[128]{0:T(128)} %slot_ref.1) | copy-start | bytes 1540
  0.7 18.0 %copy-start.1 = (f32[1024]{0:T(1024)S(1)}, f32[1024]{0:T(1024)}, u32[]{:S(2)}) copy-start(f32[1024]{0:T(1024)} %param.11) | copy-start | bytes 12292
  0.7 17.9 %copy-start.6 = (f32[8]{0:T(128)S(1)}, f32[8]{0:T(128)}, u32[]{:S(2)}) copy-start(f32[8]{0:T(128)} %param.10) | copy-start | bytes 100
  2.4 23.8 %collective-permute-start = (f32[1088,128]{1,0:T(8,128)S(1)}, f32[1088,128]{1,0:T(8,128)S(1)}, u32[]{:S(2)}, u32[]{:S(2)}) collective-permute-start(f32[1088,128]{1,0:T(8,128)S(1)} %get-tuple-element.23), channel_id=1, source_target_pairs={{0,8},{8,0},{9,17},{17,9},{2,10},{10,2},{11,19},{19,11},{4,12},{12... | collective-permute-start | bytes 1671176 | tf_op jit(solution)/shard_map/ppermute | solution.py:31
  16.6 10.6 %collective-permute-start.1 = (f32[1088,128]{1,0:T(8,128)S(1)}, f32[1088,128]{1,0:T(8,128)S(1)}, u32[]{:S(2)}, u32[]{:S(2)}) collective-permute-start(f32[1088,128]{1,0:T(8,128)S(1)} %get-tuple-element.24._), channel_id=1, source_target_pairs={{8,16},{16,8},{17,25},{25,17},{10,18},{18,10},{19,27},{27,19},{12,... | collective-permute-start | bytes 1671176 | tf_op jit(solution)/shard_map/ppermute | solution.py:31
  20.9 19.6 %collective-permute-start.4 = (f32[1024,128]{1,0:T(8,128)S(1)}, f32[1024,128]{1,0:T(8,128)S(1)}, u32[]{:S(2)}, u32[]{:S(2)}) collective-permute-start(f32[1024,128]{1,0:T(8,128)S(1)} %get-tuple-element.28), channel_id=1, source_target_pairs={{8,16},{16,8},{17,25},{25,17},{10,18},{18,10},{19,27},{27,19},{12,... | collective-permute-start | bytes 1572872 | tf_op jit(solution)/shard_map/ppermute | solution.py:31
  24.3 18.8 %collective-permute-start.5 = (f32[1024,128]{1,0:T(8,128)S(1)}, f32[1024,128]{1,0:T(8,128)S(1)}, u32[]{:S(2)}, u32[]{:S(2)}) collective-permute-start(f32[1024,128]{1,0:T(8,128)S(1)} %get-tuple-element.29), channel_id=1, source_target_pairs={{0,8},{8,0},{9,17},{17,9},{2,10},{10,2},{11,19},{19,11},{4,12},{12... | collective-permute-start | bytes 1572872 | tf_op jit(solution)/shard_map/ppermute | solution.py:31
  28.2 17.9 %collective-permute-start.2 = (f32[448,128]{1,0:T(8,128)S(1)}, f32[448,128]{1,0:T(8,128)S(1)}, u32[]{:S(2)}, u32[]{:S(2)}) collective-permute-start(f32[448,128]{1,0:T(8,128)S(1)} %get-tuple-element.26), channel_id=1, source_target_pairs={{0,8},{8,0},{9,17},{17,9},{2,10},{10,2},{11,19},{19,11},{4,12},{12... | collective-permute-start | bytes 688136 | tf_op jit(solution)/shard_map/ppermute | solution.py:31
  35.2 10.9 %collective-permute-start.3 = (f32[448,128]{1,0:T(8,128)S(1)}, f32[448,128]{1,0:T(8,128)S(1)}, u32[]{:S(2)}, u32[]{:S(2)}) collective-permute-start(f32[448,128]{1,0:T(8,128)S(1)} %get-tuple-element.27), channel_id=1, source_target_pairs={{8,16},{16,8},{17,25},{25,17},{10,18},{18,10},{19,27},{27,19},{12,... | collective-permute-start | bytes 688136 | tf_op jit(solution)/shard_map/ppermute | solution.py:31
  37.2 16.6 %collective-permute-start.6 = (f32[640,128]{1,0:T(8,128)}, f32[640,128]{1,0:T(8,128)}, u32[]{:S(2)}, u32[]{:S(2)}) collective-permute-start(f32[640,128]{1,0:T(8,128)} %get-tuple-element.38), channel_id=1, source_target_pairs={{8,16},{16,8},{17,25},{25,17},{10,18},{18,10},{19,27},{27,19},{12,... | collective-permute-start | bytes 983048 | tf_op jit(solution)/shard_map/ppermute | solution.py:31
  40.6 13.2 %collective-permute-start.7 = (f32[640,128]{1,0:T(8,128)}, f32[640,128]{1,0:T(8,128)}, u32[]{:S(2)}, u32[]{:S(2)}) collective-permute-start(f32[640,128]{1,0:T(8,128)} %get-tuple-element.39), channel_id=1, source_target_pairs={{0,8},{8,0},{9,17},{17,9},{2,10},{10,2},{11,19},{19,11},{4,12},{12... | collective-permute-start | bytes 983048 | tf_op jit(solution)/shard_map/ppermute | solution.py:31
  46.1 1.6 %copy-start.4 = (f32[448,128]{1,0:T(8,128)}, f32[448,128]{1,0:T(8,128)S(1)}, u32[]{:S(2)}) copy-start(f32[448,128]{1,0:T(8,128)S(1)} %collective-permute-done.2.lead_0) | copy-start | bytes 688132
  46.1 1.7 %copy-start.5 = (f32[448,128]{1,0:T(8,128)}, f32[448,128]{1,0:T(8,128)S(1)}, u32[]{:S(2)}) copy-start(f32[448,128]{1,0:T(8,128)S(1)} %collective-permute-done.3.lead_1) | copy-start | bytes 688132
  47.8 10.5 %all-to-all-start = ((f32[8,1,128]{2,1,0:T(1,128)}), f32[8,1,128]{2,1,0:T(1,128)S(1)}, u32[]{:S(2)}, u32[]{:S(2)}) async-start(f32[8,1,128]{2,1,0:T(1,128)} %get-tuple-element.34), calls=%async_computation | async-start | bytes 8192 | tf_op jit(solution)/shard_map/all_to_all | solution.py:498
